TPU v7x, 512 devices: a whole 4x4x16 slice. The times are simulated.
512 devices in a mesh: pair: 16 (over z_hi, x, core), aux: 32 (over z_lo, y).
Axes of the slice: x: 4, y: 4, z: 16 (z_hi: 2, z_lo: 8; z = z_hi * 8 + z_lo), core: 2. Of those that a mesh axis runs over, the one named last changes fastest.
Arguments:
- amplitudes: bfloat16 [16, 2048, 2048], P('pair', None, 'aux'), may hold values from -0.125 to 0.125
- fitting: bfloat16 [6144, 4, 2048], P('aux', None, 'pair'), may hold values from -6 to 6
- coefficients: bfloat16 [2048, 2048], P('pair'), may hold values from -0.125 to 0.125
- pair_list: int32 [16, 2], P('pair'), may hold values from 0 to 3, as said below
Outputs:
- density_ao: bfloat16 [6144, 4, 2048], P('aux', None, 'pair')
Inputs may be any that keep to these rules, and one draw needn't show every extreme that they name: `pair_list`: column 0 names every internal of the window in exactly 4 rows; column 1 names any internal of the window.
All inputs are finite; a program needn't handle non-finite values.
Results may differ from a plain program's by a relative error of at most 0.015.
Values may be sent and summed in bfloat16 or wider, within the bound.
No kernel may reach another device: no remote copies, remote signals or barrier semaphores. Data moves between devices by JAX's collectives and lax.ppermute only.
A program may use at most 64 MiB of HBM per device.

v0:
```python
import jax
import jax.numpy as jnp
from jax import lax
from jax.sharding import PartitionSpec as P


def on_device(amplitudes, fitting, coefficients, pair_list):
    whole_fit = lax.all_gather(fitting, "pair", axis=2, tiled=True)
    occ_count = whole_fit.shape[1]
    lanes = jnp.arange(occ_count, dtype=jnp.int32)
    second_onehot = (pair_list[:, 1:2] == lanes[None, :]).astype(jnp.bfloat16)
    first_onehot = (pair_list[:, 0:1] == lanes[None, :]).astype(jnp.float32)
    selected = jnp.einsum(
        "pj,qjb->pqb", second_onehot, whole_fit, preferred_element_type=jnp.float32
    ).astype(jnp.bfloat16)
    contrib = jnp.einsum(
        "pqb,pab->pqa",
        selected,
        lax.all_gather(amplitudes, "aux", axis=2, tiled=True),
        preferred_element_type=jnp.float32,
    )
    partial_value = jnp.einsum(
        "pi,pqa->qia", first_onehot, contrib, precision=lax.Precision.HIGHEST
    ).astype(jnp.bfloat16)
    density_mo = lax.psum(partial_value, "pair").astype(jnp.float32).astype(jnp.bfloat16)
    result = lax.dot_general(
        density_mo, coefficients, (((2,), (1,)), ((), ())), preferred_element_type=jnp.float32
    )
    return result.astype(jnp.bfloat16)


def solution(mesh):
    in_specs = (P("pair", None, "aux"), P("aux", None, "pair"), P("pair", None), P("pair", None))
    out_specs = P("aux", None, "pair")
    return jax.shard_map(
        on_device, mesh=mesh, in_specs=in_specs, out_specs=out_specs, check_vma=False
    )
```

profile of v0, /device:TPU:1, one launch (start us, length us, event | category | flops | bytes accessed | tf_op | source)
XLA Modules:
  0.0 686.9 jit_solution(10143305882303904690)
XLA Ops:
  6.5 0.0 copy-start
  6.5 0.0 all-gather.3.cloned.1.call-start
  6.5 0.7 all-gather.3.cloned.1.call-update
  7.3 0.0 all-gather.5.cloned.1.call-start
  7.3 0.7 all-gather.5.cloned.1.call-update
  8.0 0.0 all-reduce.2.cloned.1.call-start
  8.1 1.3 fusion.7
  9.4 0.7 compare_convert_fusion
  10.1 136.7 %all-gather.3.cloned.1.call-done = bf16[192,4,2048]{2,1,0:T(4,128)(2,1)} async-done(((bf16[192,4,128]{2,1,0:T(4,128)(2,1)}), bf16[192,4,2048]{2,1,0:T(4,128)(2,1)}) %all-gather.3.cloned.1.call-update) | async-done | bytes 3145744 | tf_op jit(solution)/shard_map/all_gather | solution.py:8
  146.8 4.3 fusion.4
  151.1 209.3 %all-gather.5.cloned.1.call-done = bf16[1,2048,2048]{1,2,0:T(8,128)(2,1)} async-done(((bf16[1,2048,64]{1,2,0:T(8,128)(2,1)}), bf16[1,2048,2048]{1,2,0:T(8,128)(2,1)}) %all-gather.5.cloned.1.call-update) | async-done | bytes 8388624 | tf_op jit(solution)/shard_map/all_gather | solution.py:19
  360.4 5.5 fusion
  365.9 2.5 fusion.2
  368.4 0.0 all-reduce.2.cloned.1.call-update
  368.4 308.3 %all-reduce.2.cloned.1.call-done = bf16[192,4,2048]{2,0,1:T(8,128)(2,1)} async-done(((bf16[192,4,2048]{2,0,1:T(8,128)(2,1)}), bf16[192,4,2048]{2,0,1:T(8,128)(2,1)}) %all-reduce.2.cloned.1.call-update) | async-done | bytes 3145744 | tf_op jit(solution)/shard_map/psum | solution.py:25
  676.7 0.0 copy-done
  676.7 2.9 convolution_convert_fusion
  679.5 0.8 copy.5
Async XLA Ops:
  6.5 670.1 %copy-start = (bf16[128,2048]{1,0:T(8,128)(2,1)S(1)}, bf16[128,2048]{1,0:T(8,128)(2,1)}, u32[]{:S(2)}) copy-start(bf16[128,2048]{1,0:T(8,128)(2,1)} %param.6) | copy-start | bytes 1572868
  6.5 140.2 %all-gather.3.cloned.1.call-start = ((), (), s32[]{:S(2)}) async-start(), calls=%async_computation | async-start | bytes 3342336 | tf_op jit(solution)/shard_map/all_gather | solution.py:8
  7.3 353.1 %all-gather.5.cloned.1.call-start = ((), (), s32[]{:S(2)}) async-start(), calls=%async_computation.1 | async-start | bytes 8650752 | tf_op jit(solution)/shard_map/all_gather | solution.py:19
  8.0 668.6 %all-reduce.2.cloned.1.call-start = ((), (), s32[]{:S(2)}) async-start(), calls=%async_computation.2 | async-start | bytes 6291456 | tf_op jit(solution)/shard_map/psum | solution.py:25
Sparse Core Ops, SparseCore 0:
  10.5 136.2 all-gather.2
  148.8 211.4 all-gather.4
  368.5 308.0 all-reduce.1
where the time goes:
time: 696 us; the launch traced here: 687 us
  waiting for transfers between devices  656 us (94%)
  between operations  13.1 us (2%)
  matrix products  12.7 us (2%)
    psum x1, waiting for transfers between devices, on_device(): lax.psum(partial_value, 'pair').astype(jnp.float32).astype(jnp.bfloat16)  308 us
    all_gather x1, waiting for transfers between devices, on_device(): lax.all_gather(amplitudes, 'aux', axis=2, tiled=True)  209 us
    all_gather x1, waiting for transfers between devices, on_device(): whole_fit = lax.all_gather(fitting, 'pair', axis=2, tiled=True)  137 us
  transfers between devices with their start and end apart: 3, of which 3 were waited for; matrix products, arithmetic and copies ran while one was open for 1% of the time, Pallas kernels for 0%

commit v1 on v0

v1 whole, which is shorter than its diff:
```python
import jax
import jax.numpy as jnp
from jax import lax
from jax.experimental import pallas as pl
from jax.experimental.pallas import tpu as pltpu
from jax.sharding import Mesh, PartitionSpec as P

H, X, C, L, Y = 2, 4, 2, 8, 4
AXES = ("h", "x", "c", "l", "y")
OCC = 4


def flat(h, x, c, l, y):
    return (((h * X + x) * C + c) * L + l) * Y + y


def coords():
    for h in range(H):
        for x in range(X):
            for c in range(C):
                for l in range(L):
                    for y in range(Y):
                        yield h, x, c, l, y


def weight_perm(k):
    return [
        (flat(h, x, c, l, y), flat(l // X, l % X, c, (h ^ k) * X + x, y))
        for h, x, c, l, y in coords()
    ]


def result_perm(k):
    return [
        (flat(h, x, c, l, y), flat(l // X, l % X, c, 2 * x + (h ^ k), y))
        for h, x, c, l, y in coords()
    ]


def shift(n, k):
    return [(i, (i + k) % n) for i in range(n)]


def contract_kernel(first_ref, second_ref, w_ref, b_ref, out_ref, acc_ref, s_ref):
    slots, rows, cols = w_ref.shape[1], w_ref.shape[2], w_ref.shape[3]

    @pl.when(pl.program_id(0) == 0)
    def _():
        acc_ref[...] = jnp.zeros_like(acc_ref)

        def add(slot, _):
            first, second = first_ref[slot], second_ref[slot]
            at_col = pl.multiple_of(first * cols, cols)
            for z in range(Y):
                half, part = z // 2, z % 2
                at_row = pl.multiple_of((half * OCC + second) * (2 * rows) + part * rows, rows)
                here = (pl.ds(at_row, rows), pl.ds(at_col, cols))
                acc_ref[here] += w_ref[z, slot].astype(jnp.float32)
            return 0

        lax.fori_loop(0, slots, add, 0)
        s_ref[...] = acc_ref[...].astype(jnp.bfloat16)

    depth = b_ref.shape[2]
    total = jnp.dot(b_ref[0], s_ref[:depth], preferred_element_type=jnp.float32)
    total += jnp.dot(b_ref[1], s_ref[depth:], preferred_element_type=jnp.float32)
    out_ref[...] = total.astype(jnp.bfloat16)


def contract(first, second, w, b, steps=4):
    _, q, depth = b.shape
    cols = w.shape[3]
    block = q // steps
    return pl.pallas_call(
        contract_kernel,
        grid_spec=pltpu.PrefetchScalarGridSpec(
            num_scalar_prefetch=2,
            grid=(steps,),
            in_specs=[
                pl.BlockSpec(w.shape, lambda s, *_: (0, 0, 0, 0)),
                pl.BlockSpec((2, block, depth), lambda s, *_: (0, s, 0)),
            ],
            out_specs=pl.BlockSpec((block, OCC * cols), lambda s, *_: (s, 0)),
            scratch_shapes=[
                pltpu.VMEM((2 * depth, OCC * cols), jnp.float32),
                pltpu.VMEM((2 * depth, OCC * cols), jnp.bfloat16),
            ],
        ),
        out_shape=jax.ShapeDtypeStruct((q, OCC * cols), jnp.bfloat16),
        compiler_params=pltpu.CompilerParams(vmem_limit_bytes=32 * 1024 * 1024),
        cost_estimate=pl.CostEstimate(
            flops=2 * q * 2 * depth * OCC * cols, bytes_accessed=6 * 2**20, transcendentals=0
        ),
    )(first, second, w, b)


def on_device(amplitudes, fitting, coefficients, pair_list):
    x, l, y = lax.axis_index("x"), lax.axis_index("l"), lax.axis_index("y")
    f32, bf16 = jnp.float32, jnp.bfloat16

    q_own, occ, b_own = fitting.shape
    b_all = lax.all_gather(fitting.reshape(q_own, occ * b_own), "l", axis=0, tiled=True)
    b_all = lax.all_gather(b_all, "c", axis=0)
    pairs = lax.all_gather(pair_list, ("h", "x", "c"), axis=0, tiled=True)

    t_own = amplitudes[0].T
    t_all = jnp.concatenate(
        [t_own] + [lax.ppermute(t_own, "x", shift(X, k)) for k in range(1, X)], axis=0
    )

    n_mu = coefficients.shape[0]
    c_near = lax.all_gather(coefficients, "c", axis=0, tiled=True)
    part = n_mu // Y
    piece = lax.dynamic_slice_in_dim(coefficients, y * part, part, 0)
    c_far = lax.all_gather(
        lax.ppermute(piece, "h", shift(H, 1)), ("c", "y"), axis=0, tiled=True
    )

    received = []
    for k, c_part in ((0, c_near), (1, c_far)):
        w = jnp.einsum(
            "na,cma->cnm", t_all, c_part.reshape(C, n_mu, -1), preferred_element_type=f32
        ).astype(bf16)
        received.append(lax.ppermute(w, AXES, weight_perm(k)))
    w = jnp.concatenate(received, axis=1)
    w = lax.all_to_all(w, "c", split_axis=0, concat_axis=0, tiled=True)
    pieces = [w] + [lax.ppermute(w, "y", shift(Y, k)) for k in range(1, Y)]
    w_all = jnp.zeros((Y,) + w.shape, bf16)
    for k, piece in enumerate(pieces):
        w_all = lax.dynamic_update_slice_in_dim(w_all, piece[None], (y - k) % Y, 0)
    rows = t_own.shape[0]
    w_all = w_all.reshape(Y, C * H * X, rows, n_mu)

    slot = jnp.arange(C * H * X, dtype=jnp.int32)
    slot_c, slot_k, slot_x = slot // (H * X), (slot // X) % H, slot % X
    slot_pair = (((l // X) ^ slot_k) * X + (l % X - slot_x) % X) * C + slot_c
    slot_info = jnp.take(pairs, slot_pair, axis=0)

    partial = contract(slot_info[:, 0], slot_info[:, 1], w_all, b_all)

    h = lax.axis_index("h")
    cols = partial.shape[1]
    partial = partial.reshape(X, 2 * q_own, cols)
    partial = lax.all_to_all(partial, "x", split_axis=0, concat_axis=0, tiled=True)
    summed = jnp.sum(partial.astype(f32), axis=0).astype(bf16)
    total = jnp.zeros((q_own, cols), f32)
    for k in range(H):
        piece = lax.dynamic_slice_in_dim(summed, (h ^ k) * q_own, q_own, 0)
        total += lax.ppermute(piece, AXES, result_perm(k)).astype(f32)
    return total.astype(bf16).reshape(q_own, occ, n_mu)


def solution(mesh):
    fine = Mesh(mesh.devices.reshape(H, X, C, L, Y), AXES)
    pair, aux = ("h", "x", "c"), ("l", "y")
    in_specs = (P(pair, None, aux), P(aux, None, pair), P(pair, None), P(pair, None))
    out_specs = P(aux, None, pair)
    return jax.shard_map(
        on_device, mesh=fine, in_specs=in_specs, out_specs=out_specs, check_vma=False
    )
```

time: 696 us -> 272 us (0.39)
  the two profiles are of different devices: /device:TPU:1 before, /device:TPU:62 now
where the time goes in v1:
time: 272 us; the launch traced here: 271 us
  waiting for transfers between devices  139 us (51%)
  starting transfers between devices  66.5 us (24%)
  blocking collectives  36.6 us (13%)
  between operations  13.5 us (5%)
  local copies, waits for them, and re-layouts  6.93 us (3%)
  Pallas kernels  4.67 us (2%)
  matrix products  3.58 us (1%)
    all_gather x1, waiting for transfers between devices, on_device(): lax.all_gather(fitting.reshape(q_own, occ * b_own), 'l', axis=0, tiled=True)  38.6 us
    all_gather x1, blocking collectives, on_device(): pairs = lax.all_gather(pair_list, ('h', 'x', 'c'), axis=0, tiled=True)  32.6 us
    ppermute x2, waiting for transfers between devices, on_device(): total += lax.ppermute(piece, AXES, result_perm(k)).astype(f32)  30.8 us
    all_to_all x1, waiting for transfers between devices, on_device(): lax.all_to_all(partial, 'x', split_axis=0, concat_axis=0, tiled=True)  18.8 us
    ppermute x2, starting transfers between devices, on_device(): total += lax.ppermute(piece, AXES, result_perm(k)).astype(f32)  16.4 us
    ppermute x1, waiting for transfers between devices, on_device(): lax.ppermute(piece, 'h', shift(H, 1))  15 us
    ppermute x1, starting transfers between devices, on_device(): lax.ppermute(piece, 'h', shift(H, 1))  14.8 us
    ppermute x2, waiting for transfers between devices, on_device(): received.append(lax.ppermute(w, AXES, weight_perm(k)))  14.7 us
  transfers between devices with their start and end apart: 16, of which 9 were waited for; matrix products, arithmetic and copies ran while one was open for 2% of the time, Pallas kernels for 0%

profile of v1, /device:TPU:62, one launch (start us, length us, event | category | flops | bytes accessed | tf_op | source)
XLA Modules:
  0.0 271.2 jit_solution(4066820811234222855)
XLA Ops:
  6.5 0.0 copy-start.3
  6.5 0.0 copy-start.2
  6.5 0.0 all-gather.11.cloned.1.call-start
  6.5 1.7 copy.18
  8.2 0.0 all-gather.11.cloned.1.call-update
  8.2 0.0 all-gather.7.cloned.1.call-start
  8.3 0.7 all-gather.7.cloned.1.call-update
  9.0 0.0 all-gather.9.cloned.1.call-start
  9.0 0.9 constant_dynamic-slice_fusion.2
  10.0 14.8 %collective-permute-start.4 = (bf16[32,2048]{1,0:T(8,128)(2,1)S(1)}, bf16[32,2048]{1,0:T(8,128)(2,1)S(1)}, u32[]{:S(2)}, u32[]{:S(2)}) collective-permute-start(bf16[32,2048]{1,0:T(8,128)(2,1)S(1)} %constant_dynamic-slice_fusion.2), channel_id=1, source_target_pairs={{0,256},{256,0},{1,257},{257,1},{2,258},{258,2},{3,259},{259,3},{4... | collective-permute-start | bytes 393224 | tf_op jit(solution)/shard_map/ppermute | solution.py:116
  24.8 15.0 %collective-permute-done.4 = bf16[32,2048]{1,0:T(8,128)(2,1)S(1)} collective-permute-done((bf16[32,2048]{1,0:T(8,128)(2,1)S(1)}, bf16[32,2048]{1,0:T(8,128)(2,1)S(1)}, u32[]{:S(2)}, u32[]{:S(2)}) %collective-permute-start.4) | collective-permute-done | bytes 131104 | tf_op jit(solution)/shard_map/ppermute | solution.py:116
  39.8 0.0 copy-start.1
  39.8 0.7 copy-done.1
  40.4 0.0 all-gather.9.cloned.1.call-update
  40.4 0.0 all-gather.13.cloned.1.call-start
  40.5 38.6 %all-gather.11.cloned.1.call-done = bf16[1536,512]{1,0:T(8,128)(2,1)} async-done(((bf16[192,512]{1,0:T(8,128)(2,1)}), bf16[1536,512]{1,0:T(8,128)(2,1)}) %all-gather.11.cloned.1.call-update) | async-done | bytes 1572880 | tf_op jit(solution)/shard_map/all_gather | solution.py:102
  79.0 0.0 all-gather.13.cloned.1.call-update
  79.1 0.0 copy-done.3
  79.1 2.2 collective-permute-start
  81.3 4.4 %collective-permute-start.1 = (bf16[64,2048]{1,0:T(8,128)(2,1)S(1)}, bf16[64,2048]{1,0:T(8,128)(2,1)S(1)}, u32[]{:S(2)}, u32[]{:S(2)}) collective-permute-start(bf16[64,2048]{1,0:T(8,128)(2,1)S(1)} %bitcast.43), channel_id=1, source_target_pairs={{0,128},{64,192},{128,0},{192,64},{1,129},{65,193},{129,1},{193,65... | collective-permute-start | bytes 786440 | tf_op jit(solution)/shard_map/ppermute | solution.py:108
  85.8 2.6 collective-permute-start.2
  88.4 0.0 copy-done.2
  88.4 32.6 %all-gather.1 = s32[16,1,2]{2,1,0:T(1,128)S(1)} all-gather(s32[1,1,2]{2,1,0:T(1,128)S(1)} %bitcast.39), channel_id=1, replica_groups=mesh['h'=2,'x'=4,'c'=2,'l'=8,'y'=4] {'h','x','c'}, dimensions={0}, use_global_device_ids=true | all-gather | bytes 136 | tf_op jit(solution)/shard_map/all_gather | solution.py:104
  121.1 0.6 gather_fusion
  121.7 0.0 collective-permute-done
  121.7 0.0 collective-permute-done.1
  121.7 0.0 collective-permute-done.2
  121.7 0.0 all-gather.7.cloned.1.call-done
  121.7 1.8 fusion
  123.5 1.9 collective-permute-start.3
  125.5 8.2 %all-gather.9.cloned.1.call-done = bf16[256,2048]{1,0:T(8,128)(2,1)} async-done(((bf16[32,2048]{1,0:T(8,128)(2,1)}), bf16[256,2048]{1,0:T(8,128)(2,1)}) %all-gather.9.cloned.1.call-update) | async-done | bytes 1048592 | tf_op jit(solution)/shard_map/all_gather | solution.py:115
  133.7 1.8 fusion.1
  135.5 10.5 %collective-permute-start.5 = (bf16[2,256,128]{2,1,0:T(8,128)(2,1)S(1)}, bf16[2,256,128]{2,1,0:T(8,128)(2,1)S(1)}, u32[]{:S(2)}, u32[]{:S(2)}) collective-permute-start(bf16[2,256,128]{2,1,0:T(8,128)(2,1)S(1)} %fusion.1), channel_id=1, source_target_pairs={{0,16},{1,17},{2,18},{3,19},{4,80},{5,81},{6,82},{7,83},{8,144},{9... | collective-permute-start | bytes 393224 | tf_op jit(solution)/shard_map/ppermute | solution.py:124
  146.0 0.1 broadcast_select_fusion
  146.0 0.0 collective-permute-done.3
  146.1 14.7 %collective-permute-done.5 = bf16[2,256,128]{2,1,0:T(8,128)(2,1)S(1)} collective-permute-done((bf16[2,256,128]{2,1,0:T(8,128)(2,1)S(1)}, bf16[2,256,128]{2,1,0:T(8,128)(2,1)S(1)}, u32[]{:S(2)}, u32[]{:S(2)}) %collective-permute-start.5) | collective-permute-done | bytes 131104 | tf_op jit(solution)/shard_map/ppermute | solution.py:124
  160.8 3.9 %all_to_all.10 = bf16[2,512,128]{2,1,0:T(8,128)(2,1)S(1)} all-to-all(bf16[2,512,128]{2,1,0:T(8,128)(2,1)S(1)} %pad_maximum_fusion), channel_id=1, replica_groups=mesh['h'=2,'x'=4,'c'=2,'l'=8,'y'=4] {'c'}, dimensions={0} | all-to-all | bytes 524288 | tf_op jit(solution)/shard_map/all_to_all | solution.py:126
  164.7 4.1 %collective-permute-start.6 = (bf16[2,512,128]{2,1,0:T(8,128)(2,1)S(1)}, bf16[2,512,128]{2,1,0:T(8,128)(2,1)S(1)}, u32[]{:S(2)}, u32[]{:S(2)}) collective-permute-start(bf16[2,512,128]{2,1,0:T(8,128)(2,1)S(1)} %all_to_all.10), channel_id=1, source_target_pairs={{0,1},{1,2},{2,3},{3,0},{4,5},{5,6},{6,7},{7,4},{8,9},{9,10},{10,1... | collective-permute-start | bytes 786440 | tf_op jit(solution)/shard_map/ppermute | solution.py:127
  168.9 0.2 slice_reduce_fusion
  169.1 2.9 %collective-permute-start.7 = (bf16[2,512,128]{2,1,0:T(8,128)(2,1)S(1)}, bf16[2,512,128]{2,1,0:T(8,128)(2,1)S(1)}, u32[]{:S(2)}, u32[]{:S(2)}) collective-permute-start(bf16[2,512,128]{2,1,0:T(8,128)(2,1)S(1)} %all_to_all.10), channel_id=1, source_target_pairs={{0,2},{1,3},{2,0},{3,1},{4,6},{5,7},{6,4},{7,5},{8,10},{9,11},{10,... | collective-permute-start | bytes 786440 | tf_op jit(solution)/shard_map/ppermute | solution.py:127
  172.0 1.9 collective-permute-start.8
  173.9 0.1 broadcast_in_dim.27
  174.1 6.3 %collective-permute-done.6 = bf16[2,512,128]{2,1,0:T(8,128)(2,1)S(1)} collective-permute-done((bf16[2,512,128]{2,1,0:T(8,128)(2,1)S(1)}, bf16[2,512,128]{2,1,0:T(8,128)(2,1)S(1)}, u32[]{:S(2)}, u32[]{:S(2)}) %collective-permute-start.6) | collective-permute-done | bytes 262176 | tf_op jit(solution)/shard_map/ppermute | solution.py:127
  180.4 1.3 collective-permute-done.7
  181.8 4.4 %collective-permute-done.8 = bf16[2,512,128]{2,1,0:T(8,128)(2,1)S(1)} collective-permute-done((bf16[2,512,128]{2,1,0:T(8,128)(2,1)S(1)}, bf16[2,512,128]{2,1,0:T(8,128)(2,1)S(1)}, u32[]{:S(2)}, u32[]{:S(2)}) %collective-permute-start.8) | collective-permute-done | bytes 262176 | tf_op jit(solution)/shard_map/ppermute | solution.py:127
  186.2 0.0 all-gather.13.cloned.1.call-done
  186.3 0.0 copy-start
  186.3 1.9 copy-done
  188.2 4.7 %shard_map.46 = bf16[1536,512]{1,0:T(8,128)(2,1)} custom-call(s32[16]{0:T(128)S(1)} %get-tuple-element.6.first_ref, s32[16]{0:T(128)S(1)} %get-tuple-element.5.second_ref, bf16[4,16,64,128]{3,2,1,0:T(8,128)(2,1)S(1)} %bitcast.34, bf16[2,1536,512]{2,1,0:T(8,128)(2,1)S(1)} %bitcast.35), custom_call_target="tpu_custom_call" | custom-call | flops 1610612736 | bytes 6291456 | tf_op jit(solution)/shard_map/pallas_call | solution.py:74
  192.8 4.5 %all-to-all-start.1 = ((bf16[4,384,512]{2,1,0:T(8,128)(2,1)}), bf16[4,384,512]{2,1,0:T(8,128)(2,1)S(1)}, u32[]{:S(2)}, u32[]{:S(2)}) async-start(bf16[4,384,512]{2,1,0:T(8,128)(2,1)} %bitcast.17), calls=%async_computation.1 | async-start | bytes 3145728 | tf_op jit(solution)/shard_map/all_to_all | solution.py:144
  197.3 18.8 %all-to-all-done.1 = bf16[4,384,512]{2,1,0:T(8,128)(2,1)S(1)} async-done(((bf16[4,384,512]{2,1,0:T(8,128)(2,1)}), bf16[4,384,512]{2,1,0:T(8,128)(2,1)S(1)}, u32[]{:S(2)}, u32[]{:S(2)}) %all-to-all-start.1) | async-done | bytes 1572896 | tf_op jit(solution)/shard_map/all_to_all | solution.py:144
  216.2 0.4 reduce_sum.12
  216.7 5.7 %collective-permute-start.10 = (bf16[192,512]{1,0:T(8,128)(2,1)S(1)}, bf16[192,512]{1,0:T(8,128)(2,1)S(1)}, u32[]{:S(2)}, u32[]{:S(2)}) collective-permute-start(bf16[192,512]{1,0:T(8,128)(2,1)S(1)} %get-tuple-element.8), channel_id=1, source_target_pairs={{0,4},{1,5},{2,6},{3,7},{4,68},{5,69},{6,70},{7,71},{8,132},{9,133... | collective-permute-start | bytes 589832 | tf_op jit(solution)/shard_map/ppermute | solution.py:149
  222.4 10.7 %collective-permute-start.9 = (bf16[192,512]{1,0:T(8,128)(2,1)S(1)}, bf16[192,512]{1,0:T(8,128)(2,1)S(1)}, u32[]{:S(2)}, u32[]{:S(2)}) collective-permute-start(bf16[192,512]{1,0:T(8,128)(2,1)S(1)} %get-tuple-element.7), channel_id=1, source_target_pairs={{0,0},{1,1},{2,2},{3,3},{4,64},{5,65},{6,66},{7,67},{8,128},{9,129... | collective-permute-start | bytes 589832 | tf_op jit(solution)/shard_map/ppermute | solution.py:149
  233.1 0.0 collective-permute-done.10
  233.1 30.8 %collective-permute-done.9 = bf16[192,512]{1,0:T(8,128)(2,1)S(1)} collective-permute-done((bf16[192,512]{1,0:T(8,128)(2,1)S(1)}, bf16[192,512]{1,0:T(8,128)(2,1)S(1)}, u32[]{:S(2)}, u32[]{:S(2)}) %collective-permute-start.9) | collective-permute-done | bytes 196640 | tf_op jit(solution)/shard_map/ppermute | solution.py:149
  263.9 0.1 add_convert_fusion
  263.9 0.7 reshape.194
  (9 shorter events, 0.2 us)
Async XLA Ops:
  6.5 72.5 %copy-start.3 = (bf16[1,2048,64]{1,2,0:T(8,128)(2,1)S(1)}, bf16[1,2048,64]{1,2,0:T(8,128)(2,1)}, u32[]{:S(2)}) copy-start(bf16[1,2048,64]{1,2,0:T(8,128)(2,1)} %param.4) | copy-start | bytes 786436
  6.5 81.9 %copy-start.2 = (s32[1,2]{1,0:T(1,128)S(1)}, s32[1,2]{1,0:T(1,128)}, u32[]{:S(2)}) copy-start(s32[1,2]{1,0:T(1,128)} %param.7) | copy-start | bytes 28
  6.5 72.5 %all-gather.11.cloned.1.call-start = ((), (), s32[]{:S(2)}) async-start(), calls=%async_computation.4 | async-start | bytes 1769472 | tf_op jit(solution)/shard_map/all_gather | solution.py:102
  8.2 113.5 %all-gather.7.cloned.1.call-start = ((), (), s32[]{:S(2)}) async-start(), calls=%async_computation.2 | async-start | bytes 1572864 | tf_op jit(solution)/shard_map/all_gather | solution.py:112
  9.0 124.7 %all-gather.9.cloned.1.call-start = ((), (), s32[]{:S(2)}) async-start(), calls=%async_computation.3 | async-start | bytes 1179648 | tf_op jit(solution)/shard_map/all_gather | solution.py:115
  10.0 29.8 %collective-permute-start.4 = (bf16[32,2048]{1,0:T(8,128)(2,1)S(1)}, bf16[32,2048]{1,0:T(8,128)(2,1)S(1)}, u32[]{:S(2)}, u32[]{:S(2)}) collective-permute-start(bf16[32,2048]{1,0:T(8,128)(2,1)S(1)} %constant_dynamic-slice_fusion.2), channel_id=1, source_target_pairs={{0,256},{256,0},{1,257},{257,1},{2,258},{258,2},{3,259},{259,3},{4... | collective-permute-start | bytes 393224 | tf_op jit(solution)/shard_map/ppermute | solution.py:116
  39.8 0.7 copy-start.1
  40.4 145.8 %all-gather.13.cloned.1.call-start = ((), (), s32[]{:S(2)}) async-start(), calls=%async_computation.5 | async-start | bytes 4718592 | tf_op jit(solution)/shard_map/all_gather | solution.py:103
  79.1 42.6 %collective-permute-start = (bf16[64,2048]{1,0:T(8,128)(2,1)S(1)}, bf16[64,2048]{1,0:T(8,128)(2,1)S(1)}, u32[]{:S(2)}, u32[]{:S(2)}) collective-permute-start(bf16[64,2048]{1,0:T(8,128)(2,1)S(1)} %bitcast.42), channel_id=1, source_target_pairs={{0,64},{64,128},{128,192},{192,0},{1,65},{65,129},{129,193},{193,1... | collective-permute-start | bytes 786440 | tf_op jit(solution)/shard_map/ppermute | solution.py:108
  81.3 40.4 %collective-permute-start.1 = (bf16[64,2048]{1,0:T(8,128)(2,1)S(1)}, bf16[64,2048]{1,0:T(8,128)(2,1)S(1)}, u32[]{:S(2)}, u32[]{:S(2)}) collective-permute-start(bf16[64,2048]{1,0:T(8,128)(2,1)S(1)} %bitcast.43), channel_id=1, source_target_pairs={{0,128},{64,192},{128,0},{192,64},{1,129},{65,193},{129,1},{193,65... | collective-permute-start | bytes 786440 | tf_op jit(solution)/shard_map/ppermute | solution.py:108
  85.8 35.9 %collective-permute-start.2 = (bf16[64,2048]{1,0:T(8,128)(2,1)S(1)}, bf16[64,2048]{1,0:T(8,128)(2,1)S(1)}, u32[]{:S(2)}, u32[]{:S(2)}) collective-permute-start(bf16[64,2048]{1,0:T(8,128)(2,1)S(1)} %bitcast.44), channel_id=1, source_target_pairs={{0,192},{64,0},{128,64},{192,128},{1,193},{65,1},{129,65},{193,129... | collective-permute-start | bytes 786440 | tf_op jit(solution)/shard_map/ppermute | solution.py:108
  123.5 22.5 %collective-permute-start.3 = (bf16[2,256,128]{2,1,0:T(8,128)(2,1)S(1)}, bf16[2,256,128]{2,1,0:T(8,128)(2,1)S(1)}, u32[]{:S(2)}, u32[]{:S(2)}) collective-permute-start(bf16[2,256,128]{2,1,0:T(8,128)(2,1)S(1)} %fusion), channel_id=1, source_target_pairs={{0,0},{1,1},{2,2},{3,3},{4,64},{5,65},{6,66},{7,67},{8,128},{9,129... | collective-permute-start | bytes 393224 | tf_op jit(solution)/shard_map/ppermute | solution.py:124
  135.5 25.3 %collective-permute-start.5 = (bf16[2,256,128]{2,1,0:T(8,128)(2,1)S(1)}, bf16[2,256,128]{2,1,0:T(8,128)(2,1)S(1)}, u32[]{:S(2)}, u32[]{:S(2)}) collective-permute-start(bf16[2,256,128]{2,1,0:T(8,128)(2,1)S(1)} %fusion.1), channel_id=1, source_target_pairs={{0,16},{1,17},{2,18},{3,19},{4,80},{5,81},{6,82},{7,83},{8,144},{9... | collective-permute-start | bytes 393224 | tf_op jit(solution)/shard_map/ppermute | solution.py:124
  164.7 15.7 %collective-permute-start.6 = (bf16[2,512,128]{2,1,0:T(8,128)(2,1)S(1)}, bf16[2,512,128]{2,1,0:T(8,128)(2,1)S(1)}, u32[]{:S(2)}, u32[]{:S(2)}) collective-permute-start(bf16[2,512,128]{2,1,0:T(8,128)(2,1)S(1)} %all_to_all.10), channel_id=1, source_target_pairs={{0,1},{1,2},{2,3},{3,0},{4,5},{5,6},{6,7},{7,4},{8,9},{9,10},{10,1... | collective-permute-start | bytes 786440 | tf_op jit(solution)/shard_map/ppermute | solution.py:127
  169.1 12.6 %collective-permute-start.7 = (bf16[2,512,128]{2,1,0:T(8,128)(2,1)S(1)}, bf16[2,512,128]{2,1,0:T(8,128)(2,1)S(1)}, u32[]{:S(2)}, u32[]{:S(2)}) collective-permute-start(bf16[2,512,128]{2,1,0:T(8,128)(2,1)S(1)} %all_to_all.10), channel_id=1, source_target_pairs={{0,2},{1,3},{2,0},{3,1},{4,6},{5,7},{6,4},{7,5},{8,10},{9,11},{10,... | collective-permute-start | bytes 786440 | tf_op jit(solution)/shard_map/ppermute | solution.py:127
  172.0 14.2 %collective-permute-start.8 = (bf16[2,512,128]{2,1,0:T(8,128)(2,1)S(1)}, bf16[2,512,128]{2,1,0:T(8,128)(2,1)S(1)}, u32[]{:S(2)}, u32[]{:S(2)}) collective-permute-start(bf16[2,512,128]{2,1,0:T(8,128)(2,1)S(1)} %all_to_all.10), channel_id=1, source_target_pairs={{0,3},{1,0},{2,1},{3,2},{4,7},{5,4},{6,5},{7,6},{8,11},{9,8},{10,9... | collective-permute-start | bytes 786440 | tf_op jit(solution)/shard_map/ppermute | solution.py:127
  186.3 1.9 copy-start
  192.8 23.3 %all-to-all-start.1 = ((bf16[4,384,512]{2,1,0:T(8,128)(2,1)}), bf16[4,384,512]{2,1,0:T(8,128)(2,1)S(1)}, u32[]{:S(2)}, u32[]{:S(2)}) async-start(bf16[4,384,512]{2,1,0:T(8,128)(2,1)} %bitcast.17), calls=%async_computation.1 | async-start | bytes 3145728 | tf_op jit(solution)/shard_map/all_to_all | solution.py:144
  216.7 16.5 %collective-permute-start.10 = (bf16[192,512]{1,0:T(8,128)(2,1)S(1)}, bf16[192,512]{1,0:T(8,128)(2,1)S(1)}, u32[]{:S(2)}, u32[]{:S(2)}) collective-permute-start(bf16[192,512]{1,0:T(8,128)(2,1)S(1)} %get-tuple-element.8), channel_id=1, source_target_pairs={{0,4},{1,5},{2,6},{3,7},{4,68},{5,69},{6,70},{7,71},{8,132},{9,133... | collective-permute-start | bytes 589832 | tf_op jit(solution)/shard_map/ppermute | solution.py:149
  222.4 41.5 %collective-permute-start.9 = (bf16[192,512]{1,0:T(8,128)(2,1)S(1)}, bf16[192,512]{1,0:T(8,128)(2,1)S(1)}, u32[]{:S(2)}, u32[]{:S(2)}) collective-permute-start(bf16[192,512]{1,0:T(8,128)(2,1)S(1)} %get-tuple-element.7), channel_id=1, source_target_pairs={{0,0},{1,1},{2,2},{3,3},{4,64},{5,65},{6,66},{7,67},{8,128},{9,129... | collective-permute-start | bytes 589832 | tf_op jit(solution)/shard_map/ppermute | solution.py:149
Sparse Core Ops, SparseCore 0:
  9.4 69.5 all-gather.10
  81.1 19.6 all-gather.6
  103.0 30.6 all-gather.8
  135.6 24.2 all-gather.12

commit v2 on v1

v2 whole, which is shorter than its diff:
```python
import jax
import jax.numpy as jnp
from jax import lax
from jax.experimental import pallas as pl
from jax.experimental.pallas import tpu as pltpu
from jax.sharding import Mesh, PartitionSpec as P

H, X, C, L, Y = 2, 4, 2, 8, 4
AXES = ("h", "x", "c", "l", "y")
OCC = 4


def flat(h, x, c, l, y):
    return (((h * X + x) * C + c) * L + l) * Y + y


def coords():
    for h in range(H):
        for x in range(X):
            for c in range(C):
                for l in range(L):
                    for y in range(Y):
                        yield h, x, c, l, y


def weight_perm(k):
    return [
        (flat(h, x, c, l, y), flat(l // X, l % X, c, (h ^ k) * X + x, y))
        for h, x, c, l, y in coords()
    ]


def result_perm(k):
    return [
        (flat(h, x, c, l, y), flat(l // X, l % X, c, 2 * x + (h ^ k), y))
        for h, x, c, l, y in coords()
    ]


def shift(n, k):
    return [(i, (i + k) % n) for i in range(n)]


def contract_kernel(first_ref, second_ref, where_ref, w_ref, near_ref, far_ref, out_ref, acc_ref, s_ref):
    slots, rows, cols = w_ref.shape[1], w_ref.shape[2], w_ref.shape[3]

    @pl.when(pl.program_id(0) == 0)
    def _():
        acc_ref[...] = jnp.zeros_like(acc_ref)

        def add(slot, _):
            first, second = first_ref[slot], second_ref[slot]
            at_col = pl.multiple_of(first * cols, cols)
            for z in range(Y):
                half, part = z // 2, z % 2
                at_row = pl.multiple_of((half * OCC + second) * (2 * rows) + part * rows, rows)
                here = (pl.ds(at_row, rows), pl.ds(at_col, cols))
                acc_ref[here] += w_ref[z, slot].astype(jnp.float32)
            return 0

        lax.fori_loop(0, slots, add, 0)
        s_ref[...] = acc_ref[...].astype(jnp.bfloat16)

    depth = near_ref.shape[1]
    at_near = pl.multiple_of(where_ref[1] * depth, depth)
    at_far = pl.multiple_of((1 - where_ref[1]) * depth, depth)
    f32 = jnp.float32
    total = jnp.dot(near_ref[...], s_ref[pl.ds(at_near, depth)], preferred_element_type=f32)
    total += jnp.dot(far_ref[...], s_ref[pl.ds(at_far, depth)], preferred_element_type=f32)
    out_ref[...] = total.astype(jnp.bfloat16)


def contract(first, second, where, w, near, far):
    q, depth = near.shape
    cols = w.shape[3]
    block = q // X

    def of_step(s, first, second, where):
        return (where[0] + s + 1) % X, 0

    return pl.pallas_call(
        contract_kernel,
        grid_spec=pltpu.PrefetchScalarGridSpec(
            num_scalar_prefetch=3,
            grid=(X,),
            in_specs=[
                pl.BlockSpec(w.shape, lambda s, *_: (0, 0, 0, 0)),
                pl.BlockSpec((block, depth), of_step),
                pl.BlockSpec((block, depth), of_step),
            ],
            out_specs=pl.BlockSpec((block, OCC * cols), lambda s, *_: (s, 0)),
            scratch_shapes=[
                pltpu.VMEM((2 * depth, OCC * cols), jnp.float32),
                pltpu.VMEM((2 * depth, OCC * cols), jnp.bfloat16),
            ],
        ),
        out_shape=jax.ShapeDtypeStruct((q, OCC * cols), jnp.bfloat16),
        compiler_params=pltpu.CompilerParams(vmem_limit_bytes=32 * 1024 * 1024),
        cost_estimate=pl.CostEstimate(
            flops=2 * q * 2 * depth * OCC * cols, bytes_accessed=6 * 2**20, transcendentals=0
        ),
    )(first, second, where, w, near, far)


def on_device(amplitudes, fitting, coefficients, pair_list):
    h, x, c = lax.axis_index("h"), lax.axis_index("x"), lax.axis_index("c")
    l, y = lax.axis_index("l"), lax.axis_index("y")
    f32, bf16 = jnp.float32, jnp.bfloat16

    def swap_core(v):
        return lax.ppermute(v, "c", shift(C, 1))

    q_own, occ, b_own = fitting.shape
    b_near = lax.all_gather(fitting.reshape(q_own, occ * b_own), "l", axis=0, tiled=True)

    n_mu, n_a = coefficients.shape
    part = n_mu // Y
    piece = lax.dynamic_slice_in_dim(coefficients, y * part, part, 0)
    piece = lax.ppermute(piece, "h", shift(H, 1))
    piece = jnp.broadcast_to(piece[None], (Y, part, n_a))
    c_far = lax.all_to_all(piece, "y", split_axis=0, concat_axis=0, tiled=True)
    c_far = c_far.reshape(n_mu, n_a)

    rows = amplitudes.shape[2]
    info = jnp.pad(pair_list.astype(bf16), ((0, rows - 1), (0, 126)))
    t_own = jnp.concatenate([amplitudes[0].T, info], axis=1)
    t_all = jnp.concatenate(
        [t_own] + [lax.ppermute(t_own, "x", shift(X, k)) for k in range(1, X)], axis=0
    )
    info = t_all.reshape(X, rows, -1)[:, 0, n_a:]
    info = jnp.broadcast_to(jnp.pad(info, ((0, 16 - X), (0, 0)))[None], (C, 16, n_mu))
    t_all = t_all[:, :n_a]

    received = []
    for k, c_part in ((0, coefficients), (1, c_far)):
        w = [
            lax.dot_general(t_all, m, (((1,), (1,)), ((), ())), preferred_element_type=f32)
            for m in (c_part, swap_core(c_part))
        ]
        w = jnp.concatenate([jnp.stack(w).astype(bf16), info], axis=1)
        received.append(lax.ppermute(w, AXES, weight_perm(k)))
    mine = jnp.stack([r[0] for r in received])
    w = jnp.stack([mine, swap_core(jnp.stack([r[1] for r in received]))])
    slots = C * H * X
    n_b = X * rows
    info = w[:, :, n_b : n_b + X, :2].reshape(slots, 2).astype(jnp.int32)
    w = w[:, :, :n_b].reshape(slots, rows, n_mu)
    w, b_near = lax.optimization_barrier((w, b_near))
    pieces = [w] + [lax.ppermute(w, "y", shift(Y, k)) for k in range(1, Y)]
    w_all = jnp.zeros((Y,) + w.shape, bf16)
    for k, piece in enumerate(pieces):
        w_all = lax.dynamic_update_slice_in_dim(w_all, piece[None], (y - k) % Y, 0)
    b_far = swap_core(b_near)

    where = jnp.stack([x, c]).astype(jnp.int32)
    partial = contract(info[:, 0], info[:, 1], where, w_all, b_near, b_far)
    cols = partial.shape[1]
    partial = partial.reshape(X, 2 * q_own, cols)
    summed = partial[X - 1].astype(f32)
    for k in range(1, X):
        summed += lax.ppermute(partial[k - 1], "x", shift(X, k)).astype(f32)
    summed = summed.astype(bf16)

    total = jnp.zeros((q_own, cols), f32)
    for k in range(H):
        piece = lax.dynamic_slice_in_dim(summed, (h ^ k) * q_own, q_own, 0)
        total += lax.ppermute(piece, AXES, result_perm(k)).astype(f32)
    return total.astype(bf16).reshape(q_own, occ, n_mu)


def solution(mesh):
    fine = Mesh(mesh.devices.reshape(H, X, C, L, Y), AXES)
    pair, aux = ("h", "x", "c"), ("l", "y")
    in_specs = (P(pair, None, aux), P(aux, None, pair), P(pair, None), P(pair, None))
    out_specs = P(aux, None, pair)
    return jax.shard_map(
        on_device, mesh=fine, in_specs=in_specs, out_specs=out_specs, check_vma=False
    )
```

time: 272 us -> 205 us (0.75)
  the two profiles are of different devices: /device:TPU:62 before, /device:TPU:136 now
where the time goes in v2:
time: 205 us; the launch traced here: 204 us
  starting transfers between devices  91.5 us (45%)
  waiting for transfers between devices  85.2 us (42%)
  between operations  13.9 us (7%)
  local copies, waits for them, and re-layouts  4.09 us (2%)
  Pallas kernels  3.65 us (2%)
  other arithmetic  3.12 us (2%)
  matrix products  2.78 us (1%)
    ppermute x2, waiting for transfers between devices, on_device(): total += lax.ppermute(piece, AXES, result_perm(k)).astype(f32)  31.8 us
    ppermute x3, starting transfers between devices, on_device(): summed += lax.ppermute(partial[k - 1], 'x', shift(X, k)).astype(f32)  28.3 us
    ppermute x1, waiting for transfers between devices, on_device(): piece = lax.ppermute(piece, 'h', shift(H, 1))  16.3 us
    ppermute x3, waiting for transfers between devices, on_device(): summed += lax.ppermute(partial[k - 1], 'x', shift(X, k)).astype(f32)  15 us
    ppermute x3, starting transfers between devices, on_device(): lax.ppermute(t_own, 'x', shift(X, k))  11.5 us
    ppermute x1, starting transfers between devices, on_device(): piece = lax.ppermute(piece, 'h', shift(H, 1))  10.9 us
    ppermute x3, starting transfers between devices, on_device(): pieces = [w] + [lax.ppermute(w, 'y', shift(Y, k)) for k in range(1, Y)]  10.3 us
    ppermute x3, waiting for transfers between devices, on_device(): pieces = [w] + [lax.ppermute(w, 'y', shift(Y, k)) for k in range(1, Y)]  9.15 us
  transfers between devices with their start and end apart: 20, of which 13 were waited for; matrix products, arithmetic and copies ran while one was open for 3% of the time, Pallas kernels for 0%

profile of v2, /device:TPU:136, one launch (start us, length us, event | category | flops | bytes accessed | tf_op | source)
XLA Modules:
  0.0 204.2 jit_solution(10054574788729251056)
XLA Ops:
  6.5 0.0 all-gather.2.cloned.1.call-start
  6.5 1.7 copy.14
  8.2 0.0 all-gather.2.cloned.1.call-update
  8.3 0.7 convert_element_type.39
  8.9 1.0 pad_maximum_fusion.1
  9.9 0.0 copy-start.1
  9.9 3.5 %collective-permute-start = (bf16[64,2176]{1,0:T(8,128)(2,1)S(1)}, bf16[64,2176]{1,0:T(8,128)(2,1)S(1)}, u32[]{:S(2)}, u32[]{:S(2)}) collective-permute-start(bf16[64,2176]{1,0:T(8,128)(2,1)S(1)} %pad_maximum_fusion.1), channel_id=1, source_target_pairs={{0,64},{64,128},{128,192},{192,0},{1,65},{65,129},{129,193},{193,1... | collective-permute-start | bytes 835592 | tf_op jit(solution)/shard_map/ppermute | solution.py:128
  13.4 4.6 %collective-permute-start.1 = (bf16[64,2176]{1,0:T(8,128)(2,1)S(1)}, bf16[64,2176]{1,0:T(8,128)(2,1)S(1)}, u32[]{:S(2)}, u32[]{:S(2)}) collective-permute-start(bf16[64,2176]{1,0:T(8,128)(2,1)S(1)} %pad_maximum_fusion.1), channel_id=1, source_target_pairs={{0,128},{64,192},{128,0},{192,64},{1,129},{65,193},{129,1},{193,65... | collective-permute-start | bytes 835592 | tf_op jit(solution)/shard_map/ppermute | solution.py:128
  18.1 3.3 %collective-permute-start.2 = (bf16[64,2176]{1,0:T(8,128)(2,1)S(1)}, bf16[64,2176]{1,0:T(8,128)(2,1)S(1)}, u32[]{:S(2)}, u32[]{:S(2)}) collective-permute-start(bf16[64,2176]{1,0:T(8,128)(2,1)S(1)} %pad_maximum_fusion.1), channel_id=1, source_target_pairs={{0,192},{64,0},{128,64},{192,128},{1,193},{65,1},{129,65},{193,129... | collective-permute-start | bytes 835592 | tf_op jit(solution)/shard_map/ppermute | solution.py:128
  21.4 0.0 copy-done.2
  21.5 10.9 %collective-permute-start.5 = (bf16[32,2048]{1,0:T(8,128)(2,1)S(1)}, bf16[32,2048]{1,0:T(8,128)(2,1)S(1)}, u32[]{:S(2)}, u32[]{:S(2)}) collective-permute-start(bf16[32,2048]{1,0:T(8,128)(2,1)S(1)} %constant_dynamic-slice_fusion.2), channel_id=1, source_target_pairs={{0,256},{256,0},{1,257},{257,1},{2,258},{258,2},{3,259},{259,3},{4... | collective-permute-start | bytes 393224 | tf_op jit(solution)/shard_map/ppermute | solution.py:119
  32.4 16.3 %collective-permute-done.5 = bf16[32,2048]{1,0:T(8,128)(2,1)S(1)} collective-permute-done((bf16[32,2048]{1,0:T(8,128)(2,1)S(1)}, bf16[32,2048]{1,0:T(8,128)(2,1)S(1)}, u32[]{:S(2)}, u32[]{:S(2)}) %collective-permute-start.5) | collective-permute-done | bytes 131104 | tf_op jit(solution)/shard_map/ppermute | solution.py:119
  48.7 0.9 broadcast_in_dim.28
  49.6 4.9 %all-to-all-start = ((bf16[4,32,2048]{2,1,0:T(8,128)(2,1)}), bf16[4,32,2048]{2,1,0:T(8,128)(2,1)S(1)}, u32[]{:S(2)}, u32[]{:S(2)}) async-start(bf16[4,32,2048]{2,1,0:T(8,128)(2,1)} %broadcast_in_dim.28), calls=%async_computation | async-start | bytes 1048576 | tf_op jit(solution)/shard_map/all_to_all | solution.py:121
  54.5 1.9 collective-permute-start.3
  56.4 0.0 collective-permute-done
  56.4 0.0 collective-permute-done.1
  56.4 0.0 collective-permute-done.2
  56.4 0.0 copy-done.1
  56.4 0.1 pad_maximum_fusion
  56.5 4.5 %all-to-all-done = bf16[4,32,2048]{2,1,0:T(8,128)(2,1)S(1)} async-done(((bf16[4,32,2048]{2,1,0:T(8,128)(2,1)}), bf16[4,32,2048]{2,1,0:T(8,128)(2,1)S(1)}, u32[]{:S(2)}, u32[]{:S(2)}) %all-to-all-start) | async-done | bytes 524320 | tf_op jit(solution)/shard_map/all_to_all | solution.py:121
  61.1 1.9 collective-permute-start.6
  63.0 0.4 fusion
  63.4 0.4 fusion.2
  63.9 0.0 collective-permute-done.3
  63.9 1.5 fusion.1
  65.4 0.0 collective-permute-done.6
  65.4 0.4 fusion.3
  65.9 1.9 collective-permute-start.4
  67.8 6.7 %collective-permute-start.7 = (bf16[2,272,128]{2,1,0:T(8,128)(2,1)S(1)}, bf16[2,272,128]{2,1,0:T(8,128)(2,1)S(1)}, u32[]{:S(2)}, u32[]{:S(2)}) collective-permute-start(bf16[2,272,128]{2,1,0:T(8,128)(2,1)S(1)} %get-tuple-element.21), channel_id=1, source_target_pairs={{0,16},{1,17},{2,18},{3,19},{4,80},{5,81},{6,82},{7,83},{8,144},{9... | collective-permute-start | bytes 417800 | tf_op jit(solution)/shard_map/ppermute | solution.py:141
  74.5 6.7 %collective-permute-done.4 = bf16[2,272,128]{2,1,0:T(8,128)(2,1)S(1)} collective-permute-done((bf16[2,272,128]{2,1,0:T(8,128)(2,1)S(1)}, bf16[2,272,128]{2,1,0:T(8,128)(2,1)S(1)}, u32[]{:S(2)}, u32[]{:S(2)}) %collective-permute-start.4) | collective-permute-done | bytes 139296 | tf_op jit(solution)/shard_map/ppermute | solution.py:141
  81.2 0.4 collective-permute-done.7
  81.6 1.9 collective-permute-start.8
  83.5 1.3 collective-permute-done.8
  84.8 0.0 all-gather.2.cloned.1.call-done.near_ref
  84.9 2.1 %collective-permute-start.12 = (bf16[1536,512]{1,0:T(8,128)(2,1)}, bf16[1536,512]{1,0:T(8,128)(2,1)S(1)}, u32[]{:S(2)}, u32[]{:S(2)}) collective-permute-start(bf16[1536,512]{1,0:T(8,128)(2,1)} %all-gather.2.cloned.1.call-done.near_ref), channel_id=1, source_target_pairs={{0,32},{32,0},{1,33},{33,1},{2,34},{34,2},{3,35},{35,3},{4,36},{36... | collective-permute-start | bytes 4718600 | tf_op jit(solution)/shard_map/ppermute | solution.py:111
  87.0 0.1 pad_add_fusion.where_ref
  87.1 2.5 %collective-permute-start.9 = (bf16[16,64,128]{2,1,0:T(8,128)(2,1)S(1)}, bf16[16,64,128]{2,1,0:T(8,128)(2,1)S(1)}, u32[]{:S(2)}, u32[]{:S(2)}) collective-permute-start(bf16[16,64,128]{2,1,0:T(8,128)(2,1)S(1)} %bitcast.47), channel_id=1, source_target_pairs={{0,1},{1,2},{2,3},{3,0},{4,5},{5,6},{6,7},{7,4},{8,9},{9,10},{10,1... | collective-permute-start | bytes 786440 | tf_op jit(solution)/shard_map/ppermute | solution.py:149
  89.6 0.1 fusion.11
  89.6 0.1 copy.9
  89.7 0.1 copy.10
  89.8 4.8 %collective-permute-start.10 = (bf16[16,64,128]{2,1,0:T(8,128)(2,1)S(1)}, bf16[16,64,128]{2,1,0:T(8,128)(2,1)S(1)}, u32[]{:S(2)}, u32[]{:S(2)}) collective-permute-start(bf16[16,64,128]{2,1,0:T(8,128)(2,1)S(1)} %bitcast.48), channel_id=1, source_target_pairs={{0,2},{1,3},{2,0},{3,1},{4,6},{5,7},{6,4},{7,5},{8,10},{9,11},{10,... | collective-permute-start | bytes 786440 | tf_op jit(solution)/shard_map/ppermute | solution.py:149
  94.6 3.1 %collective-permute-start.11 = (bf16[16,64,128]{2,1,0:T(8,128)(2,1)S(1)}, bf16[16,64,128]{2,1,0:T(8,128)(2,1)S(1)}, u32[]{:S(2)}, u32[]{:S(2)}) collective-permute-start(bf16[16,64,128]{2,1,0:T(8,128)(2,1)S(1)} %bitcast.49), channel_id=1, source_target_pairs={{0,3},{1,0},{2,1},{3,2},{4,7},{5,4},{6,5},{7,6},{8,11},{9,8},{10,9... | collective-permute-start | bytes 786440 | tf_op jit(solution)/shard_map/ppermute | solution.py:149
  97.7 0.2 broadcast_in_dim.29
  97.9 0.0 copy-start
  98.0 0.1 collective-permute-done.9
  98.2 4.2 %collective-permute-done.10 = bf16[16,64,128]{2,1,0:T(8,128)(2,1)S(1)} collective-permute-done((bf16[16,64,128]{2,1,0:T(8,128)(2,1)S(1)}, bf16[16,64,128]{2,1,0:T(8,128)(2,1)S(1)}, u32[]{:S(2)}, u32[]{:S(2)}) %collective-permute-start.10) | collective-permute-done | bytes 262176 | tf_op jit(solution)/shard_map/ppermute | solution.py:149
  102.4 4.8 %collective-permute-done.11 = bf16[16,64,128]{2,1,0:T(8,128)(2,1)S(1)} collective-permute-done((bf16[16,64,128]{2,1,0:T(8,128)(2,1)S(1)}, bf16[16,64,128]{2,1,0:T(8,128)(2,1)S(1)}, u32[]{:S(2)}, u32[]{:S(2)}) %collective-permute-start.11) | collective-permute-done | bytes 262176 | tf_op jit(solution)/shard_map/ppermute | solution.py:149
  107.3 0.0 collective-permute-done.12.far_ref
  107.3 3.6 %shard_map.46 = bf16[1536,512]{1,0:T(8,128)(2,1)S(1)} custom-call(s32[16]{0:T(128)S(1)} %bitcast.42, s32[16]{0:T(128)S(1)} %bitcast.43, s32[2]{0:T(128)S(1)} %pad_add_fusion.where_ref, bf16[4,16,64,128]{3,2,1,0:T(8,128)(2,1)S(1)} %bitcast_dynamic-update-slice_fusion.w_ref, bf16[1536,512]{1,0:T(8,128)(2,1)S(1)} %copy-done, ...), custom_call_target="tpu_custom_call" | custom-call | flops 1610612736 | bytes 6291456 | tf_op jit(solution)/shard_map/pallas_call | solution.py:81
  110.9 0.1 fusion.8
  111.0 20.0 %collective-permute-start.13 = (bf16[384,512]{1,0:T(8,128)(2,1)S(1)}, bf16[384,512]{1,0:T(8,128)(2,1)S(1)}, u32[]{:S(2)}, u32[]{:S(2)}) collective-permute-start(bf16[384,512]{1,0:T(8,128)(2,1)S(1)} %get-tuple-element.9), channel_id=1, source_target_pairs={{0,64},{64,128},{128,192},{192,0},{1,65},{65,129},{129,193},{193,1... | collective-permute-start | bytes 1179656 | tf_op jit(solution)/shard_map/ppermute | solution.py:161
  131.0 6.5 %collective-permute-start.14 = (bf16[384,512]{1,0:T(8,128)(2,1)S(1)}, bf16[384,512]{1,0:T(8,128)(2,1)S(1)}, u32[]{:S(2)}, u32[]{:S(2)}) collective-permute-start(bf16[384,512]{1,0:T(8,128)(2,1)S(1)} %get-tuple-element.11), channel_id=1, source_target_pairs={{0,128},{64,192},{128,0},{192,64},{1,129},{65,193},{129,1},{193,65... | collective-permute-start | bytes 1179656 | tf_op jit(solution)/shard_map/ppermute | solution.py:161
  137.5 1.9 collective-permute-start.15
  139.4 4.0 %collective-permute-done.13 = bf16[384,512]{1,0:T(8,128)(2,1)S(1)} collective-permute-done((bf16[384,512]{1,0:T(8,128)(2,1)S(1)}, bf16[384,512]{1,0:T(8,128)(2,1)S(1)}, u32[]{:S(2)}, u32[]{:S(2)}) %collective-permute-start.13) | collective-permute-done | bytes 393248 | tf_op jit(solution)/shard_map/ppermute | solution.py:161
  143.4 9.6 %collective-permute-done.14 = bf16[384,512]{1,0:T(8,128)(2,1)S(1)} collective-permute-done((bf16[384,512]{1,0:T(8,128)(2,1)S(1)}, bf16[384,512]{1,0:T(8,128)(2,1)S(1)}, u32[]{:S(2)}, u32[]{:S(2)}) %collective-permute-start.14) | collective-permute-done | bytes 393248 | tf_op jit(solution)/shard_map/ppermute | solution.py:161
  153.0 1.5 collective-permute-done.15
  154.4 1.2 add_convert_fusion
  155.7 2.5 %collective-permute-start.16 = (bf16[192,512]{1,0:T(8,128)(2,1)S(1)}, bf16[192,512]{1,0:T(8,128)(2,1)S(1)}, u32[]{:S(2)}, u32[]{:S(2)}) collective-permute-start(bf16[192,512]{1,0:T(8,128)(2,1)S(1)} %get-tuple-element.12), channel_id=1, source_target_pairs={{0,0},{1,1},{2,2},{3,3},{4,64},{5,65},{6,66},{7,67},{8,128},{9,129... | collective-permute-start | bytes 589832 | tf_op jit(solution)/shard_map/ppermute | solution.py:167
  158.2 6.6 %collective-permute-start.17 = (bf16[192,512]{1,0:T(8,128)(2,1)S(1)}, bf16[192,512]{1,0:T(8,128)(2,1)S(1)}, u32[]{:S(2)}, u32[]{:S(2)}) collective-permute-start(bf16[192,512]{1,0:T(8,128)(2,1)S(1)} %get-tuple-element.13), channel_id=1, source_target_pairs={{0,4},{1,5},{2,6},{3,7},{4,68},{5,69},{6,70},{7,71},{8,132},{9,133... | collective-permute-start | bytes 589832 | tf_op jit(solution)/shard_map/ppermute | solution.py:167
  164.8 5.7 %collective-permute-done.16 = bf16[192,512]{1,0:T(8,128)(2,1)S(1)} collective-permute-done((bf16[192,512]{1,0:T(8,128)(2,1)S(1)}, bf16[192,512]{1,0:T(8,128)(2,1)S(1)}, u32[]{:S(2)}, u32[]{:S(2)}) %collective-permute-start.16) | collective-permute-done | bytes 196640 | tf_op jit(solution)/shard_map/ppermute | solution.py:167
  170.5 26.1 %collective-permute-done.17 = bf16[192,512]{1,0:T(8,128)(2,1)S(1)} collective-permute-done((bf16[192,512]{1,0:T(8,128)(2,1)S(1)}, bf16[192,512]{1,0:T(8,128)(2,1)S(1)}, u32[]{:S(2)}, u32[]{:S(2)}) %collective-permute-start.17) | collective-permute-done | bytes 196640 | tf_op jit(solution)/shard_map/ppermute | solution.py:167
  196.6 0.1 add_convert_fusion.1
  196.6 0.7 reshape.33
  (21 shorter events, 0.3 us)
Async XLA Ops:
  6.5 14.9 %copy-start.2 = (bf16[128,2048]{1,0:T(8,128)(2,1)S(1)}, bf16[128,2048]{1,0:T(8,128)(2,1)}, u32[]{:S(2)}) copy-start(bf16[128,2048]{1,0:T(8,128)(2,1)} %param.6) | copy-start | bytes 1572868
  6.5 78.3 %all-gather.2.cloned.1.call-start = ((), (), s32[]{:S(2)}) async-start(), calls=%async_computation.1 | async-start | bytes 1769472 | tf_op jit(solution)/shard_map/all_gather | solution.py:114
  9.9 46.5 %copy-start.1 = (bf16[1,2048,64]{1,2,0:T(8,128)(2,1)S(1)}, bf16[1,2048,64]{1,2,0:T(8,128)(2,1)}, u32[]{:S(2)}) copy-start(bf16[1,2048,64]{1,2,0:T(8,128)(2,1)} %param.4) | copy-start | bytes 786436
  9.9 46.5 %collective-permute-start = (bf16[64,2176]{1,0:T(8,128)(2,1)S(1)}, bf16[64,2176]{1,0:T(8,128)(2,1)S(1)}, u32[]{:S(2)}, u32[]{:S(2)}) collective-permute-start(bf16[64,2176]{1,0:T(8,128)(2,1)S(1)} %pad_maximum_fusion.1), channel_id=1, source_target_pairs={{0,64},{64,128},{128,192},{192,0},{1,65},{65,129},{129,193},{193,1... | collective-permute-start | bytes 835592 | tf_op jit(solution)/shard_map/ppermute | solution.py:128
  13.4 42.9 %collective-permute-start.1 = (bf16[64,2176]{1,0:T(8,128)(2,1)S(1)}, bf16[64,2176]{1,0:T(8,128)(2,1)S(1)}, u32[]{:S(2)}, u32[]{:S(2)}) collective-permute-start(bf16[64,2176]{1,0:T(8,128)(2,1)S(1)} %pad_maximum_fusion.1), channel_id=1, source_target_pairs={{0,128},{64,192},{128,0},{192,64},{1,129},{65,193},{129,1},{193,65... | collective-permute-start | bytes 835592 | tf_op jit(solution)/shard_map/ppermute | solution.py:128
  18.1 38.3 %collective-permute-start.2 = (bf16[64,2176]{1,0:T(8,128)(2,1)S(1)}, bf16[64,2176]{1,0:T(8,128)(2,1)S(1)}, u32[]{:S(2)}, u32[]{:S(2)}) collective-permute-start(bf16[64,2176]{1,0:T(8,128)(2,1)S(1)} %pad_maximum_fusion.1), channel_id=1, source_target_pairs={{0,192},{64,0},{128,64},{192,128},{1,193},{65,1},{129,65},{193,129... | collective-permute-start | bytes 835592 | tf_op jit(solution)/shard_map/ppermute | solution.py:128
  21.5 27.2 %collective-permute-start.5 = (bf16[32,2048]{1,0:T(8,128)(2,1)S(1)}, bf16[32,2048]{1,0:T(8,128)(2,1)S(1)}, u32[]{:S(2)}, u32[]{:S(2)}) collective-permute-start(bf16[32,2048]{1,0:T(8,128)(2,1)S(1)} %constant_dynamic-slice_fusion.2), channel_id=1, source_target_pairs={{0,256},{256,0},{1,257},{257,1},{2,258},{258,2},{3,259},{259,3},{4... | collective-permute-start | bytes 393224 | tf_op jit(solution)/shard_map/ppermute | solution.py:119
  49.6 11.5 %all-to-all-start = ((bf16[4,32,2048]{2,1,0:T(8,128)(2,1)}), bf16[4,32,2048]{2,1,0:T(8,128)(2,1)S(1)}, u32[]{:S(2)}, u32[]{:S(2)}) async-start(bf16[4,32,2048]{2,1,0:T(8,128)(2,1)} %broadcast_in_dim.28), calls=%async_computation | async-start | bytes 1048576 | tf_op jit(solution)/shard_map/all_to_all | solution.py:121
  54.5 9.4 %collective-permute-start.3 = (bf16[128,2048]{1,0:T(8,128)(2,1)S(1)}, bf16[128,2048]{1,0:T(8,128)(2,1)}, u32[]{:S(2)}, u32[]{:S(2)}) collective-permute-start(bf16[128,2048]{1,0:T(8,128)(2,1)S(1)} %copy-done.2), channel_id=1, source_target_pairs={{0,32},{32,0},{1,33},{33,1},{2,34},{34,2},{3,35},{35,3},{4,36},{36... | collective-permute-start | bytes 1572872 | tf_op jit(solution)/shard_map/ppermute | solution.py:111
  61.1 4.3 %collective-permute-start.6 = (bf16[128,2048]{1,0:T(8,128)(2,1)S(1)}, bf16[128,2048]{1,0:T(8,128)(2,1)S(1)}, u32[]{:S(2)}, u32[]{:S(2)}) collective-permute-start(bf16[128,2048]{1,0:T(8,128)(2,1)S(1)} %bitcast.54), channel_id=1, source_target_pairs={{0,32},{32,0},{1,33},{33,1},{2,34},{34,2},{3,35},{35,3},{4,36},{36... | collective-permute-start | bytes 1572872 | tf_op jit(solution)/shard_map/ppermute | solution.py:111
  65.9 15.3 %collective-permute-start.4 = (bf16[2,272,128]{2,1,0:T(8,128)(2,1)S(1)}, bf16[2,272,128]{2,1,0:T(8,128)(2,1)S(1)}, u32[]{:S(2)}, u32[]{:S(2)}) collective-permute-start(bf16[2,272,128]{2,1,0:T(8,128)(2,1)S(1)} %get-tuple-element.20), channel_id=1, source_target_pairs={{0,0},{1,1},{2,2},{3,3},{4,64},{5,65},{6,66},{7,67},{8,128},{9,129... | collective-permute-start | bytes 417800 | tf_op jit(solution)/shard_map/ppermute | solution.py:141
  67.8 13.7 %collective-permute-start.7 = (bf16[2,272,128]{2,1,0:T(8,128)(2,1)S(1)}, bf16[2,272,128]{2,1,0:T(8,128)(2,1)S(1)}, u32[]{:S(2)}, u32[]{:S(2)}) collective-permute-start(bf16[2,272,128]{2,1,0:T(8,128)(2,1)S(1)} %get-tuple-element.21), channel_id=1, source_target_pairs={{0,16},{1,17},{2,18},{3,19},{4,80},{5,81},{6,82},{7,83},{8,144},{9... | collective-permute-start | bytes 417800 | tf_op jit(solution)/shard_map/ppermute | solution.py:141
  81.6 3.3 %collective-permute-start.8 = (bf16[2,272,128]{2,1,0:T(8,128)(2,1)S(1)}, bf16[2,272,128]{2,1,0:T(8,128)(2,1)S(1)}, u32[]{:S(2)}, u32[]{:S(2)}) collective-permute-start(bf16[2,272,128]{2,1,0:T(8,128)(2,1)S(1)} %pad_maximum_fusion.5), channel_id=1, source_target_pairs={{0,32},{32,0},{1,33},{33,1},{2,34},{34,2},{3,35},{35,3},{4,36},{36... | collective-permute-start | bytes 417800 | tf_op jit(solution)/shard_map/ppermute | solution.py:111
  84.9 22.4 %collective-permute-start.12 = (bf16[1536,512]{1,0:T(8,128)(2,1)}, bf16[1536,512]{1,0:T(8,128)(2,1)S(1)}, u32[]{:S(2)}, u32[]{:S(2)}) collective-permute-start(bf16[1536,512]{1,0:T(8,128)(2,1)} %all-gather.2.cloned.1.call-done.near_ref), channel_id=1, source_target_pairs={{0,32},{32,0},{1,33},{33,1},{2,34},{34,2},{3,35},{35,3},{4,36},{36... | collective-permute-start | bytes 4718600 | tf_op jit(solution)/shard_map/ppermute | solution.py:111
  87.1 11.0 %collective-permute-start.9 = (bf16[16,64,128]{2,1,0:T(8,128)(2,1)S(1)}, bf16[16,64,128]{2,1,0:T(8,128)(2,1)S(1)}, u32[]{:S(2)}, u32[]{:S(2)}) collective-permute-start(bf16[16,64,128]{2,1,0:T(8,128)(2,1)S(1)} %bitcast.47), channel_id=1, source_target_pairs={{0,1},{1,2},{2,3},{3,0},{4,5},{5,6},{6,7},{7,4},{8,9},{9,10},{10,1... | collective-permute-start | bytes 786440 | tf_op jit(solution)/shard_map/ppermute | solution.py:149
  89.8 12.6 %collective-permute-start.10 = (bf16[16,64,128]{2,1,0:T(8,128)(2,1)S(1)}, bf16[16,64,128]{2,1,0:T(8,128)(2,1)S(1)}, u32[]{:S(2)}, u32[]{:S(2)}) collective-permute-start(bf16[16,64,128]{2,1,0:T(8,128)(2,1)S(1)} %bitcast.48), channel_id=1, source_target_pairs={{0,2},{1,3},{2,0},{3,1},{4,6},{5,7},{6,4},{7,5},{8,10},{9,11},{10,... | collective-permute-start | bytes 786440 | tf_op jit(solution)/shard_map/ppermute | solution.py:149
  94.6 12.7 %collective-permute-start.11 = (bf16[16,64,128]{2,1,0:T(8,128)(2,1)S(1)}, bf16[16,64,128]{2,1,0:T(8,128)(2,1)S(1)}, u32[]{:S(2)}, u32[]{:S(2)}) collective-permute-start(bf16[16,64,128]{2,1,0:T(8,128)(2,1)S(1)} %bitcast.49), channel_id=1, source_target_pairs={{0,3},{1,0},{2,1},{3,2},{4,7},{5,4},{6,5},{7,6},{8,11},{9,8},{10,9... | collective-permute-start | bytes 786440 | tf_op jit(solution)/shard_map/ppermute | solution.py:149
  97.9 9.3 %copy-start = (bf16[1536,512]{1,0:T(8,128)(2,1)S(1)}, bf16[1536,512]{1,0:T(8,128)(2,1)}, u32[]{:S(2)}) copy-start(bf16[1536,512]{1,0:T(8,128)(2,1)} %all-gather.2.cloned.1.call-done.near_ref) | copy-start | bytes 4718596
  111.0 32.3 %collective-permute-start.13 = (bf16[384,512]{1,0:T(8,128)(2,1)S(1)}, bf16[384,512]{1,0:T(8,128)(2,1)S(1)}, u32[]{:S(2)}, u32[]{:S(2)}) collective-permute-start(bf16[384,512]{1,0:T(8,128)(2,1)S(1)} %get-tuple-element.9), channel_id=1, source_target_pairs={{0,64},{64,128},{128,192},{192,0},{1,65},{65,129},{129,193},{193,1... | collective-permute-start | bytes 1179656 | tf_op jit(solution)/shard_map/ppermute | solution.py:161
  131.0 22.0 %collective-permute-start.14 = (bf16[384,512]{1,0:T(8,128)(2,1)S(1)}, bf16[384,512]{1,0:T(8,128)(2,1)S(1)}, u32[]{:S(2)}, u32[]{:S(2)}) collective-permute-start(bf16[384,512]{1,0:T(8,128)(2,1)S(1)} %get-tuple-element.11), channel_id=1, source_target_pairs={{0,128},{64,192},{128,0},{192,64},{1,129},{65,193},{129,1},{193,65... | collective-permute-start | bytes 1179656 | tf_op jit(solution)/shard_map/ppermute | solution.py:161
  137.5 17.0 %collective-permute-start.15 = (bf16[384,512]{1,0:T(8,128)(2,1)S(1)}, bf16[384,512]{1,0:T(8,128)(2,1)}, u32[]{:S(2)}, u32[]{:S(2)}) collective-permute-start(bf16[384,512]{1,0:T(8,128)(2,1)S(1)} %get-tuple-element.10), channel_id=1, source_target_pairs={{0,192},{64,0},{128,64},{192,128},{1,193},{65,1},{129,65},{193,129... | collective-permute-start | bytes 1179656 | tf_op jit(solution)/shard_map/ppermute | solution.py:161
  155.7 14.8 %collective-permute-start.16 = (bf16[192,512]{1,0:T(8,128)(2,1)S(1)}, bf16[192,512]{1,0:T(8,128)(2,1)S(1)}, u32[]{:S(2)}, u32[]{:S(2)}) collective-permute-start(bf16[192,512]{1,0:T(8,128)(2,1)S(1)} %get-tuple-element.12), channel_id=1, source_target_pairs={{0,0},{1,1},{2,2},{3,3},{4,64},{5,65},{6,66},{7,67},{8,128},{9,129... | collective-permute-start | bytes 589832 | tf_op jit(solution)/shard_map/ppermute | solution.py:167
  158.2 38.4 %collective-permute-start.17 = (bf16[192,512]{1,0:T(8,128)(2,1)S(1)}, bf16[192,512]{1,0:T(8,128)(2,1)S(1)}, u32[]{:S(2)}, u32[]{:S(2)}) collective-permute-start(bf16[192,512]{1,0:T(8,128)(2,1)S(1)} %get-tuple-element.13), channel_id=1, source_target_pairs={{0,4},{1,5},{2,6},{3,7},{4,68},{5,69},{6,70},{7,71},{8,132},{9,133... | collective-permute-start | bytes 589832 | tf_op jit(solution)/shard_map/ppermute | solution.py:167
Sparse Core Ops, SparseCore 0:
  9.4 72.7 all-gather.1

commit v3 on v2

v3 whole, which is shorter than its diff:
```python
import jax
import jax.numpy as jnp
from jax import lax
from jax.experimental import pallas as pl
from jax.experimental.pallas import tpu as pltpu
from jax.sharding import Mesh, PartitionSpec as P

H, X, C, L, Y = 2, 4, 2, 8, 4
AXES = ("h", "x", "c", "l", "y")
OCC = 4


def flat(h, x, c, l, y):
    return (((h * X + x) * C + c) * L + l) * Y + y


def coords():
    for h in range(H):
        for x in range(X):
            for c in range(C):
                for l in range(L):
                    for y in range(Y):
                        yield h, x, c, l, y


def weight_perm(k):
    return [
        (flat(h, x, c, l, y), flat(l // X, l % X, c, (h ^ k) * X + x, y))
        for h, x, c, l, y in coords()
    ]


def result_perm(k):
    return [
        (flat(h, x, c, l, y), flat(l // X, l % X, c, 2 * x + (h ^ k), y))
        for h, x, c, l, y in coords()
    ]


def shift(n, k):
    return [(i, (i + k) % n) for i in range(n)]


def assemble(first_ref, second_ref, w_refs, acc_ref, s_ref):
    acc_ref[...] = jnp.zeros_like(acc_ref)
    offset = 0
    for w_ref in w_refs:
        slots, rows, cols = w_ref.shape[1:]

        def add(slot, _, w_ref=w_ref, offset=offset):
            first, second = first_ref[slot + offset], second_ref[slot + offset]
            at_col = pl.multiple_of(first * cols, cols)
            for z in range(Y):
                half, part = z // 2, z % 2
                at_row = pl.multiple_of((half * OCC + second) * (2 * rows) + part * rows, rows)
                here = (pl.ds(at_row, rows), pl.ds(at_col, cols))
                acc_ref[here] += w_ref[z, slot].astype(jnp.float32)
            return 0

        lax.fori_loop(0, slots, add, 0)
        offset += slots
    s_ref[...] = acc_ref[...].astype(jnp.bfloat16)


def multiply(where_ref, near_ref, far_ref, s_ref, out_ref):
    depth = near_ref.shape[1]
    at_near = pl.multiple_of(where_ref[1] * depth, depth)
    at_far = pl.multiple_of((1 - where_ref[1]) * depth, depth)
    f32 = jnp.float32
    total = jnp.dot(near_ref[...], s_ref[pl.ds(at_near, depth)], preferred_element_type=f32)
    total += jnp.dot(far_ref[...], s_ref[pl.ds(at_far, depth)], preferred_element_type=f32)
    out_ref[...] = total.astype(jnp.bfloat16)


def first_kernel(
    first_ref, second_ref, where_ref, w0_ref, w1_ref, near_ref, far_ref, out_ref, s_ref, acc_ref
):
    @pl.when(pl.program_id(0) == 0)
    def _():
        assemble(first_ref, second_ref, (w0_ref, w1_ref), acc_ref, s_ref)

    multiply(where_ref, near_ref, far_ref, s_ref, out_ref)


def second_kernel(where_ref, near_ref, far_ref, s_ref, out_ref):
    multiply(where_ref, near_ref, far_ref, s_ref, out_ref)


def part_of(k):
    return lambda s, *refs: (2 * s + (refs[-1][0] ^ k), 0)


def whole(array):
    return pl.BlockSpec(array.shape, lambda s, *_: (0,) * array.ndim)


def contract(first, second, where, w0, w1, near, far):
    q, depth = near.shape
    cols = OCC * w0.shape[3]
    block = q // (2 * X)
    out = jax.ShapeDtypeStruct((q // 2, cols), jnp.bfloat16)
    out_spec = pl.BlockSpec((block, cols), lambda s, *_: (s, 0))
    s_shape = jax.ShapeDtypeStruct((2 * depth, cols), jnp.bfloat16)
    params = pltpu.CompilerParams(vmem_limit_bytes=32 * 1024 * 1024)
    cost = pl.CostEstimate(
        flops=2 * q * depth * cols, bytes_accessed=4 * 2**20, transcendentals=0
    )
    rows = [pl.BlockSpec((block, depth), part_of(0))] * 2
    one, s = pl.pallas_call(
        first_kernel,
        grid_spec=pltpu.PrefetchScalarGridSpec(
            num_scalar_prefetch=3,
            grid=(X,),
            in_specs=[whole(w0), whole(w1)] + rows,
            out_specs=[out_spec, whole(s_shape)],
            scratch_shapes=[pltpu.VMEM(s_shape.shape, jnp.float32)],
        ),
        out_shape=[out, s_shape],
        compiler_params=params,
        cost_estimate=cost,
    )(first, second, where, w0, w1, near, far)
    rows = [pl.BlockSpec((block, depth), part_of(1))] * 2
    two = pl.pallas_call(
        second_kernel,
        grid_spec=pltpu.PrefetchScalarGridSpec(
            num_scalar_prefetch=1, grid=(X,), in_specs=rows + [whole(s)], out_specs=out_spec
        ),
        out_shape=out,
        compiler_params=params,
        cost_estimate=cost,
    )(where, near, far, s)
    return one, two


def on_device(amplitudes, fitting, coefficients, pair_list):
    h, x, c = lax.axis_index("h"), lax.axis_index("x"), lax.axis_index("c")
    y = lax.axis_index("y")
    f32, bf16 = jnp.float32, jnp.bfloat16

    def swap_core(v):
        return lax.ppermute(v, "c", shift(C, 1))

    def gather_y(v):
        v = jnp.broadcast_to(v[None], (Y,) + v.shape)
        return lax.all_to_all(v, "y", split_axis=0, concat_axis=0, tiled=True)

    q_own, occ, b_own = fitting.shape
    b_near = lax.all_gather(fitting.reshape(q_own, occ * b_own), "l", axis=0, tiled=True)

    n_mu, n_a = coefficients.shape
    part = n_mu // Y
    mirror = [(i, H * L - 1 - i) for i in range(H * L)]
    piece = lax.dynamic_slice_in_dim(coefficients, y * part, part, 0)
    piece = lax.ppermute(piece, ("h", "l"), mirror)

    rows = amplitudes.shape[2]
    info = jnp.pad(pair_list.astype(bf16), ((0, rows - 1), (0, 126)))
    t_own = jnp.concatenate([amplitudes[0].T, info], axis=1)
    t_all = jnp.concatenate(
        [t_own] + [lax.ppermute(t_own, "x", shift(X, k)) for k in range(1, X)], axis=0
    )
    info = t_all.reshape(X, rows, -1)[:, 0, n_a:]
    info = jnp.broadcast_to(jnp.pad(info, ((0, 16 - X), (0, 0)))[None], (C, 16, n_mu))
    t_all = t_all[:, :n_a]

    slots, n_b = C * X, X * rows
    w_all, w_info = [], []
    for k in range(H):
        c_part = gather_y(piece).reshape(n_mu, n_a) if k else coefficients
        w = [
            lax.dot_general(t_all, m, (((1,), (1,)), ((), ())), preferred_element_type=f32)
            for m in (c_part, swap_core(c_part))
        ]
        w = jnp.concatenate([jnp.stack(w).astype(bf16), info], axis=1)
        if k == 0:
            w, piece = lax.optimization_barrier((w, piece))
        w = lax.ppermute(w, AXES, weight_perm(k))
        w = jnp.stack([w[0], swap_core(w[1])])
        w_info.append(w[:, n_b : n_b + X, :2].reshape(slots, 2).astype(jnp.int32))
        w = w[:, :n_b].reshape(slots, rows, n_mu)
        if k:
            w, b_near = lax.optimization_barrier((w, b_near))
        w_all.append(gather_y(w).reshape(Y, slots, rows, n_mu))
    info = jnp.concatenate(w_info)
    b_far = swap_core(b_near)

    where = jnp.stack([h, c]).astype(jnp.int32)
    parts = contract(info[:, 0], info[:, 1], where, w_all[0], w_all[1], b_near, b_far)
    total = 0
    for k, v in enumerate(parts):
        v = v.reshape(X, q_own, -1)
        v = lax.all_to_all(v, "x", split_axis=0, concat_axis=0, tiled=True)
        v = jnp.sum(v.astype(f32), axis=0).astype(bf16)
        total += lax.ppermute(v, AXES, result_perm(k)).astype(f32)
    return total.astype(bf16).reshape(q_own, occ, n_mu)


def solution(mesh):
    fine = Mesh(mesh.devices.reshape(H, X, C, L, Y), AXES)
    pair, aux = ("h", "x", "c"), ("l", "y")
    in_specs = (P(pair, None, aux), P(aux, None, pair), P(pair, None), P(pair, None))
    out_specs = P(aux, None, pair)
    return jax.shard_map(
        on_device, mesh=fine, in_specs=in_specs, out_specs=out_specs, check_vma=False
    )
```

time: 205 us -> 225 us (1.098)
  the two profiles are of different devices: /device:TPU:136 before, /device:TPU:128 now
where the time goes in v3:
time: 225 us; the launch traced here: 224 us
  waiting for transfers between devices  92.1 us (41%)
  starting transfers between devices  83.7 us (37%)
  between operations  13.7 us (6%)
  blocking collectives  13.5 us (6%)
  local copies, waits for them, and re-layouts  8.53 us (4%)
  Pallas kernels  6.15 us (3%)
  other arithmetic  4.25 us (2%)
    ppermute x2, starting transfers between devices, on_device(): w = lax.ppermute(w, AXES, weight_perm(k))  28.4 us
    ppermute x2, waiting for transfers between devices, on_device(): total += lax.ppermute(v, AXES, result_perm(k)).astype(f32)  26.2 us
    all_to_all x2, waiting for transfers between devices, gather_y(): return lax.all_to_all(v, 'y', split_axis=0, concat_axis=0, tiled=True)  17.7 us
    all_to_all x2, waiting for transfers between devices, on_device(): v = lax.all_to_all(v, 'x', split_axis=0, concat_axis=0, tiled=True)  15.2 us
    ppermute x2, waiting for transfers between devices, on_device(): w = lax.ppermute(w, AXES, weight_perm(k))  14.3 us
    all_to_all x1, blocking collectives, gather_y(): return lax.all_to_all(v, 'y', split_axis=0, concat_axis=0, tiled=True)  13.5 us
    all_to_all x2, starting transfers between devices, gather_y(): return lax.all_to_all(v, 'y', split_axis=0, concat_axis=0, tiled=True)  13 us
    all_gather x1, waiting for transfers between devices, on_device(): lax.all_gather(fitting.reshape(q_own, occ * b_own), 'l', axis=0, tiled=True)  11.5 us
  transfers between devices with their start and end apart: 18, of which 13 were waited for; matrix products, arithmetic and copies ran while one was open for 4% of the time, Pallas kernels for 1%

profile of v3, /device:TPU:128, one launch (start us, length us, event | category | flops | bytes accessed | tf_op | source)
XLA Modules:
  0.0 223.7 jit_solution(4604857605730584772)
XLA Ops:
  6.5 0.0 all-gather.2.cloned.1.call-start
  6.5 0.7 convert_element_type.30
  7.3 1.0 pad_maximum_fusion.1
  8.3 4.7 %collective-permute-start.2 = (bf16[64,2176]{1,0:T(8,128)(2,1)S(1)}, bf16[64,2176]{1,0:T(8,128)(2,1)S(1)}, u32[]{:S(2)}, u32[]{:S(2)}) collective-permute-start(bf16[64,2176]{1,0:T(8,128)(2,1)S(1)} %pad_maximum_fusion.1), channel_id=1, source_target_pairs={{0,192},{64,0},{128,64},{192,128},{1,193},{65,1},{129,65},{193,129... | collective-permute-start | bytes 835592 | tf_op jit(solution)/shard_map/ppermute | solution.py:160
  12.9 2.7 %collective-permute-start.1 = (bf16[64,2176]{1,0:T(8,128)(2,1)S(1)}, bf16[64,2176]{1,0:T(8,128)(2,1)S(1)}, u32[]{:S(2)}, u32[]{:S(2)}) collective-permute-start(bf16[64,2176]{1,0:T(8,128)(2,1)S(1)} %pad_maximum_fusion.1), channel_id=1, source_target_pairs={{0,128},{64,192},{128,0},{192,64},{1,129},{65,193},{129,1},{193,65... | collective-permute-start | bytes 835592 | tf_op jit(solution)/shard_map/ppermute | solution.py:160
  15.6 2.8 %collective-permute-start = (bf16[64,2176]{1,0:T(8,128)(2,1)S(1)}, bf16[64,2176]{1,0:T(8,128)(2,1)S(1)}, u32[]{:S(2)}, u32[]{:S(2)}) collective-permute-start(bf16[64,2176]{1,0:T(8,128)(2,1)S(1)} %pad_maximum_fusion.1), channel_id=1, source_target_pairs={{0,64},{64,128},{128,192},{192,0},{1,65},{65,129},{129,193},{193,1... | collective-permute-start | bytes 835592 | tf_op jit(solution)/shard_map/ppermute | solution.py:160
  18.4 1.6 copy.14
  20.1 0.0 all-gather.2.cloned.1.call-update
  20.1 1.9 collective-permute-start.3
  22.1 10.5 %collective-permute-start.4 = (bf16[32,2048]{1,0:T(8,128)(2,1)S(1)}, bf16[32,2048]{1,0:T(8,128)(2,1)S(1)}, u32[]{:S(2)}, u32[]{:S(2)}) collective-permute-start(bf16[32,2048]{1,0:T(8,128)(2,1)S(1)} %constant_dynamic-slice_fusion), channel_id=1, source_target_pairs={{0,284},{4,280},{8,276},{12,272},{16,268},{20,264},{24,260},{28,25... | collective-permute-start | bytes 393224 | tf_op jit(solution)/shard_map/ppermute | solution.py:154
  32.5 0.0 collective-permute-done.2
  32.6 0.0 collective-permute-done.1
  32.6 0.0 collective-permute-done
  32.6 0.1 pad_maximum_fusion
  32.7 0.4 fusion
  33.2 0.0 collective-permute-done.3
  33.2 0.5 fusion.1
  33.7 3.4 %collective-permute-done.4 = bf16[32,2048]{1,0:T(8,128)(2,1)S(1)} collective-permute-done((bf16[32,2048]{1,0:T(8,128)(2,1)S(1)}, bf16[32,2048]{1,0:T(8,128)(2,1)S(1)}, u32[]{:S(2)}, u32[]{:S(2)}) %collective-permute-start.4) | collective-permute-done | bytes 131104 | tf_op jit(solution)/shard_map/ppermute | solution.py:154
  37.2 13.5 %all_to_all.25 = bf16[4,32,2048]{2,1,0:T(8,128)(2,1)S(1)} all-to-all(bf16[4,32,2048]{2,1,0:T(8,128)(2,1)S(1)} %broadcast_in_dim.11), channel_id=1, replica_groups=mesh['h'=2,'x'=4,'c'=2,'l'=8,'y'=4] {'y'}, dimensions={0} | all-to-all | bytes 1048576 | tf_op jit(solution)/shard_map/all_to_all | solution.py:145
  50.6 1.9 collective-permute-start.7
  52.6 0.4 fusion.2
  53.0 1.4 collective-permute-done.7
  54.4 0.4 fusion.3
  54.9 10.5 %collective-permute-start.8 = (bf16[2,272,128]{2,1,0:T(8,128)(2,1)S(1)}, bf16[2,272,128]{2,1,0:T(8,128)(2,1)S(1)}, u32[]{:S(2)}, u32[]{:S(2)}) collective-permute-start(bf16[2,272,128]{2,1,0:T(8,128)(2,1)S(1)} %pad_maximum_fusion.2), channel_id=1, source_target_pairs={{0,16},{1,17},{2,18},{3,19},{4,80},{5,81},{6,82},{7,83},{8,144},{9... | collective-permute-start | bytes 417800 | tf_op jit(solution)/shard_map/ppermute | solution.py:177
  65.4 6.4 %collective-permute-done.8 = bf16[2,272,128]{2,1,0:T(8,128)(2,1)S(1)} collective-permute-done((bf16[2,272,128]{2,1,0:T(8,128)(2,1)S(1)}, bf16[2,272,128]{2,1,0:T(8,128)(2,1)S(1)}, u32[]{:S(2)}, u32[]{:S(2)}) %collective-permute-start.8) | collective-permute-done | bytes 139296 | tf_op jit(solution)/shard_map/ppermute | solution.py:177
  71.8 1.9 collective-permute-start.9
  73.7 1.2 collective-permute-done.9
  75.0 11.5 %all-gather.2.cloned.1.call-done.near_ref = bf16[1536,512]{1,0:T(8,128)(2,1)} async-done(((bf16[192,512]{1,0:T(8,128)(2,1)}), bf16[1536,512]{1,0:T(8,128)(2,1)}) %all-gather.2.cloned.1.call-update) | async-done | bytes 1572880 | tf_op jit(solution)/shard_map/all_gather | solution.py:148
  86.5 1.9 collective-permute-start.10
  88.4 17.9 %collective-permute-start.5 = (bf16[2,272,128]{2,1,0:T(8,128)(2,1)S(1)}, bf16[2,272,128]{2,1,0:T(8,128)(2,1)S(1)}, u32[]{:S(2)}, u32[]{:S(2)}) collective-permute-start(bf16[2,272,128]{2,1,0:T(8,128)(2,1)S(1)} %pad_maximum_fusion.3), channel_id=1, source_target_pairs={{0,0},{1,1},{2,2},{3,3},{4,64},{5,65},{6,66},{7,67},{8,128},{9,129... | collective-permute-start | bytes 417800 | tf_op jit(solution)/shard_map/ppermute | solution.py:177
  106.3 7.9 %collective-permute-done.5 = bf16[2,272,128]{2,1,0:T(8,128)(2,1)S(1)} collective-permute-done((bf16[2,272,128]{2,1,0:T(8,128)(2,1)S(1)}, bf16[2,272,128]{2,1,0:T(8,128)(2,1)S(1)}, u32[]{:S(2)}, u32[]{:S(2)}) %collective-permute-start.5) | collective-permute-done | bytes 139296 | tf_op jit(solution)/shard_map/ppermute | solution.py:177
  114.2 2.0 collective-permute-start.6
  116.2 1.1 collective-permute-done.6
  117.4 0.9 broadcast_in_dim.13
  118.3 0.0 copy-done.6
  118.3 8.8 %all-to-all-start.1 = ((bf16[4,8,64,128]{3,2,1,0:T(8,128)(2,1)}), bf16[4,8,64,128]{3,2,1,0:T(8,128)(2,1)}, u32[]{:S(2)}, u32[]{:S(2)}) async-start(bf16[4,8,64,128]{3,2,1,0:T(8,128)(2,1)} %broadcast_in_dim.13), calls=%async_computation.1 | async-start | bytes 1048576 | tf_op jit(solution)/shard_map/all_to_all | solution.py:145
  127.2 0.1 pad_add_fusion.where_ref
  127.2 0.8 pad_maximum_fusion.7
  128.0 0.1 copy.8
  128.1 8.9 %all-to-all-done.1.w0_ref = bf16[4,8,64,128]{3,2,1,0:T(8,128)(2,1)} async-done(((bf16[4,8,64,128]{3,2,1,0:T(8,128)(2,1)}), bf16[4,8,64,128]{3,2,1,0:T(8,128)(2,1)}, u32[]{:S(2)}, u32[]{:S(2)}) %all-to-all-start.1) | async-done | bytes 524320 | tf_op jit(solution)/shard_map/all_to_all | solution.py:145
  137.1 0.9 broadcast_in_dim.14
  138.0 4.1 %all-to-all-start.2 = ((bf16[4,8,64,128]{3,2,1,0:T(8,128)(2,1)}), bf16[4,8,64,128]{3,2,1,0:T(8,128)(2,1)}, u32[]{:S(2)}, u32[]{:S(2)}) async-start(bf16[4,8,64,128]{3,2,1,0:T(8,128)(2,1)} %broadcast_in_dim.14), calls=%async_computation.2 | async-start | bytes 1048576 | tf_op jit(solution)/shard_map/all_to_all | solution.py:145
  142.1 0.1 copy.9
  142.2 0.1 maximum_convert_fusion
  142.3 8.8 %all-to-all-done.2.w1_ref = bf16[4,8,64,128]{3,2,1,0:T(8,128)(2,1)} async-done(((bf16[4,8,64,128]{3,2,1,0:T(8,128)(2,1)}), bf16[4,8,64,128]{3,2,1,0:T(8,128)(2,1)}, u32[]{:S(2)}, u32[]{:S(2)}) %all-to-all-start.2) | async-done | bytes 524320 | tf_op jit(solution)/shard_map/all_to_all | solution.py:145
  151.1 0.0 collective-permute-done.10.far_ref
  151.1 4.1 %shard_map.46 = (bf16[768,512]{1,0:T(8,128)(2,1)S(1)}, bf16[1024,512]{1,0:T(8,128)(2,1)S(1)}) custom-call(s32[16]{0:T(128)S(1)} %get-tuple-element.22.first_ref, s32[16]{0:T(128)S(1)} %get-tuple-element.21.second_ref, s32[2]{0:T(128)S(1)} %pad_add_fusion.where_ref, bf16[4,8,64,128]{3,2,1,0:T(8,128)(2,1)} %all-to-all-done.1.w0_ref, ...), custom_call_target="tpu_custom_call" | custom-call | flops 805306368 | bytes 4194304 | tf_op jit(solution)/shard_map/pallas_call | solution.py:109
  155.2 1.0 copy-done.2
  156.2 0.9 copy-done.4
  157.1 4.7 %all-to-all-start.3 = ((bf16[4,192,512]{2,1,0:T(8,128)(2,1)}), bf16[4,192,512]{2,1,0:T(8,128)(2,1)}, u32[]{:S(2)}, u32[]{:S(2)}) async-start(bf16[4,192,512]{2,1,0:T(8,128)(2,1)} %bitcast.43), calls=%async_computation.3 | async-start | bytes 1572864 | tf_op jit(solution)/shard_map/all_to_all | solution.py:192
  161.7 1.2 copy-done.3
  163.0 2.1 shard_map.47
  165.1 0.9 copy-done.1
  166.0 6.4 %all-to-all-done.3 = bf16[4,192,512]{2,1,0:T(8,128)(2,1)} async-done(((bf16[4,192,512]{2,1,0:T(8,128)(2,1)}), bf16[4,192,512]{2,1,0:T(8,128)(2,1)}, u32[]{:S(2)}, u32[]{:S(2)}) %all-to-all-start.3) | async-done | bytes 786464 | tf_op jit(solution)/shard_map/all_to_all | solution.py:192
  172.4 3.5 %all-to-all-start.4 = ((bf16[4,192,512]{2,1,0:T(8,128)(2,1)}), bf16[4,192,512]{2,1,0:T(8,128)(2,1)S(1)}, u32[]{:S(2)}, u32[]{:S(2)}) async-start(bf16[4,192,512]{2,1,0:T(8,128)(2,1)} %bitcast.42), calls=%async_computation.4 | async-start | bytes 1572864 | tf_op jit(solution)/shard_map/all_to_all | solution.py:192
  175.9 1.3 reduce_sum.24
  177.2 1.9 collective-permute-start.11
  179.1 8.7 %all-to-all-done.4 = bf16[4,192,512]{2,1,0:T(8,128)(2,1)S(1)} async-done(((bf16[4,192,512]{2,1,0:T(8,128)(2,1)}), bf16[4,192,512]{2,1,0:T(8,128)(2,1)S(1)}, u32[]{:S(2)}, u32[]{:S(2)}) %all-to-all-start.4) | async-done | bytes 786464 | tf_op jit(solution)/shard_map/all_to_all | solution.py:192
  187.9 0.1 reduce_sum.25
  188.0 1.9 collective-permute-start.12
  189.9 2.7 %collective-permute-done.11 = bf16[192,512]{1,0:T(8,128)(2,1)S(1)} collective-permute-done((bf16[192,512]{1,0:T(8,128)(2,1)S(1)}, bf16[192,512]{1,0:T(8,128)(2,1)S(1)}, u32[]{:S(2)}, u32[]{:S(2)}) %collective-permute-start.11) | collective-permute-done | bytes 196640 | tf_op jit(solution)/shard_map/ppermute | solution.py:194
  192.7 23.4 %collective-permute-done.12 = bf16[192,512]{1,0:T(8,128)(2,1)S(1)} collective-permute-done((bf16[192,512]{1,0:T(8,128)(2,1)S(1)}, bf16[192,512]{1,0:T(8,128)(2,1)S(1)}, u32[]{:S(2)}, u32[]{:S(2)}) %collective-permute-start.12) | collective-permute-done | bytes 196640 | tf_op jit(solution)/shard_map/ppermute | solution.py:194
  216.1 0.1 add_convert_fusion
  216.2 0.7 reshape.37
  (26 shorter events, 0.2 us)
Async XLA Ops:
  6.5 26.0 %copy-start.5 = (bf16[1,2048,64]{1,2,0:T(8,128)(2,1)S(1)}, bf16[1,2048,64]{1,2,0:T(8,128)(2,1)}, u32[]{:S(2)}) copy-start(bf16[1,2048,64]{1,2,0:T(8,128)(2,1)} %param.4) | copy-start | bytes 786436
  6.5 13.6 %copy-start.7 = (bf16[128,2048]{1,0:T(8,128)(2,1)S(1)}, bf16[128,2048]{1,0:T(8,128)(2,1)}, u32[]{:S(2)}) copy-start(bf16[128,2048]{1,0:T(8,128)(2,1)} %param.6) | copy-start | bytes 1572868
  6.5 79.9 %all-gather.2.cloned.1.call-start = ((), (), s32[]{:S(2)}) async-start(), calls=%async_computation.5 | async-start | bytes 1769472 | tf_op jit(solution)/shard_map/all_gather | solution.py:148
  8.3 24.3 %collective-permute-start.2 = (bf16[64,2176]{1,0:T(8,128)(2,1)S(1)}, bf16[64,2176]{1,0:T(8,128)(2,1)S(1)}, u32[]{:S(2)}, u32[]{:S(2)}) collective-permute-start(bf16[64,2176]{1,0:T(8,128)(2,1)S(1)} %pad_maximum_fusion.1), channel_id=1, source_target_pairs={{0,192},{64,0},{128,64},{192,128},{1,193},{65,1},{129,65},{193,129... | collective-permute-start | bytes 835592 | tf_op jit(solution)/shard_map/ppermute | solution.py:160
  12.9 19.6 %collective-permute-start.1 = (bf16[64,2176]{1,0:T(8,128)(2,1)S(1)}, bf16[64,2176]{1,0:T(8,128)(2,1)S(1)}, u32[]{:S(2)}, u32[]{:S(2)}) collective-permute-start(bf16[64,2176]{1,0:T(8,128)(2,1)S(1)} %pad_maximum_fusion.1), channel_id=1, source_target_pairs={{0,128},{64,192},{128,0},{192,64},{1,129},{65,193},{129,1},{193,65... | collective-permute-start | bytes 835592 | tf_op jit(solution)/shard_map/ppermute | solution.py:160
  15.6 16.9 %collective-permute-start = (bf16[64,2176]{1,0:T(8,128)(2,1)S(1)}, bf16[64,2176]{1,0:T(8,128)(2,1)S(1)}, u32[]{:S(2)}, u32[]{:S(2)}) collective-permute-start(bf16[64,2176]{1,0:T(8,128)(2,1)S(1)} %pad_maximum_fusion.1), channel_id=1, source_target_pairs={{0,64},{64,128},{128,192},{192,0},{1,65},{65,129},{129,193},{193,1... | collective-permute-start | bytes 835592 | tf_op jit(solution)/shard_map/ppermute | solution.py:160
  20.1 13.1 %collective-permute-start.3 = (bf16[128,2048]{1,0:T(8,128)(2,1)S(1)}, bf16[128,2048]{1,0:T(8,128)(2,1)S(1)}, u32[]{:S(2)}, u32[]{:S(2)}) collective-permute-start(bf16[128,2048]{1,0:T(8,128)(2,1)S(1)} %copy-done.7), channel_id=1, source_target_pairs={{0,32},{32,0},{1,33},{33,1},{2,34},{34,2},{3,35},{35,3},{4,36},{36... | collective-permute-start | bytes 1572872 | tf_op jit(solution)/shard_map/ppermute | solution.py:141
  22.1 15.0 %collective-permute-start.4 = (bf16[32,2048]{1,0:T(8,128)(2,1)S(1)}, bf16[32,2048]{1,0:T(8,128)(2,1)S(1)}, u32[]{:S(2)}, u32[]{:S(2)}) collective-permute-start(bf16[32,2048]{1,0:T(8,128)(2,1)S(1)} %constant_dynamic-slice_fusion), channel_id=1, source_target_pairs={{0,284},{4,280},{8,276},{12,272},{16,268},{20,264},{24,260},{28,25... | collective-permute-start | bytes 393224 | tf_op jit(solution)/shard_map/ppermute | solution.py:154
  50.6 3.8 %collective-permute-start.7 = (bf16[128,2048]{1,0:T(8,128)(2,1)S(1)}, bf16[128,2048]{1,0:T(8,128)(2,1)S(1)}, u32[]{:S(2)}, u32[]{:S(2)}) collective-permute-start(bf16[128,2048]{1,0:T(8,128)(2,1)S(1)} %bitcast.50), channel_id=1, source_target_pairs={{0,32},{32,0},{1,33},{33,1},{2,34},{34,2},{3,35},{35,3},{4,36},{36... | collective-permute-start | bytes 1572872 | tf_op jit(solution)/shard_map/ppermute | solution.py:141
  54.9 16.9 %collective-permute-start.8 = (bf16[2,272,128]{2,1,0:T(8,128)(2,1)S(1)}, bf16[2,272,128]{2,1,0:T(8,128)(2,1)S(1)}, u32[]{:S(2)}, u32[]{:S(2)}) collective-permute-start(bf16[2,272,128]{2,1,0:T(8,128)(2,1)S(1)} %pad_maximum_fusion.2), channel_id=1, source_target_pairs={{0,16},{1,17},{2,18},{3,19},{4,80},{5,81},{6,82},{7,83},{8,144},{9... | collective-permute-start | bytes 417800 | tf_op jit(solution)/shard_map/ppermute | solution.py:177
  71.8 3.2 %collective-permute-start.9 = (bf16[272,128]{1,0:T(8,128)(2,1)S(1)}, bf16[272,128]{1,0:T(8,128)(2,1)S(1)}, u32[]{:S(2)}, u32[]{:S(2)}) collective-permute-start(bf16[272,128]{1,0:T(8,128)(2,1)S(1)} %get-tuple-element.20), channel_id=1, source_target_pairs={{0,32},{32,0},{1,33},{33,1},{2,34},{34,2},{3,35},{35,3},{4,36},{36... | collective-permute-start | bytes 208904 | tf_op jit(solution)/shard_map/ppermute | solution.py:141
  86.5 64.6 %collective-permute-start.10 = (bf16[1536,512]{1,0:T(8,128)(2,1)}, bf16[1536,512]{1,0:T(8,128)(2,1)S(1)}, u32[]{:S(2)}, u32[]{:S(2)}) collective-permute-start(bf16[1536,512]{1,0:T(8,128)(2,1)} %all-gather.2.cloned.1.call-done.near_ref), channel_id=1, source_target_pairs={{0,32},{32,0},{1,33},{33,1},{2,34},{34,2},{3,35},{35,3},{4,36},{36... | collective-permute-start | bytes 4718600 | tf_op jit(solution)/shard_map/ppermute | solution.py:141
  88.4 25.8 %collective-permute-start.5 = (bf16[2,272,128]{2,1,0:T(8,128)(2,1)S(1)}, bf16[2,272,128]{2,1,0:T(8,128)(2,1)S(1)}, u32[]{:S(2)}, u32[]{:S(2)}) collective-permute-start(bf16[2,272,128]{2,1,0:T(8,128)(2,1)S(1)} %pad_maximum_fusion.3), channel_id=1, source_target_pairs={{0,0},{1,1},{2,2},{3,3},{4,64},{5,65},{6,66},{7,67},{8,128},{9,129... | collective-permute-start | bytes 417800 | tf_op jit(solution)/shard_map/ppermute | solution.py:177
  114.2 3.2 %collective-permute-start.6 = (bf16[272,128]{1,0:T(8,128)(2,1)S(1)}, bf16[272,128]{1,0:T(8,128)(2,1)S(1)}, u32[]{:S(2)}, u32[]{:S(2)}) collective-permute-start(bf16[272,128]{1,0:T(8,128)(2,1)S(1)} %get-tuple-element.18), channel_id=1, source_target_pairs={{0,32},{32,0},{1,33},{33,1},{2,34},{34,2},{3,35},{35,3},{4,36},{36... | collective-permute-start | bytes 208904 | tf_op jit(solution)/shard_map/ppermute | solution.py:141
  117.4 1.0 copy-start.6
  118.3 18.7 %all-to-all-start.1 = ((bf16[4,8,64,128]{3,2,1,0:T(8,128)(2,1)}), bf16[4,8,64,128]{3,2,1,0:T(8,128)(2,1)}, u32[]{:S(2)}, u32[]{:S(2)}) async-start(bf16[4,8,64,128]{3,2,1,0:T(8,128)(2,1)} %broadcast_in_dim.13), calls=%async_computation.1 | async-start | bytes 1048576 | tf_op jit(solution)/shard_map/all_to_all | solution.py:145
  127.1 24.0 %copy-start = (bf16[1536,512]{1,0:T(8,128)(2,1)S(1)}, bf16[1536,512]{1,0:T(8,128)(2,1)}, u32[]{:S(2)}) copy-start(bf16[1536,512]{1,0:T(8,128)(2,1)} %all-gather.2.cloned.1.call-done.near_ref) | copy-start | bytes 4718596
  138.0 13.1 %all-to-all-start.2 = ((bf16[4,8,64,128]{3,2,1,0:T(8,128)(2,1)}), bf16[4,8,64,128]{3,2,1,0:T(8,128)(2,1)}, u32[]{:S(2)}, u32[]{:S(2)}) async-start(bf16[4,8,64,128]{3,2,1,0:T(8,128)(2,1)} %broadcast_in_dim.14), calls=%async_computation.2 | async-start | bytes 1048576 | tf_op jit(solution)/shard_map/all_to_all | solution.py:145
  155.2 1.0 copy-start.2
  156.2 0.9 copy-start.4
  157.1 15.3 %all-to-all-start.3 = ((bf16[4,192,512]{2,1,0:T(8,128)(2,1)}), bf16[4,192,512]{2,1,0:T(8,128)(2,1)}, u32[]{:S(2)}, u32[]{:S(2)}) async-start(bf16[4,192,512]{2,1,0:T(8,128)(2,1)} %bitcast.43), calls=%async_computation.3 | async-start | bytes 1572864 | tf_op jit(solution)/shard_map/all_to_all | solution.py:192
  161.7 1.2 copy-start.3
  165.1 0.9 copy-start.1
  172.4 15.5 %all-to-all-start.4 = ((bf16[4,192,512]{2,1,0:T(8,128)(2,1)}), bf16[4,192,512]{2,1,0:T(8,128)(2,1)S(1)}, u32[]{:S(2)}, u32[]{:S(2)}) async-start(bf16[4,192,512]{2,1,0:T(8,128)(2,1)} %bitcast.42), calls=%async_computation.4 | async-start | bytes 1572864 | tf_op jit(solution)/shard_map/all_to_all | solution.py:192
  177.2 15.5 %collective-permute-start.11 = (bf16[192,512]{1,0:T(8,128)(2,1)S(1)}, bf16[192,512]{1,0:T(8,128)(2,1)S(1)}, u32[]{:S(2)}, u32[]{:S(2)}) collective-permute-start(bf16[192,512]{1,0:T(8,128)(2,1)S(1)} %reduce_sum.24), channel_id=1, source_target_pairs={{0,0},{1,1},{2,2},{3,3},{4,64},{5,65},{6,66},{7,67},{8,128},{9,129... | collective-permute-start | bytes 589832 | tf_op jit(solution)/shard_map/ppermute | solution.py:194
  188.0 28.1 %collective-permute-start.12 = (bf16[192,512]{1,0:T(8,128)(2,1)S(1)}, bf16[192,512]{1,0:T(8,128)(2,1)S(1)}, u32[]{:S(2)}, u32[]{:S(2)}) collective-permute-start(bf16[192,512]{1,0:T(8,128)(2,1)S(1)} %reduce_sum.25), channel_id=1, source_target_pairs={{0,4},{1,5},{2,6},{3,7},{4,68},{5,69},{6,70},{7,71},{8,132},{9,133... | collective-permute-start | bytes 589832 | tf_op jit(solution)/shard_map/ppermute | solution.py:194
Sparse Core Ops, SparseCore 0:
  20.2 66.1 all-gather.1

commit v4 on v2

--- a/solution.py
+++ b/solution.py
@@ -23,16 +23,28 @@
                         yield h, x, c, l, y
 
 
+INNER, OUTER = (2, 3, 4, 5), (7, 6, 1, 0)
+
+
+def place(h, h2, x2):
+    l = (INNER if h2 == h else OUTER)[x2]
+    return l if h == 0 else L - 1 - l
+
+
+def chunk(h, l):
+    return next((h2, x2) for h2 in range(H) for x2 in range(X) if place(h, h2, x2) == l)
+
+
 def weight_perm(k):
     return [
-        (flat(h, x, c, l, y), flat(l // X, l % X, c, (h ^ k) * X + x, y))
+        (flat(h, x, c, l, y), flat(l // X, l % X, c, place(l // X, h ^ k, x), y))
         for h, x, c, l, y in coords()
     ]
 
 
 def result_perm(k):
     return [
-        (flat(h, x, c, l, y), flat(l // X, l % X, c, 2 * x + (h ^ k), y))
+        (flat(h, x, c, l, y), flat(*chunk(h, l), c, L - 1 - x if h ^ k else x, y))
         for h, x, c, l, y in coords()
     ]
 
@@ -73,16 +85,17 @@
 def contract(first, second, where, w, near, far):
     q, depth = near.shape
     cols = w.shape[3]
-    block = q // X
+    block = q // L
 
     def of_step(s, first, second, where):
-        return (where[0] + s + 1) % X, 0
+        to = (where[0] + s // 2 + 1) % X
+        return jnp.where(s % 2 == 0, to, L - 1 - to), 0
 
     return pl.pallas_call(
         contract_kernel,
         grid_spec=pltpu.PrefetchScalarGridSpec(
             num_scalar_prefetch=3,
-            grid=(X,),
+            grid=(L,),
             in_specs=[
                 pl.BlockSpec(w.shape, lambda s, *_: (0, 0, 0, 0)),
                 pl.BlockSpec((block, depth), of_step),
@@ -110,23 +123,28 @@
     def swap_core(v):
         return lax.ppermute(v, "c", shift(C, 1))
 
-    q_own, occ, b_own = fitting.shape
-    b_near = lax.all_gather(fitting.reshape(q_own, occ * b_own), "l", axis=0, tiled=True)
-
     n_mu, n_a = coefficients.shape
     part = n_mu // Y
+    mirror = [(i, H * L - 1 - i) for i in range(H * L)]
     piece = lax.dynamic_slice_in_dim(coefficients, y * part, part, 0)
-    piece = lax.ppermute(piece, "h", shift(H, 1))
+    piece = lax.ppermute(piece, ("h", "l"), mirror)
+
+    q_own, occ, b_own = fitting.shape
+    rows = amplitudes.shape[2]
+    info = jnp.pad(pair_list.astype(bf16), ((0, rows - 1), (0, 126)))
+    t_own = jnp.concatenate([amplitudes[0].T, info], axis=1)
+    b_near = fitting.reshape(q_own, occ * b_own)
+    piece, t_own, b_near = lax.optimization_barrier((piece, t_own, b_near))
+
+    b_near = lax.all_gather(b_near, "l", axis=0, tiled=True)
+
+    t_all = jnp.concatenate(
+        [t_own] + [lax.ppermute(t_own, "x", shift(X, k)) for k in range(1, X)], axis=0
+    )
     piece = jnp.broadcast_to(piece[None], (Y, part, n_a))
     c_far = lax.all_to_all(piece, "y", split_axis=0, concat_axis=0, tiled=True)
     c_far = c_far.reshape(n_mu, n_a)
 
-    rows = amplitudes.shape[2]
-    info = jnp.pad(pair_list.astype(bf16), ((0, rows - 1), (0, 126)))
-    t_own = jnp.concatenate([amplitudes[0].T, info], axis=1)
-    t_all = jnp.concatenate(
-        [t_own] + [lax.ppermute(t_own, "x", shift(X, k)) for k in range(1, X)], axis=0
-    )
     info = t_all.reshape(X, rows, -1)[:, 0, n_a:]
     info = jnp.broadcast_to(jnp.pad(info, ((0, 16 - X), (0, 0)))[None], (C, 16, n_mu))
     t_all = t_all[:, :n_a]

time: 205 us -> 234 us (1.14)
  the two profiles are of different devices: /device:TPU:136 before, /device:TPU:1 now
where the time goes in v4:
time: 234 us; the launch traced here: 229 us
  waiting for transfers between devices  117 us (50%)
  starting transfers between devices  83.5 us (36%)
  between operations  13.9 us (6%)
  local copies, waits for them, and re-layouts  5.03 us (2%)
  Pallas kernels  4.48 us (2%)
  other arithmetic  3.04 us (1%)
  matrix products  2.78 us (1%)
    all_gather x1, waiting for transfers between devices, on_device(): b_near = lax.all_gather(b_near, 'l', axis=0, tiled=True)  31.6 us
    ppermute x4, starting transfers between devices, swap_core(): return lax.ppermute(v, 'c', shift(C, 1))  23.4 us
    ppermute x2, waiting for transfers between devices, on_device(): received.append(lax.ppermute(w, AXES, weight_perm(k)))  22.2 us
    ppermute x2, waiting for transfers between devices, on_device(): total += lax.ppermute(piece, AXES, result_perm(k)).astype(f32)  21.5 us
    ppermute x3, waiting for transfers between devices, on_device(): summed += lax.ppermute(partial[k - 1], 'x', shift(X, k)).astype(f32)  15.6 us
    ppermute x2, starting transfers between devices, on_device(): total += lax.ppermute(piece, AXES, result_perm(k)).astype(f32)  10.8 us
    ppermute x2, starting transfers between devices, on_device(): received.append(lax.ppermute(w, AXES, weight_perm(k)))  10.6 us
    ppermute x3, starting transfers between devices, on_device(): lax.ppermute(t_own, 'x', shift(X, k))  10.5 us
  transfers between devices with their start and end apart: 20, of which 13 were waited for; matrix products, arithmetic and copies ran while one was open for 4% of the time, Pallas kernels for 0%

profile of v4, /device:TPU:1, one launch (start us, length us, event | category | flops | bytes accessed | tf_op | source)
XLA Modules:
  0.0 229.4 jit_solution(922033709874134779)
XLA Ops:
  6.5 8.8 %collective-permute-start.4 = (bf16[128,2048]{1,0:T(8,128)(2,1)}, bf16[128,2048]{1,0:T(8,128)(2,1)}, u32[]{:S(2)}, u32[]{:S(2)}) collective-permute-start(bf16[128,2048]{1,0:T(8,128)(2,1)} %param.6), channel_id=1, source_target_pairs={{0,32},{32,0},{1,33},{33,1},{2,34},{34,2},{3,35},{35,3},{4,36},{36... | collective-permute-start | bytes 1572872 | tf_op jit(solution)/shard_map/ppermute | solution.py:124
  15.3 0.9 constant_dynamic-slice_fusion.2
  16.2 5.7 %collective-permute-start = (bf16[32,2048]{1,0:T(8,128)(2,1)S(1)}, bf16[32,2048]{1,0:T(8,128)(2,1)S(1)}, u32[]{:S(2)}, u32[]{:S(2)}) collective-permute-start(bf16[32,2048]{1,0:T(8,128)(2,1)S(1)} %constant_dynamic-slice_fusion.2), channel_id=1, source_target_pairs={{0,284},{4,280},{8,276},{12,272},{16,268},{20,264},{24,260},{28,25... | collective-permute-start | bytes 393224 | tf_op jit(solution)/shard_map/ppermute | solution.py:130
  22.0 0.7 convert_element_type.39
  22.7 1.0 fusion.9
  23.6 1.6 copy.14
  25.3 9.0 %collective-permute-done = bf16[32,2048]{1,0:T(8,128)(2,1)S(1)} collective-permute-done((bf16[32,2048]{1,0:T(8,128)(2,1)S(1)}, bf16[32,2048]{1,0:T(8,128)(2,1)S(1)}, u32[]{:S(2)}, u32[]{:S(2)}) %collective-permute-start) | collective-permute-done | bytes 131104 | tf_op jit(solution)/shard_map/ppermute | solution.py:130
  34.3 3.1 %collective-permute-start.1 = (bf16[64,2176]{1,0:T(8,128)(2,1)S(1)}, bf16[64,2176]{1,0:T(8,128)(2,1)S(1)}, u32[]{:S(2)}, u32[]{:S(2)}) collective-permute-start(bf16[64,2176]{1,0:T(8,128)(2,1)S(1)} %fusion.9), channel_id=1, source_target_pairs={{0,64},{64,128},{128,192},{192,0},{1,65},{65,129},{129,193},{193,1... | collective-permute-start | bytes 835592 | tf_op jit(solution)/shard_map/ppermute | solution.py:142
  37.4 4.4 %collective-permute-start.2 = (bf16[64,2176]{1,0:T(8,128)(2,1)S(1)}, bf16[64,2176]{1,0:T(8,128)(2,1)S(1)}, u32[]{:S(2)}, u32[]{:S(2)}) collective-permute-start(bf16[64,2176]{1,0:T(8,128)(2,1)S(1)} %fusion.9), channel_id=1, source_target_pairs={{0,128},{64,192},{128,0},{192,64},{1,129},{65,193},{129,1},{193,65... | collective-permute-start | bytes 835592 | tf_op jit(solution)/shard_map/ppermute | solution.py:142
  41.8 3.1 %collective-permute-start.3 = (bf16[64,2176]{1,0:T(8,128)(2,1)S(1)}, bf16[64,2176]{1,0:T(8,128)(2,1)S(1)}, u32[]{:S(2)}, u32[]{:S(2)}) collective-permute-start(bf16[64,2176]{1,0:T(8,128)(2,1)S(1)} %fusion.9), channel_id=1, source_target_pairs={{0,192},{64,0},{128,64},{192,128},{1,193},{65,1},{129,65},{193,129... | collective-permute-start | bytes 835592 | tf_op jit(solution)/shard_map/ppermute | solution.py:142
  44.8 0.9 broadcast_in_dim.28
  45.7 4.2 %all-to-all-start = ((bf16[4,32,2048]{2,1,0:T(8,128)(2,1)}), bf16[4,32,2048]{2,1,0:T(8,128)(2,1)S(1)}, u32[]{:S(2)}, u32[]{:S(2)}) async-start(bf16[4,32,2048]{2,1,0:T(8,128)(2,1)} %broadcast_in_dim.28), calls=%async_computation | async-start | bytes 1048576 | tf_op jit(solution)/shard_map/all_to_all | solution.py:145
  49.9 0.0 all-gather.2.cloned.1.call-start
  49.9 0.7 all-gather.2.cloned.1.call-update
  50.6 0.0 copy-start.1
  50.6 0.0 collective-permute-done.1
  50.7 1.3 collective-permute-done.2
  52.0 1.2 collective-permute-done.3
  53.2 4.2 %all-to-all-done = bf16[4,32,2048]{2,1,0:T(8,128)(2,1)S(1)} async-done(((bf16[4,32,2048]{2,1,0:T(8,128)(2,1)}), bf16[4,32,2048]{2,1,0:T(8,128)(2,1)S(1)}, u32[]{:S(2)}, u32[]{:S(2)}) %all-to-all-start) | async-done | bytes 524320 | tf_op jit(solution)/shard_map/all_to_all | solution.py:145
  57.4 4.8 %collective-permute-start.6 = (bf16[128,2048]{1,0:T(8,128)(2,1)S(1)}, bf16[128,2048]{1,0:T(8,128)(2,1)S(1)}, u32[]{:S(2)}, u32[]{:S(2)}) collective-permute-start(bf16[128,2048]{1,0:T(8,128)(2,1)S(1)} %bitcast.51), channel_id=1, source_target_pairs={{0,32},{32,0},{1,33},{33,1},{2,34},{34,2},{3,35},{35,3},{4,36},{36... | collective-permute-start | bytes 1572872 | tf_op jit(solution)/shard_map/ppermute | solution.py:124
  62.2 0.0 copy-done.1
  62.2 0.4 fusion
  62.7 0.4 fusion.2
  63.1 0.0 collective-permute-done.4
  63.1 1.5 fusion.1
  64.6 0.0 collective-permute-done.6
  64.6 0.4 fusion.3
  65.1 1.9 collective-permute-start.5
  67.0 8.7 %collective-permute-start.7 = (bf16[2,272,128]{2,1,0:T(8,128)(2,1)S(1)}, bf16[2,272,128]{2,1,0:T(8,128)(2,1)S(1)}, u32[]{:S(2)}, u32[]{:S(2)}) collective-permute-start(bf16[2,272,128]{2,1,0:T(8,128)(2,1)S(1)} %get-tuple-element.27), channel_id=1, source_target_pairs={{0,28},{1,29},{2,30},{3,31},{4,92},{5,93},{6,94},{7,95},{8,156},{9... | collective-permute-start | bytes 417800 | tf_op jit(solution)/shard_map/ppermute | solution.py:159
  75.7 22.2 %collective-permute-done.5 = bf16[2,272,128]{2,1,0:T(8,128)(2,1)S(1)} collective-permute-done((bf16[2,272,128]{2,1,0:T(8,128)(2,1)S(1)}, bf16[2,272,128]{2,1,0:T(8,128)(2,1)S(1)}, u32[]{:S(2)}, u32[]{:S(2)}) %collective-permute-start.5) | collective-permute-done | bytes 139296 | tf_op jit(solution)/shard_map/ppermute | solution.py:159
  97.9 0.0 collective-permute-done.7
  98.0 2.8 %collective-permute-start.8 = (bf16[2,272,128]{2,1,0:T(8,128)(2,1)S(1)}, bf16[2,272,128]{2,1,0:T(8,128)(2,1)S(1)}, u32[]{:S(2)}, u32[]{:S(2)}) collective-permute-start(bf16[2,272,128]{2,1,0:T(8,128)(2,1)S(1)} %pad_maximum_fusion.3), channel_id=1, source_target_pairs={{0,32},{32,0},{1,33},{33,1},{2,34},{34,2},{3,35},{35,3},{4,36},{36... | collective-permute-start | bytes 417800 | tf_op jit(solution)/shard_map/ppermute | solution.py:124
  100.8 1.0 collective-permute-done.8
  101.8 31.6 %all-gather.2.cloned.1.call-done.near_ref = bf16[1536,512]{1,0:T(8,128)(2,1)} async-done(((bf16[192,512]{1,0:T(8,128)(2,1)}), bf16[1536,512]{1,0:T(8,128)(2,1)}) %all-gather.2.cloned.1.call-update) | async-done | bytes 1572880 | tf_op jit(solution)/shard_map/all_gather | solution.py:139
  133.4 6.9 %collective-permute-start.12 = (bf16[1536,512]{1,0:T(8,128)(2,1)}, bf16[1536,512]{1,0:T(8,128)(2,1)S(1)}, u32[]{:S(2)}, u32[]{:S(2)}) collective-permute-start(bf16[1536,512]{1,0:T(8,128)(2,1)} %all-gather.2.cloned.1.call-done.near_ref), channel_id=1, source_target_pairs={{0,32},{32,0},{1,33},{33,1},{2,34},{34,2},{3,35},{35,3},{4,36},{36... | collective-permute-start | bytes 4718600 | tf_op jit(solution)/shard_map/ppermute | solution.py:124
  140.4 0.1 pad_add_fusion.where_ref
  140.5 3.1 %collective-permute-start.9 = (bf16[16,64,128]{2,1,0:T(8,128)(2,1)S(1)}, bf16[16,64,128]{2,1,0:T(8,128)(2,1)S(1)}, u32[]{:S(2)}, u32[]{:S(2)}) collective-permute-start(bf16[16,64,128]{2,1,0:T(8,128)(2,1)S(1)} %bitcast.44), channel_id=1, source_target_pairs={{0,1},{1,2},{2,3},{3,0},{4,5},{5,6},{6,7},{7,4},{8,9},{9,10},{10,1... | collective-permute-start | bytes 786440 | tf_op jit(solution)/shard_map/ppermute | solution.py:167
  143.6 0.1 fusion.13
  143.7 0.1 copy.9
  143.8 0.1 copy.10
  143.8 4.4 %collective-permute-start.10 = (bf16[16,64,128]{2,1,0:T(8,128)(2,1)S(1)}, bf16[16,64,128]{2,1,0:T(8,128)(2,1)S(1)}, u32[]{:S(2)}, u32[]{:S(2)}) collective-permute-start(bf16[16,64,128]{2,1,0:T(8,128)(2,1)S(1)} %bitcast.45), channel_id=1, source_target_pairs={{0,2},{1,3},{2,0},{3,1},{4,6},{5,7},{6,4},{7,5},{8,10},{9,11},{10,... | collective-permute-start | bytes 786440 | tf_op jit(solution)/shard_map/ppermute | solution.py:167
  148.3 2.2 collective-permute-start.11
  150.5 0.2 broadcast_in_dim.29
  150.8 0.0 copy-start
  150.8 0.7 collective-permute-done.9
  151.5 6.7 %collective-permute-done.10 = bf16[16,64,128]{2,1,0:T(8,128)(2,1)S(1)} collective-permute-done((bf16[16,64,128]{2,1,0:T(8,128)(2,1)S(1)}, bf16[16,64,128]{2,1,0:T(8,128)(2,1)S(1)}, u32[]{:S(2)}, u32[]{:S(2)}) %collective-permute-start.10) | collective-permute-done | bytes 262176 | tf_op jit(solution)/shard_map/ppermute | solution.py:167
  158.2 1.3 collective-permute-done.11
  159.6 0.0 collective-permute-done.12.far_ref
  159.6 0.0 copy-done
  159.6 4.5 %shard_map.46 = bf16[1536,512]{1,0:T(8,128)(2,1)S(1)} custom-call(s32[16]{0:T(128)S(1)} %bitcast.42, s32[16]{0:T(128)S(1)} %bitcast.43, s32[2]{0:T(128)S(1)} %pad_add_fusion.where_ref, bf16[4,16,64,128]{3,2,1,0:T(8,128)(2,1)S(1)} %bitcast_dynamic-update-slice_fusion.w_ref, bf16[1536,512]{1,0:T(8,128)(2,1)S(1)} %copy-done, ...), custom_call_target="tpu_custom_call" | custom-call | flops 1610612736 | bytes 6291456 | tf_op jit(solution)/shard_map/pallas_call | solution.py:94
  164.1 0.1 fusion.10
  164.2 1.9 collective-permute-start.13
  166.1 2.1 collective-permute-start.14
  168.2 4.4 %collective-permute-start.15 = (bf16[384,512]{1,0:T(8,128)(2,1)S(1)}, bf16[384,512]{1,0:T(8,128)(2,1)}, u32[]{:S(2)}, u32[]{:S(2)}) collective-permute-start(bf16[384,512]{1,0:T(8,128)(2,1)S(1)} %get-tuple-element.16), channel_id=1, source_target_pairs={{0,192},{64,0},{128,64},{192,128},{1,193},{65,1},{129,65},{193,129... | collective-permute-start | bytes 1179656 | tf_op jit(solution)/shard_map/ppermute | solution.py:179
  172.6 12.6 %collective-permute-done.13 = bf16[384,512]{1,0:T(8,128)(2,1)S(1)} collective-permute-done((bf16[384,512]{1,0:T(8,128)(2,1)S(1)}, bf16[384,512]{1,0:T(8,128)(2,1)S(1)}, u32[]{:S(2)}, u32[]{:S(2)}) %collective-permute-start.13) | collective-permute-done | bytes 393248 | tf_op jit(solution)/shard_map/ppermute | solution.py:179
  185.2 0.0 collective-permute-done.14
  185.2 3.0 %collective-permute-done.15 = bf16[384,512]{1,0:T(8,128)(2,1)} collective-permute-done((bf16[384,512]{1,0:T(8,128)(2,1)S(1)}, bf16[384,512]{1,0:T(8,128)(2,1)}, u32[]{:S(2)}, u32[]{:S(2)}) %collective-permute-start.15) | collective-permute-done | bytes 393248 | tf_op jit(solution)/shard_map/ppermute | solution.py:179
  188.2 1.2 add_convert_fusion
  189.5 8.9 %collective-permute-start.16 = (bf16[192,512]{1,0:T(8,128)(2,1)S(1)}, bf16[192,512]{1,0:T(8,128)(2,1)S(1)}, u32[]{:S(2)}, u32[]{:S(2)}) collective-permute-start(bf16[192,512]{1,0:T(8,128)(2,1)S(1)} %get-tuple-element.18), channel_id=1, source_target_pairs={{0,448},{1,449},{2,450},{3,451},{4,384},{5,385},{6,386},{7,387},{8... | collective-permute-start | bytes 589832 | tf_op jit(solution)/shard_map/ppermute | solution.py:185
  198.4 1.9 collective-permute-start.17
  200.3 21.5 %collective-permute-done.16 = bf16[192,512]{1,0:T(8,128)(2,1)S(1)} collective-permute-done((bf16[192,512]{1,0:T(8,128)(2,1)S(1)}, bf16[192,512]{1,0:T(8,128)(2,1)S(1)}, u32[]{:S(2)}, u32[]{:S(2)}) %collective-permute-start.16) | collective-permute-done | bytes 196640 | tf_op jit(solution)/shard_map/ppermute | solution.py:185
  221.8 0.0 collective-permute-done.17
  221.8 0.1 add_convert_fusion.1
  221.8 0.7 reshape.33
  (21 shorter events, 0.4 us)
Async XLA Ops:
  6.5 56.6 %collective-permute-start.4 = (bf16[128,2048]{1,0:T(8,128)(2,1)}, bf16[128,2048]{1,0:T(8,128)(2,1)}, u32[]{:S(2)}, u32[]{:S(2)}) collective-permute-start(bf16[128,2048]{1,0:T(8,128)(2,1)} %param.6), channel_id=1, source_target_pairs={{0,32},{32,0},{1,33},{33,1},{2,34},{34,2},{3,35},{35,3},{4,36},{36... | collective-permute-start | bytes 1572872 | tf_op jit(solution)/shard_map/ppermute | solution.py:124
  16.2 18.0 %collective-permute-start = (bf16[32,2048]{1,0:T(8,128)(2,1)S(1)}, bf16[32,2048]{1,0:T(8,128)(2,1)S(1)}, u32[]{:S(2)}, u32[]{:S(2)}) collective-permute-start(bf16[32,2048]{1,0:T(8,128)(2,1)S(1)} %constant_dynamic-slice_fusion.2), channel_id=1, source_target_pairs={{0,284},{4,280},{8,276},{12,272},{16,268},{20,264},{24,260},{28,25... | collective-permute-start | bytes 393224 | tf_op jit(solution)/shard_map/ppermute | solution.py:130
  34.3 16.4 %collective-permute-start.1 = (bf16[64,2176]{1,0:T(8,128)(2,1)S(1)}, bf16[64,2176]{1,0:T(8,128)(2,1)S(1)}, u32[]{:S(2)}, u32[]{:S(2)}) collective-permute-start(bf16[64,2176]{1,0:T(8,128)(2,1)S(1)} %fusion.9), channel_id=1, source_target_pairs={{0,64},{64,128},{128,192},{192,0},{1,65},{65,129},{129,193},{193,1... | collective-permute-start | bytes 835592 | tf_op jit(solution)/shard_map/ppermute | solution.py:142
  37.4 14.5 %collective-permute-start.2 = (bf16[64,2176]{1,0:T(8,128)(2,1)S(1)}, bf16[64,2176]{1,0:T(8,128)(2,1)S(1)}, u32[]{:S(2)}, u32[]{:S(2)}) collective-permute-start(bf16[64,2176]{1,0:T(8,128)(2,1)S(1)} %fusion.9), channel_id=1, source_target_pairs={{0,128},{64,192},{128,0},{192,64},{1,129},{65,193},{129,1},{193,65... | collective-permute-start | bytes 835592 | tf_op jit(solution)/shard_map/ppermute | solution.py:142
  41.8 11.4 %collective-permute-start.3 = (bf16[64,2176]{1,0:T(8,128)(2,1)S(1)}, bf16[64,2176]{1,0:T(8,128)(2,1)S(1)}, u32[]{:S(2)}, u32[]{:S(2)}) collective-permute-start(bf16[64,2176]{1,0:T(8,128)(2,1)S(1)} %fusion.9), channel_id=1, source_target_pairs={{0,192},{64,0},{128,64},{192,128},{1,193},{65,1},{129,65},{193,129... | collective-permute-start | bytes 835592 | tf_op jit(solution)/shard_map/ppermute | solution.py:142
  45.7 11.7 %all-to-all-start = ((bf16[4,32,2048]{2,1,0:T(8,128)(2,1)}), bf16[4,32,2048]{2,1,0:T(8,128)(2,1)S(1)}, u32[]{:S(2)}, u32[]{:S(2)}) async-start(bf16[4,32,2048]{2,1,0:T(8,128)(2,1)} %broadcast_in_dim.28), calls=%async_computation | async-start | bytes 1048576 | tf_op jit(solution)/shard_map/all_to_all | solution.py:145
  49.9 83.5 %all-gather.2.cloned.1.call-start = ((), (), s32[]{:S(2)}) async-start(), calls=%async_computation.1 | async-start | bytes 1769472 | tf_op jit(solution)/shard_map/all_gather | solution.py:139
  50.6 11.6 %copy-start.1 = (bf16[128,2048]{1,0:T(8,128)(2,1)S(1)}, bf16[128,2048]{1,0:T(8,128)(2,1)}, u32[]{:S(2)}) copy-start(bf16[128,2048]{1,0:T(8,128)(2,1)} %param.6) | copy-start | bytes 1572868
  57.4 7.2 %collective-permute-start.6 = (bf16[128,2048]{1,0:T(8,128)(2,1)S(1)}, bf16[128,2048]{1,0:T(8,128)(2,1)S(1)}, u32[]{:S(2)}, u32[]{:S(2)}) collective-permute-start(bf16[128,2048]{1,0:T(8,128)(2,1)S(1)} %bitcast.51), channel_id=1, source_target_pairs={{0,32},{32,0},{1,33},{33,1},{2,34},{34,2},{3,35},{35,3},{4,36},{36... | collective-permute-start | bytes 1572872 | tf_op jit(solution)/shard_map/ppermute | solution.py:124
  65.1 32.8 %collective-permute-start.5 = (bf16[2,272,128]{2,1,0:T(8,128)(2,1)S(1)}, bf16[2,272,128]{2,1,0:T(8,128)(2,1)S(1)}, u32[]{:S(2)}, u32[]{:S(2)}) collective-permute-start(bf16[2,272,128]{2,1,0:T(8,128)(2,1)S(1)} %get-tuple-element.26), channel_id=1, source_target_pairs={{0,8},{1,9},{2,10},{3,11},{4,72},{5,73},{6,74},{7,75},{8,136},{9,1... | collective-permute-start | bytes 417800 | tf_op jit(solution)/shard_map/ppermute | solution.py:159
  67.0 30.9 %collective-permute-start.7 = (bf16[2,272,128]{2,1,0:T(8,128)(2,1)S(1)}, bf16[2,272,128]{2,1,0:T(8,128)(2,1)S(1)}, u32[]{:S(2)}, u32[]{:S(2)}) collective-permute-start(bf16[2,272,128]{2,1,0:T(8,128)(2,1)S(1)} %get-tuple-element.27), channel_id=1, source_target_pairs={{0,28},{1,29},{2,30},{3,31},{4,92},{5,93},{6,94},{7,95},{8,156},{9... | collective-permute-start | bytes 417800 | tf_op jit(solution)/shard_map/ppermute | solution.py:159
  98.0 3.8 %collective-permute-start.8 = (bf16[2,272,128]{2,1,0:T(8,128)(2,1)S(1)}, bf16[2,272,128]{2,1,0:T(8,128)(2,1)S(1)}, u32[]{:S(2)}, u32[]{:S(2)}) collective-permute-start(bf16[2,272,128]{2,1,0:T(8,128)(2,1)S(1)} %pad_maximum_fusion.3), channel_id=1, source_target_pairs={{0,32},{32,0},{1,33},{33,1},{2,34},{34,2},{3,35},{35,3},{4,36},{36... | collective-permute-start | bytes 417800 | tf_op jit(solution)/shard_map/ppermute | solution.py:124
  133.4 26.2 %collective-permute-start.12 = (bf16[1536,512]{1,0:T(8,128)(2,1)}, bf16[1536,512]{1,0:T(8,128)(2,1)S(1)}, u32[]{:S(2)}, u32[]{:S(2)}) collective-permute-start(bf16[1536,512]{1,0:T(8,128)(2,1)} %all-gather.2.cloned.1.call-done.near_ref), channel_id=1, source_target_pairs={{0,32},{32,0},{1,33},{33,1},{2,34},{34,2},{3,35},{35,3},{4,36},{36... | collective-permute-start | bytes 4718600 | tf_op jit(solution)/shard_map/ppermute | solution.py:124
  140.5 11.0 %collective-permute-start.9 = (bf16[16,64,128]{2,1,0:T(8,128)(2,1)S(1)}, bf16[16,64,128]{2,1,0:T(8,128)(2,1)S(1)}, u32[]{:S(2)}, u32[]{:S(2)}) collective-permute-start(bf16[16,64,128]{2,1,0:T(8,128)(2,1)S(1)} %bitcast.44), channel_id=1, source_target_pairs={{0,1},{1,2},{2,3},{3,0},{4,5},{5,6},{6,7},{7,4},{8,9},{9,10},{10,1... | collective-permute-start | bytes 786440 | tf_op jit(solution)/shard_map/ppermute | solution.py:167
  143.8 14.4 %collective-permute-start.10 = (bf16[16,64,128]{2,1,0:T(8,128)(2,1)S(1)}, bf16[16,64,128]{2,1,0:T(8,128)(2,1)S(1)}, u32[]{:S(2)}, u32[]{:S(2)}) collective-permute-start(bf16[16,64,128]{2,1,0:T(8,128)(2,1)S(1)} %bitcast.45), channel_id=1, source_target_pairs={{0,2},{1,3},{2,0},{3,1},{4,6},{5,7},{6,4},{7,5},{8,10},{9,11},{10,... | collective-permute-start | bytes 786440 | tf_op jit(solution)/shard_map/ppermute | solution.py:167
  148.3 11.3 %collective-permute-start.11 = (bf16[16,64,128]{2,1,0:T(8,128)(2,1)S(1)}, bf16[16,64,128]{2,1,0:T(8,128)(2,1)S(1)}, u32[]{:S(2)}, u32[]{:S(2)}) collective-permute-start(bf16[16,64,128]{2,1,0:T(8,128)(2,1)S(1)} %bitcast.46), channel_id=1, source_target_pairs={{0,3},{1,0},{2,1},{3,2},{4,7},{5,4},{6,5},{7,6},{8,11},{9,8},{10,9... | collective-permute-start | bytes 786440 | tf_op jit(solution)/shard_map/ppermute | solution.py:167
  150.8 8.8 %copy-start = (bf16[1536,512]{1,0:T(8,128)(2,1)S(1)}, bf16[1536,512]{1,0:T(8,128)(2,1)}, u32[]{:S(2)}) copy-start(bf16[1536,512]{1,0:T(8,128)(2,1)} %all-gather.2.cloned.1.call-done.near_ref) | copy-start | bytes 4718596
  164.2 21.0 %collective-permute-start.13 = (bf16[384,512]{1,0:T(8,128)(2,1)S(1)}, bf16[384,512]{1,0:T(8,128)(2,1)S(1)}, u32[]{:S(2)}, u32[]{:S(2)}) collective-permute-start(bf16[384,512]{1,0:T(8,128)(2,1)S(1)} %get-tuple-element.15), channel_id=1, source_target_pairs={{0,64},{64,128},{128,192},{192,0},{1,65},{65,129},{129,193},{193,1... | collective-permute-start | bytes 1179656 | tf_op jit(solution)/shard_map/ppermute | solution.py:179
  166.1 19.1 %collective-permute-start.14 = (bf16[384,512]{1,0:T(8,128)(2,1)S(1)}, bf16[384,512]{1,0:T(8,128)(2,1)S(1)}, u32[]{:S(2)}, u32[]{:S(2)}) collective-permute-start(bf16[384,512]{1,0:T(8,128)(2,1)S(1)} %get-tuple-element.17), channel_id=1, source_target_pairs={{0,128},{64,192},{128,0},{192,64},{1,129},{65,193},{129,1},{193,65... | collective-permute-start | bytes 1179656 | tf_op jit(solution)/shard_map/ppermute | solution.py:179
  168.2 20.0 %collective-permute-start.15 = (bf16[384,512]{1,0:T(8,128)(2,1)S(1)}, bf16[384,512]{1,0:T(8,128)(2,1)}, u32[]{:S(2)}, u32[]{:S(2)}) collective-permute-start(bf16[384,512]{1,0:T(8,128)(2,1)S(1)} %get-tuple-element.16), channel_id=1, source_target_pairs={{0,192},{64,0},{128,64},{192,128},{1,193},{65,1},{129,65},{193,129... | collective-permute-start | bytes 1179656 | tf_op jit(solution)/shard_map/ppermute | solution.py:179
  189.5 32.3 %collective-permute-start.16 = (bf16[192,512]{1,0:T(8,128)(2,1)S(1)}, bf16[192,512]{1,0:T(8,128)(2,1)S(1)}, u32[]{:S(2)}, u32[]{:S(2)}) collective-permute-start(bf16[192,512]{1,0:T(8,128)(2,1)S(1)} %get-tuple-element.18), channel_id=1, source_target_pairs={{0,448},{1,449},{2,450},{3,451},{4,384},{5,385},{6,386},{7,387},{8... | collective-permute-start | bytes 589832 | tf_op jit(solution)/shard_map/ppermute | solution.py:185
  198.4 23.4 %collective-permute-start.17 = (bf16[192,512]{1,0:T(8,128)(2,1)S(1)}, bf16[192,512]{1,0:T(8,128)(2,1)S(1)}, u32[]{:S(2)}, u32[]{:S(2)}) collective-permute-start(bf16[192,512]{1,0:T(8,128)(2,1)S(1)} %get-tuple-element.19), channel_id=1, source_target_pairs={{0,476},{1,477},{2,478},{3,479},{4,412},{5,413},{6,414},{7,415},{8... | collective-permute-start | bytes 589832 | tf_op jit(solution)/shard_map/ppermute | solution.py:185
Sparse Core Ops, SparseCore 0:
  52.8 80.5 all-gather.1

commit v5 on v3

v5 whole, which is shorter than its diff:
```python
import jax
import jax.numpy as jnp
from jax import lax
from jax.experimental import pallas as pl
from jax.experimental.pallas import tpu as pltpu
from jax.sharding import Mesh, PartitionSpec as P

H, X, C, L, Y = 2, 4, 2, 8, 4
AXES = ("h", "x", "c", "l", "y")
OCC = 4


def flat(h, x, c, l, y):
    return (((h * X + x) * C + c) * L + l) * Y + y


def coords():
    for h in range(H):
        for x in range(X):
            for c in range(C):
                for l in range(L):
                    for y in range(Y):
                        yield h, x, c, l, y


INNER, OUTER = (2, 3, 4, 5), (7, 6, 1, 0)


def place(h, h2, x2):
    l = (INNER if h2 == h else OUTER)[x2]
    return l if h == 0 else L - 1 - l


def chunk(h, l):
    return next((h2, x2) for h2 in range(H) for x2 in range(X) if place(h, h2, x2) == l)


def weight_perm(k):
    return [
        (flat(h, x, c, l, y), flat(l // X, l % X, c, place(l // X, h ^ k, x), y))
        for h, x, c, l, y in coords()
    ]


def result_perm(k):
    return [
        (flat(h, x, c, l, y), flat(*chunk(h, l), c, L - 1 - x if h ^ k else x, y))
        for h, x, c, l, y in coords()
    ]


def shift(n, k):
    return [(i, (i + k) % n) for i in range(n)]


def assemble(first_ref, second_ref, w_ref, acc_ref, s_ref):
    slots, rows, cols = w_ref.shape[1:]
    acc_ref[...] = jnp.zeros_like(acc_ref)

    def add(slot, _):
        first, second = first_ref[slot], second_ref[slot]
        at_col = pl.multiple_of(first * cols, cols)
        for z in range(Y):
            half, part = z // 2, z % 2
            at_row = pl.multiple_of((half * OCC + second) * (2 * rows) + part * rows, rows)
            here = (pl.ds(at_row, rows), pl.ds(at_col, cols))
            acc_ref[here] += w_ref[z, slot].astype(jnp.float32)
        return 0

    lax.fori_loop(0, slots, add, 0)
    s_ref[...] = acc_ref[...].astype(jnp.bfloat16)


def multiply(where_ref, near_ref, far_ref, s_ref, out_ref):
    depth = near_ref.shape[1]
    at_near = pl.multiple_of(where_ref[1] * depth, depth)
    at_far = pl.multiple_of((1 - where_ref[1]) * depth, depth)
    f32 = jnp.float32
    total = jnp.dot(near_ref[...], s_ref[pl.ds(at_near, depth)], preferred_element_type=f32)
    total += jnp.dot(far_ref[...], s_ref[pl.ds(at_far, depth)], preferred_element_type=f32)
    out_ref[...] = total.astype(jnp.bfloat16)


def first_kernel(
    first_ref, second_ref, where_ref, w_ref, near_ref, far_ref, out_ref, s_ref, acc_ref
):
    @pl.when(pl.program_id(0) == 0)
    def _():
        assemble(first_ref, second_ref, w_ref, acc_ref, s_ref)

    multiply(where_ref, near_ref, far_ref, s_ref, out_ref)


def second_kernel(where_ref, near_ref, far_ref, s_ref, out_ref):
    multiply(where_ref, near_ref, far_ref, s_ref, out_ref)


def part_of(k):
    def block(s, *refs):
        where_ref = refs[-1]
        to = (where_ref[2] + s + 1) % X
        return jnp.where((where_ref[0] ^ k) == 0, to, L - 1 - to), 0

    return block


def whole(array):
    return pl.BlockSpec(array.shape, lambda s, *_: (0,) * array.ndim)


def contract(first, second, where, w, near, far):
    q, depth = near.shape
    cols = OCC * w.shape[3]
    block = q // (2 * X)
    out = jax.ShapeDtypeStruct((q // 2, cols), jnp.bfloat16)
    out_spec = pl.BlockSpec((block, cols), lambda s, *_: (s, 0))
    s_shape = jax.ShapeDtypeStruct((2 * depth, cols), jnp.bfloat16)
    params = pltpu.CompilerParams(vmem_limit_bytes=32 * 1024 * 1024)
    cost = pl.CostEstimate(
        flops=2 * q * depth * cols, bytes_accessed=4 * 2**20, transcendentals=0
    )
    rows = [pl.BlockSpec((block, depth), part_of(0))] * 2
    one, s = pl.pallas_call(
        first_kernel,
        grid_spec=pltpu.PrefetchScalarGridSpec(
            num_scalar_prefetch=3,
            grid=(X,),
            in_specs=[whole(w)] + rows,
            out_specs=[out_spec, whole(s_shape)],
            scratch_shapes=[pltpu.VMEM(s_shape.shape, jnp.float32)],
        ),
        out_shape=[out, s_shape],
        compiler_params=params,
        cost_estimate=cost,
    )(first, second, where, w, near, far)
    rows = [pl.BlockSpec((block, depth), part_of(1))] * 2
    two = pl.pallas_call(
        second_kernel,
        grid_spec=pltpu.PrefetchScalarGridSpec(
            num_scalar_prefetch=1, grid=(X,), in_specs=rows + [whole(s)], out_specs=out_spec
        ),
        out_shape=out,
        compiler_params=params,
        cost_estimate=cost,
    )(where, near, far, s)
    return one, two


def on_device(amplitudes, fitting, coefficients, pair_list):
    h, x, c = lax.axis_index("h"), lax.axis_index("x"), lax.axis_index("c")
    y = lax.axis_index("y")
    f32, bf16 = jnp.float32, jnp.bfloat16

    def swap_core(v):
        return lax.ppermute(v, "c", shift(C, 1))

    q_own, occ, b_own = fitting.shape
    b_near = fitting.reshape(q_own, occ * b_own)
    b_near, coefficients, amplitudes = lax.optimization_barrier(
        (b_near, coefficients, amplitudes)
    )
    b_near = lax.all_gather(b_near, "l", axis=0, tiled=True)

    n_mu, n_a = coefficients.shape
    part = n_mu // Y
    mirror = [(i, H * L - 1 - i) for i in range(H * L)]
    piece = lax.dynamic_slice_in_dim(coefficients, y * part, part, 0)
    piece = lax.ppermute(piece, ("h", "l"), mirror)

    rows = amplitudes.shape[2]
    info = jnp.pad(pair_list.astype(bf16), ((0, rows - 1), (0, 126)))
    t_own = jnp.concatenate([amplitudes[0].T, info], axis=1)
    c_other = swap_core(coefficients)
    c_other, t_own = lax.optimization_barrier((c_other, t_own))

    t_all = jnp.concatenate(
        [t_own] + [lax.ppermute(t_own, "x", shift(X, k)) for k in range(1, X)], axis=0
    )
    info = t_all.reshape(X, rows, -1)[:, 0, n_a:]
    info = jnp.broadcast_to(jnp.pad(info, ((0, 16 - X), (0, 0)))[None], (C, 16, n_mu))
    t_all = t_all[:, :n_a]

    slots, n_b = H * C * X, X * rows

    def weights(*parts):
        w = [
            lax.dot_general(t_all, m, (((1,), (1,)), ((), ())), preferred_element_type=f32)
            for m in parts
        ]
        return jnp.concatenate([jnp.stack(w).astype(bf16), info], axis=1)

    def send(w, k):
        w = lax.ppermute(w, AXES, weight_perm(k))
        return w[0], swap_core(w[1])

    w_near, piece = lax.optimization_barrier((weights(coefficients, c_other), piece))
    w_near = send(w_near, 0)
    piece = jnp.broadcast_to(piece[None], (Y, part, n_a))
    c_far = lax.all_to_all(piece, "y", split_axis=0, concat_axis=0, tiled=True)
    c_far = c_far.reshape(n_mu, n_a)
    w_far = send(weights(c_far, swap_core(c_far)), 1)

    w = jnp.stack(w_near + w_far)
    pairs = w[:, n_b : n_b + X, :2].reshape(slots, 2).astype(jnp.int32)
    w = w[:, :n_b].reshape(slots, rows, n_mu)
    w, b_near = lax.optimization_barrier((w, b_near))
    pieces = [w] + [lax.ppermute(w, "y", shift(Y, k)) for k in range(1, Y)]
    w_all = jnp.zeros((Y,) + w.shape, bf16)
    for k, piece in enumerate(pieces):
        w_all = lax.dynamic_update_slice_in_dim(w_all, piece[None], (y - k) % Y, 0)
    b_far = swap_core(b_near)

    where = jnp.stack([h, c, x]).astype(jnp.int32)
    parts = contract(pairs[:, 0], pairs[:, 1], where, w_all, b_near, b_far)
    total = 0
    for k, v in enumerate(parts):
        v = v.reshape(X, q_own, -1)
        summed = v[X - 1].astype(f32)
        for n in range(1, X):
            summed += lax.ppermute(v[n - 1], "x", shift(X, n)).astype(f32)
        total += lax.ppermute(summed.astype(bf16), AXES, result_perm(k)).astype(f32)
    return total.astype(bf16).reshape(q_own, occ, n_mu)


def solution(mesh):
    fine = Mesh(mesh.devices.reshape(H, X, C, L, Y), AXES)
    pair, aux = ("h", "x", "c"), ("l", "y")
    in_specs = (P(pair, None, aux), P(aux, None, pair), P(pair, None), P(pair, None))
    out_specs = P(aux, None, pair)
    return jax.shard_map(
        on_device, mesh=fine, in_specs=in_specs, out_specs=out_specs, check_vma=False
    )
```

time: 225 us -> 209 us (0.929)
  the two profiles are of different devices: /device:TPU:128 before, /device:TPU:1 now
where the time goes in v5:
time: 209 us; the launch traced here: 205 us
  starting transfers between devices  100 us (48%)
  waiting for transfers between devices  62.1 us (30%)
  between operations  14.1 us (7%)
  blocking collectives  11.9 us (6%)
  local copies, waits for them, and re-layouts  6.23 us (3%)
  Pallas kernels  4.97 us (2%)
  other arithmetic  3.37 us (2%)
    ppermute x6, starting transfers between devices, on_device(): summed += lax.ppermute(v[n - 1], 'x', shift(X, n)).astype(f32)  29.3 us
    ppermute x5, starting transfers between devices, swap_core(): return lax.ppermute(v, 'c', shift(C, 1))  22.9 us
    ppermute x2, waiting for transfers between devices, on_device(): total += lax.ppermute(summed.astype(bf16), AXES, result_perm(k)).astype(f32)  22.1 us
    ppermute x2, waiting for transfers between devices, send(): w = lax.ppermute(w, AXES, weight_perm(k))  20.7 us
    all_to_all x1, blocking collectives, on_device(): c_far = lax.all_to_all(piece, 'y', split_axis=0, concat_axis=0, tiled=True)  11.9 us
    ppermute x2, starting transfers between devices, on_device(): total += lax.ppermute(summed.astype(bf16), AXES, result_perm(k)).astype(f32)  11.5 us
    ppermute x2, starting transfers between devices, send(): w = lax.ppermute(w, AXES, weight_perm(k))  11.5 us
    ppermute x3, starting transfers between devices, on_device(): lax.ppermute(t_own, 'x', shift(X, k))  10.7 us
  transfers between devices with their start and end apart: 23, of which 8 were waited for; matrix products, arithmetic and copies ran while one was open for 4% of the time, Pallas kernels for 1%

profile of v5, /device:TPU:1, one launch (start us, length us, event | category | flops | bytes accessed | tf_op | source)
XLA Modules:
  0.0 204.8 jit_solution(8577940792634713957)
XLA Ops:
  6.5 1.6 copy.38
  8.2 8.8 %collective-permute-start = (bf16[128,2048]{1,0:T(8,128)(2,1)}, bf16[128,2048]{1,0:T(8,128)(2,1)S(1)}, u32[]{:S(2)}, u32[]{:S(2)}) collective-permute-start(bf16[128,2048]{1,0:T(8,128)(2,1)} %param.6), channel_id=1, source_target_pairs={{0,32},{32,0},{1,33},{33,1},{2,34},{34,2},{3,35},{35,3},{4,36},{36... | collective-permute-start | bytes 1572872 | tf_op jit(solution)/shard_map/ppermute | solution.py:155
  17.0 0.9 constant_dynamic-slice_fusion
  17.9 5.7 %collective-permute-start.4 = (bf16[32,2048]{1,0:T(8,128)(2,1)S(1)}, bf16[32,2048]{1,0:T(8,128)(2,1)S(1)}, u32[]{:S(2)}, u32[]{:S(2)}) collective-permute-start(bf16[32,2048]{1,0:T(8,128)(2,1)S(1)} %constant_dynamic-slice_fusion), channel_id=1, source_target_pairs={{0,284},{4,280},{8,276},{12,272},{16,268},{20,264},{24,260},{28,25... | collective-permute-start | bytes 393224 | tf_op jit(solution)/shard_map/ppermute | solution.py:168
  23.7 0.7 convert_element_type.54
  24.3 1.0 fusion.9
  25.3 3.3 %collective-permute-start.1 = (bf16[64,2176]{1,0:T(8,128)(2,1)S(1)}, bf16[64,2176]{1,0:T(8,128)(2,1)S(1)}, u32[]{:S(2)}, u32[]{:S(2)}) collective-permute-start(bf16[64,2176]{1,0:T(8,128)(2,1)S(1)} %fusion.9), channel_id=1, source_target_pairs={{0,64},{64,128},{128,192},{192,0},{1,65},{65,129},{129,193},{193,1... | collective-permute-start | bytes 835592 | tf_op jit(solution)/shard_map/ppermute | solution.py:177
  28.6 4.4 %collective-permute-start.2 = (bf16[64,2176]{1,0:T(8,128)(2,1)S(1)}, bf16[64,2176]{1,0:T(8,128)(2,1)S(1)}, u32[]{:S(2)}, u32[]{:S(2)}) collective-permute-start(bf16[64,2176]{1,0:T(8,128)(2,1)S(1)} %fusion.9), channel_id=1, source_target_pairs={{0,128},{64,192},{128,0},{192,64},{1,129},{65,193},{129,1},{193,65... | collective-permute-start | bytes 835592 | tf_op jit(solution)/shard_map/ppermute | solution.py:177
  32.9 3.1 %collective-permute-start.3 = (bf16[64,2176]{1,0:T(8,128)(2,1)S(1)}, bf16[64,2176]{1,0:T(8,128)(2,1)S(1)}, u32[]{:S(2)}, u32[]{:S(2)}) collective-permute-start(bf16[64,2176]{1,0:T(8,128)(2,1)S(1)} %fusion.9), channel_id=1, source_target_pairs={{0,192},{64,0},{128,64},{192,128},{1,193},{65,1},{129,65},{193,129... | collective-permute-start | bytes 835592 | tf_op jit(solution)/shard_map/ppermute | solution.py:177
  36.0 0.5 collective-permute-done.1
  36.5 6.9 %collective-permute-done.2 = bf16[64,2176]{1,0:T(8,128)(2,1)S(1)} collective-permute-done((bf16[64,2176]{1,0:T(8,128)(2,1)S(1)}, bf16[64,2176]{1,0:T(8,128)(2,1)S(1)}, u32[]{:S(2)}, u32[]{:S(2)}) %collective-permute-start.2) | collective-permute-done | bytes 278560 | tf_op jit(solution)/shard_map/ppermute | solution.py:177
  43.5 1.3 collective-permute-done.3
  44.8 0.4 fusion
  45.2 0.4 fusion.1
  45.7 0.1 copy.26
  45.8 0.1 copy.25
  46.0 0.1 copy.35
  46.2 0.4 pad_maximum_fusion.4
  46.6 11.9 %all_to_all.5 = bf16[4,32,2048]{2,1,0:T(8,128)(2,1)S(1)} all-to-all(bf16[4,32,2048]{2,1,0:T(8,128)(2,1)S(1)} %broadcast_in_dim.28), channel_id=1, replica_groups=mesh['h'=2,'x'=4,'c'=2,'l'=8,'y'=4] {'y'}, dimensions={0} | all-to-all | bytes 1048576 | tf_op jit(solution)/shard_map/all_to_all | solution.py:199
  58.5 4.4 %collective-permute-start.7 = (bf16[128,2048]{1,0:T(8,128)(2,1)S(1)}, bf16[128,2048]{1,0:T(8,128)(2,1)S(1)}, u32[]{:S(2)}, u32[]{:S(2)}) collective-permute-start(bf16[128,2048]{1,0:T(8,128)(2,1)S(1)} %bitcast.49), channel_id=1, source_target_pairs={{0,32},{32,0},{1,33},{33,1},{2,34},{34,2},{3,35},{35,3},{4,36},{36... | collective-permute-start | bytes 1572872 | tf_op jit(solution)/shard_map/ppermute | solution.py:155
  63.0 4.9 %collective-permute-start.5 = (bf16[2,272,128]{1,0,2:T(2,128)(2,1)S(1)}, bf16[2,272,128]{1,0,2:T(2,128)(2,1)S(1)}, u32[]{:S(2)}, u32[]{:S(2)}) collective-permute-start(bf16[2,272,128]{1,0,2:T(2,128)(2,1)S(1)} %pad_maximum_fusion.4), channel_id=1, source_target_pairs={{0,8},{1,9},{2,10},{3,11},{4,72},{5,73},{6,74},{7,75},{8,136},{9,1... | collective-permute-start | bytes 417800 | tf_op jit(solution)/shard_map/ppermute | solution.py:193
  67.8 0.4 fusion.2
  68.3 0.1 copy.29
  68.4 0.4 fusion.3
  68.9 0.1 copy.30
  69.0 0.4 pad_maximum_fusion.3
  69.4 6.6 %collective-permute-start.8 = (bf16[2,272,128]{1,0,2:T(2,128)(2,1)S(1)}, bf16[2,272,128]{1,0,2:T(2,128)(2,1)S(1)}, u32[]{:S(2)}, u32[]{:S(2)}) collective-permute-start(bf16[2,272,128]{1,0,2:T(2,128)(2,1)S(1)} %pad_maximum_fusion.3), channel_id=1, source_target_pairs={{0,28},{1,29},{2,30},{3,31},{4,92},{5,93},{6,94},{7,95},{8,156},{9... | collective-permute-start | bytes 417800 | tf_op jit(solution)/shard_map/ppermute | solution.py:193
  76.0 20.7 %collective-permute-done.5 = bf16[2,272,128]{1,0,2:T(2,128)(2,1)S(1)} collective-permute-done((bf16[2,272,128]{1,0,2:T(2,128)(2,1)S(1)}, bf16[2,272,128]{1,0,2:T(2,128)(2,1)S(1)}, u32[]{:S(2)}, u32[]{:S(2)}) %collective-permute-start.5) | collective-permute-done | bytes 139296 | tf_op jit(solution)/shard_map/ppermute | solution.py:193
  96.7 0.3 fusion.12
  97.0 0.2 copy.28
  97.2 4.6 %collective-permute-start.6 = (bf16[272,128]{1,0:T(8,128)(2,1)S(1)}, bf16[272,128]{1,0:T(8,128)(2,1)S(1)}, u32[]{:S(2)}, u32[]{:S(2)}) collective-permute-start(bf16[272,128]{1,0:T(8,128)(2,1)S(1)} %bitcast.55), channel_id=1, source_target_pairs={{0,32},{32,0},{1,33},{33,1},{2,34},{34,2},{3,35},{35,3},{4,36},{36... | collective-permute-start | bytes 208904 | tf_op jit(solution)/shard_map/ppermute | solution.py:155
  101.8 0.3 fusion.13
  102.1 0.2 copy.31
  102.3 1.9 collective-permute-start.9
  104.2 0.2 copy.32
  104.4 1.0 collective-permute-done.9
  105.4 0.2 copy.33
  105.6 0.6 pad_maximum_fusion
  106.3 0.2 copy.34
  106.5 0.0 all-gather.2.cloned.1.call-done.near_ref
  106.5 3.2 %collective-permute-start.13 = (bf16[1536,512]{1,0:T(8,128)(2,1)}, bf16[1536,512]{1,0:T(8,128)(2,1)S(1)}, u32[]{:S(2)}, u32[]{:S(2)}) collective-permute-start(bf16[1536,512]{1,0:T(8,128)(2,1)} %all-gather.2.cloned.1.call-done.near_ref), channel_id=1, source_target_pairs={{0,32},{32,0},{1,33},{33,1},{2,34},{34,2},{3,35},{35,3},{4,36},{36... | collective-permute-start | bytes 4718600 | tf_op jit(solution)/shard_map/ppermute | solution.py:155
  109.8 0.1 pad_add_fusion.where_ref
  109.9 0.1 reshape.43
  110.0 1.9 collective-permute-start.10
  111.9 2.9 %collective-permute-start.11 = (bf16[16,64,128]{2,1,0:T(8,128)(2,1)S(1)}, bf16[16,64,128]{2,1,0:T(8,128)(2,1)S(1)}, u32[]{:S(2)}, u32[]{:S(2)}) collective-permute-start(bf16[16,64,128]{2,1,0:T(8,128)(2,1)S(1)} %bitcast.45), channel_id=1, source_target_pairs={{0,2},{1,3},{2,0},{3,1},{4,6},{5,7},{6,4},{7,5},{8,10},{9,11},{10,... | collective-permute-start | bytes 786440 | tf_op jit(solution)/shard_map/ppermute | solution.py:207
  114.8 4.0 %collective-permute-start.12 = (bf16[16,64,128]{2,1,0:T(8,128)(2,1)S(1)}, bf16[16,64,128]{2,1,0:T(8,128)(2,1)S(1)}, u32[]{:S(2)}, u32[]{:S(2)}) collective-permute-start(bf16[16,64,128]{2,1,0:T(8,128)(2,1)S(1)} %bitcast.46), channel_id=1, source_target_pairs={{0,3},{1,0},{2,1},{3,2},{4,7},{5,4},{6,5},{7,6},{8,11},{9,8},{10,9... | collective-permute-start | bytes 786440 | tf_op jit(solution)/shard_map/ppermute | solution.py:207
  118.8 0.2 broadcast_in_dim.29
  119.1 7.5 %collective-permute-done.10 = bf16[16,64,128]{2,1,0:T(8,128)(2,1)S(1)} collective-permute-done((bf16[16,64,128]{2,1,0:T(8,128)(2,1)S(1)}, bf16[16,64,128]{2,1,0:T(8,128)(2,1)S(1)}, u32[]{:S(2)}, u32[]{:S(2)}) %collective-permute-start.10) | collective-permute-done | bytes 262176 | tf_op jit(solution)/shard_map/ppermute | solution.py:207
  126.7 2.1 %collective-permute-done.12 = bf16[16,64,128]{2,1,0:T(8,128)(2,1)S(1)} collective-permute-done((bf16[16,64,128]{2,1,0:T(8,128)(2,1)S(1)}, bf16[16,64,128]{2,1,0:T(8,128)(2,1)S(1)}, u32[]{:S(2)}, u32[]{:S(2)}) %collective-permute-start.12) | collective-permute-done | bytes 262176 | tf_op jit(solution)/shard_map/ppermute | solution.py:207
  128.9 2.9 %shard_map.46 = (bf16[768,512]{1,0:T(8,128)(2,1)S(1)}, bf16[1024,512]{1,0:T(8,128)(2,1)S(1)}) custom-call(s32[16]{0:T(128)S(1)} %get-tuple-element.38.first_ref, s32[16]{0:T(128)S(1)} %get-tuple-element.37.second_ref, s32[3]{0:T(128)S(1)} %pad_add_fusion.where_ref, bf16[4,16,64,128]{3,2,1,0:T(8,128)(2,1)S(1)} %bitcast_dynamic-update-slice_fusion.w_ref, ...), custom_call_target="tpu_custom_call" | custom-call | flops 805306368 | bytes 4194304 | tf_op jit(solution)/shard_map/pallas_call | solution.py:123
  131.8 14.6 %collective-permute-start.14 = (bf16[192,512]{1,0:T(8,128)(2,1)S(1)}, bf16[192,512]{1,0:T(8,128)(2,1)S(1)}, u32[]{:S(2)}, u32[]{:S(2)}) collective-permute-start(bf16[192,512]{1,0:T(8,128)(2,1)S(1)} %get-tuple-element.27), channel_id=1, source_target_pairs={{0,64},{64,128},{128,192},{192,0},{1,65},{65,129},{129,193},{193,1... | collective-permute-start | bytes 589832 | tf_op jit(solution)/shard_map/ppermute | solution.py:220
  146.4 1.9 collective-permute-start.15
  148.4 4.3 %collective-permute-start.16 = (bf16[192,512]{1,0:T(8,128)(2,1)S(1)}, bf16[192,512]{1,0:T(8,128)(2,1)S(1)}, u32[]{:S(2)}, u32[]{:S(2)}) collective-permute-start(bf16[192,512]{1,0:T(8,128)(2,1)S(1)} %get-tuple-element.28), channel_id=1, source_target_pairs={{0,192},{64,0},{128,64},{192,128},{1,193},{65,1},{129,65},{193,129... | collective-permute-start | bytes 589832 | tf_op jit(solution)/shard_map/ppermute | solution.py:220
  152.7 2.1 %shard_map.47 = bf16[768,512]{1,0:T(8,128)(2,1)S(1)} custom-call(s32[3]{0:T(128)S(1)} %pad_add_fusion.where_ref, bf16[1536,512]{1,0:T(8,128)(2,1)S(1)} %copy-done, bf16[1536,512]{1,0:T(8,128)(2,1)S(1)} %collective-permute-done.13.far_ref, bf16[1024,512]{1,0:T(8,128)(2,1)S(1)} %get-tuple-element.26.s_ref), custom_call_target="tpu_custom_call" | custom-call | flops 805306368 | bytes 4194304 | tf_op jit(solution)/shard_map/pallas_call | solution.py:137
  154.8 1.9 collective-permute-start.18
  156.8 3.9 %collective-permute-start.19 = (bf16[192,512]{1,0:T(8,128)(2,1)S(1)}, bf16[192,512]{1,0:T(8,128)(2,1)S(1)}, u32[]{:S(2)}, u32[]{:S(2)}) collective-permute-start(bf16[192,512]{1,0:T(8,128)(2,1)S(1)} %get-tuple-element.32), channel_id=1, source_target_pairs={{0,128},{64,192},{128,0},{192,64},{1,129},{65,193},{129,1},{193,65... | collective-permute-start | bytes 589832 | tf_op jit(solution)/shard_map/ppermute | solution.py:220
  160.7 2.6 %collective-permute-start.20 = (bf16[192,512]{1,0:T(8,128)(2,1)S(1)}, bf16[192,512]{1,0:T(8,128)(2,1)S(1)}, u32[]{:S(2)}, u32[]{:S(2)}) collective-permute-start(bf16[192,512]{1,0:T(8,128)(2,1)S(1)} %get-tuple-element.31), channel_id=1, source_target_pairs={{0,192},{64,0},{128,64},{192,128},{1,193},{65,1},{129,65},{193,129... | collective-permute-start | bytes 589832 | tf_op jit(solution)/shard_map/ppermute | solution.py:220
  163.3 0.1 add_convert_fusion.2
  163.4 6.6 %collective-permute-start.17 = (bf16[192,512]{1,0:T(8,128)(2,1)S(1)}, bf16[192,512]{1,0:T(8,128)(2,1)S(1)}, u32[]{:S(2)}, u32[]{:S(2)}) collective-permute-start(bf16[192,512]{1,0:T(8,128)(2,1)S(1)} %add_convert_fusion.2), channel_id=1, source_target_pairs={{0,448},{1,449},{2,450},{3,451},{4,384},{5,385},{6,386},{7,387},{8... | collective-permute-start | bytes 589832 | tf_op jit(solution)/shard_map/ppermute | solution.py:221
  170.1 0.1 add_convert_fusion.1
  170.2 4.9 %collective-permute-start.21 = (bf16[192,512]{1,0:T(8,128)(2,1)S(1)}, bf16[192,512]{1,0:T(8,128)(2,1)S(1)}, u32[]{:S(2)}, u32[]{:S(2)}) collective-permute-start(bf16[192,512]{1,0:T(8,128)(2,1)S(1)} %add_convert_fusion.1), channel_id=1, source_target_pairs={{0,476},{1,477},{2,478},{3,479},{4,412},{5,413},{6,414},{7,415},{8... | collective-permute-start | bytes 589832 | tf_op jit(solution)/shard_map/ppermute | solution.py:221
  175.1 22.1 %collective-permute-done.17 = bf16[192,512]{1,0:T(8,128)(2,1)S(1)} collective-permute-done((bf16[192,512]{1,0:T(8,128)(2,1)S(1)}, bf16[192,512]{1,0:T(8,128)(2,1)S(1)}, u32[]{:S(2)}, u32[]{:S(2)}) %collective-permute-start.17) | collective-permute-done | bytes 196640 | tf_op jit(solution)/shard_map/ppermute | solution.py:221
  197.2 0.1 add_convert_fusion
  197.3 0.7 reshape.42
  (36 shorter events, 0.5 us)
Async XLA Ops:
  6.5 100.0 %all-gather.2.cloned.1.call-start = ((), (), s32[]{:S(2)}) async-start(), calls=%async_computation.1 | async-start | bytes 1769472 | tf_op jit(solution)/shard_map/all_gather | solution.py:162
  8.2 17.1 %collective-permute-start = (bf16[128,2048]{1,0:T(8,128)(2,1)}, bf16[128,2048]{1,0:T(8,128)(2,1)S(1)}, u32[]{:S(2)}, u32[]{:S(2)}) collective-permute-start(bf16[128,2048]{1,0:T(8,128)(2,1)} %param.6), channel_id=1, source_target_pairs={{0,32},{32,0},{1,33},{33,1},{2,34},{34,2},{3,35},{35,3},{4,36},{36... | collective-permute-start | bytes 1572872 | tf_op jit(solution)/shard_map/ppermute | solution.py:155
  17.9 28.7 %collective-permute-start.4 = (bf16[32,2048]{1,0:T(8,128)(2,1)S(1)}, bf16[32,2048]{1,0:T(8,128)(2,1)S(1)}, u32[]{:S(2)}, u32[]{:S(2)}) collective-permute-start(bf16[32,2048]{1,0:T(8,128)(2,1)S(1)} %constant_dynamic-slice_fusion), channel_id=1, source_target_pairs={{0,284},{4,280},{8,276},{12,272},{16,268},{20,264},{24,260},{28,25... | collective-permute-start | bytes 393224 | tf_op jit(solution)/shard_map/ppermute | solution.py:168
  25.3 19.5 %copy-start.1 = (bf16[128,2048]{1,0:T(8,128)(2,1)S(1)}, bf16[128,2048]{1,0:T(8,128)(2,1)}, u32[]{:S(2)}) copy-start(bf16[128,2048]{1,0:T(8,128)(2,1)} %param.6) | copy-start | bytes 1572868
  25.3 11.2 %collective-permute-start.1 = (bf16[64,2176]{1,0:T(8,128)(2,1)S(1)}, bf16[64,2176]{1,0:T(8,128)(2,1)S(1)}, u32[]{:S(2)}, u32[]{:S(2)}) collective-permute-start(bf16[64,2176]{1,0:T(8,128)(2,1)S(1)} %fusion.9), channel_id=1, source_target_pairs={{0,64},{64,128},{128,192},{192,0},{1,65},{65,129},{129,193},{193,1... | collective-permute-start | bytes 835592 | tf_op jit(solution)/shard_map/ppermute | solution.py:177
  28.6 14.9 %collective-permute-start.2 = (bf16[64,2176]{1,0:T(8,128)(2,1)S(1)}, bf16[64,2176]{1,0:T(8,128)(2,1)S(1)}, u32[]{:S(2)}, u32[]{:S(2)}) collective-permute-start(bf16[64,2176]{1,0:T(8,128)(2,1)S(1)} %fusion.9), channel_id=1, source_target_pairs={{0,128},{64,192},{128,0},{192,64},{1,129},{65,193},{129,1},{193,65... | collective-permute-start | bytes 835592 | tf_op jit(solution)/shard_map/ppermute | solution.py:177
  32.9 11.8 %collective-permute-start.3 = (bf16[64,2176]{1,0:T(8,128)(2,1)S(1)}, bf16[64,2176]{1,0:T(8,128)(2,1)S(1)}, u32[]{:S(2)}, u32[]{:S(2)}) collective-permute-start(bf16[64,2176]{1,0:T(8,128)(2,1)S(1)} %fusion.9), channel_id=1, source_target_pairs={{0,192},{64,0},{128,64},{192,128},{1,193},{65,1},{129,65},{193,129... | collective-permute-start | bytes 835592 | tf_op jit(solution)/shard_map/ppermute | solution.py:177
  58.5 9.9 %collective-permute-start.7 = (bf16[128,2048]{1,0:T(8,128)(2,1)S(1)}, bf16[128,2048]{1,0:T(8,128)(2,1)S(1)}, u32[]{:S(2)}, u32[]{:S(2)}) collective-permute-start(bf16[128,2048]{1,0:T(8,128)(2,1)S(1)} %bitcast.49), channel_id=1, source_target_pairs={{0,32},{32,0},{1,33},{33,1},{2,34},{34,2},{3,35},{35,3},{4,36},{36... | collective-permute-start | bytes 1572872 | tf_op jit(solution)/shard_map/ppermute | solution.py:155
  63.0 33.8 %collective-permute-start.5 = (bf16[2,272,128]{1,0,2:T(2,128)(2,1)S(1)}, bf16[2,272,128]{1,0,2:T(2,128)(2,1)S(1)}, u32[]{:S(2)}, u32[]{:S(2)}) collective-permute-start(bf16[2,272,128]{1,0,2:T(2,128)(2,1)S(1)} %pad_maximum_fusion.4), channel_id=1, source_target_pairs={{0,8},{1,9},{2,10},{3,11},{4,72},{5,73},{6,74},{7,75},{8,136},{9,1... | collective-permute-start | bytes 417800 | tf_op jit(solution)/shard_map/ppermute | solution.py:193
  69.4 32.4 %collective-permute-start.8 = (bf16[2,272,128]{1,0,2:T(2,128)(2,1)S(1)}, bf16[2,272,128]{1,0,2:T(2,128)(2,1)S(1)}, u32[]{:S(2)}, u32[]{:S(2)}) collective-permute-start(bf16[2,272,128]{1,0,2:T(2,128)(2,1)S(1)} %pad_maximum_fusion.3), channel_id=1, source_target_pairs={{0,28},{1,29},{2,30},{3,31},{4,92},{5,93},{6,94},{7,95},{8,156},{9... | collective-permute-start | bytes 417800 | tf_op jit(solution)/shard_map/ppermute | solution.py:193
  97.2 7.0 %collective-permute-start.6 = (bf16[272,128]{1,0:T(8,128)(2,1)S(1)}, bf16[272,128]{1,0:T(8,128)(2,1)S(1)}, u32[]{:S(2)}, u32[]{:S(2)}) collective-permute-start(bf16[272,128]{1,0:T(8,128)(2,1)S(1)} %bitcast.55), channel_id=1, source_target_pairs={{0,32},{32,0},{1,33},{33,1},{2,34},{34,2},{3,35},{35,3},{4,36},{36... | collective-permute-start | bytes 208904 | tf_op jit(solution)/shard_map/ppermute | solution.py:155
  102.3 3.2 %collective-permute-start.9 = (bf16[272,128]{1,0:T(8,128)(2,1)S(1)}, bf16[272,128]{1,0:T(8,128)(2,1)S(1)}, u32[]{:S(2)}, u32[]{:S(2)}) collective-permute-start(bf16[272,128]{1,0:T(8,128)(2,1)S(1)} %bitcast.57), channel_id=1, source_target_pairs={{0,32},{32,0},{1,33},{33,1},{2,34},{34,2},{3,35},{35,3},{4,36},{36... | collective-permute-start | bytes 208904 | tf_op jit(solution)/shard_map/ppermute | solution.py:155
  106.5 22.3 %collective-permute-start.13 = (bf16[1536,512]{1,0:T(8,128)(2,1)}, bf16[1536,512]{1,0:T(8,128)(2,1)S(1)}, u32[]{:S(2)}, u32[]{:S(2)}) collective-permute-start(bf16[1536,512]{1,0:T(8,128)(2,1)} %all-gather.2.cloned.1.call-done.near_ref), channel_id=1, source_target_pairs={{0,32},{32,0},{1,33},{33,1},{2,34},{34,2},{3,35},{35,3},{4,36},{36... | collective-permute-start | bytes 4718600 | tf_op jit(solution)/shard_map/ppermute | solution.py:155
  110.0 16.6 %collective-permute-start.10 = (bf16[16,64,128]{2,1,0:T(8,128)(2,1)S(1)}, bf16[16,64,128]{2,1,0:T(8,128)(2,1)S(1)}, u32[]{:S(2)}, u32[]{:S(2)}) collective-permute-start(bf16[16,64,128]{2,1,0:T(8,128)(2,1)S(1)} %bitcast.44), channel_id=1, source_target_pairs={{0,1},{1,2},{2,3},{3,0},{4,5},{5,6},{6,7},{7,4},{8,9},{9,10},{10,1... | collective-permute-start | bytes 786440 | tf_op jit(solution)/shard_map/ppermute | solution.py:207
  111.9 14.8 %collective-permute-start.11 = (bf16[16,64,128]{2,1,0:T(8,128)(2,1)S(1)}, bf16[16,64,128]{2,1,0:T(8,128)(2,1)S(1)}, u32[]{:S(2)}, u32[]{:S(2)}) collective-permute-start(bf16[16,64,128]{2,1,0:T(8,128)(2,1)S(1)} %bitcast.45), channel_id=1, source_target_pairs={{0,2},{1,3},{2,0},{3,1},{4,6},{5,7},{6,4},{7,5},{8,10},{9,11},{10,... | collective-permute-start | bytes 786440 | tf_op jit(solution)/shard_map/ppermute | solution.py:207
  114.8 14.0 %collective-permute-start.12 = (bf16[16,64,128]{2,1,0:T(8,128)(2,1)S(1)}, bf16[16,64,128]{2,1,0:T(8,128)(2,1)S(1)}, u32[]{:S(2)}, u32[]{:S(2)}) collective-permute-start(bf16[16,64,128]{2,1,0:T(8,128)(2,1)S(1)} %bitcast.46), channel_id=1, source_target_pairs={{0,3},{1,0},{2,1},{3,2},{4,7},{5,4},{6,5},{7,6},{8,11},{9,8},{10,9... | collective-permute-start | bytes 786440 | tf_op jit(solution)/shard_map/ppermute | solution.py:207
  119.1 9.8 %copy-start = (bf16[1536,512]{1,0:T(8,128)(2,1)S(1)}, bf16[1536,512]{1,0:T(8,128)(2,1)}, u32[]{:S(2)}) copy-start(bf16[1536,512]{1,0:T(8,128)(2,1)} %all-gather.2.cloned.1.call-done.near_ref) | copy-start | bytes 4718596
  131.8 28.9 %collective-permute-start.14 = (bf16[192,512]{1,0:T(8,128)(2,1)S(1)}, bf16[192,512]{1,0:T(8,128)(2,1)S(1)}, u32[]{:S(2)}, u32[]{:S(2)}) collective-permute-start(bf16[192,512]{1,0:T(8,128)(2,1)S(1)} %get-tuple-element.27), channel_id=1, source_target_pairs={{0,64},{64,128},{128,192},{192,0},{1,65},{65,129},{129,193},{193,1... | collective-permute-start | bytes 589832 | tf_op jit(solution)/shard_map/ppermute | solution.py:220
  146.4 16.9 %collective-permute-start.15 = (bf16[192,512]{1,0:T(8,128)(2,1)S(1)}, bf16[192,512]{1,0:T(8,128)(2,1)S(1)}, u32[]{:S(2)}, u32[]{:S(2)}) collective-permute-start(bf16[192,512]{1,0:T(8,128)(2,1)S(1)} %get-tuple-element.29), channel_id=1, source_target_pairs={{0,128},{64,192},{128,0},{192,64},{1,129},{65,193},{129,1},{193,65... | collective-permute-start | bytes 589832 | tf_op jit(solution)/shard_map/ppermute | solution.py:220
  148.4 14.9 %collective-permute-start.16 = (bf16[192,512]{1,0:T(8,128)(2,1)S(1)}, bf16[192,512]{1,0:T(8,128)(2,1)S(1)}, u32[]{:S(2)}, u32[]{:S(2)}) collective-permute-start(bf16[192,512]{1,0:T(8,128)(2,1)S(1)} %get-tuple-element.28), channel_id=1, source_target_pairs={{0,192},{64,0},{128,64},{192,128},{1,193},{65,1},{129,65},{193,129... | collective-permute-start | bytes 589832 | tf_op jit(solution)/shard_map/ppermute | solution.py:220
  154.8 15.2 %collective-permute-start.18 = (bf16[192,512]{1,0:T(8,128)(2,1)S(1)}, bf16[192,512]{1,0:T(8,128)(2,1)S(1)}, u32[]{:S(2)}, u32[]{:S(2)}) collective-permute-start(bf16[192,512]{1,0:T(8,128)(2,1)S(1)} %get-tuple-element.30), channel_id=1, source_target_pairs={{0,64},{64,128},{128,192},{192,0},{1,65},{65,129},{129,193},{193,1... | collective-permute-start | bytes 589832 | tf_op jit(solution)/shard_map/ppermute | solution.py:220
  156.8 13.3 %collective-permute-start.19 = (bf16[192,512]{1,0:T(8,128)(2,1)S(1)}, bf16[192,512]{1,0:T(8,128)(2,1)S(1)}, u32[]{:S(2)}, u32[]{:S(2)}) collective-permute-start(bf16[192,512]{1,0:T(8,128)(2,1)S(1)} %get-tuple-element.32), channel_id=1, source_target_pairs={{0,128},{64,192},{128,0},{192,64},{1,129},{65,193},{129,1},{193,65... | collective-permute-start | bytes 589832 | tf_op jit(solution)/shard_map/ppermute | solution.py:220
  160.7 9.4 %collective-permute-start.20 = (bf16[192,512]{1,0:T(8,128)(2,1)S(1)}, bf16[192,512]{1,0:T(8,128)(2,1)S(1)}, u32[]{:S(2)}, u32[]{:S(2)}) collective-permute-start(bf16[192,512]{1,0:T(8,128)(2,1)S(1)} %get-tuple-element.31), channel_id=1, source_target_pairs={{0,192},{64,0},{128,64},{192,128},{1,193},{65,1},{129,65},{193,129... | collective-permute-start | bytes 589832 | tf_op jit(solution)/shard_map/ppermute | solution.py:220
  163.4 33.8 %collective-permute-start.17 = (bf16[192,512]{1,0:T(8,128)(2,1)S(1)}, bf16[192,512]{1,0:T(8,128)(2,1)S(1)}, u32[]{:S(2)}, u32[]{:S(2)}) collective-permute-start(bf16[192,512]{1,0:T(8,128)(2,1)S(1)} %add_convert_fusion.2), channel_id=1, source_target_pairs={{0,448},{1,449},{2,450},{3,451},{4,384},{5,385},{6,386},{7,387},{8... | collective-permute-start | bytes 589832 | tf_op jit(solution)/shard_map/ppermute | solution.py:221
  170.2 27.0 %collective-permute-start.21 = (bf16[192,512]{1,0:T(8,128)(2,1)S(1)}, bf16[192,512]{1,0:T(8,128)(2,1)S(1)}, u32[]{:S(2)}, u32[]{:S(2)}) collective-permute-start(bf16[192,512]{1,0:T(8,128)(2,1)S(1)} %add_convert_fusion.1), channel_id=1, source_target_pairs={{0,476},{1,477},{2,478},{3,479},{4,412},{5,413},{6,414},{7,415},{8... | collective-permute-start | bytes 589832 | tf_op jit(solution)/shard_map/ppermute | solution.py:221
Sparse Core Ops, SparseCore 0:
  23.8 65.3 all-gather.1

commit v6 on v4

--- a/solution.py
+++ b/solution.py
@@ -35,9 +35,9 @@
     return next((h2, x2) for h2 in range(H) for x2 in range(X) if place(h, h2, x2) == l)
 
 
-def weight_perm(k):
+def weight_perm(k, d):
     return [
-        (flat(h, x, c, l, y), flat(l // X, l % X, c, place(l // X, h ^ k, x), y))
+        (flat(h, x, c, l, y), flat(l // X, l % X, c ^ d, place(l // X, h ^ k, x), y))
         for h, x, c, l, y in coords()
     ]
 
@@ -117,61 +117,65 @@
 
 def on_device(amplitudes, fitting, coefficients, pair_list):
     h, x, c = lax.axis_index("h"), lax.axis_index("x"), lax.axis_index("c")
-    l, y = lax.axis_index("l"), lax.axis_index("y")
+    y = lax.axis_index("y")
     f32, bf16 = jnp.float32, jnp.bfloat16
 
     def swap_core(v):
         return lax.ppermute(v, "c", shift(C, 1))
 
+    def gather(v, axes, n):
+        v = jnp.broadcast_to(v[None], (n,) + v.shape)
+        return lax.all_to_all(v, axes, split_axis=0, concat_axis=0, tiled=True)
+
+    q_own, occ, b_own = fitting.shape
+    b_near = lax.all_gather(fitting, "l", axis=0, tiled=True)
+
     n_mu, n_a = coefficients.shape
     part = n_mu // Y
+    c_other = swap_core(coefficients)
     mirror = [(i, H * L - 1 - i) for i in range(H * L)]
     piece = lax.dynamic_slice_in_dim(coefficients, y * part, part, 0)
     piece = lax.ppermute(piece, ("h", "l"), mirror)
 
-    q_own, occ, b_own = fitting.shape
     rows = amplitudes.shape[2]
     info = jnp.pad(pair_list.astype(bf16), ((0, rows - 1), (0, 126)))
     t_own = jnp.concatenate([amplitudes[0].T, info], axis=1)
-    b_near = fitting.reshape(q_own, occ * b_own)
-    piece, t_own, b_near = lax.optimization_barrier((piece, t_own, b_near))
-
-    b_near = lax.all_gather(b_near, "l", axis=0, tiled=True)
-
-    t_all = jnp.concatenate(
-        [t_own] + [lax.ppermute(t_own, "x", shift(X, k)) for k in range(1, X)], axis=0
-    )
-    piece = jnp.broadcast_to(piece[None], (Y, part, n_a))
-    c_far = lax.all_to_all(piece, "y", split_axis=0, concat_axis=0, tiled=True)
-    c_far = c_far.reshape(n_mu, n_a)
-
-    info = t_all.reshape(X, rows, -1)[:, 0, n_a:]
-    info = jnp.broadcast_to(jnp.pad(info, ((0, 16 - X), (0, 0)))[None], (C, 16, n_mu))
-    t_all = t_all[:, :n_a]
-
-    received = []
-    for k, c_part in ((0, coefficients), (1, c_far)):
-        w = [
-            lax.dot_general(t_all, m, (((1,), (1,)), ((), ())), preferred_element_type=f32)
-            for m in (c_part, swap_core(c_part))
-        ]
-        w = jnp.concatenate([jnp.stack(w).astype(bf16), info], axis=1)
-        received.append(lax.ppermute(w, AXES, weight_perm(k)))
-    mine = jnp.stack([r[0] for r in received])
-    w = jnp.stack([mine, swap_core(jnp.stack([r[1] for r in received]))])
-    slots = C * H * X
-    n_b = X * rows
-    info = w[:, :, n_b : n_b + X, :2].reshape(slots, 2).astype(jnp.int32)
-    w = w[:, :, :n_b].reshape(slots, rows, n_mu)
+    c_other, t_own = lax.optimization_barrier((c_other, t_own))
+    t_all = gather(t_own, "x", X)
+    t_all, piece = lax.optimization_barrier((t_all, piece))
+    info = t_all[:, 0, n_a:]
+    info = jnp.pad(info, ((0, 16 - X), (0, 0)))
+    t_all = t_all.reshape(X * rows, -1)[:, :n_a]
+    c_far = gather(piece, ("c", "y"), C * Y).reshape(C * n_mu, n_a)
+
+    def weights(m):
+        return lax.dot_general(
+            t_all, m, (((1,), (1,)), ((), ())), preferred_element_type=f32
+        ).astype(bf16)
+
+    near = [weights(coefficients), weights(c_other)]
+    far = weights(c_far)
+    far = [lax.dynamic_slice_in_dim(far, (c ^ d) * n_mu, n_mu, 1) for d in range(C)]
+    w = [
+        lax.ppermute(jnp.concatenate([v, info], axis=0), AXES, weight_perm(k, d))
+        for k, pieces in enumerate((near, far))
+        for d, v in enumerate(pieces)
+    ]
+    w = jnp.stack(w)
+    slots, n_b = H * C * X, X * rows
+    pairs = w[:, n_b : n_b + X, :2].reshape(slots, 2).astype(jnp.int32)
+    w = w[:, :n_b].reshape(slots, rows, n_mu)
+
     w, b_near = lax.optimization_barrier((w, b_near))
     pieces = [w] + [lax.ppermute(w, "y", shift(Y, k)) for k in range(1, Y)]
     w_all = jnp.zeros((Y,) + w.shape, bf16)
     for k, piece in enumerate(pieces):
         w_all = lax.dynamic_update_slice_in_dim(w_all, piece[None], (y - k) % Y, 0)
+    b_near = b_near.reshape(-1, occ * b_own)
     b_far = swap_core(b_near)
 
     where = jnp.stack([x, c]).astype(jnp.int32)
-    partial = contract(info[:, 0], info[:, 1], where, w_all, b_near, b_far)
+    partial = contract(pairs[:, 0], pairs[:, 1], where, w_all, b_near, b_far)
     cols = partial.shape[1]
     partial = partial.reshape(X, 2 * q_own, cols)
     summed = partial[X - 1].astype(f32)

time: 234 us -> 208 us (0.89)
  the two profiles are of different devices: /device:TPU:1 before, /device:TPU:13 now
where the time goes in v6:
time: 208 us; the launch traced here: 207 us
  waiting for transfers between devices  90.4 us (43%)
  starting transfers between devices  82.1 us (39%)
  between operations  13.8 us (7%)
  local copies, waits for them, and re-layouts  10.4 us (5%)
  Pallas kernels  4.48 us (2%)
  other arithmetic  4.29 us (2%)
    ppermute x2, waiting for transfers between devices, on_device(): total += lax.ppermute(piece, AXES, result_perm(k)).astype(f32)  28.8 us
    ppermute x4, starting transfers between devices, on_device(): lax.ppermute(jnp.concatenate([v, info], axis=0), AXES, weight_perm(k, d))  22.3 us
    ppermute x3, waiting for transfers between devices, on_device(): summed += lax.ppermute(partial[k - 1], 'x', shift(X, k)).astype(f32)  16 us
    all_to_all x2, waiting for transfers between devices, gather(): return lax.all_to_all(v, axes, split_axis=0, concat_axis=0, tiled=True)  12.8 us
    ppermute x3, starting transfers between devices, on_device(): summed += lax.ppermute(partial[k - 1], 'x', shift(X, k)).astype(f32)  12 us
    ppermute x2, starting transfers between devices, on_device(): total += lax.ppermute(piece, AXES, result_perm(k)).astype(f32)  11.5 us
    ppermute x1, waiting for transfers between devices, on_device(): piece = lax.ppermute(piece, ('h', 'l'), mirror)  11.5 us
    ppermute x1, starting transfers between devices, on_device(): piece = lax.ppermute(piece, ('h', 'l'), mirror)  11.1 us
  transfers between devices with their start and end apart: 18, of which 13 were waited for; matrix products, arithmetic and copies ran while one was open for 5% of the time, Pallas kernels for 0%

profile of v6, /device:TPU:13, one launch (start us, length us, event | category | flops | bytes accessed | tf_op | source)
XLA Modules:
  0.0 206.8 jit_solution(3468504795996615627)
XLA Ops:
  6.5 2.6 %collective-permute-start = (bf16[128,2048]{1,0:T(8,128)(2,1)}, bf16[128,2048]{1,0:T(8,128)(2,1)S(1)}, u32[]{:S(2)}, u32[]{:S(2)}) collective-permute-start(bf16[128,2048]{1,0:T(8,128)(2,1)} %param.6), channel_id=1, source_target_pairs={{0,32},{32,0},{1,33},{33,1},{2,34},{34,2},{3,35},{35,3},{4,36},{36... | collective-permute-start | bytes 1572872 | tf_op jit(solution)/shard_map/ppermute | solution.py:124
  9.1 0.0 all-gather.2.cloned.1.call-update
  9.1 0.7 convert_element_type.46
  9.8 1.0 fusion.4
  10.8 0.1 collective-permute-done
  10.8 1.1 broadcast_in_dim.27
  11.9 4.4 %all-to-all-start = ((bf16[4,64,2176]{2,1,0:T(8,128)(2,1)}), bf16[4,64,2176]{2,1,0:T(8,128)(2,1)S(1)}, u32[]{:S(2)}, u32[]{:S(2)}) async-start(bf16[4,64,2176]{2,1,0:T(8,128)(2,1)} %broadcast_in_dim.27), calls=%async_computation | async-start | bytes 2228224 | tf_op jit(solution)/shard_map/all_to_all | solution.py:128
  16.3 11.1 %collective-permute-start.1 = (bf16[32,2048]{1,0:T(8,128)(2,1)S(1)}, bf16[32,2048]{1,0:T(8,128)(2,1)S(1)}, u32[]{:S(2)}, u32[]{:S(2)}) collective-permute-start(bf16[32,2048]{1,0:T(8,128)(2,1)S(1)} %constant_dynamic-slice_fusion.4), channel_id=1, source_target_pairs={{0,284},{4,280},{8,276},{12,272},{16,268},{20,264},{24,260},{28,25... | collective-permute-start | bytes 393224 | tf_op jit(solution)/shard_map/ppermute | solution.py:138
  27.5 11.5 %collective-permute-done.1 = bf16[32,2048]{1,0:T(8,128)(2,1)S(1)} collective-permute-done((bf16[32,2048]{1,0:T(8,128)(2,1)S(1)}, bf16[32,2048]{1,0:T(8,128)(2,1)S(1)}, u32[]{:S(2)}, u32[]{:S(2)}) %collective-permute-start.1) | collective-permute-done | bytes 131104 | tf_op jit(solution)/shard_map/ppermute | solution.py:138
  38.9 0.0 all-to-all-done
  38.9 1.1 broadcast_in_dim.28
  40.1 5.7 %all-to-all-start.1 = ((bf16[8,32,2048]{2,1,0:T(8,128)(2,1)}), bf16[8,32,2048]{2,1,0:T(8,128)(2,1)S(1)}, u32[]{:S(2)}, u32[]{:S(2)}) async-start(bf16[8,32,2048]{2,1,0:T(8,128)(2,1)} %broadcast_in_dim.28), calls=%async_computation.1 | async-start | bytes 2097152 | tf_op jit(solution)/shard_map/all_to_all | solution.py:128
  45.8 0.9 copy.25
  46.7 0.4 convolution_convert_fusion.2
  47.1 0.4 convolution_convert_fusion.1
  47.6 12.8 %all-to-all-done.1 = bf16[8,32,2048]{2,1,0:T(8,128)(2,1)S(1)} async-done(((bf16[8,32,2048]{2,1,0:T(8,128)(2,1)}), bf16[8,32,2048]{2,1,0:T(8,128)(2,1)S(1)}, u32[]{:S(2)}, u32[]{:S(2)}) %all-to-all-start.1) | async-done | bytes 1048608 | tf_op jit(solution)/shard_map/all_to_all | solution.py:128
  60.4 0.5 convolution_convert_fusion
  60.9 1.9 collective-permute-start.2
  62.8 8.5 %collective-permute-start.3 = (bf16[272,128]{1,0:T(8,128)(2,1)S(1)}, bf16[272,128]{1,0:T(8,128)(2,1)S(1)}, u32[]{:S(2)}, u32[]{:S(2)}) collective-permute-start(bf16[272,128]{1,0:T(8,128)(2,1)S(1)} %get-tuple-element.27), channel_id=1, source_target_pairs={{0,40},{1,41},{2,42},{3,43},{4,104},{5,105},{6,106},{7,107},{8,168... | collective-permute-start | bytes 208904 | tf_op jit(solution)/shard_map/ppermute | solution.py:160
  71.3 1.9 collective-permute-start.4
  73.2 10.0 %collective-permute-start.5 = (bf16[272,128]{1,0:T(8,128)(2,1)S(1)}, bf16[272,128]{1,0:T(8,128)(2,1)S(1)}, u32[]{:S(2)}, u32[]{:S(2)}) collective-permute-start(bf16[272,128]{1,0:T(8,128)(2,1)S(1)} %get-tuple-element.29), channel_id=1, source_target_pairs={{0,60},{1,61},{2,62},{3,63},{4,124},{5,125},{6,126},{7,127},{8,188... | collective-permute-start | bytes 208904 | tf_op jit(solution)/shard_map/ppermute | solution.py:160
  83.2 0.0 collective-permute-done.2
  83.2 0.2 copy.26
  83.4 3.6 %collective-permute-done.3 = bf16[272,128]{1,0:T(8,128)(2,1)S(1)} collective-permute-done((bf16[272,128]{1,0:T(8,128)(2,1)S(1)}, bf16[272,128]{1,0:T(8,128)(2,1)S(1)}, u32[]{:S(2)}, u32[]{:S(2)}) %collective-permute-start.3) | collective-permute-done | bytes 69664 | tf_op jit(solution)/shard_map/ppermute | solution.py:160
  87.0 0.2 copy.27
  87.2 6.2 %collective-permute-done.4 = bf16[272,128]{1,0:T(8,128)(2,1)S(1)} collective-permute-done((bf16[272,128]{1,0:T(8,128)(2,1)S(1)}, bf16[272,128]{1,0:T(8,128)(2,1)S(1)}, u32[]{:S(2)}, u32[]{:S(2)}) %collective-permute-start.4) | collective-permute-done | bytes 69664 | tf_op jit(solution)/shard_map/ppermute | solution.py:160
  93.4 0.2 copy.28
  93.6 1.2 collective-permute-done.5
  94.8 0.2 copy.29
  95.0 0.0 copy-start.3
  95.0 0.6 pad_maximum_fusion
  95.6 0.9 copy.30
  96.6 0.0 copy-done.3
  96.6 1.7 copy.33
  98.2 2.3 %collective-permute-start.9 = (bf16[1536,512]{1,0:T(8,128)(2,1)S(1)}, bf16[1536,512]{1,0:T(8,128)(2,1)S(1)}, u32[]{:S(2)}, u32[]{:S(2)}) collective-permute-start(bf16[1536,512]{1,0:T(8,128)(2,1)S(1)} %bitcast.35), channel_id=1, source_target_pairs={{0,32},{32,0},{1,33},{33,1},{2,34},{34,2},{3,35},{35,3},{4,36},{36... | collective-permute-start | bytes 4718600 | tf_op jit(solution)/shard_map/ppermute | solution.py:124
  100.6 0.1 pad_add_fusion.where_ref
  100.7 0.7 maximum_convert_fusion
  101.4 0.1 reshape.34
  101.5 3.4 %collective-permute-start.6 = (bf16[16,64,128]{2,1,0:T(8,128)(2,1)}, bf16[16,64,128]{2,1,0:T(8,128)(2,1)S(1)}, u32[]{:S(2)}, u32[]{:S(2)}) collective-permute-start(bf16[16,64,128]{2,1,0:T(8,128)(2,1)} %bitcast.41), channel_id=1, source_target_pairs={{0,1},{1,2},{2,3},{3,0},{4,5},{5,6},{6,7},{7,4},{8,9},{9,10},{10,1... | collective-permute-start | bytes 786440 | tf_op jit(solution)/shard_map/ppermute | solution.py:170
  104.9 3.1 %collective-permute-start.7 = (bf16[16,64,128]{2,1,0:T(8,128)(2,1)}, bf16[16,64,128]{2,1,0:T(8,128)(2,1)S(1)}, u32[]{:S(2)}, u32[]{:S(2)}) collective-permute-start(bf16[16,64,128]{2,1,0:T(8,128)(2,1)} %bitcast.42), channel_id=1, source_target_pairs={{0,2},{1,3},{2,0},{3,1},{4,6},{5,7},{6,4},{7,5},{8,10},{9,11},{10,... | collective-permute-start | bytes 786440 | tf_op jit(solution)/shard_map/ppermute | solution.py:170
  108.0 3.7 %collective-permute-start.8 = (bf16[16,64,128]{2,1,0:T(8,128)(2,1)}, bf16[16,64,128]{2,1,0:T(8,128)(2,1)S(1)}, u32[]{:S(2)}, u32[]{:S(2)}) collective-permute-start(bf16[16,64,128]{2,1,0:T(8,128)(2,1)} %bitcast.43), channel_id=1, source_target_pairs={{0,3},{1,0},{2,1},{3,2},{4,7},{5,4},{6,5},{7,6},{8,11},{9,8},{10,9... | collective-permute-start | bytes 786440 | tf_op jit(solution)/shard_map/ppermute | solution.py:170
  111.7 0.2 broadcast_in_dim.29
  112.0 0.0 copy-done.4
  112.0 0.0 collective-permute-done.6
  112.1 3.8 %collective-permute-done.7 = bf16[16,64,128]{2,1,0:T(8,128)(2,1)S(1)} collective-permute-done((bf16[16,64,128]{2,1,0:T(8,128)(2,1)}, bf16[16,64,128]{2,1,0:T(8,128)(2,1)S(1)}, u32[]{:S(2)}, u32[]{:S(2)}) %collective-permute-start.7) | collective-permute-done | bytes 262176 | tf_op jit(solution)/shard_map/ppermute | solution.py:170
  116.0 6.4 %collective-permute-done.8 = bf16[16,64,128]{2,1,0:T(8,128)(2,1)S(1)} collective-permute-done((bf16[16,64,128]{2,1,0:T(8,128)(2,1)}, bf16[16,64,128]{2,1,0:T(8,128)(2,1)S(1)}, u32[]{:S(2)}, u32[]{:S(2)}) %collective-permute-start.8) | collective-permute-done | bytes 262176 | tf_op jit(solution)/shard_map/ppermute | solution.py:170
  122.4 0.0 collective-permute-done.9.far_ref
  122.4 1.2 copy-done
  123.6 1.4 copy-done.1
  125.0 4.5 %shard_map.46 = bf16[1536,512]{1,0:T(8,128)(2,1)S(1)} custom-call(s32[16]{0:T(128)S(1)} %get-tuple-element.25.first_ref, s32[16]{0:T(128)S(1)} %get-tuple-element.24.second_ref, s32[2]{0:T(128)S(1)} %pad_add_fusion.where_ref, bf16[4,16,64,128]{3,2,1,0:T(8,128)(2,1)S(1)} %bitcast_dynamic-update-slice_fusion.w_ref, bf16[1536,512]{1,0:T(8,128)(2,1)S(1)} %bitcast.36, ...), custom_call_target="tpu_custom_call" | custom-call | flops 1610612736 | bytes 6291456 | tf_op jit(solution)/shard_map/pallas_call | solution.py:94
  129.5 0.1 fusion.10
  129.6 3.3 %collective-permute-start.10 = (bf16[384,512]{1,0:T(8,128)(2,1)S(1)}, bf16[384,512]{1,0:T(8,128)(2,1)S(1)}, u32[]{:S(2)}, u32[]{:S(2)}) collective-permute-start(bf16[384,512]{1,0:T(8,128)(2,1)S(1)} %get-tuple-element.17), channel_id=1, source_target_pairs={{0,64},{64,128},{128,192},{192,0},{1,65},{65,129},{129,193},{193,1... | collective-permute-start | bytes 1179656 | tf_op jit(solution)/shard_map/ppermute | solution.py:183
  132.8 6.8 %collective-permute-start.11 = (bf16[384,512]{1,0:T(8,128)(2,1)S(1)}, bf16[384,512]{1,0:T(8,128)(2,1)S(1)}, u32[]{:S(2)}, u32[]{:S(2)}) collective-permute-start(bf16[384,512]{1,0:T(8,128)(2,1)S(1)} %get-tuple-element.19), channel_id=1, source_target_pairs={{0,128},{64,192},{128,0},{192,64},{1,129},{65,193},{129,1},{193,65... | collective-permute-start | bytes 1179656 | tf_op jit(solution)/shard_map/ppermute | solution.py:183
  139.7 1.9 collective-permute-start.12
  141.6 4.0 %collective-permute-done.10 = bf16[384,512]{1,0:T(8,128)(2,1)S(1)} collective-permute-done((bf16[384,512]{1,0:T(8,128)(2,1)S(1)}, bf16[384,512]{1,0:T(8,128)(2,1)S(1)}, u32[]{:S(2)}, u32[]{:S(2)}) %collective-permute-start.10) | collective-permute-done | bytes 393248 | tf_op jit(solution)/shard_map/ppermute | solution.py:183
  145.6 9.3 %collective-permute-done.11 = bf16[384,512]{1,0:T(8,128)(2,1)S(1)} collective-permute-done((bf16[384,512]{1,0:T(8,128)(2,1)S(1)}, bf16[384,512]{1,0:T(8,128)(2,1)S(1)}, u32[]{:S(2)}, u32[]{:S(2)}) %collective-permute-start.11) | collective-permute-done | bytes 393248 | tf_op jit(solution)/shard_map/ppermute | solution.py:183
  154.9 2.7 %collective-permute-done.12 = bf16[384,512]{1,0:T(8,128)(2,1)} collective-permute-done((bf16[384,512]{1,0:T(8,128)(2,1)S(1)}, bf16[384,512]{1,0:T(8,128)(2,1)}, u32[]{:S(2)}, u32[]{:S(2)}) %collective-permute-start.12) | collective-permute-done | bytes 393248 | tf_op jit(solution)/shard_map/ppermute | solution.py:183
  157.6 1.2 add_convert_fusion
  158.8 8.0 %collective-permute-start.13 = (bf16[192,512]{1,0:T(8,128)(2,1)S(1)}, bf16[192,512]{1,0:T(8,128)(2,1)S(1)}, u32[]{:S(2)}, u32[]{:S(2)}) collective-permute-start(bf16[192,512]{1,0:T(8,128)(2,1)S(1)} %get-tuple-element.20), channel_id=1, source_target_pairs={{0,448},{1,449},{2,450},{3,451},{4,384},{5,385},{6,386},{7,387},{8... | collective-permute-start | bytes 589832 | tf_op jit(solution)/shard_map/ppermute | solution.py:189
  166.8 3.6 %collective-permute-start.14 = (bf16[192,512]{1,0:T(8,128)(2,1)S(1)}, bf16[192,512]{1,0:T(8,128)(2,1)S(1)}, u32[]{:S(2)}, u32[]{:S(2)}) collective-permute-start(bf16[192,512]{1,0:T(8,128)(2,1)S(1)} %get-tuple-element.21), channel_id=1, source_target_pairs={{0,476},{1,477},{2,478},{3,479},{4,412},{5,413},{6,414},{7,415},{8... | collective-permute-start | bytes 589832 | tf_op jit(solution)/shard_map/ppermute | solution.py:189
  170.3 9.1 %collective-permute-done.13 = bf16[192,512]{1,0:T(8,128)(2,1)S(1)} collective-permute-done((bf16[192,512]{1,0:T(8,128)(2,1)S(1)}, bf16[192,512]{1,0:T(8,128)(2,1)S(1)}, u32[]{:S(2)}, u32[]{:S(2)}) %collective-permute-start.13) | collective-permute-done | bytes 196640 | tf_op jit(solution)/shard_map/ppermute | solution.py:189
  179.4 19.8 %collective-permute-done.14 = bf16[192,512]{1,0:T(8,128)(2,1)S(1)} collective-permute-done((bf16[192,512]{1,0:T(8,128)(2,1)S(1)}, bf16[192,512]{1,0:T(8,128)(2,1)S(1)}, u32[]{:S(2)}, u32[]{:S(2)}) %collective-permute-start.14) | collective-permute-done | bytes 196640 | tf_op jit(solution)/shard_map/ppermute | solution.py:189
  199.2 0.1 add_convert_fusion.1
  199.2 0.7 reshape.33
  (19 shorter events, 0.3 us)
Async XLA Ops:
  6.5 90.0 %all-gather.2.cloned.1.call-start = ((), (), s32[]{:S(2)}) async-start(), calls=%async_computation.2 | async-start | bytes 1769472 | tf_op jit(solution)/shard_map/all_gather | solution.py:131
  6.5 4.3 %collective-permute-start = (bf16[128,2048]{1,0:T(8,128)(2,1)}, bf16[128,2048]{1,0:T(8,128)(2,1)S(1)}, u32[]{:S(2)}, u32[]{:S(2)}) collective-permute-start(bf16[128,2048]{1,0:T(8,128)(2,1)} %param.6), channel_id=1, source_target_pairs={{0,32},{32,0},{1,33},{33,1},{2,34},{34,2},{3,35},{35,3},{4,36},{36... | collective-permute-start | bytes 1572872 | tf_op jit(solution)/shard_map/ppermute | solution.py:124
  11.9 4.4 %copy-start.5 = (bf16[128,2048]{1,0:T(8,128)(2,1)S(1)}, bf16[128,2048]{1,0:T(8,128)(2,1)}, u32[]{:S(2)}) copy-start(bf16[128,2048]{1,0:T(8,128)(2,1)} %param.6) | copy-start | bytes 1572868
  11.9 27.0 %all-to-all-start = ((bf16[4,64,2176]{2,1,0:T(8,128)(2,1)}), bf16[4,64,2176]{2,1,0:T(8,128)(2,1)S(1)}, u32[]{:S(2)}, u32[]{:S(2)}) async-start(bf16[4,64,2176]{2,1,0:T(8,128)(2,1)} %broadcast_in_dim.27), calls=%async_computation | async-start | bytes 2228224 | tf_op jit(solution)/shard_map/all_to_all | solution.py:128
  16.3 22.6 %collective-permute-start.1 = (bf16[32,2048]{1,0:T(8,128)(2,1)S(1)}, bf16[32,2048]{1,0:T(8,128)(2,1)S(1)}, u32[]{:S(2)}, u32[]{:S(2)}) collective-permute-start(bf16[32,2048]{1,0:T(8,128)(2,1)S(1)} %constant_dynamic-slice_fusion.4), channel_id=1, source_target_pairs={{0,284},{4,280},{8,276},{12,272},{16,268},{20,264},{24,260},{28,25... | collective-permute-start | bytes 393224 | tf_op jit(solution)/shard_map/ppermute | solution.py:138
  40.1 20.3 %all-to-all-start.1 = ((bf16[8,32,2048]{2,1,0:T(8,128)(2,1)}), bf16[8,32,2048]{2,1,0:T(8,128)(2,1)S(1)}, u32[]{:S(2)}, u32[]{:S(2)}) async-start(bf16[8,32,2048]{2,1,0:T(8,128)(2,1)} %broadcast_in_dim.28), calls=%async_computation.1 | async-start | bytes 2097152 | tf_op jit(solution)/shard_map/all_to_all | solution.py:128
  60.9 22.3 %collective-permute-start.2 = (bf16[272,128]{1,0:T(8,128)(2,1)S(1)}, bf16[272,128]{1,0:T(8,128)(2,1)S(1)}, u32[]{:S(2)}, u32[]{:S(2)}) collective-permute-start(bf16[272,128]{1,0:T(8,128)(2,1)S(1)} %get-tuple-element.26), channel_id=1, source_target_pairs={{0,8},{1,9},{2,10},{3,11},{4,72},{5,73},{6,74},{7,75},{8,136},{9,1... | collective-permute-start | bytes 208904 | tf_op jit(solution)/shard_map/ppermute | solution.py:160
  62.8 24.1 %collective-permute-start.3 = (bf16[272,128]{1,0:T(8,128)(2,1)S(1)}, bf16[272,128]{1,0:T(8,128)(2,1)S(1)}, u32[]{:S(2)}, u32[]{:S(2)}) collective-permute-start(bf16[272,128]{1,0:T(8,128)(2,1)S(1)} %get-tuple-element.27), channel_id=1, source_target_pairs={{0,40},{1,41},{2,42},{3,43},{4,104},{5,105},{6,106},{7,107},{8,168... | collective-permute-start | bytes 208904 | tf_op jit(solution)/shard_map/ppermute | solution.py:160
  71.3 22.1 %collective-permute-start.4 = (bf16[272,128]{1,0:T(8,128)(2,1)S(1)}, bf16[272,128]{1,0:T(8,128)(2,1)S(1)}, u32[]{:S(2)}, u32[]{:S(2)}) collective-permute-start(bf16[272,128]{1,0:T(8,128)(2,1)S(1)} %get-tuple-element.28), channel_id=1, source_target_pairs={{0,28},{1,29},{2,30},{3,31},{4,92},{5,93},{6,94},{7,95},{8,156},{9... | collective-permute-start | bytes 208904 | tf_op jit(solution)/shard_map/ppermute | solution.py:160
  73.2 21.6 %collective-permute-start.5 = (bf16[272,128]{1,0:T(8,128)(2,1)S(1)}, bf16[272,128]{1,0:T(8,128)(2,1)S(1)}, u32[]{:S(2)}, u32[]{:S(2)}) collective-permute-start(bf16[272,128]{1,0:T(8,128)(2,1)S(1)} %get-tuple-element.29), channel_id=1, source_target_pairs={{0,60},{1,61},{2,62},{3,63},{4,124},{5,125},{6,126},{7,127},{8,188... | collective-permute-start | bytes 208904 | tf_op jit(solution)/shard_map/ppermute | solution.py:160
  93.6 3.0 %copy-start.2 = (bf16[1,272,128]{1,0,2:T(2,128)(2,1)}, bf16[1,272,128]{1,0,2:T(2,128)(2,1)S(1)}, u32[]{:S(2)}) copy-start(bf16[1,272,128]{1,0,2:T(2,128)(2,1)S(1)} %copy.28) | copy-start | bytes 208900
  95.0 1.6 copy-start.3
  98.2 24.1 %collective-permute-start.9 = (bf16[1536,512]{1,0:T(8,128)(2,1)S(1)}, bf16[1536,512]{1,0:T(8,128)(2,1)S(1)}, u32[]{:S(2)}, u32[]{:S(2)}) collective-permute-start(bf16[1536,512]{1,0:T(8,128)(2,1)S(1)} %bitcast.35), channel_id=1, source_target_pairs={{0,32},{32,0},{1,33},{33,1},{2,34},{34,2},{3,35},{35,3},{4,36},{36... | collective-permute-start | bytes 4718600 | tf_op jit(solution)/shard_map/ppermute | solution.py:124
  101.5 10.5 %copy-start.4 = (bf16[4,256,128]{2,1,0:T(8,128)(2,1)S(1)}, bf16[4,256,128]{2,1,0:T(8,128)(2,1)}, u32[]{:S(2)}) copy-start(bf16[4,256,128]{2,1,0:T(8,128)(2,1)} %copy.30) | copy-start | bytes 786436
  101.5 10.5 %collective-permute-start.6 = (bf16[16,64,128]{2,1,0:T(8,128)(2,1)}, bf16[16,64,128]{2,1,0:T(8,128)(2,1)S(1)}, u32[]{:S(2)}, u32[]{:S(2)}) collective-permute-start(bf16[16,64,128]{2,1,0:T(8,128)(2,1)} %bitcast.41), channel_id=1, source_target_pairs={{0,1},{1,2},{2,3},{3,0},{4,5},{5,6},{6,7},{7,4},{8,9},{9,10},{10,1... | collective-permute-start | bytes 786440 | tf_op jit(solution)/shard_map/ppermute | solution.py:170
  104.9 11.0 %collective-permute-start.7 = (bf16[16,64,128]{2,1,0:T(8,128)(2,1)}, bf16[16,64,128]{2,1,0:T(8,128)(2,1)S(1)}, u32[]{:S(2)}, u32[]{:S(2)}) collective-permute-start(bf16[16,64,128]{2,1,0:T(8,128)(2,1)} %bitcast.42), channel_id=1, source_target_pairs={{0,2},{1,3},{2,0},{3,1},{4,6},{5,7},{6,4},{7,5},{8,10},{9,11},{10,... | collective-permute-start | bytes 786440 | tf_op jit(solution)/shard_map/ppermute | solution.py:170
  108.0 14.3 %collective-permute-start.8 = (bf16[16,64,128]{2,1,0:T(8,128)(2,1)}, bf16[16,64,128]{2,1,0:T(8,128)(2,1)S(1)}, u32[]{:S(2)}, u32[]{:S(2)}) collective-permute-start(bf16[16,64,128]{2,1,0:T(8,128)(2,1)} %bitcast.43), channel_id=1, source_target_pairs={{0,3},{1,0},{2,1},{3,2},{4,7},{5,4},{6,5},{7,6},{8,11},{9,8},{10,9... | collective-permute-start | bytes 786440 | tf_op jit(solution)/shard_map/ppermute | solution.py:170
  122.4 1.2 copy-start
  123.6 1.4 copy-start.1
  129.6 16.0 %collective-permute-start.10 = (bf16[384,512]{1,0:T(8,128)(2,1)S(1)}, bf16[384,512]{1,0:T(8,128)(2,1)S(1)}, u32[]{:S(2)}, u32[]{:S(2)}) collective-permute-start(bf16[384,512]{1,0:T(8,128)(2,1)S(1)} %get-tuple-element.17), channel_id=1, source_target_pairs={{0,64},{64,128},{128,192},{192,0},{1,65},{65,129},{129,193},{193,1... | collective-permute-start | bytes 1179656 | tf_op jit(solution)/shard_map/ppermute | solution.py:183
  132.8 22.0 %collective-permute-start.11 = (bf16[384,512]{1,0:T(8,128)(2,1)S(1)}, bf16[384,512]{1,0:T(8,128)(2,1)S(1)}, u32[]{:S(2)}, u32[]{:S(2)}) collective-permute-start(bf16[384,512]{1,0:T(8,128)(2,1)S(1)} %get-tuple-element.19), channel_id=1, source_target_pairs={{0,128},{64,192},{128,0},{192,64},{1,129},{65,193},{129,1},{193,65... | collective-permute-start | bytes 1179656 | tf_op jit(solution)/shard_map/ppermute | solution.py:183
  139.7 17.9 %collective-permute-start.12 = (bf16[384,512]{1,0:T(8,128)(2,1)S(1)}, bf16[384,512]{1,0:T(8,128)(2,1)}, u32[]{:S(2)}, u32[]{:S(2)}) collective-permute-start(bf16[384,512]{1,0:T(8,128)(2,1)S(1)} %get-tuple-element.18), channel_id=1, source_target_pairs={{0,192},{64,0},{128,64},{192,128},{1,193},{65,1},{129,65},{193,129... | collective-permute-start | bytes 1179656 | tf_op jit(solution)/shard_map/ppermute | solution.py:183
  158.8 20.6 %collective-permute-start.13 = (bf16[192,512]{1,0:T(8,128)(2,1)S(1)}, bf16[192,512]{1,0:T(8,128)(2,1)S(1)}, u32[]{:S(2)}, u32[]{:S(2)}) collective-permute-start(bf16[192,512]{1,0:T(8,128)(2,1)S(1)} %get-tuple-element.20), channel_id=1, source_target_pairs={{0,448},{1,449},{2,450},{3,451},{4,384},{5,385},{6,386},{7,387},{8... | collective-permute-start | bytes 589832 | tf_op jit(solution)/shard_map/ppermute | solution.py:189
  166.8 32.4 %collective-permute-start.14 = (bf16[192,512]{1,0:T(8,128)(2,1)S(1)}, bf16[192,512]{1,0:T(8,128)(2,1)S(1)}, u32[]{:S(2)}, u32[]{:S(2)}) collective-permute-start(bf16[192,512]{1,0:T(8,128)(2,1)S(1)} %get-tuple-element.21), channel_id=1, source_target_pairs={{0,476},{1,477},{2,478},{3,479},{4,412},{5,413},{6,414},{7,415},{8... | collective-permute-start | bytes 589832 | tf_op jit(solution)/shard_map/ppermute | solution.py:189
Sparse Core Ops, SparseCore 0:
  9.4 84.0 all-gather.1

commit v7 on v6

--- a/solution.py
+++ b/solution.py
@@ -74,8 +74,8 @@
         s_ref[...] = acc_ref[...].astype(jnp.bfloat16)
 
     depth = near_ref.shape[1]
-    at_near = pl.multiple_of(where_ref[1] * depth, depth)
-    at_far = pl.multiple_of((1 - where_ref[1]) * depth, depth)
+    at_near = pl.multiple_of(where_ref[0] * depth, depth)
+    at_far = pl.multiple_of((1 - where_ref[0]) * depth, depth)
     f32 = jnp.float32
     total = jnp.dot(near_ref[...], s_ref[pl.ds(at_near, depth)], preferred_element_type=f32)
     total += jnp.dot(far_ref[...], s_ref[pl.ds(at_far, depth)], preferred_element_type=f32)
@@ -87,8 +87,8 @@
     cols = w.shape[3]
     block = q // L
 
-    def of_step(s, first, second, where):
-        to = (where[0] + s // 2 + 1) % X
+    def of_step(s, *_):
+        to = s // 2
         return jnp.where(s % 2 == 0, to, L - 1 - to), 0
 
     return pl.pallas_call(
@@ -116,8 +116,7 @@
 
 
 def on_device(amplitudes, fitting, coefficients, pair_list):
-    h, x, c = lax.axis_index("h"), lax.axis_index("x"), lax.axis_index("c")
-    y = lax.axis_index("y")
+    h, c, y = lax.axis_index("h"), lax.axis_index("c"), lax.axis_index("y")
     f32, bf16 = jnp.float32, jnp.bfloat16
 
     def swap_core(v):
@@ -167,21 +166,17 @@
     w = w[:, :n_b].reshape(slots, rows, n_mu)
 
     w, b_near = lax.optimization_barrier((w, b_near))
-    pieces = [w] + [lax.ppermute(w, "y", shift(Y, k)) for k in range(1, Y)]
-    w_all = jnp.zeros((Y,) + w.shape, bf16)
-    for k, piece in enumerate(pieces):
-        w_all = lax.dynamic_update_slice_in_dim(w_all, piece[None], (y - k) % Y, 0)
+    w_all = gather(w, "y", Y)
+    w_all = w_all.reshape(Y, slots, rows, n_mu)
     b_near = b_near.reshape(-1, occ * b_own)
     b_far = swap_core(b_near)
 
-    where = jnp.stack([x, c]).astype(jnp.int32)
+    where = c.astype(jnp.int32)[None]
     partial = contract(pairs[:, 0], pairs[:, 1], where, w_all, b_near, b_far)
     cols = partial.shape[1]
     partial = partial.reshape(X, 2 * q_own, cols)
-    summed = partial[X - 1].astype(f32)
-    for k in range(1, X):
-        summed += lax.ppermute(partial[k - 1], "x", shift(X, k)).astype(f32)
-    summed = summed.astype(bf16)
+    partial = lax.all_to_all(partial, "x", split_axis=0, concat_axis=0, tiled=True)
+    summed = jnp.sum(partial.astype(f32), axis=0).astype(bf16)
 
     total = jnp.zeros((q_own, cols), f32)
     for k in range(H):

time: 208 us -> 206 us (level)
  the two profiles are of different devices: /device:TPU:13 before, /device:TPU:1 now
where the time goes in v7:
time: 206 us
  waiting for transfers between devices  101 us (49%)
  starting transfers between devices  70.8 us (34%)
  between operations  13.6 us (7%)
  Pallas kernels  8.12 us (4%)
  local copies, waits for them, and re-layouts  7.82 us (4%)
  other arithmetic  2.77 us (1%)
    all_to_all x3, waiting for transfers between devices, gather(): return lax.all_to_all(v, axes, split_axis=0, concat_axis=0, tiled=True)  28.4 us
    ppermute x2, waiting for transfers between devices, on_device(): total += lax.ppermute(piece, AXES, result_perm(k)).astype(f32)  24.5 us
    ppermute x4, starting transfers between devices, on_device(): lax.ppermute(jnp.concatenate([v, info], axis=0), AXES, weight_perm(k, d))  19.7 us
    all_to_all x1, waiting for transfers between devices, on_device(): lax.all_to_all(partial, 'x', split_axis=0, concat_axis=0, tiled=True)  19.4 us
    ppermute x4, waiting for transfers between devices, on_device(): lax.ppermute(jnp.concatenate([v, info], axis=0), AXES, weight_perm(k, d))  16.8 us
    ppermute x2, starting transfers between devices, on_device(): total += lax.ppermute(piece, AXES, result_perm(k)).astype(f32)  14 us
    all_to_all x3, starting transfers between devices, gather(): return lax.all_to_all(v, axes, split_axis=0, concat_axis=0, tiled=True)  13.7 us
    ppermute x2, starting transfers between devices, swap_core(): return lax.ppermute(v, 'c', shift(C, 1))  13.2 us
  transfers between devices with their start and end apart: 14, of which 9 were waited for; matrix products, arithmetic and copies ran while one was open for 4% of the time, Pallas kernels for 0%

profile of v7, /device:TPU:1, one launch (start us, length us, event | category | flops | bytes accessed | tf_op | source)
XLA Modules:
  0.0 205.5 jit_solution(8131921040737413568)
XLA Ops:
  6.5 0.0 all-gather.2.cloned.1.call-start
  6.5 8.8 %collective-permute-start = (bf16[128,2048]{1,0:T(8,128)(2,1)}, bf16[128,2048]{1,0:T(8,128)(2,1)S(1)}, u32[]{:S(2)}, u32[]{:S(2)}) collective-permute-start(bf16[128,2048]{1,0:T(8,128)(2,1)} %param.6), channel_id=1, source_target_pairs={{0,32},{32,0},{1,33},{33,1},{2,34},{34,2},{3,35},{35,3},{4,36},{36... | collective-permute-start | bytes 1572872 | tf_op jit(solution)/shard_map/ppermute | solution.py:123
  15.3 0.0 all-gather.2.cloned.1.call-update
  15.3 0.7 convert_element_type.33
  16.0 1.0 fusion.4
  17.0 0.1 collective-permute-done
  17.0 1.1 broadcast_in_dim.8
  18.1 0.0 copy-start
  18.1 3.7 %all-to-all-start = ((bf16[4,64,2176]{2,1,0:T(8,128)(2,1)}), bf16[4,64,2176]{2,1,0:T(8,128)(2,1)S(1)}, u32[]{:S(2)}, u32[]{:S(2)}) async-start(bf16[4,64,2176]{2,1,0:T(8,128)(2,1)} %broadcast_in_dim.8), calls=%async_computation | async-start | bytes 2228224 | tf_op jit(solution)/shard_map/all_to_all | solution.py:127
  21.8 0.0 copy-done
  21.8 6.2 %collective-permute-start.1 = (bf16[32,2048]{1,0:T(8,128)(2,1)S(1)}, bf16[32,2048]{1,0:T(8,128)(2,1)S(1)}, u32[]{:S(2)}, u32[]{:S(2)}) collective-permute-start(bf16[32,2048]{1,0:T(8,128)(2,1)S(1)} %constant_dynamic-slice_fusion.4), channel_id=1, source_target_pairs={{0,284},{4,280},{8,276},{12,272},{16,268},{20,264},{24,260},{28,25... | collective-permute-start | bytes 393224 | tf_op jit(solution)/shard_map/ppermute | solution.py:137
  28.0 11.7 %collective-permute-done.1 = bf16[32,2048]{1,0:T(8,128)(2,1)S(1)} collective-permute-done((bf16[32,2048]{1,0:T(8,128)(2,1)S(1)}, bf16[32,2048]{1,0:T(8,128)(2,1)S(1)}, u32[]{:S(2)}, u32[]{:S(2)}) %collective-permute-start.1) | collective-permute-done | bytes 131104 | tf_op jit(solution)/shard_map/ppermute | solution.py:137
  39.8 0.0 all-to-all-done
  39.8 1.1 broadcast_in_dim.9
  40.9 5.6 %all-to-all-start.1 = ((bf16[8,32,2048]{2,1,0:T(8,128)(2,1)}), bf16[8,32,2048]{2,1,0:T(8,128)(2,1)S(1)}, u32[]{:S(2)}, u32[]{:S(2)}) async-start(bf16[8,32,2048]{2,1,0:T(8,128)(2,1)} %broadcast_in_dim.9), calls=%async_computation.1 | async-start | bytes 2097152 | tf_op jit(solution)/shard_map/all_to_all | solution.py:127
  46.5 0.9 copy.25
  47.3 0.4 convolution_convert_fusion.2
  47.8 0.4 convolution_convert_fusion.1
  48.2 13.6 %all-to-all-done.1 = bf16[8,32,2048]{2,1,0:T(8,128)(2,1)S(1)} async-done(((bf16[8,32,2048]{2,1,0:T(8,128)(2,1)}), bf16[8,32,2048]{2,1,0:T(8,128)(2,1)S(1)}, u32[]{:S(2)}, u32[]{:S(2)}) %all-to-all-start.1) | async-done | bytes 1048608 | tf_op jit(solution)/shard_map/all_to_all | solution.py:127
  61.9 0.5 convolution_convert_fusion
  62.4 6.4 %collective-permute-start.5 = (bf16[272,128]{1,0:T(8,128)(2,1)S(1)}, bf16[272,128]{1,0:T(8,128)(2,1)S(1)}, u32[]{:S(2)}, u32[]{:S(2)}) collective-permute-start(bf16[272,128]{1,0:T(8,128)(2,1)S(1)} %get-tuple-element.26), channel_id=1, source_target_pairs={{0,60},{1,61},{2,62},{3,63},{4,124},{5,125},{6,126},{7,127},{8,188... | collective-permute-start | bytes 208904 | tf_op jit(solution)/shard_map/ppermute | solution.py:159
  68.8 9.5 %collective-permute-start.4 = (bf16[272,128]{1,0:T(8,128)(2,1)S(1)}, bf16[272,128]{1,0:T(8,128)(2,1)S(1)}, u32[]{:S(2)}, u32[]{:S(2)}) collective-permute-start(bf16[272,128]{1,0:T(8,128)(2,1)S(1)} %get-tuple-element.25), channel_id=1, source_target_pairs={{0,28},{1,29},{2,30},{3,31},{4,92},{5,93},{6,94},{7,95},{8,156},{9... | collective-permute-start | bytes 208904 | tf_op jit(solution)/shard_map/ppermute | solution.py:159
  78.2 1.9 collective-permute-start.3
  80.1 1.9 collective-permute-start.2
  82.1 0.0 collective-permute-done.5
  82.1 0.2 copy.29
  82.3 0.0 collective-permute-done.4
  82.3 0.2 copy.28
  82.5 14.4 %collective-permute-done.3 = bf16[272,128]{1,0:T(8,128)(2,1)S(1)} collective-permute-done((bf16[272,128]{1,0:T(8,128)(2,1)S(1)}, bf16[272,128]{1,0:T(8,128)(2,1)S(1)}, u32[]{:S(2)}, u32[]{:S(2)}) %collective-permute-start.3) | collective-permute-done | bytes 69664 | tf_op jit(solution)/shard_map/ppermute | solution.py:159
  96.9 0.2 copy.27
  97.1 2.4 %collective-permute-done.2 = bf16[272,128]{1,0:T(8,128)(2,1)S(1)} collective-permute-done((bf16[272,128]{1,0:T(8,128)(2,1)S(1)}, bf16[272,128]{1,0:T(8,128)(2,1)S(1)}, u32[]{:S(2)}, u32[]{:S(2)}) %collective-permute-start.2) | collective-permute-done | bytes 69664 | tf_op jit(solution)/shard_map/ppermute | solution.py:159
  99.4 0.2 copy.26
  99.6 0.6 pad_maximum_fusion
  100.3 0.2 copy.30
  100.5 0.0 all-gather.2.cloned.1.call-done
  100.5 1.7 copy.33
  102.2 4.4 %collective-permute-start.6 = (bf16[1536,512]{1,0:T(8,128)(2,1)S(1)}, bf16[1536,512]{1,0:T(8,128)(2,1)}, u32[]{:S(2)}, u32[]{:S(2)}) collective-permute-start(bf16[1536,512]{1,0:T(8,128)(2,1)S(1)} %bitcast.27), channel_id=1, source_target_pairs={{0,32},{32,0},{1,33},{33,1},{2,34},{34,2},{3,35},{35,3},{4,36},{36... | collective-permute-start | bytes 4718600 | tf_op jit(solution)/shard_map/ppermute | solution.py:123
  106.7 1.2 broadcast_in_dim.11
  107.9 4.5 %all-to-all-start.2 = ((bf16[4,16,64,128]{3,2,1,0:T(8,128)(2,1)}), bf16[4,16,64,128]{3,2,1,0:T(8,128)(2,1)S(1)}, u32[]{:S(2)}, u32[]{:S(2)}) async-start(bf16[4,16,64,128]{3,2,1,0:T(8,128)(2,1)} %broadcast_in_dim.11), calls=%async_computation.2 | async-start | bytes 2097152 | tf_op jit(solution)/shard_map/all_to_all | solution.py:127
  112.4 0.1 reshape.30
  112.5 14.8 %all-to-all-done.2.w_ref = bf16[4,16,64,128]{3,2,1,0:T(8,128)(2,1)S(1)} async-done(((bf16[4,16,64,128]{3,2,1,0:T(8,128)(2,1)}), bf16[4,16,64,128]{3,2,1,0:T(8,128)(2,1)S(1)}, u32[]{:S(2)}, u32[]{:S(2)}) %all-to-all-start.2) | async-done | bytes 1048608 | tf_op jit(solution)/shard_map/all_to_all | solution.py:127
  127.3 0.0 collective-permute-done.6.far_ref
  127.3 8.1 %shard_map.46 = bf16[1536,512]{1,0:T(8,128)(2,1)} custom-call(s32[16]{0:T(128)S(1)} %get-tuple-element.22.first_ref, s32[16]{0:T(128)S(1)} %get-tuple-element.21.second_ref, s32[1]{0:T(128)} %bitcast.11.where_ref, bf16[4,16,64,128]{3,2,1,0:T(8,128)(2,1)S(1)} %all-to-all-done.2.w_ref, bf16[1536,512]{1,0:T(8,128)(2,1)S(1)} %bitcast.28, ...), custom_call_target="tpu_custom_call" | custom-call | flops 1610612736 | bytes 6291456 | tf_op jit(solution)/shard_map/pallas_call | solution.py:94
  135.4 4.0 %all-to-all-start.3 = ((bf16[4,384,512]{2,1,0:T(8,128)(2,1)}), bf16[4,384,512]{2,1,0:T(8,128)(2,1)S(1)}, u32[]{:S(2)}, u32[]{:S(2)}) async-start(bf16[4,384,512]{2,1,0:T(8,128)(2,1)} %bitcast.13), calls=%async_computation.3 | async-start | bytes 3145728 | tf_op jit(solution)/shard_map/all_to_all | solution.py:178
  139.4 19.4 %all-to-all-done.3 = bf16[4,384,512]{2,1,0:T(8,128)(2,1)S(1)} async-done(((bf16[4,384,512]{2,1,0:T(8,128)(2,1)}), bf16[4,384,512]{2,1,0:T(8,128)(2,1)S(1)}, u32[]{:S(2)}, u32[]{:S(2)}) %all-to-all-start.3) | async-done | bytes 1572896 | tf_op jit(solution)/shard_map/all_to_all | solution.py:178
  158.8 0.4 reduce_sum.12
  159.3 7.5 %collective-permute-start.8 = (bf16[192,512]{1,0:T(8,128)(2,1)S(1)}, bf16[192,512]{1,0:T(8,128)(2,1)S(1)}, u32[]{:S(2)}, u32[]{:S(2)}) collective-permute-start(bf16[192,512]{1,0:T(8,128)(2,1)S(1)} %get-tuple-element.18), channel_id=1, source_target_pairs={{0,476},{1,477},{2,478},{3,479},{4,412},{5,413},{6,414},{7,415},{8... | collective-permute-start | bytes 589832 | tf_op jit(solution)/shard_map/ppermute | solution.py:184
  166.8 6.5 %collective-permute-start.7 = (bf16[192,512]{1,0:T(8,128)(2,1)S(1)}, bf16[192,512]{1,0:T(8,128)(2,1)S(1)}, u32[]{:S(2)}, u32[]{:S(2)}) collective-permute-start(bf16[192,512]{1,0:T(8,128)(2,1)S(1)} %get-tuple-element.17), channel_id=1, source_target_pairs={{0,448},{1,449},{2,450},{3,451},{4,384},{5,385},{6,386},{7,387},{8... | collective-permute-start | bytes 589832 | tf_op jit(solution)/shard_map/ppermute | solution.py:184
  173.3 7.9 %collective-permute-done.8 = bf16[192,512]{1,0:T(8,128)(2,1)S(1)} collective-permute-done((bf16[192,512]{1,0:T(8,128)(2,1)S(1)}, bf16[192,512]{1,0:T(8,128)(2,1)S(1)}, u32[]{:S(2)}, u32[]{:S(2)}) %collective-permute-start.8) | collective-permute-done | bytes 196640 | tf_op jit(solution)/shard_map/ppermute | solution.py:184
  181.2 16.6 %collective-permute-done.7 = bf16[192,512]{1,0:T(8,128)(2,1)S(1)} collective-permute-done((bf16[192,512]{1,0:T(8,128)(2,1)S(1)}, bf16[192,512]{1,0:T(8,128)(2,1)S(1)}, u32[]{:S(2)}, u32[]{:S(2)}) %collective-permute-start.7) | collective-permute-done | bytes 196640 | tf_op jit(solution)/shard_map/ppermute | solution.py:184
  197.9 0.1 add_convert_fusion
  197.9 0.7 reshape.29
  (7 shorter events, 0.1 us)
Async XLA Ops:
  6.5 94.0 %all-gather.2.cloned.1.call-start = ((), (), s32[]{:S(2)}) async-start(), calls=%async_computation.4 | async-start | bytes 1769472 | tf_op jit(solution)/shard_map/all_gather | solution.py:130
  6.5 10.5 %collective-permute-start = (bf16[128,2048]{1,0:T(8,128)(2,1)}, bf16[128,2048]{1,0:T(8,128)(2,1)S(1)}, u32[]{:S(2)}, u32[]{:S(2)}) collective-permute-start(bf16[128,2048]{1,0:T(8,128)(2,1)} %param.6), channel_id=1, source_target_pairs={{0,32},{32,0},{1,33},{33,1},{2,34},{34,2},{3,35},{35,3},{4,36},{36... | collective-permute-start | bytes 1572872 | tf_op jit(solution)/shard_map/ppermute | solution.py:123
  18.1 3.7 %copy-start = (bf16[128,2048]{1,0:T(8,128)(2,1)S(1)}, bf16[128,2048]{1,0:T(8,128)(2,1)}, u32[]{:S(2)}) copy-start(bf16[128,2048]{1,0:T(8,128)(2,1)} %param.6) | copy-start | bytes 1572868
  18.1 21.7 %all-to-all-start = ((bf16[4,64,2176]{2,1,0:T(8,128)(2,1)}), bf16[4,64,2176]{2,1,0:T(8,128)(2,1)S(1)}, u32[]{:S(2)}, u32[]{:S(2)}) async-start(bf16[4,64,2176]{2,1,0:T(8,128)(2,1)} %broadcast_in_dim.8), calls=%async_computation | async-start | bytes 2228224 | tf_op jit(solution)/shard_map/all_to_all | solution.py:127
  21.8 18.0 %collective-permute-start.1 = (bf16[32,2048]{1,0:T(8,128)(2,1)S(1)}, bf16[32,2048]{1,0:T(8,128)(2,1)S(1)}, u32[]{:S(2)}, u32[]{:S(2)}) collective-permute-start(bf16[32,2048]{1,0:T(8,128)(2,1)S(1)} %constant_dynamic-slice_fusion.4), channel_id=1, source_target_pairs={{0,284},{4,280},{8,276},{12,272},{16,268},{20,264},{24,260},{28,25... | collective-permute-start | bytes 393224 | tf_op jit(solution)/shard_map/ppermute | solution.py:137
  40.9 21.0 %all-to-all-start.1 = ((bf16[8,32,2048]{2,1,0:T(8,128)(2,1)}), bf16[8,32,2048]{2,1,0:T(8,128)(2,1)S(1)}, u32[]{:S(2)}, u32[]{:S(2)}) async-start(bf16[8,32,2048]{2,1,0:T(8,128)(2,1)} %broadcast_in_dim.9), calls=%async_computation.1 | async-start | bytes 2097152 | tf_op jit(solution)/shard_map/all_to_all | solution.py:127
  62.4 19.7 %collective-permute-start.5 = (bf16[272,128]{1,0:T(8,128)(2,1)S(1)}, bf16[272,128]{1,0:T(8,128)(2,1)S(1)}, u32[]{:S(2)}, u32[]{:S(2)}) collective-permute-start(bf16[272,128]{1,0:T(8,128)(2,1)S(1)} %get-tuple-element.26), channel_id=1, source_target_pairs={{0,60},{1,61},{2,62},{3,63},{4,124},{5,125},{6,126},{7,127},{8,188... | collective-permute-start | bytes 208904 | tf_op jit(solution)/shard_map/ppermute | solution.py:159
  68.8 13.5 %collective-permute-start.4 = (bf16[272,128]{1,0:T(8,128)(2,1)S(1)}, bf16[272,128]{1,0:T(8,128)(2,1)S(1)}, u32[]{:S(2)}, u32[]{:S(2)}) collective-permute-start(bf16[272,128]{1,0:T(8,128)(2,1)S(1)} %get-tuple-element.25), channel_id=1, source_target_pairs={{0,28},{1,29},{2,30},{3,31},{4,92},{5,93},{6,94},{7,95},{8,156},{9... | collective-permute-start | bytes 208904 | tf_op jit(solution)/shard_map/ppermute | solution.py:159
  78.2 18.6 %collective-permute-start.3 = (bf16[272,128]{1,0:T(8,128)(2,1)S(1)}, bf16[272,128]{1,0:T(8,128)(2,1)S(1)}, u32[]{:S(2)}, u32[]{:S(2)}) collective-permute-start(bf16[272,128]{1,0:T(8,128)(2,1)S(1)} %get-tuple-element.24), channel_id=1, source_target_pairs={{0,40},{1,41},{2,42},{3,43},{4,104},{5,105},{6,106},{7,107},{8,168... | collective-permute-start | bytes 208904 | tf_op jit(solution)/shard_map/ppermute | solution.py:159
  80.1 19.3 %collective-permute-start.2 = (bf16[272,128]{1,0:T(8,128)(2,1)S(1)}, bf16[272,128]{1,0:T(8,128)(2,1)S(1)}, u32[]{:S(2)}, u32[]{:S(2)}) collective-permute-start(bf16[272,128]{1,0:T(8,128)(2,1)S(1)} %get-tuple-element.23), channel_id=1, source_target_pairs={{0,8},{1,9},{2,10},{3,11},{4,72},{5,73},{6,74},{7,75},{8,136},{9,1... | collective-permute-start | bytes 208904 | tf_op jit(solution)/shard_map/ppermute | solution.py:159
  102.2 25.1 %collective-permute-start.6 = (bf16[1536,512]{1,0:T(8,128)(2,1)S(1)}, bf16[1536,512]{1,0:T(8,128)(2,1)}, u32[]{:S(2)}, u32[]{:S(2)}) collective-permute-start(bf16[1536,512]{1,0:T(8,128)(2,1)S(1)} %bitcast.27), channel_id=1, source_target_pairs={{0,32},{32,0},{1,33},{33,1},{2,34},{34,2},{3,35},{35,3},{4,36},{36... | collective-permute-start | bytes 4718600 | tf_op jit(solution)/shard_map/ppermute | solution.py:123
  107.9 19.4 %all-to-all-start.2 = ((bf16[4,16,64,128]{3,2,1,0:T(8,128)(2,1)}), bf16[4,16,64,128]{3,2,1,0:T(8,128)(2,1)S(1)}, u32[]{:S(2)}, u32[]{:S(2)}) async-start(bf16[4,16,64,128]{3,2,1,0:T(8,128)(2,1)} %broadcast_in_dim.11), calls=%async_computation.2 | async-start | bytes 2097152 | tf_op jit(solution)/shard_map/all_to_all | solution.py:127
  135.4 23.4 %all-to-all-start.3 = ((bf16[4,384,512]{2,1,0:T(8,128)(2,1)}), bf16[4,384,512]{2,1,0:T(8,128)(2,1)S(1)}, u32[]{:S(2)}, u32[]{:S(2)}) async-start(bf16[4,384,512]{2,1,0:T(8,128)(2,1)} %bitcast.13), calls=%async_computation.3 | async-start | bytes 3145728 | tf_op jit(solution)/shard_map/all_to_all | solution.py:178
  159.3 21.9 %collective-permute-start.8 = (bf16[192,512]{1,0:T(8,128)(2,1)S(1)}, bf16[192,512]{1,0:T(8,128)(2,1)S(1)}, u32[]{:S(2)}, u32[]{:S(2)}) collective-permute-start(bf16[192,512]{1,0:T(8,128)(2,1)S(1)} %get-tuple-element.18), channel_id=1, source_target_pairs={{0,476},{1,477},{2,478},{3,479},{4,412},{5,413},{6,414},{7,415},{8... | collective-permute-start | bytes 589832 | tf_op jit(solution)/shard_map/ppermute | solution.py:184
  166.8 31.0 %collective-permute-start.7 = (bf16[192,512]{1,0:T(8,128)(2,1)S(1)}, bf16[192,512]{1,0:T(8,128)(2,1)S(1)}, u32[]{:S(2)}, u32[]{:S(2)}) collective-permute-start(bf16[192,512]{1,0:T(8,128)(2,1)S(1)} %get-tuple-element.17), channel_id=1, source_target_pairs={{0,448},{1,449},{2,450},{3,451},{4,384},{5,385},{6,386},{7,387},{8... | collective-permute-start | bytes 589832 | tf_op jit(solution)/shard_map/ppermute | solution.py:184
Sparse Core Ops, SparseCore 0:
  15.5 65.8 all-gather.1

commit v8 on v7

--- a/solution.py
+++ b/solution.py
@@ -8,6 +8,9 @@
 H, X, C, L, Y = 2, 4, 2, 8, 4
 AXES = ("h", "x", "c", "l", "y")
 OCC = 4
+
+
+RING = [0, 2, 4, 6, 7, 5, 3, 1]
 
 
 def flat(h, x, c, l, y):
@@ -88,8 +91,8 @@
     block = q // L
 
     def of_step(s, *_):
-        to = s // 2
-        return jnp.where(s % 2 == 0, to, L - 1 - to), 0
+        l = jnp.where(s % 2 == 0, s // 2, L - 1 - s // 2)
+        return jnp.where(l % 2 == 0, l // 2, (2 * L - 1 - l) // 2), 0
 
     return pl.pallas_call(
         contract_kernel,
@@ -127,7 +130,7 @@
         return lax.all_to_all(v, axes, split_axis=0, concat_axis=0, tiled=True)
 
     q_own, occ, b_own = fitting.shape
-    b_near = lax.all_gather(fitting, "l", axis=0, tiled=True)
+    b_near = lax.all_gather(fitting, "l", axis=0, tiled=True, axis_index_groups=[RING])
 
     n_mu, n_a = coefficients.shape
     part = n_mu // Y

time: 206 us -> 204 us (level)
  the two profiles are of different devices: /device:TPU:1 before, /device:TPU:4 now
where the time goes in v8:
time: 204 us
  waiting for transfers between devices  97.7 us (48%)
  starting transfers between devices  72.2 us (35%)
  between operations  13.6 us (7%)
  Pallas kernels  8.15 us (4%)
  local copies, waits for them, and re-layouts  7.82 us (4%)
  other arithmetic  2.77 us (1%)
    ppermute x2, waiting for transfers between devices, on_device(): total += lax.ppermute(piece, AXES, result_perm(k)).astype(f32)  30.3 us
    all_to_all x3, waiting for transfers between devices, gather(): return lax.all_to_all(v, axes, split_axis=0, concat_axis=0, tiled=True)  29.5 us
    ppermute x4, starting transfers between devices, on_device(): lax.ppermute(jnp.concatenate([v, info], axis=0), AXES, weight_perm(k, d))  24.6 us
    all_to_all x1, waiting for transfers between devices, on_device(): lax.all_to_all(partial, 'x', split_axis=0, concat_axis=0, tiled=True)  17.5 us
    all_to_all x3, starting transfers between devices, gather(): return lax.all_to_all(v, axes, split_axis=0, concat_axis=0, tiled=True)  17.3 us
    all_to_all x1, starting transfers between devices, on_device(): lax.all_to_all(partial, 'x', split_axis=0, concat_axis=0, tiled=True)  13 us
    ppermute x1, waiting for transfers between devices, on_device(): piece = lax.ppermute(piece, ('h', 'l'), mirror)  11.1 us
    ppermute x4, waiting for transfers between devices, on_device(): lax.ppermute(jnp.concatenate([v, info], axis=0), AXES, weight_perm(k, d))  8.76 us
  transfers between devices with their start and end apart: 14, of which 7 were waited for; matrix products, arithmetic and copies ran while one was open for 4% of the time, Pallas kernels for 0%

profile of v8, /device:TPU:4, one launch (start us, length us, event | category | flops | bytes accessed | tf_op | source)
XLA Modules:
  0.0 203.6 jit_solution(1401037862343038555)
XLA Ops:
  6.5 0.0 all-gather.2.cloned.1.call-start
  6.5 1.9 collective-permute-start
  8.5 0.0 all-gather.2.cloned.1.call-update
  8.5 0.7 convert_element_type.33
  9.1 1.0 fusion.4
  10.1 0.4 collective-permute-done
  10.5 1.1 broadcast_in_dim.8
  11.6 0.0 copy-start
  11.6 9.5 %all-to-all-start = ((bf16[4,64,2176]{2,1,0:T(8,128)(2,1)}), bf16[4,64,2176]{2,1,0:T(8,128)(2,1)S(1)}, u32[]{:S(2)}, u32[]{:S(2)}) async-start(bf16[4,64,2176]{2,1,0:T(8,128)(2,1)} %broadcast_in_dim.8), calls=%async_computation | async-start | bytes 2228224 | tf_op jit(solution)/shard_map/all_to_all | solution.py:130
  21.1 0.0 copy-done
  21.1 6.8 %collective-permute-start.1 = (bf16[32,2048]{1,0:T(8,128)(2,1)S(1)}, bf16[32,2048]{1,0:T(8,128)(2,1)S(1)}, u32[]{:S(2)}, u32[]{:S(2)}) collective-permute-start(bf16[32,2048]{1,0:T(8,128)(2,1)S(1)} %constant_dynamic-slice_fusion.4), channel_id=1, source_target_pairs={{0,284},{4,280},{8,276},{12,272},{16,268},{20,264},{24,260},{28,25... | collective-permute-start | bytes 393224 | tf_op jit(solution)/shard_map/ppermute | solution.py:140
  28.0 11.1 %collective-permute-done.1 = bf16[32,2048]{1,0:T(8,128)(2,1)S(1)} collective-permute-done((bf16[32,2048]{1,0:T(8,128)(2,1)S(1)}, bf16[32,2048]{1,0:T(8,128)(2,1)S(1)}, u32[]{:S(2)}, u32[]{:S(2)}) %collective-permute-start.1) | collective-permute-done | bytes 131104 | tf_op jit(solution)/shard_map/ppermute | solution.py:140
  39.1 0.0 all-to-all-done
  39.1 1.1 broadcast_in_dim.9
  40.2 4.3 %all-to-all-start.1 = ((bf16[8,32,2048]{2,1,0:T(8,128)(2,1)}), bf16[8,32,2048]{2,1,0:T(8,128)(2,1)S(1)}, u32[]{:S(2)}, u32[]{:S(2)}) async-start(bf16[8,32,2048]{2,1,0:T(8,128)(2,1)} %broadcast_in_dim.9), calls=%async_computation.1 | async-start | bytes 2097152 | tf_op jit(solution)/shard_map/all_to_all | solution.py:130
  44.5 0.9 copy.25
  45.3 0.4 convolution_convert_fusion.2
  45.8 0.4 convolution_convert_fusion.1
  46.2 13.6 %all-to-all-done.1 = bf16[8,32,2048]{2,1,0:T(8,128)(2,1)S(1)} async-done(((bf16[8,32,2048]{2,1,0:T(8,128)(2,1)}), bf16[8,32,2048]{2,1,0:T(8,128)(2,1)S(1)}, u32[]{:S(2)}, u32[]{:S(2)}) %all-to-all-start.1) | async-done | bytes 1048608 | tf_op jit(solution)/shard_map/all_to_all | solution.py:130
  59.8 0.5 convolution_convert_fusion
  60.3 6.1 %collective-permute-start.5 = (bf16[272,128]{1,0:T(8,128)(2,1)S(1)}, bf16[272,128]{1,0:T(8,128)(2,1)S(1)}, u32[]{:S(2)}, u32[]{:S(2)}) collective-permute-start(bf16[272,128]{1,0:T(8,128)(2,1)S(1)} %get-tuple-element.26), channel_id=1, source_target_pairs={{0,60},{1,61},{2,62},{3,63},{4,124},{5,125},{6,126},{7,127},{8,188... | collective-permute-start | bytes 208904 | tf_op jit(solution)/shard_map/ppermute | solution.py:162
  66.4 4.9 %collective-permute-start.4 = (bf16[272,128]{1,0:T(8,128)(2,1)S(1)}, bf16[272,128]{1,0:T(8,128)(2,1)S(1)}, u32[]{:S(2)}, u32[]{:S(2)}) collective-permute-start(bf16[272,128]{1,0:T(8,128)(2,1)S(1)} %get-tuple-element.25), channel_id=1, source_target_pairs={{0,28},{1,29},{2,30},{3,31},{4,92},{5,93},{6,94},{7,95},{8,156},{9... | collective-permute-start | bytes 208904 | tf_op jit(solution)/shard_map/ppermute | solution.py:162
  71.3 8.8 %collective-permute-start.3 = (bf16[272,128]{1,0:T(8,128)(2,1)S(1)}, bf16[272,128]{1,0:T(8,128)(2,1)S(1)}, u32[]{:S(2)}, u32[]{:S(2)}) collective-permute-start(bf16[272,128]{1,0:T(8,128)(2,1)S(1)} %get-tuple-element.24), channel_id=1, source_target_pairs={{0,40},{1,41},{2,42},{3,43},{4,104},{5,105},{6,106},{7,107},{8,168... | collective-permute-start | bytes 208904 | tf_op jit(solution)/shard_map/ppermute | solution.py:162
  80.1 4.8 %collective-permute-start.2 = (bf16[272,128]{1,0:T(8,128)(2,1)S(1)}, bf16[272,128]{1,0:T(8,128)(2,1)S(1)}, u32[]{:S(2)}, u32[]{:S(2)}) collective-permute-start(bf16[272,128]{1,0:T(8,128)(2,1)S(1)} %get-tuple-element.23), channel_id=1, source_target_pairs={{0,8},{1,9},{2,10},{3,11},{4,72},{5,73},{6,74},{7,75},{8,136},{9,1... | collective-permute-start | bytes 208904 | tf_op jit(solution)/shard_map/ppermute | solution.py:162
  85.0 0.0 collective-permute-done.5
  85.0 0.2 copy.29
  85.2 0.0 collective-permute-done.4
  85.2 0.2 copy.28
  85.4 0.0 collective-permute-done.3
  85.4 0.2 copy.27
  85.6 8.8 %collective-permute-done.2 = bf16[272,128]{1,0:T(8,128)(2,1)S(1)} collective-permute-done((bf16[272,128]{1,0:T(8,128)(2,1)S(1)}, bf16[272,128]{1,0:T(8,128)(2,1)S(1)}, u32[]{:S(2)}, u32[]{:S(2)}) %collective-permute-start.2) | collective-permute-done | bytes 69664 | tf_op jit(solution)/shard_map/ppermute | solution.py:162
  94.3 0.2 copy.26
  94.5 0.6 pad_maximum_fusion
  95.2 0.2 copy.30
  95.4 0.0 all-gather.2.cloned.1.call-done
  95.4 1.7 copy.33
  97.1 1.9 collective-permute-start.6
  99.0 1.2 broadcast_in_dim.11
  100.3 3.5 %all-to-all-start.2 = ((bf16[4,16,64,128]{3,2,1,0:T(8,128)(2,1)}), bf16[4,16,64,128]{3,2,1,0:T(8,128)(2,1)S(1)}, u32[]{:S(2)}, u32[]{:S(2)}) async-start(bf16[4,16,64,128]{3,2,1,0:T(8,128)(2,1)} %broadcast_in_dim.11), calls=%async_computation.2 | async-start | bytes 2097152 | tf_op jit(solution)/shard_map/all_to_all | solution.py:130
  103.8 0.1 reshape.30
  103.9 15.9 %all-to-all-done.2.w_ref = bf16[4,16,64,128]{3,2,1,0:T(8,128)(2,1)S(1)} async-done(((bf16[4,16,64,128]{3,2,1,0:T(8,128)(2,1)}), bf16[4,16,64,128]{3,2,1,0:T(8,128)(2,1)S(1)}, u32[]{:S(2)}, u32[]{:S(2)}) %all-to-all-start.2) | async-done | bytes 1048608 | tf_op jit(solution)/shard_map/all_to_all | solution.py:130
  119.8 0.0 collective-permute-done.6.far_ref
  119.8 8.1 %shard_map.46 = bf16[1536,512]{1,0:T(8,128)(2,1)} custom-call(s32[16]{0:T(128)S(1)} %get-tuple-element.22.first_ref, s32[16]{0:T(128)S(1)} %get-tuple-element.21.second_ref, s32[1]{0:T(128)} %bitcast.11.where_ref, bf16[4,16,64,128]{3,2,1,0:T(8,128)(2,1)S(1)} %all-to-all-done.2.w_ref, bf16[1536,512]{1,0:T(8,128)(2,1)S(1)} %bitcast.28, ...), custom_call_target="tpu_custom_call" | custom-call | flops 1610612736 | bytes 6291456 | tf_op jit(solution)/shard_map/pallas_call | solution.py:97
  127.9 13.0 %all-to-all-start.3 = ((bf16[4,384,512]{2,1,0:T(8,128)(2,1)}), bf16[4,384,512]{2,1,0:T(8,128)(2,1)S(1)}, u32[]{:S(2)}, u32[]{:S(2)}) async-start(bf16[4,384,512]{2,1,0:T(8,128)(2,1)} %bitcast.13), calls=%async_computation.3 | async-start | bytes 3145728 | tf_op jit(solution)/shard_map/all_to_all | solution.py:181
  140.9 17.5 %all-to-all-done.3 = bf16[4,384,512]{2,1,0:T(8,128)(2,1)S(1)} async-done(((bf16[4,384,512]{2,1,0:T(8,128)(2,1)}), bf16[4,384,512]{2,1,0:T(8,128)(2,1)S(1)}, u32[]{:S(2)}, u32[]{:S(2)}) %all-to-all-start.3) | async-done | bytes 1572896 | tf_op jit(solution)/shard_map/all_to_all | solution.py:181
  158.4 0.4 reduce_sum.12
  158.9 3.0 %collective-permute-start.8 = (bf16[192,512]{1,0:T(8,128)(2,1)S(1)}, bf16[192,512]{1,0:T(8,128)(2,1)S(1)}, u32[]{:S(2)}, u32[]{:S(2)}) collective-permute-start(bf16[192,512]{1,0:T(8,128)(2,1)S(1)} %get-tuple-element.18), channel_id=1, source_target_pairs={{0,476},{1,477},{2,478},{3,479},{4,412},{5,413},{6,414},{7,415},{8... | collective-permute-start | bytes 589832 | tf_op jit(solution)/shard_map/ppermute | solution.py:187
  161.9 3.7 %collective-permute-start.7 = (bf16[192,512]{1,0:T(8,128)(2,1)S(1)}, bf16[192,512]{1,0:T(8,128)(2,1)S(1)}, u32[]{:S(2)}, u32[]{:S(2)}) collective-permute-start(bf16[192,512]{1,0:T(8,128)(2,1)S(1)} %get-tuple-element.17), channel_id=1, source_target_pairs={{0,448},{1,449},{2,450},{3,451},{4,384},{5,385},{6,386},{7,387},{8... | collective-permute-start | bytes 589832 | tf_op jit(solution)/shard_map/ppermute | solution.py:187
  165.7 30.3 %collective-permute-done.8 = bf16[192,512]{1,0:T(8,128)(2,1)S(1)} collective-permute-done((bf16[192,512]{1,0:T(8,128)(2,1)S(1)}, bf16[192,512]{1,0:T(8,128)(2,1)S(1)}, u32[]{:S(2)}, u32[]{:S(2)}) %collective-permute-start.8) | collective-permute-done | bytes 196640 | tf_op jit(solution)/shard_map/ppermute | solution.py:187
  196.0 0.0 collective-permute-done.7
  196.0 0.1 add_convert_fusion
  196.0 0.7 reshape.29
  (7 shorter events, 0.1 us)
Async XLA Ops:
  6.5 88.9 %all-gather.2.cloned.1.call-start = ((), (), s32[]{:S(2)}) async-start(), calls=%async_computation.4 | async-start | bytes 1769472 | tf_op jit(solution)/shard_map/all_gather | solution.py:133
  6.5 4.0 %collective-permute-start = (bf16[128,2048]{1,0:T(8,128)(2,1)}, bf16[128,2048]{1,0:T(8,128)(2,1)S(1)}, u32[]{:S(2)}, u32[]{:S(2)}) collective-permute-start(bf16[128,2048]{1,0:T(8,128)(2,1)} %param.6), channel_id=1, source_target_pairs={{0,32},{32,0},{1,33},{33,1},{2,34},{34,2},{3,35},{35,3},{4,36},{36... | collective-permute-start | bytes 1572872 | tf_op jit(solution)/shard_map/ppermute | solution.py:126
  11.6 9.5 %copy-start = (bf16[128,2048]{1,0:T(8,128)(2,1)S(1)}, bf16[128,2048]{1,0:T(8,128)(2,1)}, u32[]{:S(2)}) copy-start(bf16[128,2048]{1,0:T(8,128)(2,1)} %param.6) | copy-start | bytes 1572868
  11.6 27.5 %all-to-all-start = ((bf16[4,64,2176]{2,1,0:T(8,128)(2,1)}), bf16[4,64,2176]{2,1,0:T(8,128)(2,1)S(1)}, u32[]{:S(2)}, u32[]{:S(2)}) async-start(bf16[4,64,2176]{2,1,0:T(8,128)(2,1)} %broadcast_in_dim.8), calls=%async_computation | async-start | bytes 2228224 | tf_op jit(solution)/shard_map/all_to_all | solution.py:130
  21.1 17.9 %collective-permute-start.1 = (bf16[32,2048]{1,0:T(8,128)(2,1)S(1)}, bf16[32,2048]{1,0:T(8,128)(2,1)S(1)}, u32[]{:S(2)}, u32[]{:S(2)}) collective-permute-start(bf16[32,2048]{1,0:T(8,128)(2,1)S(1)} %constant_dynamic-slice_fusion.4), channel_id=1, source_target_pairs={{0,284},{4,280},{8,276},{12,272},{16,268},{20,264},{24,260},{28,25... | collective-permute-start | bytes 393224 | tf_op jit(solution)/shard_map/ppermute | solution.py:140
  40.2 19.6 %all-to-all-start.1 = ((bf16[8,32,2048]{2,1,0:T(8,128)(2,1)}), bf16[8,32,2048]{2,1,0:T(8,128)(2,1)S(1)}, u32[]{:S(2)}, u32[]{:S(2)}) async-start(bf16[8,32,2048]{2,1,0:T(8,128)(2,1)} %broadcast_in_dim.9), calls=%async_computation.1 | async-start | bytes 2097152 | tf_op jit(solution)/shard_map/all_to_all | solution.py:130
  60.3 24.6 %collective-permute-start.5 = (bf16[272,128]{1,0:T(8,128)(2,1)S(1)}, bf16[272,128]{1,0:T(8,128)(2,1)S(1)}, u32[]{:S(2)}, u32[]{:S(2)}) collective-permute-start(bf16[272,128]{1,0:T(8,128)(2,1)S(1)} %get-tuple-element.26), channel_id=1, source_target_pairs={{0,60},{1,61},{2,62},{3,63},{4,124},{5,125},{6,126},{7,127},{8,188... | collective-permute-start | bytes 208904 | tf_op jit(solution)/shard_map/ppermute | solution.py:162
  66.4 18.8 %collective-permute-start.4 = (bf16[272,128]{1,0:T(8,128)(2,1)S(1)}, bf16[272,128]{1,0:T(8,128)(2,1)S(1)}, u32[]{:S(2)}, u32[]{:S(2)}) collective-permute-start(bf16[272,128]{1,0:T(8,128)(2,1)S(1)} %get-tuple-element.25), channel_id=1, source_target_pairs={{0,28},{1,29},{2,30},{3,31},{4,92},{5,93},{6,94},{7,95},{8,156},{9... | collective-permute-start | bytes 208904 | tf_op jit(solution)/shard_map/ppermute | solution.py:162
  71.3 14.0 %collective-permute-start.3 = (bf16[272,128]{1,0:T(8,128)(2,1)S(1)}, bf16[272,128]{1,0:T(8,128)(2,1)S(1)}, u32[]{:S(2)}, u32[]{:S(2)}) collective-permute-start(bf16[272,128]{1,0:T(8,128)(2,1)S(1)} %get-tuple-element.24), channel_id=1, source_target_pairs={{0,40},{1,41},{2,42},{3,43},{4,104},{5,105},{6,106},{7,107},{8,168... | collective-permute-start | bytes 208904 | tf_op jit(solution)/shard_map/ppermute | solution.py:162
  80.1 14.2 %collective-permute-start.2 = (bf16[272,128]{1,0:T(8,128)(2,1)S(1)}, bf16[272,128]{1,0:T(8,128)(2,1)S(1)}, u32[]{:S(2)}, u32[]{:S(2)}) collective-permute-start(bf16[272,128]{1,0:T(8,128)(2,1)S(1)} %get-tuple-element.23), channel_id=1, source_target_pairs={{0,8},{1,9},{2,10},{3,11},{4,72},{5,73},{6,74},{7,75},{8,136},{9,1... | collective-permute-start | bytes 208904 | tf_op jit(solution)/shard_map/ppermute | solution.py:162
  97.1 22.7 %collective-permute-start.6 = (bf16[1536,512]{1,0:T(8,128)(2,1)S(1)}, bf16[1536,512]{1,0:T(8,128)(2,1)}, u32[]{:S(2)}, u32[]{:S(2)}) collective-permute-start(bf16[1536,512]{1,0:T(8,128)(2,1)S(1)} %bitcast.27), channel_id=1, source_target_pairs={{0,32},{32,0},{1,33},{33,1},{2,34},{34,2},{3,35},{35,3},{4,36},{36... | collective-permute-start | bytes 4718600 | tf_op jit(solution)/shard_map/ppermute | solution.py:126
  100.3 19.5 %all-to-all-start.2 = ((bf16[4,16,64,128]{3,2,1,0:T(8,128)(2,1)}), bf16[4,16,64,128]{3,2,1,0:T(8,128)(2,1)S(1)}, u32[]{:S(2)}, u32[]{:S(2)}) async-start(bf16[4,16,64,128]{3,2,1,0:T(8,128)(2,1)} %broadcast_in_dim.11), calls=%async_computation.2 | async-start | bytes 2097152 | tf_op jit(solution)/shard_map/all_to_all | solution.py:130
  127.9 30.5 %all-to-all-start.3 = ((bf16[4,384,512]{2,1,0:T(8,128)(2,1)}), bf16[4,384,512]{2,1,0:T(8,128)(2,1)S(1)}, u32[]{:S(2)}, u32[]{:S(2)}) async-start(bf16[4,384,512]{2,1,0:T(8,128)(2,1)} %bitcast.13), calls=%async_computation.3 | async-start | bytes 3145728 | tf_op jit(solution)/shard_map/all_to_all | solution.py:181
  158.9 37.0 %collective-permute-start.8 = (bf16[192,512]{1,0:T(8,128)(2,1)S(1)}, bf16[192,512]{1,0:T(8,128)(2,1)S(1)}, u32[]{:S(2)}, u32[]{:S(2)}) collective-permute-start(bf16[192,512]{1,0:T(8,128)(2,1)S(1)} %get-tuple-element.18), channel_id=1, source_target_pairs={{0,476},{1,477},{2,478},{3,479},{4,412},{5,413},{6,414},{7,415},{8... | collective-permute-start | bytes 589832 | tf_op jit(solution)/shard_map/ppermute | solution.py:187
  161.9 34.0 %collective-permute-start.7 = (bf16[192,512]{1,0:T(8,128)(2,1)S(1)}, bf16[192,512]{1,0:T(8,128)(2,1)S(1)}, u32[]{:S(2)}, u32[]{:S(2)}) collective-permute-start(bf16[192,512]{1,0:T(8,128)(2,1)S(1)} %get-tuple-element.17), channel_id=1, source_target_pairs={{0,448},{1,449},{2,450},{3,451},{4,384},{5,385},{6,386},{7,387},{8... | collective-permute-start | bytes 589832 | tf_op jit(solution)/shard_map/ppermute | solution.py:187
Sparse Core Ops, SparseCore 0:
  9.4 61.3 all-gather.1

commit v9 on v8

--- a/solution.py
+++ b/solution.py
@@ -56,8 +56,11 @@
     return [(i, (i + k) % n) for i in range(n)]
 
 
-def contract_kernel(first_ref, second_ref, where_ref, w_ref, near_ref, far_ref, out_ref, acc_ref, s_ref):
-    slots, rows, cols = w_ref.shape[1], w_ref.shape[2], w_ref.shape[3]
+def contract_kernel(
+    first_ref, second_ref, where_ref, w_ref, near_ref, near2_ref, far_ref, far2_ref, out_ref,
+    acc_ref, s_ref
+):
+    slots, rows, cols = w_ref.shape[1:]
 
     @pl.when(pl.program_id(0) == 0)
     def _():
@@ -76,13 +79,14 @@
         lax.fori_loop(0, slots, add, 0)
         s_ref[...] = acc_ref[...].astype(jnp.bfloat16)
 
-    depth = near_ref.shape[1]
+    block, depth = near_ref.shape
     at_near = pl.multiple_of(where_ref[0] * depth, depth)
     at_far = pl.multiple_of((1 - where_ref[0]) * depth, depth)
     f32 = jnp.float32
-    total = jnp.dot(near_ref[...], s_ref[pl.ds(at_near, depth)], preferred_element_type=f32)
-    total += jnp.dot(far_ref[...], s_ref[pl.ds(at_far, depth)], preferred_element_type=f32)
-    out_ref[...] = total.astype(jnp.bfloat16)
+    for part, (near, far) in enumerate(((near_ref, far_ref), (near2_ref, far2_ref))):
+        total = jnp.dot(near[...], s_ref[pl.ds(at_near, depth)], preferred_element_type=f32)
+        total += jnp.dot(far[...], s_ref[pl.ds(at_far, depth)], preferred_element_type=f32)
+        out_ref[part * block : (part + 1) * block] = total.astype(jnp.bfloat16)
 
 
 def contract(first, second, where, w, near, far):
@@ -90,21 +94,21 @@
     cols = w.shape[3]
     block = q // L
 
-    def of_step(s, *_):
-        l = jnp.where(s % 2 == 0, s // 2, L - 1 - s // 2)
-        return jnp.where(l % 2 == 0, l // 2, (2 * L - 1 - l) // 2), 0
+    def rows_of(part):
+        def of_step(x, *_):
+            l = L - 1 - x if part else x
+            return jnp.where(l % 2 == 0, l // 2, (2 * L - 1 - l) // 2), 0
+
+        return pl.BlockSpec((block, depth), of_step)
 
     return pl.pallas_call(
         contract_kernel,
         grid_spec=pltpu.PrefetchScalarGridSpec(
             num_scalar_prefetch=3,
-            grid=(L,),
-            in_specs=[
-                pl.BlockSpec(w.shape, lambda s, *_: (0, 0, 0, 0)),
-                pl.BlockSpec((block, depth), of_step),
-                pl.BlockSpec((block, depth), of_step),
-            ],
-            out_specs=pl.BlockSpec((block, OCC * cols), lambda s, *_: (s, 0)),
+            grid=(X,),
+            in_specs=[pl.BlockSpec(w.shape, lambda s, *_: (0, 0, 0, 0))]
+            + [rows_of(0), rows_of(1)] * 2,
+            out_specs=pl.BlockSpec((2 * block, OCC * cols), lambda s, *_: (s, 0)),
             scratch_shapes=[
                 pltpu.VMEM((2 * depth, OCC * cols), jnp.float32),
                 pltpu.VMEM((2 * depth, OCC * cols), jnp.bfloat16),
@@ -115,7 +119,7 @@
         cost_estimate=pl.CostEstimate(
             flops=2 * q * 2 * depth * OCC * cols, bytes_accessed=6 * 2**20, transcendentals=0
         ),
-    )(first, second, where, w, near, far)
+    )(first, second, where, w, near, near, far, far)
 
 
 def on_device(amplitudes, fitting, coefficients, pair_list):
@@ -130,7 +134,8 @@
         return lax.all_to_all(v, axes, split_axis=0, concat_axis=0, tiled=True)
 
     q_own, occ, b_own = fitting.shape
-    b_near = lax.all_gather(fitting, "l", axis=0, tiled=True, axis_index_groups=[RING])
+    b_near = fitting.reshape(q_own, occ * b_own)
+    b_near = lax.all_gather(b_near, "l", axis=0, tiled=True, axis_index_groups=[RING])
 
     n_mu, n_a = coefficients.shape
     part = n_mu // Y
@@ -142,13 +147,14 @@
     rows = amplitudes.shape[2]
     info = jnp.pad(pair_list.astype(bf16), ((0, rows - 1), (0, 126)))
     t_own = jnp.concatenate([amplitudes[0].T, info], axis=1)
-    c_other, t_own = lax.optimization_barrier((c_other, t_own))
     t_all = gather(t_own, "x", X)
-    t_all, piece = lax.optimization_barrier((t_all, piece))
     info = t_all[:, 0, n_a:]
     info = jnp.pad(info, ((0, 16 - X), (0, 0)))
     t_all = t_all.reshape(X * rows, -1)[:, :n_a]
-    c_far = gather(piece, ("c", "y"), C * Y).reshape(C * n_mu, n_a)
+    c_far = jnp.zeros((n_mu, n_a), bf16)
+    for k in range(Y):
+        v = lax.ppermute(piece, "y", shift(Y, k)) if k else piece
+        c_far = lax.dynamic_update_slice_in_dim(c_far, v, (y - k) % Y * part, 0)
 
     def weights(m):
         return lax.dot_general(
@@ -156,8 +162,7 @@
         ).astype(bf16)
 
     near = [weights(coefficients), weights(c_other)]
-    far = weights(c_far)
-    far = [lax.dynamic_slice_in_dim(far, (c ^ d) * n_mu, n_mu, 1) for d in range(C)]
+    far = [weights(c_far), weights(swap_core(c_far))]
     w = [
         lax.ppermute(jnp.concatenate([v, info], axis=0), AXES, weight_perm(k, d))
         for k, pieces in enumerate((near, far))
@@ -169,10 +174,10 @@
     w = w[:, :n_b].reshape(slots, rows, n_mu)
 
     w, b_near = lax.optimization_barrier((w, b_near))
+    b_far = swap_core(b_near)
+
     w_all = gather(w, "y", Y)
     w_all = w_all.reshape(Y, slots, rows, n_mu)
-    b_near = b_near.reshape(-1, occ * b_own)
-    b_far = swap_core(b_near)
 
     where = c.astype(jnp.int32)[None]
     partial = contract(pairs[:, 0], pairs[:, 1], where, w_all, b_near, b_far)

time: 204 us -> 190 us (0.931)
  the two profiles are of different devices: /device:TPU:4 before, /device:TPU:1 now
where the time goes in v9:
time: 190 us; the launch traced here: 189 us
  starting transfers between devices  79.8 us (42%)
  waiting for transfers between devices  77.2 us (41%)
  between operations  13.8 us (7%)
  local copies, waits for them, and re-layouts  8.02 us (4%)
  Pallas kernels  4.94 us (3%)
  other arithmetic  3.46 us (2%)
    all_to_all x1, waiting for transfers between devices, on_device(): lax.all_to_all(partial, 'x', split_axis=0, concat_axis=0, tiled=True)  19.7 us
    ppermute x2, waiting for transfers between devices, on_device(): total += lax.ppermute(piece, AXES, result_perm(k)).astype(f32)  18.4 us
    ppermute x4, starting transfers between devices, on_device(): lax.ppermute(jnp.concatenate([v, info], axis=0), AXES, weight_perm(k, d))  17.8 us
    ppermute x4, waiting for transfers between devices, on_device(): lax.ppermute(jnp.concatenate([v, info], axis=0), AXES, weight_perm(k, d))  15.8 us
    ppermute x2, starting transfers between devices, on_device(): total += lax.ppermute(piece, AXES, result_perm(k)).astype(f32)  15.8 us
    ppermute x3, starting transfers between devices, swap_core(): return lax.ppermute(v, 'c', shift(C, 1))  15 us
    all_to_all x2, waiting for transfers between devices, gather(): return lax.all_to_all(v, axes, split_axis=0, concat_axis=0, tiled=True)  14.5 us
    ppermute x3, starting transfers between devices, on_device(): v = lax.ppermute(piece, 'y', shift(Y, k)) if k else piece  10.7 us
  transfers between devices with their start and end apart: 17, of which 10 were waited for; matrix products, arithmetic and copies ran while one was open for 6% of the time, Pallas kernels for 0%

profile of v9, /device:TPU:1, one launch (start us, length us, event | category | flops | bytes accessed | tf_op | source)
XLA Modules:
  0.0 188.9 jit_solution(2644332021345797803)
XLA Ops:
  6.5 0.0 all-gather.2.cloned.1.call-start
  6.5 8.8 %collective-permute-start.1 = (bf16[128,2048]{1,0:T(8,128)(2,1)}, bf16[128,2048]{1,0:T(8,128)(2,1)S(1)}, u32[]{:S(2)}, u32[]{:S(2)}) collective-permute-start(bf16[128,2048]{1,0:T(8,128)(2,1)} %param.6), channel_id=1, source_target_pairs={{0,32},{32,0},{1,33},{33,1},{2,34},{34,2},{3,35},{35,3},{4,36},{36... | collective-permute-start | bytes 1572872 | tf_op jit(solution)/shard_map/ppermute | solution.py:130
  15.3 1.6 copy.26
  17.0 0.0 all-gather.2.cloned.1.call-update
  17.0 0.9 constant_dynamic-slice_fusion.2
  17.9 5.7 %collective-permute-start.3 = (bf16[32,2048]{1,0:T(8,128)(2,1)S(1)}, bf16[32,2048]{1,0:T(8,128)(2,1)S(1)}, u32[]{:S(2)}, u32[]{:S(2)}) collective-permute-start(bf16[32,2048]{1,0:T(8,128)(2,1)S(1)} %constant_dynamic-slice_fusion.2), channel_id=1, source_target_pairs={{0,284},{4,280},{8,276},{12,272},{16,268},{20,264},{24,260},{28,25... | collective-permute-start | bytes 393224 | tf_op jit(solution)/shard_map/ppermute | solution.py:145
  23.7 0.7 convert_element_type.36
  24.3 1.0 fusion.5
  25.3 1.1 broadcast_in_dim.8
  26.4 4.0 %all-to-all-start = ((bf16[4,64,2176]{2,1,0:T(8,128)(2,1)}), bf16[4,64,2176]{2,1,0:T(8,128)(2,1)S(1)}, u32[]{:S(2)}, u32[]{:S(2)}) async-start(bf16[4,64,2176]{2,1,0:T(8,128)(2,1)} %broadcast_in_dim.8), calls=%async_computation | async-start | bytes 2228224 | tf_op jit(solution)/shard_map/all_to_all | solution.py:134
  30.4 5.6 %collective-permute-done.3 = bf16[32,2048]{1,0:T(8,128)(2,1)S(1)} collective-permute-done((bf16[32,2048]{1,0:T(8,128)(2,1)S(1)}, bf16[32,2048]{1,0:T(8,128)(2,1)S(1)}, u32[]{:S(2)}, u32[]{:S(2)}) %collective-permute-start.3) | collective-permute-done | bytes 131104 | tf_op jit(solution)/shard_map/ppermute | solution.py:145
  36.0 3.2 %collective-permute-start.4 = (bf16[32,2048]{1,0:T(8,128)(2,1)S(1)}, bf16[32,2048]{1,0:T(8,128)(2,1)S(1)}, u32[]{:S(2)}, u32[]{:S(2)}) collective-permute-start(bf16[32,2048]{1,0:T(8,128)(2,1)S(1)} %collective-permute-done.3), channel_id=1, source_target_pairs={{0,1},{1,2},{2,3},{3,0},{4,5},{5,6},{6,7},{7,4},{8,9},{9,10},{10,1... | collective-permute-start | bytes 393224 | tf_op jit(solution)/shard_map/ppermute | solution.py:156
  39.2 4.5 %collective-permute-start.5 = (bf16[32,2048]{1,0:T(8,128)(2,1)S(1)}, bf16[32,2048]{1,0:T(8,128)(2,1)S(1)}, u32[]{:S(2)}, u32[]{:S(2)}) collective-permute-start(bf16[32,2048]{1,0:T(8,128)(2,1)S(1)} %collective-permute-done.3), channel_id=1, source_target_pairs={{0,2},{1,3},{2,0},{3,1},{4,6},{5,7},{6,4},{7,5},{8,10},{9,11},{10,... | collective-permute-start | bytes 393224 | tf_op jit(solution)/shard_map/ppermute | solution.py:156
  43.7 3.0 %collective-permute-start.6 = (bf16[32,2048]{1,0:T(8,128)(2,1)S(1)}, bf16[32,2048]{1,0:T(8,128)(2,1)S(1)}, u32[]{:S(2)}, u32[]{:S(2)}) collective-permute-start(bf16[32,2048]{1,0:T(8,128)(2,1)S(1)} %collective-permute-done.3), channel_id=1, source_target_pairs={{0,3},{1,0},{2,1},{3,2},{4,7},{5,4},{6,5},{7,6},{8,11},{9,8},{10,9... | collective-permute-start | bytes 393224 | tf_op jit(solution)/shard_map/ppermute | solution.py:156
  46.8 0.0 collective-permute-done.4
  46.8 1.0 collective-permute-done.5
  47.9 2.0 %collective-permute-done.6 = bf16[32,2048]{1,0:T(8,128)(2,1)S(1)} collective-permute-done((bf16[32,2048]{1,0:T(8,128)(2,1)S(1)}, bf16[32,2048]{1,0:T(8,128)(2,1)S(1)}, u32[]{:S(2)}, u32[]{:S(2)}) %collective-permute-start.6) | collective-permute-done | bytes 131104 | tf_op jit(solution)/shard_map/ppermute | solution.py:156
  49.9 3.8 %collective-permute-start.8 = (bf16[128,2048]{1,0:T(8,128)(2,1)S(1)}, bf16[128,2048]{1,0:T(8,128)(2,1)S(1)}, u32[]{:S(2)}, u32[]{:S(2)}) collective-permute-start(bf16[128,2048]{1,0:T(8,128)(2,1)S(1)} %constant_dynamic-update-slice_fusion), channel_id=1, source_target_pairs={{0,32},{32,0},{1,33},{33,1},{2,34},{34,2},{3,35},{35,3},{4,36},{36... | collective-permute-start | bytes 1572872 | tf_op jit(solution)/shard_map/ppermute | solution.py:130
  53.6 0.0 all-to-all-done
  53.7 0.0 copy-done.4
  53.7 0.4 convolution_convert_fusion.3
  54.1 0.4 convolution_convert_fusion.1
  54.6 0.0 collective-permute-done.1
  54.6 0.4 convolution_convert_fusion.2
  55.0 0.1 collective-permute-done.8
  55.1 0.4 convolution_convert_fusion
  55.6 6.8 %collective-permute-start.9 = (bf16[272,128]{1,0:T(8,128)(2,1)S(1)}, bf16[272,128]{1,0:T(8,128)(2,1)S(1)}, u32[]{:S(2)}, u32[]{:S(2)}) collective-permute-start(bf16[272,128]{1,0:T(8,128)(2,1)S(1)} %get-tuple-element.16), channel_id=1, source_target_pairs={{0,60},{1,61},{2,62},{3,63},{4,124},{5,125},{6,126},{7,127},{8,188... | collective-permute-start | bytes 208904 | tf_op jit(solution)/shard_map/ppermute | solution.py:167
  62.4 7.2 %collective-permute-start.7 = (bf16[272,128]{1,0:T(8,128)(2,1)S(1)}, bf16[272,128]{1,0:T(8,128)(2,1)S(1)}, u32[]{:S(2)}, u32[]{:S(2)}) collective-permute-start(bf16[272,128]{1,0:T(8,128)(2,1)S(1)} %get-tuple-element.15), channel_id=1, source_target_pairs={{0,28},{1,29},{2,30},{3,31},{4,92},{5,93},{6,94},{7,95},{8,156},{9... | collective-permute-start | bytes 208904 | tf_op jit(solution)/shard_map/ppermute | solution.py:167
  69.6 1.9 %collective-permute-start.2 = (bf16[272,128]{1,0:T(8,128)(2,1)S(1)}, bf16[272,128]{1,0:T(8,128)(2,1)S(1)}, u32[]{:S(2)}, u32[]{:S(2)}) collective-permute-start(bf16[272,128]{1,0:T(8,128)(2,1)S(1)} %get-tuple-element.14), channel_id=1, source_target_pairs={{0,40},{1,41},{2,42},{3,43},{4,104},{5,105},{6,106},{7,107},{8,168... | collective-permute-start | bytes 208904 | tf_op jit(solution)/shard_map/ppermute | solution.py:167
  71.5 1.9 %collective-permute-start = (bf16[272,128]{1,0:T(8,128)(2,1)S(1)}, bf16[272,128]{1,0:T(8,128)(2,1)S(1)}, u32[]{:S(2)}, u32[]{:S(2)}) collective-permute-start(bf16[272,128]{1,0:T(8,128)(2,1)S(1)} %get-tuple-element.13), channel_id=1, source_target_pairs={{0,8},{1,9},{2,10},{3,11},{4,72},{5,73},{6,74},{7,75},{8,136},{9,1... | collective-permute-start | bytes 208904 | tf_op jit(solution)/shard_map/ppermute | solution.py:167
  73.4 0.0 collective-permute-done.9
  73.4 0.2 copy.20
  73.6 0.0 collective-permute-done.7
  73.6 0.2 copy.19
  73.8 13.8 %collective-permute-done.2 = bf16[272,128]{1,0:T(8,128)(2,1)S(1)} collective-permute-done((bf16[272,128]{1,0:T(8,128)(2,1)S(1)}, bf16[272,128]{1,0:T(8,128)(2,1)S(1)}, u32[]{:S(2)}, u32[]{:S(2)}) %collective-permute-start.2) | collective-permute-done | bytes 69664 | tf_op jit(solution)/shard_map/ppermute | solution.py:167
  87.6 0.2 copy.18
  87.8 0.0 copy-start.2
  87.8 2.0 %collective-permute-done = bf16[272,128]{1,0:T(8,128)(2,1)S(1)} collective-permute-done((bf16[272,128]{1,0:T(8,128)(2,1)S(1)}, bf16[272,128]{1,0:T(8,128)(2,1)S(1)}, u32[]{:S(2)}, u32[]{:S(2)}) %collective-permute-start) | collective-permute-done | bytes 69664 | tf_op jit(solution)/shard_map/ppermute | solution.py:167
  89.9 0.2 copy.17
  90.1 0.6 pad_maximum_fusion
  90.7 0.2 copy.21
  90.9 0.0 all-gather.2.cloned.1.call-done.near_ref.near2_ref
  91.0 0.0 copy-done.2
  91.0 0.0 copy-done.3
  91.0 2.5 %collective-permute-start.10 = (bf16[1536,512]{1,0:T(8,128)(2,1)}, bf16[1536,512]{1,0:T(8,128)(2,1)S(1)}, u32[]{:S(2)}, u32[]{:S(2)}) collective-permute-start(bf16[1536,512]{1,0:T(8,128)(2,1)} %all-gather.2.cloned.1.call-done.near_ref.near2_ref), channel_id=1, source_target_pairs={{0,32},{32,0},{1,33},{33,1},{2,34},{34,2},{3,35},{35,3},{4,36},{36... | collective-permute-start | bytes 4718600 | tf_op jit(solution)/shard_map/ppermute | solution.py:130
  93.5 1.2 broadcast_in_dim.21
  94.7 4.4 %all-to-all-start.1 = ((bf16[4,16,64,128]{3,2,1,0:T(8,128)(2,1)}), bf16[4,16,64,128]{3,2,1,0:T(8,128)(2,1)}, u32[]{:S(2)}, u32[]{:S(2)}) async-start(bf16[4,16,64,128]{3,2,1,0:T(8,128)(2,1)} %broadcast_in_dim.21), calls=%async_computation.1 | async-start | bytes 2097152 | tf_op jit(solution)/shard_map/all_to_all | solution.py:134
  99.1 0.7 maximum_convert_fusion
  99.8 0.1 reshape.25
  99.9 14.5 %all-to-all-done.1.w_ref = bf16[4,16,64,128]{3,2,1,0:T(8,128)(2,1)} async-done(((bf16[4,16,64,128]{3,2,1,0:T(8,128)(2,1)}), bf16[4,16,64,128]{3,2,1,0:T(8,128)(2,1)}, u32[]{:S(2)}, u32[]{:S(2)}) %all-to-all-start.1) | async-done | bytes 1048608 | tf_op jit(solution)/shard_map/all_to_all | solution.py:134
  114.4 0.0 collective-permute-done.10.far_ref.far2_ref
  114.4 0.0 copy-done
  114.4 4.9 %shard_map.46 = bf16[1536,512]{1,0:T(8,128)(2,1)S(1)} custom-call(s32[16]{0:T(128)S(1)} %get-tuple-element.12.first_ref, s32[16]{0:T(128)S(1)} %get-tuple-element.11.second_ref, s32[1]{0:T(128)} %bitcast.10.where_ref, bf16[4,16,64,128]{3,2,1,0:T(8,128)(2,1)} %all-to-all-done.1.w_ref, bf16[1536,512]{1,0:T(8,128)(2,1)S(1)} %copy-done, ...), custom_call_target="tpu_custom_call" | custom-call | flops 1610612736 | bytes 6291456 | tf_op jit(solution)/shard_map/pallas_call | solution.py:104
  119.4 0.0 copy-start.1
  119.4 1.2 copy-done.1
  120.5 6.4 %all-to-all-start.2 = ((bf16[4,384,512]{2,1,0:T(8,128)(2,1)}), bf16[4,384,512]{2,1,0:T(8,128)(2,1)S(1)}, u32[]{:S(2)}, u32[]{:S(2)}) async-start(bf16[4,384,512]{2,1,0:T(8,128)(2,1)} %bitcast.28), calls=%async_computation.2 | async-start | bytes 3145728 | tf_op jit(solution)/shard_map/all_to_all | solution.py:186
  126.9 19.7 %all-to-all-done.2 = bf16[4,384,512]{2,1,0:T(8,128)(2,1)S(1)} async-done(((bf16[4,384,512]{2,1,0:T(8,128)(2,1)}), bf16[4,384,512]{2,1,0:T(8,128)(2,1)S(1)}, u32[]{:S(2)}, u32[]{:S(2)}) %all-to-all-start.2) | async-done | bytes 1572896 | tf_op jit(solution)/shard_map/all_to_all | solution.py:186
  146.6 0.4 reduce_sum.12
  147.1 4.3 %collective-permute-start.12 = (bf16[192,512]{1,0:T(8,128)(2,1)S(1)}, bf16[192,512]{1,0:T(8,128)(2,1)S(1)}, u32[]{:S(2)}, u32[]{:S(2)}) collective-permute-start(bf16[192,512]{1,0:T(8,128)(2,1)S(1)} %get-tuple-element.10), channel_id=1, source_target_pairs={{0,476},{1,477},{2,478},{3,479},{4,412},{5,413},{6,414},{7,415},{8... | collective-permute-start | bytes 589832 | tf_op jit(solution)/shard_map/ppermute | solution.py:192
  151.4 11.5 %collective-permute-start.11 = (bf16[192,512]{1,0:T(8,128)(2,1)S(1)}, bf16[192,512]{1,0:T(8,128)(2,1)S(1)}, u32[]{:S(2)}, u32[]{:S(2)}) collective-permute-start(bf16[192,512]{1,0:T(8,128)(2,1)S(1)} %get-tuple-element.9), channel_id=1, source_target_pairs={{0,448},{1,449},{2,450},{3,451},{4,384},{5,385},{6,386},{7,387},{8... | collective-permute-start | bytes 589832 | tf_op jit(solution)/shard_map/ppermute | solution.py:192
  162.9 4.6 %collective-permute-done.12 = bf16[192,512]{1,0:T(8,128)(2,1)S(1)} collective-permute-done((bf16[192,512]{1,0:T(8,128)(2,1)S(1)}, bf16[192,512]{1,0:T(8,128)(2,1)S(1)}, u32[]{:S(2)}, u32[]{:S(2)}) %collective-permute-start.12) | collective-permute-done | bytes 196640 | tf_op jit(solution)/shard_map/ppermute | solution.py:192
  167.4 13.8 %collective-permute-done.11 = bf16[192,512]{1,0:T(8,128)(2,1)S(1)} collective-permute-done((bf16[192,512]{1,0:T(8,128)(2,1)S(1)}, bf16[192,512]{1,0:T(8,128)(2,1)S(1)}, u32[]{:S(2)}, u32[]{:S(2)}) %collective-permute-start.11) | collective-permute-done | bytes 196640 | tf_op jit(solution)/shard_map/ppermute | solution.py:192
  181.3 0.1 add_convert_fusion
  181.3 0.7 reshape.24
  (13 shorter events, 0.2 us)
Async XLA Ops:
  6.5 84.4 %all-gather.2.cloned.1.call-start = ((), (), s32[]{:S(2)}) async-start(), calls=%async_computation.3 | async-start | bytes 1769472 | tf_op jit(solution)/shard_map/all_gather | solution.py:138
  6.5 48.0 %collective-permute-start.1 = (bf16[128,2048]{1,0:T(8,128)(2,1)}, bf16[128,2048]{1,0:T(8,128)(2,1)S(1)}, u32[]{:S(2)}, u32[]{:S(2)}) collective-permute-start(bf16[128,2048]{1,0:T(8,128)(2,1)} %param.6), channel_id=1, source_target_pairs={{0,32},{32,0},{1,33},{33,1},{2,34},{34,2},{3,35},{35,3},{4,36},{36... | collective-permute-start | bytes 1572872 | tf_op jit(solution)/shard_map/ppermute | solution.py:130
  17.9 18.1 %collective-permute-start.3 = (bf16[32,2048]{1,0:T(8,128)(2,1)S(1)}, bf16[32,2048]{1,0:T(8,128)(2,1)S(1)}, u32[]{:S(2)}, u32[]{:S(2)}) collective-permute-start(bf16[32,2048]{1,0:T(8,128)(2,1)S(1)} %constant_dynamic-slice_fusion.2), channel_id=1, source_target_pairs={{0,284},{4,280},{8,276},{12,272},{16,268},{20,264},{24,260},{28,25... | collective-permute-start | bytes 393224 | tf_op jit(solution)/shard_map/ppermute | solution.py:145
  26.4 27.2 %all-to-all-start = ((bf16[4,64,2176]{2,1,0:T(8,128)(2,1)}), bf16[4,64,2176]{2,1,0:T(8,128)(2,1)S(1)}, u32[]{:S(2)}, u32[]{:S(2)}) async-start(bf16[4,64,2176]{2,1,0:T(8,128)(2,1)} %broadcast_in_dim.8), calls=%async_computation | async-start | bytes 2228224 | tf_op jit(solution)/shard_map/all_to_all | solution.py:134
  30.4 23.3 %copy-start.4 = (bf16[128,2048]{1,0:T(8,128)(2,1)S(1)}, bf16[128,2048]{1,0:T(8,128)(2,1)}, u32[]{:S(2)}) copy-start(bf16[128,2048]{1,0:T(8,128)(2,1)} %param.6) | copy-start | bytes 1572868
  36.0 10.8 %collective-permute-start.4 = (bf16[32,2048]{1,0:T(8,128)(2,1)S(1)}, bf16[32,2048]{1,0:T(8,128)(2,1)S(1)}, u32[]{:S(2)}, u32[]{:S(2)}) collective-permute-start(bf16[32,2048]{1,0:T(8,128)(2,1)S(1)} %collective-permute-done.3), channel_id=1, source_target_pairs={{0,1},{1,2},{2,3},{3,0},{4,5},{5,6},{6,7},{7,4},{8,9},{9,10},{10,1... | collective-permute-start | bytes 393224 | tf_op jit(solution)/shard_map/ppermute | solution.py:156
  39.2 8.7 %collective-permute-start.5 = (bf16[32,2048]{1,0:T(8,128)(2,1)S(1)}, bf16[32,2048]{1,0:T(8,128)(2,1)S(1)}, u32[]{:S(2)}, u32[]{:S(2)}) collective-permute-start(bf16[32,2048]{1,0:T(8,128)(2,1)S(1)} %collective-permute-done.3), channel_id=1, source_target_pairs={{0,2},{1,3},{2,0},{3,1},{4,6},{5,7},{6,4},{7,5},{8,10},{9,11},{10,... | collective-permute-start | bytes 393224 | tf_op jit(solution)/shard_map/ppermute | solution.py:156
  43.7 6.1 %collective-permute-start.6 = (bf16[32,2048]{1,0:T(8,128)(2,1)S(1)}, bf16[32,2048]{1,0:T(8,128)(2,1)S(1)}, u32[]{:S(2)}, u32[]{:S(2)}) collective-permute-start(bf16[32,2048]{1,0:T(8,128)(2,1)S(1)} %collective-permute-done.3), channel_id=1, source_target_pairs={{0,3},{1,0},{2,1},{3,2},{4,7},{5,4},{6,5},{7,6},{8,11},{9,8},{10,9... | collective-permute-start | bytes 393224 | tf_op jit(solution)/shard_map/ppermute | solution.py:156
  49.9 5.3 %collective-permute-start.8 = (bf16[128,2048]{1,0:T(8,128)(2,1)S(1)}, bf16[128,2048]{1,0:T(8,128)(2,1)S(1)}, u32[]{:S(2)}, u32[]{:S(2)}) collective-permute-start(bf16[128,2048]{1,0:T(8,128)(2,1)S(1)} %constant_dynamic-update-slice_fusion), channel_id=1, source_target_pairs={{0,32},{32,0},{1,33},{33,1},{2,34},{34,2},{3,35},{35,3},{4,36},{36... | collective-permute-start | bytes 1572872 | tf_op jit(solution)/shard_map/ppermute | solution.py:130
  55.6 17.8 %collective-permute-start.9 = (bf16[272,128]{1,0:T(8,128)(2,1)S(1)}, bf16[272,128]{1,0:T(8,128)(2,1)S(1)}, u32[]{:S(2)}, u32[]{:S(2)}) collective-permute-start(bf16[272,128]{1,0:T(8,128)(2,1)S(1)} %get-tuple-element.16), channel_id=1, source_target_pairs={{0,60},{1,61},{2,62},{3,63},{4,124},{5,125},{6,126},{7,127},{8,188... | collective-permute-start | bytes 208904 | tf_op jit(solution)/shard_map/ppermute | solution.py:167
  62.4 11.2 %collective-permute-start.7 = (bf16[272,128]{1,0:T(8,128)(2,1)S(1)}, bf16[272,128]{1,0:T(8,128)(2,1)S(1)}, u32[]{:S(2)}, u32[]{:S(2)}) collective-permute-start(bf16[272,128]{1,0:T(8,128)(2,1)S(1)} %get-tuple-element.15), channel_id=1, source_target_pairs={{0,28},{1,29},{2,30},{3,31},{4,92},{5,93},{6,94},{7,95},{8,156},{9... | collective-permute-start | bytes 208904 | tf_op jit(solution)/shard_map/ppermute | solution.py:167
  69.6 18.1 %collective-permute-start.2 = (bf16[272,128]{1,0:T(8,128)(2,1)S(1)}, bf16[272,128]{1,0:T(8,128)(2,1)S(1)}, u32[]{:S(2)}, u32[]{:S(2)}) collective-permute-start(bf16[272,128]{1,0:T(8,128)(2,1)S(1)} %get-tuple-element.14), channel_id=1, source_target_pairs={{0,40},{1,41},{2,42},{3,43},{4,104},{5,105},{6,106},{7,107},{8,168... | collective-permute-start | bytes 208904 | tf_op jit(solution)/shard_map/ppermute | solution.py:167
  71.5 18.4 %collective-permute-start = (bf16[272,128]{1,0:T(8,128)(2,1)S(1)}, bf16[272,128]{1,0:T(8,128)(2,1)S(1)}, u32[]{:S(2)}, u32[]{:S(2)}) collective-permute-start(bf16[272,128]{1,0:T(8,128)(2,1)S(1)} %get-tuple-element.13), channel_id=1, source_target_pairs={{0,8},{1,9},{2,10},{3,11},{4,72},{5,73},{6,74},{7,75},{8,136},{9,1... | collective-permute-start | bytes 208904 | tf_op jit(solution)/shard_map/ppermute | solution.py:167
  87.8 3.1 %copy-start.2 = (bf16[1,272,128]{1,0,2:T(2,128)(2,1)}, bf16[1,272,128]{1,0,2:T(2,128)(2,1)S(1)}, u32[]{:S(2)}) copy-start(bf16[1,272,128]{1,0,2:T(2,128)(2,1)S(1)} %copy.18) | copy-start | bytes 208900
  90.1 0.9 copy-start.3
  91.0 23.4 %collective-permute-start.10 = (bf16[1536,512]{1,0:T(8,128)(2,1)}, bf16[1536,512]{1,0:T(8,128)(2,1)S(1)}, u32[]{:S(2)}, u32[]{:S(2)}) collective-permute-start(bf16[1536,512]{1,0:T(8,128)(2,1)} %all-gather.2.cloned.1.call-done.near_ref.near2_ref), channel_id=1, source_target_pairs={{0,32},{32,0},{1,33},{33,1},{2,34},{34,2},{3,35},{35,3},{4,36},{36... | collective-permute-start | bytes 4718600 | tf_op jit(solution)/shard_map/ppermute | solution.py:130
  94.7 19.7 %copy-start = (bf16[1536,512]{1,0:T(8,128)(2,1)S(1)}, bf16[1536,512]{1,0:T(8,128)(2,1)}, u32[]{:S(2)}) copy-start(bf16[1536,512]{1,0:T(8,128)(2,1)} %all-gather.2.cloned.1.call-done.near_ref.near2_ref) | copy-start | bytes 4718596
  94.7 19.7 %all-to-all-start.1 = ((bf16[4,16,64,128]{3,2,1,0:T(8,128)(2,1)}), bf16[4,16,64,128]{3,2,1,0:T(8,128)(2,1)}, u32[]{:S(2)}, u32[]{:S(2)}) async-start(bf16[4,16,64,128]{3,2,1,0:T(8,128)(2,1)} %broadcast_in_dim.21), calls=%async_computation.1 | async-start | bytes 2097152 | tf_op jit(solution)/shard_map/all_to_all | solution.py:134
  119.4 1.2 copy-start.1
  120.5 26.0 %all-to-all-start.2 = ((bf16[4,384,512]{2,1,0:T(8,128)(2,1)}), bf16[4,384,512]{2,1,0:T(8,128)(2,1)S(1)}, u32[]{:S(2)}, u32[]{:S(2)}) async-start(bf16[4,384,512]{2,1,0:T(8,128)(2,1)} %bitcast.28), calls=%async_computation.2 | async-start | bytes 3145728 | tf_op jit(solution)/shard_map/all_to_all | solution.py:186
  147.1 20.4 %collective-permute-start.12 = (bf16[192,512]{1,0:T(8,128)(2,1)S(1)}, bf16[192,512]{1,0:T(8,128)(2,1)S(1)}, u32[]{:S(2)}, u32[]{:S(2)}) collective-permute-start(bf16[192,512]{1,0:T(8,128)(2,1)S(1)} %get-tuple-element.10), channel_id=1, source_target_pairs={{0,476},{1,477},{2,478},{3,479},{4,412},{5,413},{6,414},{7,415},{8... | collective-permute-start | bytes 589832 | tf_op jit(solution)/shard_map/ppermute | solution.py:192
  151.4 29.9 %collective-permute-start.11 = (bf16[192,512]{1,0:T(8,128)(2,1)S(1)}, bf16[192,512]{1,0:T(8,128)(2,1)S(1)}, u32[]{:S(2)}, u32[]{:S(2)}) collective-permute-start(bf16[192,512]{1,0:T(8,128)(2,1)S(1)} %get-tuple-element.9), channel_id=1, source_target_pairs={{0,448},{1,449},{2,450},{3,451},{4,384},{5,385},{6,386},{7,387},{8... | collective-permute-start | bytes 589832 | tf_op jit(solution)/shard_map/ppermute | solution.py:192
Sparse Core Ops, SparseCore 0:
  17.1 50.0 all-gather.1

commit v10 on v9

--- a/solution.py
+++ b/solution.py
@@ -26,16 +26,16 @@
                         yield h, x, c, l, y
 
 
-INNER, OUTER = (2, 3, 4, 5), (7, 6, 1, 0)
+PLACE = ((6, 7, 3, 2, 1, 0, 4, 5), (7, 6, 2, 3, 0, 1, 4, 5))
+ROWS = ((2, 6), (3, 7), (4, 0), (5, 1))
 
 
 def place(h, h2, x2):
-    l = (INNER if h2 == h else OUTER)[x2]
-    return l if h == 0 else L - 1 - l
+    return PLACE[h][h2 * X + x2]
 
 
 def chunk(h, l):
-    return next((h2, x2) for h2 in range(H) for x2 in range(X) if place(h, h2, x2) == l)
+    return divmod(PLACE[h].index(l), X)
 
 
 def weight_perm(k, d):
@@ -47,7 +47,7 @@
 
 def result_perm(k):
     return [
-        (flat(h, x, c, l, y), flat(*chunk(h, l), c, L - 1 - x if h ^ k else x, y))
+        (flat(h, x, c, l, y), flat(*chunk(h, l), c, ROWS[x][h ^ k], y))
         for h, x, c, l, y in coords()
     ]
 
@@ -57,8 +57,7 @@
 
 
 def contract_kernel(
-    first_ref, second_ref, where_ref, w_ref, near_ref, near2_ref, far_ref, far2_ref, out_ref,
-    acc_ref, s_ref
+    where_ref, first_ref, second_ref, w_ref, near_ref, far_ref, out_ref, acc_ref, s_ref
 ):
     slots, rows, cols = w_ref.shape[1:]
 
@@ -79,47 +78,38 @@
         lax.fori_loop(0, slots, add, 0)
         s_ref[...] = acc_ref[...].astype(jnp.bfloat16)
 
-    block, depth = near_ref.shape
+    depth = near_ref.shape[1]
     at_near = pl.multiple_of(where_ref[0] * depth, depth)
     at_far = pl.multiple_of((1 - where_ref[0]) * depth, depth)
     f32 = jnp.float32
-    for part, (near, far) in enumerate(((near_ref, far_ref), (near2_ref, far2_ref))):
-        total = jnp.dot(near[...], s_ref[pl.ds(at_near, depth)], preferred_element_type=f32)
-        total += jnp.dot(far[...], s_ref[pl.ds(at_far, depth)], preferred_element_type=f32)
-        out_ref[part * block : (part + 1) * block] = total.astype(jnp.bfloat16)
+    total = jnp.dot(near_ref[...], s_ref[pl.ds(at_near, depth)], preferred_element_type=f32)
+    total += jnp.dot(far_ref[...], s_ref[pl.ds(at_far, depth)], preferred_element_type=f32)
+    out_ref[...] = total.astype(jnp.bfloat16)
 
 
-def contract(first, second, where, w, near, far):
+def contract(where, first, second, w, near, far):
     q, depth = near.shape
-    cols = w.shape[3]
+    cols = OCC * w.shape[3]
     block = q // L
-
-    def rows_of(part):
-        def of_step(x, *_):
-            l = L - 1 - x if part else x
-            return jnp.where(l % 2 == 0, l // 2, (2 * L - 1 - l) // 2), 0
-
-        return pl.BlockSpec((block, depth), of_step)
-
+    rows = [pl.BlockSpec((block, depth), lambda x, where, *_: (where[1 + x], 0))] * 2
     return pl.pallas_call(
         contract_kernel,
         grid_spec=pltpu.PrefetchScalarGridSpec(
             num_scalar_prefetch=3,
             grid=(X,),
-            in_specs=[pl.BlockSpec(w.shape, lambda s, *_: (0, 0, 0, 0))]
-            + [rows_of(0), rows_of(1)] * 2,
-            out_specs=pl.BlockSpec((2 * block, OCC * cols), lambda s, *_: (s, 0)),
+            in_specs=[pl.BlockSpec(w.shape, lambda x, *_: (0, 0, 0, 0))] + rows,
+            out_specs=pl.BlockSpec((block, cols), lambda x, *_: (x, 0)),
             scratch_shapes=[
-                pltpu.VMEM((2 * depth, OCC * cols), jnp.float32),
-                pltpu.VMEM((2 * depth, OCC * cols), jnp.bfloat16),
+                pltpu.VMEM((2 * depth, cols), jnp.float32),
+                pltpu.VMEM((2 * depth, cols), jnp.bfloat16),
             ],
         ),
-        out_shape=jax.ShapeDtypeStruct((q, OCC * cols), jnp.bfloat16),
+        out_shape=jax.ShapeDtypeStruct((X * block, cols), jnp.bfloat16),
         compiler_params=pltpu.CompilerParams(vmem_limit_bytes=32 * 1024 * 1024),
         cost_estimate=pl.CostEstimate(
-            flops=2 * q * 2 * depth * OCC * cols, bytes_accessed=6 * 2**20, transcendentals=0
+            flops=2 * q * depth * cols, bytes_accessed=4 * 2**20, transcendentals=0
         ),
-    )(first, second, where, w, near, near, far, far)
+    )(where, first, second, w, near, far)
 
 
 def on_device(amplitudes, fitting, coefficients, pair_list):
@@ -179,17 +169,16 @@
     w_all = gather(w, "y", Y)
     w_all = w_all.reshape(Y, slots, rows, n_mu)
 
-    where = c.astype(jnp.int32)[None]
-    partial = contract(pairs[:, 0], pairs[:, 1], where, w_all, b_near, b_far)
-    cols = partial.shape[1]
-    partial = partial.reshape(X, 2 * q_own, cols)
-    partial = lax.all_to_all(partial, "x", split_axis=0, concat_axis=0, tiled=True)
-    summed = jnp.sum(partial.astype(f32), axis=0).astype(bf16)
-
-    total = jnp.zeros((q_own, cols), f32)
+    at = jnp.asarray([[RING.index(two[s]) for two in ROWS] for s in range(H)], jnp.int32)
+    total = 0
     for k in range(H):
-        piece = lax.dynamic_slice_in_dim(summed, (h ^ k) * q_own, q_own, 0)
-        total += lax.ppermute(piece, AXES, result_perm(k)).astype(f32)
+        where = jnp.where(h == k, at[0], at[1])
+        where = jnp.concatenate([c.astype(jnp.int32)[None], where])
+        v = contract(where, pairs[:, 0], pairs[:, 1], w_all, b_near, b_far)
+        v = v.reshape(X, q_own, -1)
+        v = lax.all_to_all(v, "x", split_axis=0, concat_axis=0, tiled=True)
+        v = jnp.sum(v.astype(f32), axis=0).astype(bf16)
+        total += lax.ppermute(v, AXES, result_perm(k)).astype(f32)
     return total.astype(bf16).reshape(q_own, occ, n_mu)
 
 

time: 190 us -> 192 us (1.011)
  Pallas kernels: 4.94 us -> 10.6 us
  waiting for transfers between devices: 77.2 us -> 74.6 us
    ppermute x2, starting transfers between devices: 15.8 us -> 3.84 us  [on_device(): total += lax.ppermute(v, AXES, result_perm(k)).astype(f32)]
    all_to_all x1 -> x2, starting transfers between devices: 6.35 us -> 14.2 us  [on_device(): v = lax.all_to_all(v, 'x', split_axis=0, concat_axis=0, tiled=True)]
    ppermute x4, waiting for transfers between devices: 15.8 us -> 8.92 us  [on_device(): lax.ppermute(jnp.concatenate([v, info], axis=0), AXES, weight_perm(k, d))]
    ppermute x4, starting transfers between devices: 17.8 us -> 24.6 us  [on_device(): lax.ppermute(jnp.concatenate([v, info], axis=0), AXES, weight_perm(k, d))]
    pallas_call x1 -> x2, Pallas kernels: 4.94 us -> 10.6 us  [contract(): pl.pallas_call(contract_kernel, grid_spec=pltpu.PrefetchScalarGridSpec(nu...]
    ppermute x2, waiting for transfers between devices: 18.4 us -> 24 us  [on_device(): total += lax.ppermute(v, AXES, result_perm(k)).astype(f32)]
    all_to_all x1 -> x2, waiting for transfers between devices: 19.7 us -> 14.9 us  [on_device(): v = lax.all_to_all(v, 'x', split_axis=0, concat_axis=0, tiled=True)]
    ppermute x3, waiting for transfers between devices: 3 us -> 6 us  [on_device(): v = lax.ppermute(piece, 'y', shift(Y, k)) if k else piece]
  transfers between devices with their start and end apart: 17 -> 18, of which waited for: 10 -> 10; matrix products, arithmetic and copies ran while one was open for 6% -> 5% of each run, Pallas kernels for 0% -> 3%
where the time goes in v10:
time: 192 us; the launch traced here: 190 us
  starting transfers between devices  80 us (42%)
  waiting for transfers between devices  74.6 us (39%)
  between operations  13.8 us (7%)
  Pallas kernels  10.6 us (6%)
  local copies, waits for them, and re-layouts  6.8 us (4%)
  other arithmetic  2.71 us (1%)
    ppermute x4, starting transfers between devices, on_device(): lax.ppermute(jnp.concatenate([v, info], axis=0), AXES, weight_perm(k, d))  24.6 us
    ppermute x2, waiting for transfers between devices, on_device(): total += lax.ppermute(v, AXES, result_perm(k)).astype(f32)  24 us
    all_to_all x2, waiting for transfers between devices, gather(): return lax.all_to_all(v, axes, split_axis=0, concat_axis=0, tiled=True)  14.9 us
    all_to_all x2, waiting for transfers between devices, on_device(): v = lax.all_to_all(v, 'x', split_axis=0, concat_axis=0, tiled=True)  14.9 us
    ppermute x3, starting transfers between devices, swap_core(): return lax.ppermute(v, 'c', shift(C, 1))  14.4 us
    all_to_all x2, starting transfers between devices, on_device(): v = lax.all_to_all(v, 'x', split_axis=0, concat_axis=0, tiled=True)  14.2 us
    pallas_call x2, Pallas kernels, contract(): pl.pallas_call(contract_kernel, grid_spec=pltpu.PrefetchScalarGridSpec(nu...  10.6 us
    ppermute x3, starting transfers between devices, on_device(): v = lax.ppermute(piece, 'y', shift(Y, k)) if k else piece  9.49 us
  transfers between devices with their start and end apart: 18, of which 10 were waited for; matrix products, arithmetic and copies ran while one was open for 5% of the time, Pallas kernels for 3%

profile of v10, /device:TPU:1, one launch (start us, length us, event | category | flops | bytes accessed | tf_op | source)
XLA Modules:
  0.0 190.2 jit_solution(13355820972231480161)
XLA Ops:
  6.5 0.0 all-gather.2.cloned.1.call-start
  6.5 1.6 copy.27
  8.2 0.0 all-gather.2.cloned.1.call-update
  8.2 8.8 %collective-permute-start.1 = (bf16[128,2048]{1,0:T(8,128)(2,1)}, bf16[128,2048]{1,0:T(8,128)(2,1)S(1)}, u32[]{:S(2)}, u32[]{:S(2)}) collective-permute-start(bf16[128,2048]{1,0:T(8,128)(2,1)} %param.7), channel_id=1, source_target_pairs={{0,32},{32,0},{1,33},{33,1},{2,34},{34,2},{3,35},{35,3},{4,36},{36... | collective-permute-start | bytes 1572872 | tf_op jit(solution)/shard_map/ppermute | solution.py:120
  17.0 0.9 constant_dynamic-slice_fusion
  17.9 5.7 %collective-permute-start.3 = (bf16[32,2048]{1,0:T(8,128)(2,1)S(1)}, bf16[32,2048]{1,0:T(8,128)(2,1)S(1)}, u32[]{:S(2)}, u32[]{:S(2)}) collective-permute-start(bf16[32,2048]{1,0:T(8,128)(2,1)S(1)} %constant_dynamic-slice_fusion), channel_id=1, source_target_pairs={{0,284},{4,280},{8,276},{12,272},{16,268},{20,264},{24,260},{28,25... | collective-permute-start | bytes 393224 | tf_op jit(solution)/shard_map/ppermute | solution.py:135
  23.7 0.7 convert_element_type.38
  24.3 1.0 fusion.5
  25.3 1.1 broadcast_in_dim.9
  26.4 4.0 %all-to-all-start = ((bf16[4,64,2176]{2,1,0:T(8,128)(2,1)}), bf16[4,64,2176]{2,1,0:T(8,128)(2,1)S(1)}, u32[]{:S(2)}, u32[]{:S(2)}) async-start(bf16[4,64,2176]{2,1,0:T(8,128)(2,1)} %broadcast_in_dim.9), calls=%async_computation | async-start | bytes 2228224 | tf_op jit(solution)/shard_map/all_to_all | solution.py:124
  30.4 5.6 %collective-permute-done.3 = bf16[32,2048]{1,0:T(8,128)(2,1)S(1)} collective-permute-done((bf16[32,2048]{1,0:T(8,128)(2,1)S(1)}, bf16[32,2048]{1,0:T(8,128)(2,1)S(1)}, u32[]{:S(2)}, u32[]{:S(2)}) %collective-permute-start.3) | collective-permute-done | bytes 131104 | tf_op jit(solution)/shard_map/ppermute | solution.py:135
  36.0 4.6 %collective-permute-start.6 = (bf16[32,2048]{1,0:T(8,128)(2,1)S(1)}, bf16[32,2048]{1,0:T(8,128)(2,1)S(1)}, u32[]{:S(2)}, u32[]{:S(2)}) collective-permute-start(bf16[32,2048]{1,0:T(8,128)(2,1)S(1)} %collective-permute-done.3), channel_id=1, source_target_pairs={{0,3},{1,0},{2,1},{3,2},{4,7},{5,4},{6,5},{7,6},{8,11},{9,8},{10,9... | collective-permute-start | bytes 393224 | tf_op jit(solution)/shard_map/ppermute | solution.py:146
  40.6 2.3 %collective-permute-start.5 = (bf16[32,2048]{1,0:T(8,128)(2,1)S(1)}, bf16[32,2048]{1,0:T(8,128)(2,1)S(1)}, u32[]{:S(2)}, u32[]{:S(2)}) collective-permute-start(bf16[32,2048]{1,0:T(8,128)(2,1)S(1)} %collective-permute-done.3), channel_id=1, source_target_pairs={{0,2},{1,3},{2,0},{3,1},{4,6},{5,7},{6,4},{7,5},{8,10},{9,11},{10,... | collective-permute-start | bytes 393224 | tf_op jit(solution)/shard_map/ppermute | solution.py:146
  42.9 2.6 %collective-permute-start.4 = (bf16[32,2048]{1,0:T(8,128)(2,1)S(1)}, bf16[32,2048]{1,0:T(8,128)(2,1)S(1)}, u32[]{:S(2)}, u32[]{:S(2)}) collective-permute-start(bf16[32,2048]{1,0:T(8,128)(2,1)S(1)} %collective-permute-done.3), channel_id=1, source_target_pairs={{0,1},{1,2},{2,3},{3,0},{4,5},{5,6},{6,7},{7,4},{8,9},{9,10},{10,1... | collective-permute-start | bytes 393224 | tf_op jit(solution)/shard_map/ppermute | solution.py:146
  45.6 6.0 %collective-permute-done.4 = bf16[32,2048]{1,0:T(8,128)(2,1)S(1)} collective-permute-done((bf16[32,2048]{1,0:T(8,128)(2,1)S(1)}, bf16[32,2048]{1,0:T(8,128)(2,1)S(1)}, u32[]{:S(2)}, u32[]{:S(2)}) %collective-permute-start.4) | collective-permute-done | bytes 131104 | tf_op jit(solution)/shard_map/ppermute | solution.py:146
  51.6 0.0 collective-permute-done.5
  51.6 0.0 copy-start.1
  51.6 0.0 collective-permute-done.6
  51.7 3.3 %collective-permute-start.8 = (bf16[128,2048]{1,0:T(8,128)(2,1)S(1)}, bf16[128,2048]{1,0:T(8,128)(2,1)S(1)}, u32[]{:S(2)}, u32[]{:S(2)}) collective-permute-start(bf16[128,2048]{1,0:T(8,128)(2,1)S(1)} %constant_dynamic-update-slice_fusion), channel_id=1, source_target_pairs={{0,32},{32,0},{1,33},{33,1},{2,34},{34,2},{3,35},{35,3},{4,36},{36... | collective-permute-start | bytes 1572872 | tf_op jit(solution)/shard_map/ppermute | solution.py:120
  54.9 0.0 all-to-all-done
  55.0 0.4 convolution_convert_fusion.1
  55.4 0.0 copy-done.1
  55.4 0.4 convolution_convert_fusion.3
  55.9 0.0 collective-permute-done.1
  55.9 0.4 convolution_convert_fusion.2
  56.3 0.1 collective-permute-done.8
  56.4 0.4 convolution_convert_fusion
  56.9 2.5 %collective-permute-start.9 = (bf16[272,128]{1,0:T(8,128)(2,1)S(1)}, bf16[272,128]{1,0:T(8,128)(2,1)S(1)}, u32[]{:S(2)}, u32[]{:S(2)}) collective-permute-start(bf16[272,128]{1,0:T(8,128)(2,1)S(1)} %get-tuple-element.16), channel_id=1, source_target_pairs={{0,36},{1,37},{2,38},{3,39},{4,100},{5,101},{6,102},{7,103},{8,164... | collective-permute-start | bytes 208904 | tf_op jit(solution)/shard_map/ppermute | solution.py:157
  59.4 3.1 %collective-permute-start.7 = (bf16[272,128]{1,0:T(8,128)(2,1)S(1)}, bf16[272,128]{1,0:T(8,128)(2,1)S(1)}, u32[]{:S(2)}, u32[]{:S(2)}) collective-permute-start(bf16[272,128]{1,0:T(8,128)(2,1)S(1)} %get-tuple-element.15), channel_id=1, source_target_pairs={{0,4},{1,5},{2,6},{3,7},{4,68},{5,69},{6,70},{7,71},{8,132},{9,133... | collective-permute-start | bytes 208904 | tf_op jit(solution)/shard_map/ppermute | solution.py:157
  62.6 10.3 %collective-permute-start.2 = (bf16[272,128]{1,0:T(8,128)(2,1)S(1)}, bf16[272,128]{1,0:T(8,128)(2,1)S(1)}, u32[]{:S(2)}, u32[]{:S(2)}) collective-permute-start(bf16[272,128]{1,0:T(8,128)(2,1)S(1)} %get-tuple-element.14), channel_id=1, source_target_pairs={{0,56},{1,57},{2,58},{3,59},{4,120},{5,121},{6,122},{7,123},{8,184... | collective-permute-start | bytes 208904 | tf_op jit(solution)/shard_map/ppermute | solution.py:157
  72.8 8.7 %collective-permute-start = (bf16[272,128]{1,0:T(8,128)(2,1)S(1)}, bf16[272,128]{1,0:T(8,128)(2,1)S(1)}, u32[]{:S(2)}, u32[]{:S(2)}) collective-permute-start(bf16[272,128]{1,0:T(8,128)(2,1)S(1)} %get-tuple-element.13), channel_id=1, source_target_pairs={{0,24},{1,25},{2,26},{3,27},{4,88},{5,89},{6,90},{7,91},{8,152},{9... | collective-permute-start | bytes 208904 | tf_op jit(solution)/shard_map/ppermute | solution.py:157
  81.6 0.0 collective-permute-done.9
  81.6 0.2 copy.21
  81.8 0.0 collective-permute-done.7
  81.8 0.2 copy.20
  82.0 7.0 %collective-permute-done.2 = bf16[272,128]{1,0:T(8,128)(2,1)S(1)} collective-permute-done((bf16[272,128]{1,0:T(8,128)(2,1)S(1)}, bf16[272,128]{1,0:T(8,128)(2,1)S(1)}, u32[]{:S(2)}, u32[]{:S(2)}) %collective-permute-start.2) | collective-permute-done | bytes 69664 | tf_op jit(solution)/shard_map/ppermute | solution.py:157
  89.0 0.2 copy.19
  89.2 1.9 collective-permute-done
  91.1 0.2 copy.18
  91.3 0.6 pad_maximum_fusion
  91.9 0.2 copy.22
  92.2 0.0 all-gather.2.cloned.1.call-done.near_ref
  92.2 2.3 %collective-permute-start.10 = (bf16[1536,512]{1,0:T(8,128)(2,1)}, bf16[1536,512]{1,0:T(8,128)(2,1)}, u32[]{:S(2)}, u32[]{:S(2)}) collective-permute-start(bf16[1536,512]{1,0:T(8,128)(2,1)} %all-gather.2.cloned.1.call-done.near_ref), channel_id=1, source_target_pairs={{0,32},{32,0},{1,33},{33,1},{2,34},{34,2},{3,35},{35,3},{4,36},{36... | collective-permute-start | bytes 4718600 | tf_op jit(solution)/shard_map/ppermute | solution.py:120
  94.5 1.2 broadcast_in_dim.22
  95.7 3.6 %all-to-all-start.1 = ((bf16[4,16,64,128]{3,2,1,0:T(8,128)(2,1)}), bf16[4,16,64,128]{3,2,1,0:T(8,128)(2,1)S(1)}, u32[]{:S(2)}, u32[]{:S(2)}) async-start(bf16[4,16,64,128]{3,2,1,0:T(8,128)(2,1)} %broadcast_in_dim.22), calls=%async_computation.1 | async-start | bytes 2097152 | tf_op jit(solution)/shard_map/all_to_all | solution.py:124
  99.4 0.0 copy-done.2
  99.4 0.1 pad_add_fusion
  99.5 0.1 reshape.33
  99.6 14.9 %all-to-all-done.1.w_ref = bf16[4,16,64,128]{3,2,1,0:T(8,128)(2,1)S(1)} async-done(((bf16[4,16,64,128]{3,2,1,0:T(8,128)(2,1)}), bf16[4,16,64,128]{3,2,1,0:T(8,128)(2,1)S(1)}, u32[]{:S(2)}, u32[]{:S(2)}) %all-to-all-start.1) | async-done | bytes 1048608 | tf_op jit(solution)/shard_map/all_to_all | solution.py:124
  114.6 0.0 collective-permute-done.10.far_ref
  114.6 5.3 %shard_map.55 = bf16[768,512]{1,0:T(8,128)(2,1)} custom-call(s32[5]{0:T(128)S(1)} %get-tuple-element.17.where_ref, s32[16]{0:T(128)S(1)} %get-tuple-element.12.first_ref, s32[16]{0:T(128)S(1)} %get-tuple-element.11.second_ref, bf16[4,16,64,128]{3,2,1,0:T(8,128)(2,1)S(1)} %all-to-all-done.1.w_ref, bf16[1536,512]{1,0:T(8,128)(2,1)S(1)} %copy-done, ...), custom_call_target="tpu_custom_call" | custom-call | flops 805306368 | bytes 4194304 | tf_op jit(solution)/shard_map/pallas_call | solution.py:95
  119.9 10.7 %all-to-all-start.2 = ((bf16[4,192,512]{2,1,0:T(8,128)(2,1)}), bf16[4,192,512]{2,1,0:T(8,128)(2,1)S(1)}, u32[]{:S(2)}, u32[]{:S(2)}) async-start(bf16[4,192,512]{2,1,0:T(8,128)(2,1)} %bitcast.13), calls=%async_computation.2 | async-start | bytes 1572864 | tf_op jit(solution)/shard_map/all_to_all | solution.py:179
  130.6 5.3 %shard_map.56 = bf16[768,512]{1,0:T(8,128)(2,1)} custom-call(s32[5]{0:T(128)S(1)} %get-tuple-element.18.where_ref, s32[16]{0:T(128)S(1)} %get-tuple-element.12.first_ref, s32[16]{0:T(128)S(1)} %get-tuple-element.11.second_ref, bf16[4,16,64,128]{3,2,1,0:T(8,128)(2,1)S(1)} %all-to-all-done.1.w_ref, bf16[1536,512]{1,0:T(8,128)(2,1)S(1)} %copy-done, ...), custom_call_target="tpu_custom_call" | custom-call | flops 805306368 | bytes 4194304 | tf_op jit(solution)/shard_map/pallas_call | solution.py:95
  135.9 5.8 %all-to-all-done.2 = bf16[4,192,512]{2,1,0:T(8,128)(2,1)S(1)} async-done(((bf16[4,192,512]{2,1,0:T(8,128)(2,1)}), bf16[4,192,512]{2,1,0:T(8,128)(2,1)S(1)}, u32[]{:S(2)}, u32[]{:S(2)}) %all-to-all-start.2) | async-done | bytes 786464 | tf_op jit(solution)/shard_map/all_to_all | solution.py:179
  141.8 3.5 %all-to-all-start.3 = ((bf16[4,192,512]{2,1,0:T(8,128)(2,1)}), bf16[4,192,512]{2,1,0:T(8,128)(2,1)S(1)}, u32[]{:S(2)}, u32[]{:S(2)}) async-start(bf16[4,192,512]{2,1,0:T(8,128)(2,1)} %bitcast.15), calls=%async_computation.3 | async-start | bytes 1572864 | tf_op jit(solution)/shard_map/all_to_all | solution.py:179
  145.3 0.1 reduce_sum.24
  145.4 1.9 %collective-permute-start.11 = (bf16[192,512]{1,0:T(8,128)(2,1)S(1)}, bf16[192,512]{1,0:T(8,128)(2,1)S(1)}, u32[]{:S(2)}, u32[]{:S(2)}) collective-permute-start(bf16[192,512]{1,0:T(8,128)(2,1)S(1)} %reduce_sum.24), channel_id=1, source_target_pairs={{0,328},{1,329},{2,330},{3,331},{4,264},{5,265},{6,266},{7,267},{8... | collective-permute-start | bytes 589832 | tf_op jit(solution)/shard_map/ppermute | solution.py:181
  147.4 9.1 %all-to-all-done.3 = bf16[4,192,512]{2,1,0:T(8,128)(2,1)S(1)} async-done(((bf16[4,192,512]{2,1,0:T(8,128)(2,1)}), bf16[4,192,512]{2,1,0:T(8,128)(2,1)S(1)}, u32[]{:S(2)}, u32[]{:S(2)}) %all-to-all-start.3) | async-done | bytes 786464 | tf_op jit(solution)/shard_map/all_to_all | solution.py:179
  156.4 0.1 reduce_sum.25
  156.6 1.9 %collective-permute-start.12 = (bf16[192,512]{1,0:T(8,128)(2,1)S(1)}, bf16[192,512]{1,0:T(8,128)(2,1)S(1)}, u32[]{:S(2)}, u32[]{:S(2)}) collective-permute-start(bf16[192,512]{1,0:T(8,128)(2,1)S(1)} %reduce_sum.25), channel_id=1, source_target_pairs={{0,344},{1,345},{2,346},{3,347},{4,280},{5,281},{6,282},{7,283},{8... | collective-permute-start | bytes 589832 | tf_op jit(solution)/shard_map/ppermute | solution.py:181
  158.5 2.5 %collective-permute-done.11 = bf16[192,512]{1,0:T(8,128)(2,1)S(1)} collective-permute-done((bf16[192,512]{1,0:T(8,128)(2,1)S(1)}, bf16[192,512]{1,0:T(8,128)(2,1)S(1)}, u32[]{:S(2)}, u32[]{:S(2)}) %collective-permute-start.11) | collective-permute-done | bytes 196640 | tf_op jit(solution)/shard_map/ppermute | solution.py:181
  161.0 21.6 %collective-permute-done.12 = bf16[192,512]{1,0:T(8,128)(2,1)S(1)} collective-permute-done((bf16[192,512]{1,0:T(8,128)(2,1)S(1)}, bf16[192,512]{1,0:T(8,128)(2,1)S(1)}, u32[]{:S(2)}, u32[]{:S(2)}) %collective-permute-start.12) | collective-permute-done | bytes 196640 | tf_op jit(solution)/shard_map/ppermute | solution.py:181
  182.5 0.1 add_convert_fusion
  182.6 0.7 reshape.32
  (16 shorter events, 0.2 us)
Async XLA Ops:
  6.5 85.7 %all-gather.2.cloned.1.call-start = ((), (), s32[]{:S(2)}) async-start(), calls=%async_computation.4 | async-start | bytes 1769472 | tf_op jit(solution)/shard_map/all_gather | solution.py:128
  8.2 47.7 %collective-permute-start.1 = (bf16[128,2048]{1,0:T(8,128)(2,1)}, bf16[128,2048]{1,0:T(8,128)(2,1)S(1)}, u32[]{:S(2)}, u32[]{:S(2)}) collective-permute-start(bf16[128,2048]{1,0:T(8,128)(2,1)} %param.7), channel_id=1, source_target_pairs={{0,32},{32,0},{1,33},{33,1},{2,34},{34,2},{3,35},{35,3},{4,36},{36... | collective-permute-start | bytes 1572872 | tf_op jit(solution)/shard_map/ppermute | solution.py:120
  17.9 18.1 %collective-permute-start.3 = (bf16[32,2048]{1,0:T(8,128)(2,1)S(1)}, bf16[32,2048]{1,0:T(8,128)(2,1)S(1)}, u32[]{:S(2)}, u32[]{:S(2)}) collective-permute-start(bf16[32,2048]{1,0:T(8,128)(2,1)S(1)} %constant_dynamic-slice_fusion), channel_id=1, source_target_pairs={{0,284},{4,280},{8,276},{12,272},{16,268},{20,264},{24,260},{28,25... | collective-permute-start | bytes 393224 | tf_op jit(solution)/shard_map/ppermute | solution.py:135
  26.4 28.5 %all-to-all-start = ((bf16[4,64,2176]{2,1,0:T(8,128)(2,1)}), bf16[4,64,2176]{2,1,0:T(8,128)(2,1)S(1)}, u32[]{:S(2)}, u32[]{:S(2)}) async-start(bf16[4,64,2176]{2,1,0:T(8,128)(2,1)} %broadcast_in_dim.9), calls=%async_computation | async-start | bytes 2228224 | tf_op jit(solution)/shard_map/all_to_all | solution.py:124
  36.0 15.7 %collective-permute-start.6 = (bf16[32,2048]{1,0:T(8,128)(2,1)S(1)}, bf16[32,2048]{1,0:T(8,128)(2,1)S(1)}, u32[]{:S(2)}, u32[]{:S(2)}) collective-permute-start(bf16[32,2048]{1,0:T(8,128)(2,1)S(1)} %collective-permute-done.3), channel_id=1, source_target_pairs={{0,3},{1,0},{2,1},{3,2},{4,7},{5,4},{6,5},{7,6},{8,11},{9,8},{10,9... | collective-permute-start | bytes 393224 | tf_op jit(solution)/shard_map/ppermute | solution.py:146
  40.6 11.0 %collective-permute-start.5 = (bf16[32,2048]{1,0:T(8,128)(2,1)S(1)}, bf16[32,2048]{1,0:T(8,128)(2,1)S(1)}, u32[]{:S(2)}, u32[]{:S(2)}) collective-permute-start(bf16[32,2048]{1,0:T(8,128)(2,1)S(1)} %collective-permute-done.3), channel_id=1, source_target_pairs={{0,2},{1,3},{2,0},{3,1},{4,6},{5,7},{6,4},{7,5},{8,10},{9,11},{10,... | collective-permute-start | bytes 393224 | tf_op jit(solution)/shard_map/ppermute | solution.py:146
  42.9 8.7 %collective-permute-start.4 = (bf16[32,2048]{1,0:T(8,128)(2,1)S(1)}, bf16[32,2048]{1,0:T(8,128)(2,1)S(1)}, u32[]{:S(2)}, u32[]{:S(2)}) collective-permute-start(bf16[32,2048]{1,0:T(8,128)(2,1)S(1)} %collective-permute-done.3), channel_id=1, source_target_pairs={{0,1},{1,2},{2,3},{3,0},{4,5},{5,6},{6,7},{7,4},{8,9},{9,10},{10,1... | collective-permute-start | bytes 393224 | tf_op jit(solution)/shard_map/ppermute | solution.py:146
  51.6 3.8 %copy-start.1 = (bf16[128,2048]{1,0:T(8,128)(2,1)S(1)}, bf16[128,2048]{1,0:T(8,128)(2,1)}, u32[]{:S(2)}) copy-start(bf16[128,2048]{1,0:T(8,128)(2,1)} %param.7) | copy-start | bytes 1572868
  51.7 4.8 %collective-permute-start.8 = (bf16[128,2048]{1,0:T(8,128)(2,1)S(1)}, bf16[128,2048]{1,0:T(8,128)(2,1)S(1)}, u32[]{:S(2)}, u32[]{:S(2)}) collective-permute-start(bf16[128,2048]{1,0:T(8,128)(2,1)S(1)} %constant_dynamic-update-slice_fusion), channel_id=1, source_target_pairs={{0,32},{32,0},{1,33},{33,1},{2,34},{34,2},{3,35},{35,3},{4,36},{36... | collective-permute-start | bytes 1572872 | tf_op jit(solution)/shard_map/ppermute | solution.py:120
  56.9 24.7 %collective-permute-start.9 = (bf16[272,128]{1,0:T(8,128)(2,1)S(1)}, bf16[272,128]{1,0:T(8,128)(2,1)S(1)}, u32[]{:S(2)}, u32[]{:S(2)}) collective-permute-start(bf16[272,128]{1,0:T(8,128)(2,1)S(1)} %get-tuple-element.16), channel_id=1, source_target_pairs={{0,36},{1,37},{2,38},{3,39},{4,100},{5,101},{6,102},{7,103},{8,164... | collective-permute-start | bytes 208904 | tf_op jit(solution)/shard_map/ppermute | solution.py:157
  59.4 22.4 %collective-permute-start.7 = (bf16[272,128]{1,0:T(8,128)(2,1)S(1)}, bf16[272,128]{1,0:T(8,128)(2,1)S(1)}, u32[]{:S(2)}, u32[]{:S(2)}) collective-permute-start(bf16[272,128]{1,0:T(8,128)(2,1)S(1)} %get-tuple-element.15), channel_id=1, source_target_pairs={{0,4},{1,5},{2,6},{3,7},{4,68},{5,69},{6,70},{7,71},{8,132},{9,133... | collective-permute-start | bytes 208904 | tf_op jit(solution)/shard_map/ppermute | solution.py:157
  62.6 26.5 %collective-permute-start.2 = (bf16[272,128]{1,0:T(8,128)(2,1)S(1)}, bf16[272,128]{1,0:T(8,128)(2,1)S(1)}, u32[]{:S(2)}, u32[]{:S(2)}) collective-permute-start(bf16[272,128]{1,0:T(8,128)(2,1)S(1)} %get-tuple-element.14), channel_id=1, source_target_pairs={{0,56},{1,57},{2,58},{3,59},{4,120},{5,121},{6,122},{7,123},{8,184... | collective-permute-start | bytes 208904 | tf_op jit(solution)/shard_map/ppermute | solution.py:157
  72.8 18.3 %collective-permute-start = (bf16[272,128]{1,0:T(8,128)(2,1)S(1)}, bf16[272,128]{1,0:T(8,128)(2,1)S(1)}, u32[]{:S(2)}, u32[]{:S(2)}) collective-permute-start(bf16[272,128]{1,0:T(8,128)(2,1)S(1)} %get-tuple-element.13), channel_id=1, source_target_pairs={{0,24},{1,25},{2,26},{3,27},{4,88},{5,89},{6,90},{7,91},{8,152},{9... | collective-permute-start | bytes 208904 | tf_op jit(solution)/shard_map/ppermute | solution.py:157
  92.2 22.4 %collective-permute-start.10 = (bf16[1536,512]{1,0:T(8,128)(2,1)}, bf16[1536,512]{1,0:T(8,128)(2,1)}, u32[]{:S(2)}, u32[]{:S(2)}) collective-permute-start(bf16[1536,512]{1,0:T(8,128)(2,1)} %all-gather.2.cloned.1.call-done.near_ref), channel_id=1, source_target_pairs={{0,32},{32,0},{1,33},{33,1},{2,34},{34,2},{3,35},{35,3},{4,36},{36... | collective-permute-start | bytes 4718600 | tf_op jit(solution)/shard_map/ppermute | solution.py:120
  95.7 3.7 %copy-start.2 = (s32[1,4]{1,0:T(1,128)S(1)}, s32[1,4]{1,0:T(1,128)}, u32[]{:S(2)}) copy-start(s32[1,4]{1,0:T(1,128)} %constant.70) | copy-start | bytes 52
  95.7 3.7 %copy-start.3 = (s32[1,4]{1,0:T(1,128)S(1)}, s32[1,4]{1,0:T(1,128)}, u32[]{:S(2)}) copy-start(s32[1,4]{1,0:T(1,128)} %constant.69) | copy-start | bytes 52
  95.7 18.8 %copy-start = (bf16[1536,512]{1,0:T(8,128)(2,1)S(1)}, bf16[1536,512]{1,0:T(8,128)(2,1)}, u32[]{:S(2)}) copy-start(bf16[1536,512]{1,0:T(8,128)(2,1)} %all-gather.2.cloned.1.call-done.near_ref) | copy-start | bytes 4718596
  95.7 18.8 %all-to-all-start.1 = ((bf16[4,16,64,128]{3,2,1,0:T(8,128)(2,1)}), bf16[4,16,64,128]{3,2,1,0:T(8,128)(2,1)S(1)}, u32[]{:S(2)}, u32[]{:S(2)}) async-start(bf16[4,16,64,128]{3,2,1,0:T(8,128)(2,1)} %broadcast_in_dim.22), calls=%async_computation.1 | async-start | bytes 2097152 | tf_op jit(solution)/shard_map/all_to_all | solution.py:124
  119.9 21.9 %all-to-all-start.2 = ((bf16[4,192,512]{2,1,0:T(8,128)(2,1)}), bf16[4,192,512]{2,1,0:T(8,128)(2,1)S(1)}, u32[]{:S(2)}, u32[]{:S(2)}) async-start(bf16[4,192,512]{2,1,0:T(8,128)(2,1)} %bitcast.13), calls=%async_computation.2 | async-start | bytes 1572864 | tf_op jit(solution)/shard_map/all_to_all | solution.py:179
  141.8 14.7 %all-to-all-start.3 = ((bf16[4,192,512]{2,1,0:T(8,128)(2,1)}), bf16[4,192,512]{2,1,0:T(8,128)(2,1)S(1)}, u32[]{:S(2)}, u32[]{:S(2)}) async-start(bf16[4,192,512]{2,1,0:T(8,128)(2,1)} %bitcast.15), calls=%async_computation.3 | async-start | bytes 1572864 | tf_op jit(solution)/shard_map/all_to_all | solution.py:179
  145.4 15.5 %collective-permute-start.11 = (bf16[192,512]{1,0:T(8,128)(2,1)S(1)}, bf16[192,512]{1,0:T(8,128)(2,1)S(1)}, u32[]{:S(2)}, u32[]{:S(2)}) collective-permute-start(bf16[192,512]{1,0:T(8,128)(2,1)S(1)} %reduce_sum.24), channel_id=1, source_target_pairs={{0,328},{1,329},{2,330},{3,331},{4,264},{5,265},{6,266},{7,267},{8... | collective-permute-start | bytes 589832 | tf_op jit(solution)/shard_map/ppermute | solution.py:181
  156.6 26.0 %collective-permute-start.12 = (bf16[192,512]{1,0:T(8,128)(2,1)S(1)}, bf16[192,512]{1,0:T(8,128)(2,1)S(1)}, u32[]{:S(2)}, u32[]{:S(2)}) collective-permute-start(bf16[192,512]{1,0:T(8,128)(2,1)S(1)} %reduce_sum.25), channel_id=1, source_target_pairs={{0,344},{1,345},{2,346},{3,347},{4,280},{5,281},{6,282},{7,283},{8... | collective-permute-start | bytes 589832 | tf_op jit(solution)/shard_map/ppermute | solution.py:181
Sparse Core Ops, SparseCore 0:
  9.4 57.3 all-gather.1

commit v11 on v10

--- a/solution.py
+++ b/solution.py
@@ -26,28 +26,28 @@
                         yield h, x, c, l, y
 
 
-PLACE = ((6, 7, 3, 2, 1, 0, 4, 5), (7, 6, 2, 3, 0, 1, 4, 5))
-ROWS = ((2, 6), (3, 7), (4, 0), (5, 1))
+INNER, OUTER = (2, 3, 4, 5), (7, 6, 1, 0)
 
 
 def place(h, h2, x2):
-    return PLACE[h][h2 * X + x2]
+    l = (INNER if h2 == h else OUTER)[x2]
+    return l if h == 0 else L - 1 - l
 
 
 def chunk(h, l):
-    return divmod(PLACE[h].index(l), X)
+    return next((h2, x2) for h2 in range(H) for x2 in range(X) if place(h, h2, x2) == l)
 
 
-def weight_perm(k, d):
+def weight_perm(k):
     return [
-        (flat(h, x, c, l, y), flat(l // X, l % X, c ^ d, place(l // X, h ^ k, x), y))
+        (flat(h, x, c, l, y), flat(l // X, l % X, c, place(l // X, h ^ k, x), y))
         for h, x, c, l, y in coords()
     ]
 
 
 def result_perm(k):
     return [
-        (flat(h, x, c, l, y), flat(*chunk(h, l), c, ROWS[x][h ^ k], y))
+        (flat(h, x, c, l, y), flat(*chunk(h, l), c, L - 1 - x if h ^ k else x, y))
         for h, x, c, l, y in coords()
     ]
 
@@ -56,27 +56,19 @@
     return [(i, (i + k) % n) for i in range(n)]
 
 
-def contract_kernel(
-    where_ref, first_ref, second_ref, w_ref, near_ref, far_ref, out_ref, acc_ref, s_ref
-):
+def contract_kernel(where_ref, first_ref, second_ref, w_ref, near_ref, far_ref, out_ref, s_ref):
     slots, rows, cols = w_ref.shape[1:]
 
     @pl.when(pl.program_id(0) == 0)
     def _():
-        acc_ref[...] = jnp.zeros_like(acc_ref)
-
-        def add(slot, _):
-            first, second = first_ref[slot], second_ref[slot]
-            at_col = pl.multiple_of(first * cols, cols)
+        s_ref[...] = jnp.zeros_like(s_ref)
+        for slot in range(slots):
+            at_row = second_ref[slot] * (2 * rows)
+            at_col = pl.ds(pl.multiple_of(first_ref[slot] * cols, cols), cols)
             for z in range(Y):
-                half, part = z // 2, z % 2
-                at_row = pl.multiple_of((half * OCC + second) * (2 * rows) + part * rows, rows)
-                here = (pl.ds(at_row, rows), pl.ds(at_col, cols))
-                acc_ref[here] += w_ref[z, slot].astype(jnp.float32)
-            return 0
-
-        lax.fori_loop(0, slots, add, 0)
-        s_ref[...] = acc_ref[...].astype(jnp.bfloat16)
+                row = (z // 2) * OCC * 2 * rows + at_row + (z % 2) * rows
+                here = (pl.ds(pl.multiple_of(row, rows), rows), at_col)
+                s_ref[here] += w_ref[z, slot]
 
     depth = near_ref.shape[1]
     at_near = pl.multiple_of(where_ref[0] * depth, depth)
@@ -99,10 +91,7 @@
             grid=(X,),
             in_specs=[pl.BlockSpec(w.shape, lambda x, *_: (0, 0, 0, 0))] + rows,
             out_specs=pl.BlockSpec((block, cols), lambda x, *_: (x, 0)),
-            scratch_shapes=[
-                pltpu.VMEM((2 * depth, cols), jnp.float32),
-                pltpu.VMEM((2 * depth, cols), jnp.bfloat16),
-            ],
+            scratch_shapes=[pltpu.VMEM((2 * depth, cols), jnp.bfloat16)],
         ),
         out_shape=jax.ShapeDtypeStruct((X * block, cols), jnp.bfloat16),
         compiler_params=pltpu.CompilerParams(vmem_limit_bytes=32 * 1024 * 1024),
@@ -129,7 +118,6 @@
 
     n_mu, n_a = coefficients.shape
     part = n_mu // Y
-    c_other = swap_core(coefficients)
     mirror = [(i, H * L - 1 - i) for i in range(H * L)]
     piece = lax.dynamic_slice_in_dim(coefficients, y * part, part, 0)
     piece = lax.ppermute(piece, ("h", "l"), mirror)
@@ -138,29 +126,28 @@
     info = jnp.pad(pair_list.astype(bf16), ((0, rows - 1), (0, 126)))
     t_own = jnp.concatenate([amplitudes[0].T, info], axis=1)
     t_all = gather(t_own, "x", X)
-    info = t_all[:, 0, n_a:]
-    info = jnp.pad(info, ((0, 16 - X), (0, 0)))
-    t_all = t_all.reshape(X * rows, -1)[:, :n_a]
+    t_all, piece = lax.optimization_barrier((t_all, piece))
+    halves = (t_all, swap_core(t_all))
+    slots, n_b = C * X, C * X * rows
+    info = [v[:, 0, n_a:] for v in halves] + [jnp.zeros((16 - slots, n_mu), bf16)]
+    halves = [v.reshape(X * rows, -1)[:, :n_a] for v in halves]
+
     c_far = jnp.zeros((n_mu, n_a), bf16)
     for k in range(Y):
         v = lax.ppermute(piece, "y", shift(Y, k)) if k else piece
         c_far = lax.dynamic_update_slice_in_dim(c_far, v, (y - k) % Y * part, 0)
 
-    def weights(m):
-        return lax.dot_general(
-            t_all, m, (((1,), (1,)), ((), ())), preferred_element_type=f32
-        ).astype(bf16)
-
-    near = [weights(coefficients), weights(c_other)]
-    far = [weights(c_far), weights(swap_core(c_far))]
-    w = [
-        lax.ppermute(jnp.concatenate([v, info], axis=0), AXES, weight_perm(k, d))
-        for k, pieces in enumerate((near, far))
-        for d, v in enumerate(pieces)
-    ]
+    w = []
+    for k, m in enumerate((coefficients, c_far)):
+        v = [
+            lax.dot_general(t, m, (((1,), (1,)), ((), ())), preferred_element_type=f32)
+            for t in halves
+        ]
+        v = jnp.concatenate([t.astype(bf16) for t in v] + info, axis=0)
+        w.append(lax.ppermute(v, AXES, weight_perm(k)))
     w = jnp.stack(w)
-    slots, n_b = H * C * X, X * rows
-    pairs = w[:, n_b : n_b + X, :2].reshape(slots, 2).astype(jnp.int32)
+    slots *= H
+    pairs = w[:, n_b : n_b + C * X, :2].reshape(slots, 2).astype(jnp.int32)
     w = w[:, :n_b].reshape(slots, rows, n_mu)
 
     w, b_near = lax.optimization_barrier((w, b_near))
@@ -169,7 +156,8 @@
     w_all = gather(w, "y", Y)
     w_all = w_all.reshape(Y, slots, rows, n_mu)
 
-    at = jnp.asarray([[RING.index(two[s]) for two in ROWS] for s in range(H)], jnp.int32)
+    at = [[RING.index(x) for x in range(X)], [RING.index(L - 1 - x) for x in range(X)]]
+    at = jnp.asarray(at, jnp.int32)
     total = 0
     for k in range(H):
         where = jnp.where(h == k, at[0], at[1])

time: 192 us -> 192 us (level)
  the two profiles are of different devices: /device:TPU:1 before, /device:TPU:5 now
where the time goes in v11:
time: 192 us; the launch traced here: 191 us
  waiting for transfers between devices  84.2 us (44%)
  starting transfers between devices  72.5 us (38%)
  between operations  13.8 us (7%)
  Pallas kernels  8.2 us (4%)
  local copies, waits for them, and re-layouts  7.03 us (4%)
  other arithmetic  3.26 us (2%)
    ppermute x2, waiting for transfers between devices, on_device(): total += lax.ppermute(v, AXES, result_perm(k)).astype(f32)  24.3 us
    all_gather x1, waiting for transfers between devices, on_device(): lax.all_gather(b_near, 'l', axis=0, tiled=True, axis_index_groups=[RING])  21.1 us
    all_to_all x2, waiting for transfers between devices, gather(): return lax.all_to_all(v, axes, split_axis=0, concat_axis=0, tiled=True)  14.6 us
    ppermute x2, starting transfers between devices, on_device(): total += lax.ppermute(v, AXES, result_perm(k)).astype(f32)  12.6 us
    ppermute x2, starting transfers between devices, on_device(): w.append(lax.ppermute(v, AXES, weight_perm(k)))  11.4 us
    ppermute x1, starting transfers between devices, on_device(): piece = lax.ppermute(piece, ('h', 'l'), mirror)  11.1 us
    ppermute x1, waiting for transfers between devices, on_device(): piece = lax.ppermute(piece, ('h', 'l'), mirror)  11.1 us
    all_to_all x2, starting transfers between devices, on_device(): v = lax.all_to_all(v, 'x', split_axis=0, concat_axis=0, tiled=True)  10.4 us
  transfers between devices with their start and end apart: 15, of which 9 were waited for; matrix products, arithmetic and copies ran while one was open for 4% of the time, Pallas kernels for 2%

profile of v11, /device:TPU:5, one launch (start us, length us, event | category | flops | bytes accessed | tf_op | source)
XLA Modules:
  0.0 190.7 jit_solution(14560163798524476454)
XLA Ops:
  6.5 0.0 copy-start
  6.5 0.7 convert_element_type.36
  7.3 1.0 fusion.5
  8.2 1.1 broadcast_in_dim.11
  9.3 4.4 %all-to-all-start = ((bf16[4,64,2176]{2,1,0:T(8,128)(2,1)}), bf16[4,64,2176]{2,1,0:T(8,128)(2,1)S(1)}, u32[]{:S(2)}, u32[]{:S(2)}) async-start(bf16[4,64,2176]{2,1,0:T(8,128)(2,1)} %broadcast_in_dim.11), calls=%async_computation | async-start | bytes 2228224 | tf_op jit(solution)/shard_map/all_to_all | solution.py:113
  13.7 0.0 all-gather.2.cloned.1.call-start
  13.7 0.0 copy-done
  13.7 11.1 %collective-permute-start = (bf16[32,2048]{1,0:T(8,128)(2,1)S(1)}, bf16[32,2048]{1,0:T(8,128)(2,1)S(1)}, u32[]{:S(2)}, u32[]{:S(2)}) collective-permute-start(bf16[32,2048]{1,0:T(8,128)(2,1)S(1)} %constant_dynamic-slice_fusion), channel_id=1, source_target_pairs={{0,284},{4,280},{8,276},{12,272},{16,268},{20,264},{24,260},{28,25... | collective-permute-start | bytes 393224 | tf_op jit(solution)/shard_map/ppermute | solution.py:123
  24.8 0.0 copy-done.4
  24.9 0.7 copy.19
  25.6 0.0 all-gather.2.cloned.1.call-update
  25.7 11.1 %collective-permute-done = bf16[32,2048]{1,0:T(8,128)(2,1)S(1)} collective-permute-done((bf16[32,2048]{1,0:T(8,128)(2,1)S(1)}, bf16[32,2048]{1,0:T(8,128)(2,1)S(1)}, u32[]{:S(2)}, u32[]{:S(2)}) %collective-permute-start) | collective-permute-done | bytes 131104 | tf_op jit(solution)/shard_map/ppermute | solution.py:123
  36.7 0.0 all-to-all-done
  36.7 4.6 %collective-permute-start.5 = (bf16[32,2048]{1,0:T(8,128)(2,1)S(1)}, bf16[32,2048]{1,0:T(8,128)(2,1)S(1)}, u32[]{:S(2)}, u32[]{:S(2)}) collective-permute-start(bf16[32,2048]{1,0:T(8,128)(2,1)S(1)} %collective-permute-done), channel_id=1, source_target_pairs={{0,3},{1,0},{2,1},{3,2},{4,7},{5,4},{6,5},{7,6},{8,11},{9,8},{10,9... | collective-permute-start | bytes 393224 | tf_op jit(solution)/shard_map/ppermute | solution.py:137
  41.4 2.3 %collective-permute-start.4 = (bf16[32,2048]{1,0:T(8,128)(2,1)S(1)}, bf16[32,2048]{1,0:T(8,128)(2,1)S(1)}, u32[]{:S(2)}, u32[]{:S(2)}) collective-permute-start(bf16[32,2048]{1,0:T(8,128)(2,1)S(1)} %collective-permute-done), channel_id=1, source_target_pairs={{0,2},{1,3},{2,0},{3,1},{4,6},{5,7},{6,4},{7,5},{8,10},{9,11},{10,... | collective-permute-start | bytes 393224 | tf_op jit(solution)/shard_map/ppermute | solution.py:137
  43.6 2.6 %collective-permute-start.3 = (bf16[32,2048]{1,0:T(8,128)(2,1)S(1)}, bf16[32,2048]{1,0:T(8,128)(2,1)S(1)}, u32[]{:S(2)}, u32[]{:S(2)}) collective-permute-start(bf16[32,2048]{1,0:T(8,128)(2,1)S(1)} %collective-permute-done), channel_id=1, source_target_pairs={{0,1},{1,2},{2,3},{3,0},{4,5},{5,6},{6,7},{7,4},{8,9},{9,10},{10,1... | collective-permute-start | bytes 393224 | tf_op jit(solution)/shard_map/ppermute | solution.py:137
  46.2 0.9 copy.10
  47.1 3.7 %collective-permute-start.1 = (bf16[4,64,2176]{2,0,1:T(4,128)(2,1)S(1)}, bf16[4,64,2176]{2,0,1:T(4,128)(2,1)S(1)}, u32[]{:S(2)}, u32[]{:S(2)}) collective-permute-start(bf16[4,64,2176]{2,0,1:T(4,128)(2,1)S(1)} %copy.10), channel_id=1, source_target_pairs={{0,32},{32,0},{1,33},{33,1},{2,34},{34,2},{3,35},{35,3},{4,36},{36... | collective-permute-start | bytes 3342344 | tf_op jit(solution)/shard_map/ppermute | solution.py:109
  50.9 0.4 convolution_convert_fusion.3
  51.4 1.0 collective-permute-done.3
  52.4 0.0 collective-permute-done.4
  52.5 0.0 collective-permute-done.5
  52.5 0.4 convolution_convert_fusion.1
  52.9 0.3 collective-permute-done.1
  53.2 0.1 copy.11
  53.3 0.4 convolution_convert_fusion
  53.8 0.1 concatenate.18
  53.9 1.9 %collective-permute-start.6 = (bf16[528,128]{1,0:T(8,128)(2,1)S(1)}, bf16[528,128]{1,0:T(8,128)(2,1)S(1)}, u32[]{:S(2)}, u32[]{:S(2)}) collective-permute-start(bf16[528,128]{1,0:T(8,128)(2,1)S(1)} %concatenate.18), channel_id=1, source_target_pairs={{0,28},{1,29},{2,30},{3,31},{4,92},{5,93},{6,94},{7,95},{8,156},{9... | collective-permute-start | bytes 405512 | tf_op jit(solution)/shard_map/ppermute | solution.py:147
  55.8 0.4 convolution_convert_fusion.2
  56.2 0.1 concatenate.17
  56.3 9.5 %collective-permute-start.2 = (bf16[528,128]{1,0:T(8,128)(2,1)S(1)}, bf16[528,128]{1,0:T(8,128)(2,1)S(1)}, u32[]{:S(2)}, u32[]{:S(2)}) collective-permute-start(bf16[528,128]{1,0:T(8,128)(2,1)S(1)} %concatenate.17), channel_id=1, source_target_pairs={{0,8},{1,9},{2,10},{3,11},{4,72},{5,73},{6,74},{7,75},{8,136},{9,1... | collective-permute-start | bytes 405512 | tf_op jit(solution)/shard_map/ppermute | solution.py:147
  65.8 8.4 %collective-permute-done.6 = bf16[528,128]{1,0:T(8,128)(2,1)S(1)} collective-permute-done((bf16[528,128]{1,0:T(8,128)(2,1)S(1)}, bf16[528,128]{1,0:T(8,128)(2,1)S(1)}, u32[]{:S(2)}, u32[]{:S(2)}) %collective-permute-start.6) | collective-permute-done | bytes 135200 | tf_op jit(solution)/shard_map/ppermute | solution.py:147
  74.3 0.0 collective-permute-done.2
  74.3 21.1 %all-gather.2.cloned.1.call-done.near_ref = bf16[1536,512]{1,0:T(8,128)(2,1)} async-done(((bf16[192,512]{1,0:T(8,128)(2,1)}), bf16[1536,512]{1,0:T(8,128)(2,1)}) %all-gather.2.cloned.1.call-update) | async-done | bytes 1572880 | tf_op jit(solution)/shard_map/all_gather | solution.py:117
  95.4 5.0 %collective-permute-start.7 = (bf16[1536,512]{1,0:T(8,128)(2,1)}, bf16[1536,512]{1,0:T(8,128)(2,1)}, u32[]{:S(2)}, u32[]{:S(2)}) collective-permute-start(bf16[1536,512]{1,0:T(8,128)(2,1)} %all-gather.2.cloned.1.call-done.near_ref), channel_id=1, source_target_pairs={{0,32},{32,0},{1,33},{33,1},{2,34},{34,2},{3,35},{35,3},{4,36},{36... | collective-permute-start | bytes 4718600 | tf_op jit(solution)/shard_map/ppermute | solution.py:109
  100.4 1.2 broadcast_in_dim.26
  101.7 4.4 %all-to-all-start.1 = ((bf16[4,16,64,128]{3,2,1,0:T(8,128)(2,1)}), bf16[4,16,64,128]{3,2,1,0:T(8,128)(2,1)S(1)}, u32[]{:S(2)}, u32[]{:S(2)}) async-start(bf16[4,16,64,128]{3,2,1,0:T(8,128)(2,1)} %broadcast_in_dim.26), calls=%async_computation.1 | async-start | bytes 2097152 | tf_op jit(solution)/shard_map/all_to_all | solution.py:113
  106.0 0.0 copy-done.5
  106.1 0.0 copy-done.6
  106.1 0.1 pad_add_fusion
  106.1 0.1 fusion.9
  106.2 0.1 copy.16
  106.3 0.1 copy.15
  106.4 14.6 %all-to-all-done.1.w_ref = bf16[4,16,64,128]{3,2,1,0:T(8,128)(2,1)S(1)} async-done(((bf16[4,16,64,128]{3,2,1,0:T(8,128)(2,1)}), bf16[4,16,64,128]{3,2,1,0:T(8,128)(2,1)S(1)}, u32[]{:S(2)}, u32[]{:S(2)}) %all-to-all-start.1) | async-done | bytes 1048608 | tf_op jit(solution)/shard_map/all_to_all | solution.py:113
  121.0 0.0 collective-permute-done.7.far_ref
  121.0 0.0 copy-done.1
  121.0 4.1 %shard_map.55 = bf16[768,512]{1,0:T(8,128)(2,1)S(1)} custom-call(s32[5]{0:T(128)S(1)} %get-tuple-element.17.where_ref, s32[16]{0:T(128)S(1)} %bitcast.38, s32[16]{0:T(128)S(1)} %bitcast.36, bf16[4,16,64,128]{3,2,1,0:T(8,128)(2,1)S(1)} %all-to-all-done.1.w_ref, bf16[1536,512]{1,0:T(8,128)(2,1)S(1)} %copy-done.1, bf16[1536,512]{1,0:T(8,128)(2,1)} %collective-permute-done.7.far_ref), custom_call_target="tpu_custom_call" | custom-call | flops 805306368 | bytes 4194304 | tf_op jit(solution)/shard_map/pallas_call | solution.py:87
  125.1 0.0 copy-start.3
  125.1 0.9 copy-done.3
  126.0 4.2 %all-to-all-start.2 = ((bf16[4,192,512]{2,1,0:T(8,128)(2,1)}), bf16[4,192,512]{2,1,0:T(8,128)(2,1)}, u32[]{:S(2)}, u32[]{:S(2)}) async-start(bf16[4,192,512]{2,1,0:T(8,128)(2,1)} %bitcast.35), calls=%async_computation.2 | async-start | bytes 1572864 | tf_op jit(solution)/shard_map/all_to_all | solution.py:167
  130.2 4.1 %shard_map.56 = bf16[768,512]{1,0:T(8,128)(2,1)S(1)} custom-call(s32[5]{0:T(128)S(1)} %get-tuple-element.18.where_ref, s32[16]{0:T(128)S(1)} %bitcast.39, s32[16]{0:T(128)S(1)} %bitcast.37, bf16[4,16,64,128]{3,2,1,0:T(8,128)(2,1)S(1)} %all-to-all-done.1.w_ref, bf16[1536,512]{1,0:T(8,128)(2,1)S(1)} %copy-done.1, bf16[1536,512]{1,0:T(8,128)(2,1)} %collective-permute-done.7.far_ref), custom_call_target="tpu_custom_call" | custom-call | flops 805306368 | bytes 4194304 | tf_op jit(solution)/shard_map/pallas_call | solution.py:87
  134.3 0.0 copy-start.2
  134.3 0.9 copy-done.2
  135.2 3.4 %all-to-all-done.2 = bf16[4,192,512]{2,1,0:T(8,128)(2,1)} async-done(((bf16[4,192,512]{2,1,0:T(8,128)(2,1)}), bf16[4,192,512]{2,1,0:T(8,128)(2,1)}, u32[]{:S(2)}, u32[]{:S(2)}) %all-to-all-start.2) | async-done | bytes 786464 | tf_op jit(solution)/shard_map/all_to_all | solution.py:167
  138.6 6.2 %all-to-all-start.3 = ((bf16[4,192,512]{2,1,0:T(8,128)(2,1)}), bf16[4,192,512]{2,1,0:T(8,128)(2,1)S(1)}, u32[]{:S(2)}, u32[]{:S(2)}) async-start(bf16[4,192,512]{2,1,0:T(8,128)(2,1)} %bitcast.34), calls=%async_computation.3 | async-start | bytes 1572864 | tf_op jit(solution)/shard_map/all_to_all | solution.py:167
  144.7 1.3 reduce_sum.24
  146.0 10.7 %collective-permute-start.8 = (bf16[192,512]{1,0:T(8,128)(2,1)S(1)}, bf16[192,512]{1,0:T(8,128)(2,1)S(1)}, u32[]{:S(2)}, u32[]{:S(2)}) collective-permute-start(bf16[192,512]{1,0:T(8,128)(2,1)S(1)} %reduce_sum.24), channel_id=1, source_target_pairs={{0,448},{1,449},{2,450},{3,451},{4,384},{5,385},{6,386},{7,387},{8... | collective-permute-start | bytes 589832 | tf_op jit(solution)/shard_map/ppermute | solution.py:169
  156.7 0.0 all-to-all-done.3
  156.7 0.1 reduce_sum.25
  156.9 1.9 %collective-permute-start.9 = (bf16[192,512]{1,0:T(8,128)(2,1)S(1)}, bf16[192,512]{1,0:T(8,128)(2,1)S(1)}, u32[]{:S(2)}, u32[]{:S(2)}) collective-permute-start(bf16[192,512]{1,0:T(8,128)(2,1)S(1)} %reduce_sum.25), channel_id=1, source_target_pairs={{0,476},{1,477},{2,478},{3,479},{4,412},{5,413},{6,414},{7,415},{8... | collective-permute-start | bytes 589832 | tf_op jit(solution)/shard_map/ppermute | solution.py:169
  158.8 10.4 %collective-permute-done.8 = bf16[192,512]{1,0:T(8,128)(2,1)S(1)} collective-permute-done((bf16[192,512]{1,0:T(8,128)(2,1)S(1)}, bf16[192,512]{1,0:T(8,128)(2,1)S(1)}, u32[]{:S(2)}, u32[]{:S(2)}) %collective-permute-start.8) | collective-permute-done | bytes 196640 | tf_op jit(solution)/shard_map/ppermute | solution.py:169
  169.2 13.9 %collective-permute-done.9 = bf16[192,512]{1,0:T(8,128)(2,1)S(1)} collective-permute-done((bf16[192,512]{1,0:T(8,128)(2,1)S(1)}, bf16[192,512]{1,0:T(8,128)(2,1)S(1)}, u32[]{:S(2)}, u32[]{:S(2)}) %collective-permute-start.9) | collective-permute-done | bytes 196640 | tf_op jit(solution)/shard_map/ppermute | solution.py:169
  183.1 0.1 add_convert_fusion
  183.2 0.7 reshape.36
  (16 shorter events, 0.2 us)
Async XLA Ops:
  6.5 7.2 %copy-start = (bf16[128,2048]{1,0:T(8,128)(2,1)S(1)}, bf16[128,2048]{1,0:T(8,128)(2,1)}, u32[]{:S(2)}) copy-start(bf16[128,2048]{1,0:T(8,128)(2,1)} %param.7) | copy-start | bytes 1572868
  9.3 15.5 %copy-start.4 = (bf16[192,4,128]{2,1,0:T(4,128)(2,1)S(1)}, bf16[192,4,128]{2,1,0:T(4,128)(2,1)}, u32[]{:S(2)}) copy-start(bf16[192,4,128]{2,1,0:T(4,128)(2,1)} %param.6) | copy-start | bytes 589828
  9.3 27.4 %all-to-all-start = ((bf16[4,64,2176]{2,1,0:T(8,128)(2,1)}), bf16[4,64,2176]{2,1,0:T(8,128)(2,1)S(1)}, u32[]{:S(2)}, u32[]{:S(2)}) async-start(bf16[4,64,2176]{2,1,0:T(8,128)(2,1)} %broadcast_in_dim.11), calls=%async_computation | async-start | bytes 2228224 | tf_op jit(solution)/shard_map/all_to_all | solution.py:113
  13.7 81.7 %all-gather.2.cloned.1.call-start = ((), (), s32[]{:S(2)}) async-start(), calls=%async_computation.4 | async-start | bytes 1769472 | tf_op jit(solution)/shard_map/all_gather | solution.py:117
  13.7 23.0 %collective-permute-start = (bf16[32,2048]{1,0:T(8,128)(2,1)S(1)}, bf16[32,2048]{1,0:T(8,128)(2,1)S(1)}, u32[]{:S(2)}, u32[]{:S(2)}) collective-permute-start(bf16[32,2048]{1,0:T(8,128)(2,1)S(1)} %constant_dynamic-slice_fusion), channel_id=1, source_target_pairs={{0,284},{4,280},{8,276},{12,272},{16,268},{20,264},{24,260},{28,25... | collective-permute-start | bytes 393224 | tf_op jit(solution)/shard_map/ppermute | solution.py:123
  36.7 15.7 %collective-permute-start.5 = (bf16[32,2048]{1,0:T(8,128)(2,1)S(1)}, bf16[32,2048]{1,0:T(8,128)(2,1)S(1)}, u32[]{:S(2)}, u32[]{:S(2)}) collective-permute-start(bf16[32,2048]{1,0:T(8,128)(2,1)S(1)} %collective-permute-done), channel_id=1, source_target_pairs={{0,3},{1,0},{2,1},{3,2},{4,7},{5,4},{6,5},{7,6},{8,11},{9,8},{10,9... | collective-permute-start | bytes 393224 | tf_op jit(solution)/shard_map/ppermute | solution.py:137
  41.4 11.1 %collective-permute-start.4 = (bf16[32,2048]{1,0:T(8,128)(2,1)S(1)}, bf16[32,2048]{1,0:T(8,128)(2,1)S(1)}, u32[]{:S(2)}, u32[]{:S(2)}) collective-permute-start(bf16[32,2048]{1,0:T(8,128)(2,1)S(1)} %collective-permute-done), channel_id=1, source_target_pairs={{0,2},{1,3},{2,0},{3,1},{4,6},{5,7},{6,4},{7,5},{8,10},{9,11},{10,... | collective-permute-start | bytes 393224 | tf_op jit(solution)/shard_map/ppermute | solution.py:137
  43.6 8.8 %collective-permute-start.3 = (bf16[32,2048]{1,0:T(8,128)(2,1)S(1)}, bf16[32,2048]{1,0:T(8,128)(2,1)S(1)}, u32[]{:S(2)}, u32[]{:S(2)}) collective-permute-start(bf16[32,2048]{1,0:T(8,128)(2,1)S(1)} %collective-permute-done), channel_id=1, source_target_pairs={{0,1},{1,2},{2,3},{3,0},{4,5},{5,6},{6,7},{7,4},{8,9},{9,10},{10,1... | collective-permute-start | bytes 393224 | tf_op jit(solution)/shard_map/ppermute | solution.py:137
  47.1 6.1 %collective-permute-start.1 = (bf16[4,64,2176]{2,0,1:T(4,128)(2,1)S(1)}, bf16[4,64,2176]{2,0,1:T(4,128)(2,1)S(1)}, u32[]{:S(2)}, u32[]{:S(2)}) collective-permute-start(bf16[4,64,2176]{2,0,1:T(4,128)(2,1)S(1)} %copy.10), channel_id=1, source_target_pairs={{0,32},{32,0},{1,33},{33,1},{2,34},{34,2},{3,35},{35,3},{4,36},{36... | collective-permute-start | bytes 3342344 | tf_op jit(solution)/shard_map/ppermute | solution.py:109
  53.9 20.4 %collective-permute-start.6 = (bf16[528,128]{1,0:T(8,128)(2,1)S(1)}, bf16[528,128]{1,0:T(8,128)(2,1)S(1)}, u32[]{:S(2)}, u32[]{:S(2)}) collective-permute-start(bf16[528,128]{1,0:T(8,128)(2,1)S(1)} %concatenate.18), channel_id=1, source_target_pairs={{0,28},{1,29},{2,30},{3,31},{4,92},{5,93},{6,94},{7,95},{8,156},{9... | collective-permute-start | bytes 405512 | tf_op jit(solution)/shard_map/ppermute | solution.py:147
  56.3 18.0 %collective-permute-start.2 = (bf16[528,128]{1,0:T(8,128)(2,1)S(1)}, bf16[528,128]{1,0:T(8,128)(2,1)S(1)}, u32[]{:S(2)}, u32[]{:S(2)}) collective-permute-start(bf16[528,128]{1,0:T(8,128)(2,1)S(1)} %concatenate.17), channel_id=1, source_target_pairs={{0,8},{1,9},{2,10},{3,11},{4,72},{5,73},{6,74},{7,75},{8,136},{9,1... | collective-permute-start | bytes 405512 | tf_op jit(solution)/shard_map/ppermute | solution.py:147
  95.4 25.6 %collective-permute-start.7 = (bf16[1536,512]{1,0:T(8,128)(2,1)}, bf16[1536,512]{1,0:T(8,128)(2,1)}, u32[]{:S(2)}, u32[]{:S(2)}) collective-permute-start(bf16[1536,512]{1,0:T(8,128)(2,1)} %all-gather.2.cloned.1.call-done.near_ref), channel_id=1, source_target_pairs={{0,32},{32,0},{1,33},{33,1},{2,34},{34,2},{3,35},{35,3},{4,36},{36... | collective-permute-start | bytes 4718600 | tf_op jit(solution)/shard_map/ppermute | solution.py:109
  101.7 4.4 %copy-start.5 = (s32[1,4]{1,0:T(1,128)S(1)}, s32[1,4]{1,0:T(1,128)}, u32[]{:S(2)}) copy-start(s32[1,4]{1,0:T(1,128)} %constant.69) | copy-start | bytes 52
  101.7 4.4 %copy-start.6 = (s32[1,4]{1,0:T(1,128)S(1)}, s32[1,4]{1,0:T(1,128)}, u32[]{:S(2)}) copy-start(s32[1,4]{1,0:T(1,128)} %constant.68) | copy-start | bytes 52
  101.7 19.3 %copy-start.1 = (bf16[1536,512]{1,0:T(8,128)(2,1)S(1)}, bf16[1536,512]{1,0:T(8,128)(2,1)}, u32[]{:S(2)}) copy-start(bf16[1536,512]{1,0:T(8,128)(2,1)} %all-gather.2.cloned.1.call-done.near_ref) | copy-start | bytes 4718596
  101.7 19.3 %all-to-all-start.1 = ((bf16[4,16,64,128]{3,2,1,0:T(8,128)(2,1)}), bf16[4,16,64,128]{3,2,1,0:T(8,128)(2,1)S(1)}, u32[]{:S(2)}, u32[]{:S(2)}) async-start(bf16[4,16,64,128]{3,2,1,0:T(8,128)(2,1)} %broadcast_in_dim.26), calls=%async_computation.1 | async-start | bytes 2097152 | tf_op jit(solution)/shard_map/all_to_all | solution.py:113
  125.1 0.9 copy-start.3
  126.0 12.6 %all-to-all-start.2 = ((bf16[4,192,512]{2,1,0:T(8,128)(2,1)}), bf16[4,192,512]{2,1,0:T(8,128)(2,1)}, u32[]{:S(2)}, u32[]{:S(2)}) async-start(bf16[4,192,512]{2,1,0:T(8,128)(2,1)} %bitcast.35), calls=%async_computation.2 | async-start | bytes 1572864 | tf_op jit(solution)/shard_map/all_to_all | solution.py:167
  134.3 0.9 copy-start.2
  138.6 18.1 %all-to-all-start.3 = ((bf16[4,192,512]{2,1,0:T(8,128)(2,1)}), bf16[4,192,512]{2,1,0:T(8,128)(2,1)S(1)}, u32[]{:S(2)}, u32[]{:S(2)}) async-start(bf16[4,192,512]{2,1,0:T(8,128)(2,1)} %bitcast.34), calls=%async_computation.3 | async-start | bytes 1572864 | tf_op jit(solution)/shard_map/all_to_all | solution.py:167
  146.0 23.2 %collective-permute-start.8 = (bf16[192,512]{1,0:T(8,128)(2,1)S(1)}, bf16[192,512]{1,0:T(8,128)(2,1)S(1)}, u32[]{:S(2)}, u32[]{:S(2)}) collective-permute-start(bf16[192,512]{1,0:T(8,128)(2,1)S(1)} %reduce_sum.24), channel_id=1, source_target_pairs={{0,448},{1,449},{2,450},{3,451},{4,384},{5,385},{6,386},{7,387},{8... | collective-permute-start | bytes 589832 | tf_op jit(solution)/shard_map/ppermute | solution.py:169
  156.9 26.2 %collective-permute-start.9 = (bf16[192,512]{1,0:T(8,128)(2,1)S(1)}, bf16[192,512]{1,0:T(8,128)(2,1)S(1)}, u32[]{:S(2)}, u32[]{:S(2)}) collective-permute-start(bf16[192,512]{1,0:T(8,128)(2,1)S(1)} %reduce_sum.25), channel_id=1, source_target_pairs={{0,476},{1,477},{2,478},{3,479},{4,412},{5,413},{6,414},{7,415},{8... | collective-permute-start | bytes 589832 | tf_op jit(solution)/shard_map/ppermute | solution.py:169
Sparse Core Ops, SparseCore 0:
  25.7 69.6 all-gather.1

commit v12 on v11

--- a/solution.py
+++ b/solution.py
@@ -38,9 +38,9 @@
     return next((h2, x2) for h2 in range(H) for x2 in range(X) if place(h, h2, x2) == l)
 
 
-def weight_perm(k):
+def weight_perm(k, d):
     return [
-        (flat(h, x, c, l, y), flat(l // X, l % X, c, place(l // X, h ^ k, x), y))
+        (flat(h, x, c, l, y), flat(l // X, l % X, c ^ d, place(l // X, h ^ k, x), y))
         for h, x, c, l, y in coords()
     ]
 
@@ -118,6 +118,7 @@
 
     n_mu, n_a = coefficients.shape
     part = n_mu // Y
+    c_other = swap_core(coefficients)
     mirror = [(i, H * L - 1 - i) for i in range(H * L)]
     piece = lax.dynamic_slice_in_dim(coefficients, y * part, part, 0)
     piece = lax.ppermute(piece, ("h", "l"), mirror)
@@ -126,28 +127,29 @@
     info = jnp.pad(pair_list.astype(bf16), ((0, rows - 1), (0, 126)))
     t_own = jnp.concatenate([amplitudes[0].T, info], axis=1)
     t_all = gather(t_own, "x", X)
-    t_all, piece = lax.optimization_barrier((t_all, piece))
-    halves = (t_all, swap_core(t_all))
-    slots, n_b = C * X, C * X * rows
-    info = [v[:, 0, n_a:] for v in halves] + [jnp.zeros((16 - slots, n_mu), bf16)]
-    halves = [v.reshape(X * rows, -1)[:, :n_a] for v in halves]
-
+    info = t_all[:, 0, n_a:]
+    info = jnp.pad(info, ((0, 16 - X), (0, 0)))
+    t_all = t_all.reshape(X * rows, -1)[:, :n_a]
     c_far = jnp.zeros((n_mu, n_a), bf16)
     for k in range(Y):
         v = lax.ppermute(piece, "y", shift(Y, k)) if k else piece
         c_far = lax.dynamic_update_slice_in_dim(c_far, v, (y - k) % Y * part, 0)
 
-    w = []
-    for k, m in enumerate((coefficients, c_far)):
-        v = [
-            lax.dot_general(t, m, (((1,), (1,)), ((), ())), preferred_element_type=f32)
-            for t in halves
-        ]
-        v = jnp.concatenate([t.astype(bf16) for t in v] + info, axis=0)
-        w.append(lax.ppermute(v, AXES, weight_perm(k)))
+    def weights(m):
+        return lax.dot_general(
+            t_all, m, (((1,), (1,)), ((), ())), preferred_element_type=f32
+        ).astype(bf16)
+
+    near = [weights(coefficients), weights(c_other)]
+    far = [weights(c_far), weights(swap_core(c_far))]
+    w = [
+        lax.ppermute(jnp.concatenate([v, info], axis=0), AXES, weight_perm(k, d))
+        for k, pieces in enumerate((near, far))
+        for d, v in enumerate(pieces)
+    ]
     w = jnp.stack(w)
-    slots *= H
-    pairs = w[:, n_b : n_b + C * X, :2].reshape(slots, 2).astype(jnp.int32)
+    slots, n_b = H * C * X, X * rows
+    pairs = w[:, n_b : n_b + X, :2].reshape(slots, 2).astype(jnp.int32)
     w = w[:, :n_b].reshape(slots, rows, n_mu)
 
     w, b_near = lax.optimization_barrier((w, b_near))

time: 192 us -> 185 us (0.964)
  the two profiles are of different devices: /device:TPU:5 before, /device:TPU:199 now
where the time goes in v12:
time: 185 us; the launch traced here: 184 us
  starting transfers between devices  77.1 us (42%)
  waiting for transfers between devices  71.7 us (39%)
  between operations  13.7 us (7%)
  Pallas kernels  10 us (5%)
  local copies, waits for them, and re-layouts  6.8 us (4%)
  other arithmetic  2.71 us (1%)
    ppermute x2, waiting for transfers between devices, on_device(): total += lax.ppermute(v, AXES, result_perm(k)).astype(f32)  28.4 us
    ppermute x4, starting transfers between devices, on_device(): lax.ppermute(jnp.concatenate([v, info], axis=0), AXES, weight_perm(k, d))  25.3 us
    all_to_all x2, starting transfers between devices, on_device(): v = lax.all_to_all(v, 'x', split_axis=0, concat_axis=0, tiled=True)  15.4 us
    all_to_all x2, waiting for transfers between devices, gather(): return lax.all_to_all(v, axes, split_axis=0, concat_axis=0, tiled=True)  14.7 us
    all_to_all x2, waiting for transfers between devices, on_device(): v = lax.all_to_all(v, 'x', split_axis=0, concat_axis=0, tiled=True)  12.3 us
    pallas_call x2, Pallas kernels, contract(): pl.pallas_call(contract_kernel, grid_spec=pltpu.PrefetchScalarGridSpec(nu...  10 us
    ppermute x3, starting transfers between devices, on_device(): v = lax.ppermute(piece, 'y', shift(Y, k)) if k else piece  9.49 us
    ppermute x3, starting transfers between devices, swap_core(): return lax.ppermute(v, 'c', shift(C, 1))  8.3 us
  transfers between devices with their start and end apart: 18, of which 10 were waited for; matrix products, arithmetic and copies ran while one was open for 5% of the time, Pallas kernels for 3%

profile of v12, /device:TPU:199, one launch (start us, length us, event | category | flops | bytes accessed | tf_op | source)
XLA Modules:
  0.0 183.8 jit_solution(7827808384128495227)
XLA Ops:
  6.5 0.0 all-gather.2.cloned.1.call-start
  6.5 1.6 copy.27
  8.2 0.0 all-gather.2.cloned.1.call-update
  8.2 2.6 %collective-permute-start.1 = (bf16[128,2048]{1,0:T(8,128)(2,1)}, bf16[128,2048]{1,0:T(8,128)(2,1)S(1)}, u32[]{:S(2)}, u32[]{:S(2)}) collective-permute-start(bf16[128,2048]{1,0:T(8,128)(2,1)} %param.7), channel_id=1, source_target_pairs={{0,32},{32,0},{1,33},{33,1},{2,34},{34,2},{3,35},{35,3},{4,36},{36... | collective-permute-start | bytes 1572872 | tf_op jit(solution)/shard_map/ppermute | solution.py:109
  10.8 0.9 constant_dynamic-slice_fusion
  11.7 6.6 %collective-permute-start.3 = (bf16[32,2048]{1,0:T(8,128)(2,1)S(1)}, bf16[32,2048]{1,0:T(8,128)(2,1)S(1)}, u32[]{:S(2)}, u32[]{:S(2)}) collective-permute-start(bf16[32,2048]{1,0:T(8,128)(2,1)S(1)} %constant_dynamic-slice_fusion), channel_id=1, source_target_pairs={{0,284},{4,280},{8,276},{12,272},{16,268},{20,264},{24,260},{28,25... | collective-permute-start | bytes 393224 | tf_op jit(solution)/shard_map/ppermute | solution.py:124
  18.3 0.7 convert_element_type.38
  18.9 1.0 fusion.5
  19.9 1.1 broadcast_in_dim.9
  21.0 4.2 %all-to-all-start = ((bf16[4,64,2176]{2,1,0:T(8,128)(2,1)}), bf16[4,64,2176]{2,1,0:T(8,128)(2,1)S(1)}, u32[]{:S(2)}, u32[]{:S(2)}) async-start(bf16[4,64,2176]{2,1,0:T(8,128)(2,1)} %broadcast_in_dim.9), calls=%async_computation | async-start | bytes 2228224 | tf_op jit(solution)/shard_map/all_to_all | solution.py:113
  25.2 2.5 %collective-permute-done.3 = bf16[32,2048]{1,0:T(8,128)(2,1)S(1)} collective-permute-done((bf16[32,2048]{1,0:T(8,128)(2,1)S(1)}, bf16[32,2048]{1,0:T(8,128)(2,1)S(1)}, u32[]{:S(2)}, u32[]{:S(2)}) %collective-permute-start.3) | collective-permute-done | bytes 131104 | tf_op jit(solution)/shard_map/ppermute | solution.py:124
  27.7 4.6 %collective-permute-start.6 = (bf16[32,2048]{1,0:T(8,128)(2,1)S(1)}, bf16[32,2048]{1,0:T(8,128)(2,1)S(1)}, u32[]{:S(2)}, u32[]{:S(2)}) collective-permute-start(bf16[32,2048]{1,0:T(8,128)(2,1)S(1)} %collective-permute-done.3), channel_id=1, source_target_pairs={{0,3},{1,0},{2,1},{3,2},{4,7},{5,4},{6,5},{7,6},{8,11},{9,8},{10,9... | collective-permute-start | bytes 393224 | tf_op jit(solution)/shard_map/ppermute | solution.py:135
  32.3 2.3 %collective-permute-start.5 = (bf16[32,2048]{1,0:T(8,128)(2,1)S(1)}, bf16[32,2048]{1,0:T(8,128)(2,1)S(1)}, u32[]{:S(2)}, u32[]{:S(2)}) collective-permute-start(bf16[32,2048]{1,0:T(8,128)(2,1)S(1)} %collective-permute-done.3), channel_id=1, source_target_pairs={{0,2},{1,3},{2,0},{3,1},{4,6},{5,7},{6,4},{7,5},{8,10},{9,11},{10,... | collective-permute-start | bytes 393224 | tf_op jit(solution)/shard_map/ppermute | solution.py:135
  34.6 2.6 %collective-permute-start.4 = (bf16[32,2048]{1,0:T(8,128)(2,1)S(1)}, bf16[32,2048]{1,0:T(8,128)(2,1)S(1)}, u32[]{:S(2)}, u32[]{:S(2)}) collective-permute-start(bf16[32,2048]{1,0:T(8,128)(2,1)S(1)} %collective-permute-done.3), channel_id=1, source_target_pairs={{0,1},{1,2},{2,3},{3,0},{4,5},{5,6},{6,7},{7,4},{8,9},{9,10},{10,1... | collective-permute-start | bytes 393224 | tf_op jit(solution)/shard_map/ppermute | solution.py:135
  37.3 6.0 %collective-permute-done.4 = bf16[32,2048]{1,0:T(8,128)(2,1)S(1)} collective-permute-done((bf16[32,2048]{1,0:T(8,128)(2,1)S(1)}, bf16[32,2048]{1,0:T(8,128)(2,1)S(1)}, u32[]{:S(2)}, u32[]{:S(2)}) %collective-permute-start.4) | collective-permute-done | bytes 131104 | tf_op jit(solution)/shard_map/ppermute | solution.py:135
  43.3 0.0 collective-permute-done.5
  43.3 0.0 copy-start.1
  43.3 0.0 collective-permute-done.6
  43.4 3.4 %collective-permute-start.8 = (bf16[128,2048]{1,0:T(8,128)(2,1)S(1)}, bf16[128,2048]{1,0:T(8,128)(2,1)S(1)}, u32[]{:S(2)}, u32[]{:S(2)}) collective-permute-start(bf16[128,2048]{1,0:T(8,128)(2,1)S(1)} %constant_dynamic-update-slice_fusion), channel_id=1, source_target_pairs={{0,32},{32,0},{1,33},{33,1},{2,34},{34,2},{3,35},{35,3},{4,36},{36... | collective-permute-start | bytes 1572872 | tf_op jit(solution)/shard_map/ppermute | solution.py:109
  46.7 0.0 all-to-all-done
  46.8 0.4 convolution_convert_fusion.1
  47.2 0.0 copy-done.1
  47.2 0.4 convolution_convert_fusion.3
  47.7 0.0 collective-permute-done.1
  47.7 0.4 convolution_convert_fusion.2
  48.1 0.1 collective-permute-done.8
  48.2 0.4 convolution_convert_fusion
  48.7 6.4 %collective-permute-start.9 = (bf16[272,128]{1,0:T(8,128)(2,1)S(1)}, bf16[272,128]{1,0:T(8,128)(2,1)S(1)}, u32[]{:S(2)}, u32[]{:S(2)}) collective-permute-start(bf16[272,128]{1,0:T(8,128)(2,1)S(1)} %get-tuple-element.16), channel_id=1, source_target_pairs={{0,60},{1,61},{2,62},{3,63},{4,124},{5,125},{6,126},{7,127},{8,188... | collective-permute-start | bytes 208904 | tf_op jit(solution)/shard_map/ppermute | solution.py:146
  55.1 3.7 %collective-permute-start.7 = (bf16[272,128]{1,0:T(8,128)(2,1)S(1)}, bf16[272,128]{1,0:T(8,128)(2,1)S(1)}, u32[]{:S(2)}, u32[]{:S(2)}) collective-permute-start(bf16[272,128]{1,0:T(8,128)(2,1)S(1)} %get-tuple-element.15), channel_id=1, source_target_pairs={{0,28},{1,29},{2,30},{3,31},{4,92},{5,93},{6,94},{7,95},{8,156},{9... | collective-permute-start | bytes 208904 | tf_op jit(solution)/shard_map/ppermute | solution.py:146
  58.8 7.3 %collective-permute-start.2 = (bf16[272,128]{1,0:T(8,128)(2,1)S(1)}, bf16[272,128]{1,0:T(8,128)(2,1)S(1)}, u32[]{:S(2)}, u32[]{:S(2)}) collective-permute-start(bf16[272,128]{1,0:T(8,128)(2,1)S(1)} %get-tuple-element.14), channel_id=1, source_target_pairs={{0,40},{1,41},{2,42},{3,43},{4,104},{5,105},{6,106},{7,107},{8,168... | collective-permute-start | bytes 208904 | tf_op jit(solution)/shard_map/ppermute | solution.py:146
  66.1 7.9 %collective-permute-start = (bf16[272,128]{1,0:T(8,128)(2,1)S(1)}, bf16[272,128]{1,0:T(8,128)(2,1)S(1)}, u32[]{:S(2)}, u32[]{:S(2)}) collective-permute-start(bf16[272,128]{1,0:T(8,128)(2,1)S(1)} %get-tuple-element.13), channel_id=1, source_target_pairs={{0,8},{1,9},{2,10},{3,11},{4,72},{5,73},{6,74},{7,75},{8,136},{9,1... | collective-permute-start | bytes 208904 | tf_op jit(solution)/shard_map/ppermute | solution.py:146
  74.0 0.0 collective-permute-done.9
  74.0 0.2 copy.21
  74.2 0.0 collective-permute-done.7
  74.2 0.2 copy.20
  74.4 6.4 %collective-permute-done.2 = bf16[272,128]{1,0:T(8,128)(2,1)S(1)} collective-permute-done((bf16[272,128]{1,0:T(8,128)(2,1)S(1)}, bf16[272,128]{1,0:T(8,128)(2,1)S(1)}, u32[]{:S(2)}, u32[]{:S(2)}) %collective-permute-start.2) | collective-permute-done | bytes 69664 | tf_op jit(solution)/shard_map/ppermute | solution.py:146
  80.8 0.2 copy.19
  81.0 1.3 collective-permute-done
  82.3 0.2 copy.18
  82.5 0.6 pad_maximum_fusion
  83.1 0.2 copy.22
  83.3 0.0 all-gather.2.cloned.1.call-done.near_ref
  83.4 2.4 %collective-permute-start.10 = (bf16[1536,512]{1,0:T(8,128)(2,1)}, bf16[1536,512]{1,0:T(8,128)(2,1)}, u32[]{:S(2)}, u32[]{:S(2)}) collective-permute-start(bf16[1536,512]{1,0:T(8,128)(2,1)} %all-gather.2.cloned.1.call-done.near_ref), channel_id=1, source_target_pairs={{0,32},{32,0},{1,33},{33,1},{2,34},{34,2},{3,35},{35,3},{4,36},{36... | collective-permute-start | bytes 4718600 | tf_op jit(solution)/shard_map/ppermute | solution.py:109
  85.7 1.2 broadcast_in_dim.22
  86.9 4.0 %all-to-all-start.1 = ((bf16[4,16,64,128]{3,2,1,0:T(8,128)(2,1)}), bf16[4,16,64,128]{3,2,1,0:T(8,128)(2,1)S(1)}, u32[]{:S(2)}, u32[]{:S(2)}) async-start(bf16[4,16,64,128]{3,2,1,0:T(8,128)(2,1)} %broadcast_in_dim.22), calls=%async_computation.1 | async-start | bytes 2097152 | tf_op jit(solution)/shard_map/all_to_all | solution.py:113
  91.0 0.0 copy-done.2
  91.0 0.1 pad_add_fusion
  91.1 0.1 reshape.33
  91.2 14.7 %all-to-all-done.1.w_ref = bf16[4,16,64,128]{3,2,1,0:T(8,128)(2,1)S(1)} async-done(((bf16[4,16,64,128]{3,2,1,0:T(8,128)(2,1)}), bf16[4,16,64,128]{3,2,1,0:T(8,128)(2,1)S(1)}, u32[]{:S(2)}, u32[]{:S(2)}) %all-to-all-start.1) | async-done | bytes 1048608 | tf_op jit(solution)/shard_map/all_to_all | solution.py:113
  105.9 0.0 collective-permute-done.10.far_ref
  105.9 5.0 %shard_map.55 = bf16[768,512]{1,0:T(8,128)(2,1)} custom-call(s32[5]{0:T(128)S(1)} %get-tuple-element.17.where_ref, s32[16]{0:T(128)S(1)} %get-tuple-element.12.first_ref, s32[16]{0:T(128)S(1)} %get-tuple-element.11.second_ref, bf16[4,16,64,128]{3,2,1,0:T(8,128)(2,1)S(1)} %all-to-all-done.1.w_ref, bf16[1536,512]{1,0:T(8,128)(2,1)S(1)} %copy-done, ...), custom_call_target="tpu_custom_call" | custom-call | flops 805306368 | bytes 4194304 | tf_op jit(solution)/shard_map/pallas_call | solution.py:87
  110.9 10.1 %all-to-all-start.2 = ((bf16[4,192,512]{2,1,0:T(8,128)(2,1)}), bf16[4,192,512]{2,1,0:T(8,128)(2,1)S(1)}, u32[]{:S(2)}, u32[]{:S(2)}) async-start(bf16[4,192,512]{2,1,0:T(8,128)(2,1)} %bitcast.13), calls=%async_computation.2 | async-start | bytes 1572864 | tf_op jit(solution)/shard_map/all_to_all | solution.py:169
  121.1 5.0 %shard_map.56 = bf16[768,512]{1,0:T(8,128)(2,1)} custom-call(s32[5]{0:T(128)S(1)} %get-tuple-element.18.where_ref, s32[16]{0:T(128)S(1)} %get-tuple-element.12.first_ref, s32[16]{0:T(128)S(1)} %get-tuple-element.11.second_ref, bf16[4,16,64,128]{3,2,1,0:T(8,128)(2,1)S(1)} %all-to-all-done.1.w_ref, bf16[1536,512]{1,0:T(8,128)(2,1)S(1)} %copy-done, ...), custom_call_target="tpu_custom_call" | custom-call | flops 805306368 | bytes 4194304 | tf_op jit(solution)/shard_map/pallas_call | solution.py:87
  126.1 4.7 %all-to-all-done.2 = bf16[4,192,512]{2,1,0:T(8,128)(2,1)S(1)} async-done(((bf16[4,192,512]{2,1,0:T(8,128)(2,1)}), bf16[4,192,512]{2,1,0:T(8,128)(2,1)S(1)}, u32[]{:S(2)}, u32[]{:S(2)}) %all-to-all-start.2) | async-done | bytes 786464 | tf_op jit(solution)/shard_map/all_to_all | solution.py:169
  130.7 5.3 %all-to-all-start.3 = ((bf16[4,192,512]{2,1,0:T(8,128)(2,1)}), bf16[4,192,512]{2,1,0:T(8,128)(2,1)S(1)}, u32[]{:S(2)}, u32[]{:S(2)}) async-start(bf16[4,192,512]{2,1,0:T(8,128)(2,1)} %bitcast.15), calls=%async_computation.3 | async-start | bytes 1572864 | tf_op jit(solution)/shard_map/all_to_all | solution.py:169
  136.0 0.1 reduce_sum.24
  136.1 1.9 %collective-permute-start.11 = (bf16[192,512]{1,0:T(8,128)(2,1)S(1)}, bf16[192,512]{1,0:T(8,128)(2,1)S(1)}, u32[]{:S(2)}, u32[]{:S(2)}) collective-permute-start(bf16[192,512]{1,0:T(8,128)(2,1)S(1)} %reduce_sum.24), channel_id=1, source_target_pairs={{0,448},{1,449},{2,450},{3,451},{4,384},{5,385},{6,386},{7,387},{8... | collective-permute-start | bytes 589832 | tf_op jit(solution)/shard_map/ppermute | solution.py:171
  138.1 7.6 %all-to-all-done.3 = bf16[4,192,512]{2,1,0:T(8,128)(2,1)S(1)} async-done(((bf16[4,192,512]{2,1,0:T(8,128)(2,1)}), bf16[4,192,512]{2,1,0:T(8,128)(2,1)S(1)}, u32[]{:S(2)}, u32[]{:S(2)}) %all-to-all-start.3) | async-done | bytes 786464 | tf_op jit(solution)/shard_map/all_to_all | solution.py:169
  145.7 0.1 reduce_sum.25
  145.8 1.9 %collective-permute-start.12 = (bf16[192,512]{1,0:T(8,128)(2,1)S(1)}, bf16[192,512]{1,0:T(8,128)(2,1)S(1)}, u32[]{:S(2)}, u32[]{:S(2)}) collective-permute-start(bf16[192,512]{1,0:T(8,128)(2,1)S(1)} %reduce_sum.25), channel_id=1, source_target_pairs={{0,476},{1,477},{2,478},{3,479},{4,412},{5,413},{6,414},{7,415},{8... | collective-permute-start | bytes 589832 | tf_op jit(solution)/shard_map/ppermute | solution.py:171
  147.8 15.4 %collective-permute-done.11 = bf16[192,512]{1,0:T(8,128)(2,1)S(1)} collective-permute-done((bf16[192,512]{1,0:T(8,128)(2,1)S(1)}, bf16[192,512]{1,0:T(8,128)(2,1)S(1)}, u32[]{:S(2)}, u32[]{:S(2)}) %collective-permute-start.11) | collective-permute-done | bytes 196640 | tf_op jit(solution)/shard_map/ppermute | solution.py:171
  163.1 13.0 %collective-permute-done.12 = bf16[192,512]{1,0:T(8,128)(2,1)S(1)} collective-permute-done((bf16[192,512]{1,0:T(8,128)(2,1)S(1)}, bf16[192,512]{1,0:T(8,128)(2,1)S(1)}, u32[]{:S(2)}, u32[]{:S(2)}) %collective-permute-start.12) | collective-permute-done | bytes 196640 | tf_op jit(solution)/shard_map/ppermute | solution.py:171
  176.1 0.1 add_convert_fusion
  176.2 0.7 reshape.32
  (16 shorter events, 0.2 us)
Async XLA Ops:
  6.5 76.8 %all-gather.2.cloned.1.call-start = ((), (), s32[]{:S(2)}) async-start(), calls=%async_computation.4 | async-start | bytes 1769472 | tf_op jit(solution)/shard_map/all_gather | solution.py:117
  8.2 39.5 %collective-permute-start.1 = (bf16[128,2048]{1,0:T(8,128)(2,1)}, bf16[128,2048]{1,0:T(8,128)(2,1)S(1)}, u32[]{:S(2)}, u32[]{:S(2)}) collective-permute-start(bf16[128,2048]{1,0:T(8,128)(2,1)} %param.7), channel_id=1, source_target_pairs={{0,32},{32,0},{1,33},{33,1},{2,34},{34,2},{3,35},{35,3},{4,36},{36... | collective-permute-start | bytes 1572872 | tf_op jit(solution)/shard_map/ppermute | solution.py:109
  11.7 16.0 %collective-permute-start.3 = (bf16[32,2048]{1,0:T(8,128)(2,1)S(1)}, bf16[32,2048]{1,0:T(8,128)(2,1)S(1)}, u32[]{:S(2)}, u32[]{:S(2)}) collective-permute-start(bf16[32,2048]{1,0:T(8,128)(2,1)S(1)} %constant_dynamic-slice_fusion), channel_id=1, source_target_pairs={{0,284},{4,280},{8,276},{12,272},{16,268},{20,264},{24,260},{28,25... | collective-permute-start | bytes 393224 | tf_op jit(solution)/shard_map/ppermute | solution.py:124
  21.0 25.7 %all-to-all-start = ((bf16[4,64,2176]{2,1,0:T(8,128)(2,1)}), bf16[4,64,2176]{2,1,0:T(8,128)(2,1)S(1)}, u32[]{:S(2)}, u32[]{:S(2)}) async-start(bf16[4,64,2176]{2,1,0:T(8,128)(2,1)} %broadcast_in_dim.9), calls=%async_computation | async-start | bytes 2228224 | tf_op jit(solution)/shard_map/all_to_all | solution.py:113
  27.7 15.6 %collective-permute-start.6 = (bf16[32,2048]{1,0:T(8,128)(2,1)S(1)}, bf16[32,2048]{1,0:T(8,128)(2,1)S(1)}, u32[]{:S(2)}, u32[]{:S(2)}) collective-permute-start(bf16[32,2048]{1,0:T(8,128)(2,1)S(1)} %collective-permute-done.3), channel_id=1, source_target_pairs={{0,3},{1,0},{2,1},{3,2},{4,7},{5,4},{6,5},{7,6},{8,11},{9,8},{10,9... | collective-permute-start | bytes 393224 | tf_op jit(solution)/shard_map/ppermute | solution.py:135
  32.3 10.9 %collective-permute-start.5 = (bf16[32,2048]{1,0:T(8,128)(2,1)S(1)}, bf16[32,2048]{1,0:T(8,128)(2,1)S(1)}, u32[]{:S(2)}, u32[]{:S(2)}) collective-permute-start(bf16[32,2048]{1,0:T(8,128)(2,1)S(1)} %collective-permute-done.3), channel_id=1, source_target_pairs={{0,2},{1,3},{2,0},{3,1},{4,6},{5,7},{6,4},{7,5},{8,10},{9,11},{10,... | collective-permute-start | bytes 393224 | tf_op jit(solution)/shard_map/ppermute | solution.py:135
  34.6 8.6 %collective-permute-start.4 = (bf16[32,2048]{1,0:T(8,128)(2,1)S(1)}, bf16[32,2048]{1,0:T(8,128)(2,1)S(1)}, u32[]{:S(2)}, u32[]{:S(2)}) collective-permute-start(bf16[32,2048]{1,0:T(8,128)(2,1)S(1)} %collective-permute-done.3), channel_id=1, source_target_pairs={{0,1},{1,2},{2,3},{3,0},{4,5},{5,6},{6,7},{7,4},{8,9},{9,10},{10,1... | collective-permute-start | bytes 393224 | tf_op jit(solution)/shard_map/ppermute | solution.py:135
  43.3 3.9 %copy-start.1 = (bf16[128,2048]{1,0:T(8,128)(2,1)S(1)}, bf16[128,2048]{1,0:T(8,128)(2,1)}, u32[]{:S(2)}) copy-start(bf16[128,2048]{1,0:T(8,128)(2,1)} %param.7) | copy-start | bytes 1572868
  43.4 4.9 %collective-permute-start.8 = (bf16[128,2048]{1,0:T(8,128)(2,1)S(1)}, bf16[128,2048]{1,0:T(8,128)(2,1)S(1)}, u32[]{:S(2)}, u32[]{:S(2)}) collective-permute-start(bf16[128,2048]{1,0:T(8,128)(2,1)S(1)} %constant_dynamic-update-slice_fusion), channel_id=1, source_target_pairs={{0,32},{32,0},{1,33},{33,1},{2,34},{34,2},{3,35},{35,3},{4,36},{36... | collective-permute-start | bytes 1572872 | tf_op jit(solution)/shard_map/ppermute | solution.py:109
  48.7 25.3 %collective-permute-start.9 = (bf16[272,128]{1,0:T(8,128)(2,1)S(1)}, bf16[272,128]{1,0:T(8,128)(2,1)S(1)}, u32[]{:S(2)}, u32[]{:S(2)}) collective-permute-start(bf16[272,128]{1,0:T(8,128)(2,1)S(1)} %get-tuple-element.16), channel_id=1, source_target_pairs={{0,60},{1,61},{2,62},{3,63},{4,124},{5,125},{6,126},{7,127},{8,188... | collective-permute-start | bytes 208904 | tf_op jit(solution)/shard_map/ppermute | solution.py:146
  55.1 19.1 %collective-permute-start.7 = (bf16[272,128]{1,0:T(8,128)(2,1)S(1)}, bf16[272,128]{1,0:T(8,128)(2,1)S(1)}, u32[]{:S(2)}, u32[]{:S(2)}) collective-permute-start(bf16[272,128]{1,0:T(8,128)(2,1)S(1)} %get-tuple-element.15), channel_id=1, source_target_pairs={{0,28},{1,29},{2,30},{3,31},{4,92},{5,93},{6,94},{7,95},{8,156},{9... | collective-permute-start | bytes 208904 | tf_op jit(solution)/shard_map/ppermute | solution.py:146
  58.8 22.0 %collective-permute-start.2 = (bf16[272,128]{1,0:T(8,128)(2,1)S(1)}, bf16[272,128]{1,0:T(8,128)(2,1)S(1)}, u32[]{:S(2)}, u32[]{:S(2)}) collective-permute-start(bf16[272,128]{1,0:T(8,128)(2,1)S(1)} %get-tuple-element.14), channel_id=1, source_target_pairs={{0,40},{1,41},{2,42},{3,43},{4,104},{5,105},{6,106},{7,107},{8,168... | collective-permute-start | bytes 208904 | tf_op jit(solution)/shard_map/ppermute | solution.py:146
  66.1 16.2 %collective-permute-start = (bf16[272,128]{1,0:T(8,128)(2,1)S(1)}, bf16[272,128]{1,0:T(8,128)(2,1)S(1)}, u32[]{:S(2)}, u32[]{:S(2)}) collective-permute-start(bf16[272,128]{1,0:T(8,128)(2,1)S(1)} %get-tuple-element.13), channel_id=1, source_target_pairs={{0,8},{1,9},{2,10},{3,11},{4,72},{5,73},{6,74},{7,75},{8,136},{9,1... | collective-permute-start | bytes 208904 | tf_op jit(solution)/shard_map/ppermute | solution.py:146
  83.4 22.5 %collective-permute-start.10 = (bf16[1536,512]{1,0:T(8,128)(2,1)}, bf16[1536,512]{1,0:T(8,128)(2,1)}, u32[]{:S(2)}, u32[]{:S(2)}) collective-permute-start(bf16[1536,512]{1,0:T(8,128)(2,1)} %all-gather.2.cloned.1.call-done.near_ref), channel_id=1, source_target_pairs={{0,32},{32,0},{1,33},{33,1},{2,34},{34,2},{3,35},{35,3},{4,36},{36... | collective-permute-start | bytes 4718600 | tf_op jit(solution)/shard_map/ppermute | solution.py:109
  86.9 4.1 %copy-start.2 = (s32[1,4]{1,0:T(1,128)S(1)}, s32[1,4]{1,0:T(1,128)}, u32[]{:S(2)}) copy-start(s32[1,4]{1,0:T(1,128)} %constant.70) | copy-start | bytes 52
  86.9 4.1 %copy-start.3 = (s32[1,4]{1,0:T(1,128)S(1)}, s32[1,4]{1,0:T(1,128)}, u32[]{:S(2)}) copy-start(s32[1,4]{1,0:T(1,128)} %constant.69) | copy-start | bytes 52
  86.9 19.0 %copy-start = (bf16[1536,512]{1,0:T(8,128)(2,1)S(1)}, bf16[1536,512]{1,0:T(8,128)(2,1)}, u32[]{:S(2)}) copy-start(bf16[1536,512]{1,0:T(8,128)(2,1)} %all-gather.2.cloned.1.call-done.near_ref) | copy-start | bytes 4718596
  86.9 18.9 %all-to-all-start.1 = ((bf16[4,16,64,128]{3,2,1,0:T(8,128)(2,1)}), bf16[4,16,64,128]{3,2,1,0:T(8,128)(2,1)S(1)}, u32[]{:S(2)}, u32[]{:S(2)}) async-start(bf16[4,16,64,128]{3,2,1,0:T(8,128)(2,1)} %broadcast_in_dim.22), calls=%async_computation.1 | async-start | bytes 2097152 | tf_op jit(solution)/shard_map/all_to_all | solution.py:113
  110.9 19.8 %all-to-all-start.2 = ((bf16[4,192,512]{2,1,0:T(8,128)(2,1)}), bf16[4,192,512]{2,1,0:T(8,128)(2,1)S(1)}, u32[]{:S(2)}, u32[]{:S(2)}) async-start(bf16[4,192,512]{2,1,0:T(8,128)(2,1)} %bitcast.13), calls=%async_computation.2 | async-start | bytes 1572864 | tf_op jit(solution)/shard_map/all_to_all | solution.py:169
  130.7 15.0 %all-to-all-start.3 = ((bf16[4,192,512]{2,1,0:T(8,128)(2,1)}), bf16[4,192,512]{2,1,0:T(8,128)(2,1)S(1)}, u32[]{:S(2)}, u32[]{:S(2)}) async-start(bf16[4,192,512]{2,1,0:T(8,128)(2,1)} %bitcast.15), calls=%async_computation.3 | async-start | bytes 1572864 | tf_op jit(solution)/shard_map/all_to_all | solution.py:169
  136.1 27.0 %collective-permute-start.11 = (bf16[192,512]{1,0:T(8,128)(2,1)S(1)}, bf16[192,512]{1,0:T(8,128)(2,1)S(1)}, u32[]{:S(2)}, u32[]{:S(2)}) collective-permute-start(bf16[192,512]{1,0:T(8,128)(2,1)S(1)} %reduce_sum.24), channel_id=1, source_target_pairs={{0,448},{1,449},{2,450},{3,451},{4,384},{5,385},{6,386},{7,387},{8... | collective-permute-start | bytes 589832 | tf_op jit(solution)/shard_map/ppermute | solution.py:171
  145.8 30.3 %collective-permute-start.12 = (bf16[192,512]{1,0:T(8,128)(2,1)S(1)}, bf16[192,512]{1,0:T(8,128)(2,1)S(1)}, u32[]{:S(2)}, u32[]{:S(2)}) collective-permute-start(bf16[192,512]{1,0:T(8,128)(2,1)S(1)} %reduce_sum.25), channel_id=1, source_target_pairs={{0,476},{1,477},{2,478},{3,479},{4,412},{5,413},{6,414},{7,415},{8... | collective-permute-start | bytes 589832 | tf_op jit(solution)/shard_map/ppermute | solution.py:171
Sparse Core Ops, SparseCore 0:
  9.4 63.0 all-gather.1

commit v13 on v12

--- a/solution.py
+++ b/solution.py
@@ -26,12 +26,11 @@
                         yield h, x, c, l, y
 
 
-INNER, OUTER = (2, 3, 4, 5), (7, 6, 1, 0)
+INNER, OUTER = (2, 3, 4, 5), (0, 1, 6, 7)
 
 
 def place(h, h2, x2):
-    l = (INNER if h2 == h else OUTER)[x2]
-    return l if h == 0 else L - 1 - l
+    return (INNER if h2 == h else OUTER)[x2]
 
 
 def chunk(h, l):

time: 185 us -> 187 us (1.011)
  the two profiles are of different devices: /device:TPU:199 before, /device:TPU:5 now
where the time goes in v13:
time: 187 us; the launch traced here: 186 us
  starting transfers between devices  77 us (41%)
  waiting for transfers between devices  74 us (40%)
  between operations  13.8 us (7%)
  Pallas kernels  10 us (5%)
  local copies, waits for them, and re-layouts  6.8 us (4%)
  other arithmetic  2.71 us (1%)
    ppermute x2, waiting for transfers between devices, on_device(): total += lax.ppermute(v, AXES, result_perm(k)).astype(f32)  26.7 us
    ppermute x4, starting transfers between devices, on_device(): lax.ppermute(jnp.concatenate([v, info], axis=0), AXES, weight_perm(k, d))  21.4 us
    all_to_all x2, waiting for transfers between devices, gather(): return lax.all_to_all(v, axes, split_axis=0, concat_axis=0, tiled=True)  14.9 us
    ppermute x4, waiting for transfers between devices, on_device(): lax.ppermute(jnp.concatenate([v, info], axis=0), AXES, weight_perm(k, d))  12.7 us
    all_to_all x2, starting transfers between devices, on_device(): v = lax.all_to_all(v, 'x', split_axis=0, concat_axis=0, tiled=True)  12.4 us
    ppermute x1, starting transfers between devices, on_device(): piece = lax.ppermute(piece, ('h', 'l'), mirror)  11.1 us
    pallas_call x2, Pallas kernels, contract(): pl.pallas_call(contract_kernel, grid_spec=pltpu.PrefetchScalarGridSpec(nu...  10 us
    ppermute x3, starting transfers between devices, on_device(): v = lax.ppermute(piece, 'y', shift(Y, k)) if k else piece  9.49 us
  transfers between devices with their start and end apart: 18, of which 10 were waited for; matrix products, arithmetic and copies ran while one was open for 5% of the time, Pallas kernels for 3%

profile of v13, /device:TPU:5, one launch (start us, length us, event | category | flops | bytes accessed | tf_op | source)
XLA Modules:
  0.0 186.0 jit_solution(7797956313722640129)
XLA Ops:
  6.5 0.0 all-gather.2.cloned.1.call-start
  6.5 1.6 copy.27
  8.2 0.0 all-gather.2.cloned.1.call-update
  8.2 2.6 %collective-permute-start.1 = (bf16[128,2048]{1,0:T(8,128)(2,1)}, bf16[128,2048]{1,0:T(8,128)(2,1)S(1)}, u32[]{:S(2)}, u32[]{:S(2)}) collective-permute-start(bf16[128,2048]{1,0:T(8,128)(2,1)} %param.7), channel_id=1, source_target_pairs={{0,32},{32,0},{1,33},{33,1},{2,34},{34,2},{3,35},{35,3},{4,36},{36... | collective-permute-start | bytes 1572872 | tf_op jit(solution)/shard_map/ppermute | solution.py:108
  10.8 0.9 constant_dynamic-slice_fusion
  11.7 11.1 %collective-permute-start.3 = (bf16[32,2048]{1,0:T(8,128)(2,1)S(1)}, bf16[32,2048]{1,0:T(8,128)(2,1)S(1)}, u32[]{:S(2)}, u32[]{:S(2)}) collective-permute-start(bf16[32,2048]{1,0:T(8,128)(2,1)S(1)} %constant_dynamic-slice_fusion), channel_id=1, source_target_pairs={{0,284},{4,280},{8,276},{12,272},{16,268},{20,264},{24,260},{28,25... | collective-permute-start | bytes 393224 | tf_op jit(solution)/shard_map/ppermute | solution.py:123
  22.8 0.7 convert_element_type.38
  23.5 1.0 fusion.5
  24.5 1.1 broadcast_in_dim.9
  25.6 4.2 %all-to-all-start = ((bf16[4,64,2176]{2,1,0:T(8,128)(2,1)}), bf16[4,64,2176]{2,1,0:T(8,128)(2,1)S(1)}, u32[]{:S(2)}, u32[]{:S(2)}) async-start(bf16[4,64,2176]{2,1,0:T(8,128)(2,1)} %broadcast_in_dim.9), calls=%async_computation | async-start | bytes 2228224 | tf_op jit(solution)/shard_map/all_to_all | solution.py:112
  29.8 5.4 %collective-permute-done.3 = bf16[32,2048]{1,0:T(8,128)(2,1)S(1)} collective-permute-done((bf16[32,2048]{1,0:T(8,128)(2,1)S(1)}, bf16[32,2048]{1,0:T(8,128)(2,1)S(1)}, u32[]{:S(2)}, u32[]{:S(2)}) %collective-permute-start.3) | collective-permute-done | bytes 131104 | tf_op jit(solution)/shard_map/ppermute | solution.py:123
  35.2 4.6 %collective-permute-start.6 = (bf16[32,2048]{1,0:T(8,128)(2,1)S(1)}, bf16[32,2048]{1,0:T(8,128)(2,1)S(1)}, u32[]{:S(2)}, u32[]{:S(2)}) collective-permute-start(bf16[32,2048]{1,0:T(8,128)(2,1)S(1)} %collective-permute-done.3), channel_id=1, source_target_pairs={{0,3},{1,0},{2,1},{3,2},{4,7},{5,4},{6,5},{7,6},{8,11},{9,8},{10,9... | collective-permute-start | bytes 393224 | tf_op jit(solution)/shard_map/ppermute | solution.py:134
  39.8 2.3 %collective-permute-start.5 = (bf16[32,2048]{1,0:T(8,128)(2,1)S(1)}, bf16[32,2048]{1,0:T(8,128)(2,1)S(1)}, u32[]{:S(2)}, u32[]{:S(2)}) collective-permute-start(bf16[32,2048]{1,0:T(8,128)(2,1)S(1)} %collective-permute-done.3), channel_id=1, source_target_pairs={{0,2},{1,3},{2,0},{3,1},{4,6},{5,7},{6,4},{7,5},{8,10},{9,11},{10,... | collective-permute-start | bytes 393224 | tf_op jit(solution)/shard_map/ppermute | solution.py:134
  42.1 2.6 %collective-permute-start.4 = (bf16[32,2048]{1,0:T(8,128)(2,1)S(1)}, bf16[32,2048]{1,0:T(8,128)(2,1)S(1)}, u32[]{:S(2)}, u32[]{:S(2)}) collective-permute-start(bf16[32,2048]{1,0:T(8,128)(2,1)S(1)} %collective-permute-done.3), channel_id=1, source_target_pairs={{0,1},{1,2},{2,3},{3,0},{4,5},{5,6},{6,7},{7,4},{8,9},{9,10},{10,1... | collective-permute-start | bytes 393224 | tf_op jit(solution)/shard_map/ppermute | solution.py:134
  44.7 6.0 %collective-permute-done.4 = bf16[32,2048]{1,0:T(8,128)(2,1)S(1)} collective-permute-done((bf16[32,2048]{1,0:T(8,128)(2,1)S(1)}, bf16[32,2048]{1,0:T(8,128)(2,1)S(1)}, u32[]{:S(2)}, u32[]{:S(2)}) %collective-permute-start.4) | collective-permute-done | bytes 131104 | tf_op jit(solution)/shard_map/ppermute | solution.py:134
  50.8 0.0 collective-permute-done.5
  50.8 0.0 copy-start.1
  50.8 0.0 collective-permute-done.6
  50.8 3.3 %collective-permute-start.8 = (bf16[128,2048]{1,0:T(8,128)(2,1)S(1)}, bf16[128,2048]{1,0:T(8,128)(2,1)S(1)}, u32[]{:S(2)}, u32[]{:S(2)}) collective-permute-start(bf16[128,2048]{1,0:T(8,128)(2,1)S(1)} %constant_dynamic-update-slice_fusion), channel_id=1, source_target_pairs={{0,32},{32,0},{1,33},{33,1},{2,34},{34,2},{3,35},{35,3},{4,36},{36... | collective-permute-start | bytes 1572872 | tf_op jit(solution)/shard_map/ppermute | solution.py:108
  54.1 0.0 all-to-all-done
  54.1 0.4 convolution_convert_fusion.1
  54.6 0.4 convolution_convert_fusion.3
  55.0 0.0 collective-permute-done.1
  55.0 0.4 convolution_convert_fusion.2
  55.5 0.1 collective-permute-done.8
  55.6 0.4 convolution_convert_fusion
  56.1 4.3 %collective-permute-start.9 = (bf16[272,128]{1,0:T(8,128)(2,1)S(1)}, bf16[272,128]{1,0:T(8,128)(2,1)S(1)}, u32[]{:S(2)}, u32[]{:S(2)}) collective-permute-start(bf16[272,128]{1,0:T(8,128)(2,1)S(1)} %get-tuple-element.16), channel_id=1, source_target_pairs={{0,32},{1,33},{2,34},{3,35},{4,96},{5,97},{6,98},{7,99},{8,160},{9... | collective-permute-start | bytes 208904 | tf_op jit(solution)/shard_map/ppermute | solution.py:145
  60.4 8.3 %collective-permute-start.7 = (bf16[272,128]{1,0:T(8,128)(2,1)S(1)}, bf16[272,128]{1,0:T(8,128)(2,1)S(1)}, u32[]{:S(2)}, u32[]{:S(2)}) collective-permute-start(bf16[272,128]{1,0:T(8,128)(2,1)S(1)} %get-tuple-element.15), channel_id=1, source_target_pairs={{0,0},{1,1},{2,2},{3,3},{4,64},{5,65},{6,66},{7,67},{8,128},{9,129... | collective-permute-start | bytes 208904 | tf_op jit(solution)/shard_map/ppermute | solution.py:145
  68.8 4.0 %collective-permute-start.2 = (bf16[272,128]{1,0:T(8,128)(2,1)S(1)}, bf16[272,128]{1,0:T(8,128)(2,1)S(1)}, u32[]{:S(2)}, u32[]{:S(2)}) collective-permute-start(bf16[272,128]{1,0:T(8,128)(2,1)S(1)} %get-tuple-element.14), channel_id=1, source_target_pairs={{0,40},{1,41},{2,42},{3,43},{4,104},{5,105},{6,106},{7,107},{8,168... | collective-permute-start | bytes 208904 | tf_op jit(solution)/shard_map/ppermute | solution.py:145
  72.8 4.7 %collective-permute-start = (bf16[272,128]{1,0:T(8,128)(2,1)S(1)}, bf16[272,128]{1,0:T(8,128)(2,1)S(1)}, u32[]{:S(2)}, u32[]{:S(2)}) collective-permute-start(bf16[272,128]{1,0:T(8,128)(2,1)S(1)} %get-tuple-element.13), channel_id=1, source_target_pairs={{0,8},{1,9},{2,10},{3,11},{4,72},{5,73},{6,74},{7,75},{8,136},{9,1... | collective-permute-start | bytes 208904 | tf_op jit(solution)/shard_map/ppermute | solution.py:145
  77.5 0.0 collective-permute-done.9
  77.5 0.2 copy.21
  77.7 0.0 collective-permute-done.7
  77.7 0.2 copy.20
  77.9 11.4 %collective-permute-done.2 = bf16[272,128]{1,0:T(8,128)(2,1)S(1)} collective-permute-done((bf16[272,128]{1,0:T(8,128)(2,1)S(1)}, bf16[272,128]{1,0:T(8,128)(2,1)S(1)}, u32[]{:S(2)}, u32[]{:S(2)}) %collective-permute-start.2) | collective-permute-done | bytes 69664 | tf_op jit(solution)/shard_map/ppermute | solution.py:145
  89.3 0.2 copy.19
  89.5 1.3 collective-permute-done
  90.8 0.2 copy.18
  91.0 0.6 pad_maximum_fusion
  91.6 0.2 copy.22
  91.8 0.0 all-gather.2.cloned.1.call-done.near_ref
  91.9 2.3 %collective-permute-start.10 = (bf16[1536,512]{1,0:T(8,128)(2,1)}, bf16[1536,512]{1,0:T(8,128)(2,1)}, u32[]{:S(2)}, u32[]{:S(2)}) collective-permute-start(bf16[1536,512]{1,0:T(8,128)(2,1)} %all-gather.2.cloned.1.call-done.near_ref), channel_id=1, source_target_pairs={{0,32},{32,0},{1,33},{33,1},{2,34},{34,2},{3,35},{35,3},{4,36},{36... | collective-permute-start | bytes 4718600 | tf_op jit(solution)/shard_map/ppermute | solution.py:108
  94.2 1.2 broadcast_in_dim.22
  95.4 3.6 %all-to-all-start.1 = ((bf16[4,16,64,128]{3,2,1,0:T(8,128)(2,1)}), bf16[4,16,64,128]{3,2,1,0:T(8,128)(2,1)S(1)}, u32[]{:S(2)}, u32[]{:S(2)}) async-start(bf16[4,16,64,128]{3,2,1,0:T(8,128)(2,1)} %broadcast_in_dim.22), calls=%async_computation.1 | async-start | bytes 2097152 | tf_op jit(solution)/shard_map/all_to_all | solution.py:112
  99.1 0.0 copy-done.2
  99.1 0.0 copy-done.3
  99.1 0.1 pad_add_fusion
  99.2 0.1 reshape.33
  99.3 14.9 %all-to-all-done.1.w_ref = bf16[4,16,64,128]{3,2,1,0:T(8,128)(2,1)S(1)} async-done(((bf16[4,16,64,128]{3,2,1,0:T(8,128)(2,1)}), bf16[4,16,64,128]{3,2,1,0:T(8,128)(2,1)S(1)}, u32[]{:S(2)}, u32[]{:S(2)}) %all-to-all-start.1) | async-done | bytes 1048608 | tf_op jit(solution)/shard_map/all_to_all | solution.py:112
  114.2 0.0 collective-permute-done.10.far_ref
  114.2 5.0 %shard_map.55 = bf16[768,512]{1,0:T(8,128)(2,1)} custom-call(s32[5]{0:T(128)S(1)} %get-tuple-element.17.where_ref, s32[16]{0:T(128)S(1)} %get-tuple-element.12.first_ref, s32[16]{0:T(128)S(1)} %get-tuple-element.11.second_ref, bf16[4,16,64,128]{3,2,1,0:T(8,128)(2,1)S(1)} %all-to-all-done.1.w_ref, bf16[1536,512]{1,0:T(8,128)(2,1)S(1)} %copy-done, ...), custom_call_target="tpu_custom_call" | custom-call | flops 805306368 | bytes 4194304 | tf_op jit(solution)/shard_map/pallas_call | solution.py:86
  119.3 6.3 %all-to-all-start.2 = ((bf16[4,192,512]{2,1,0:T(8,128)(2,1)}), bf16[4,192,512]{2,1,0:T(8,128)(2,1)S(1)}, u32[]{:S(2)}, u32[]{:S(2)}) async-start(bf16[4,192,512]{2,1,0:T(8,128)(2,1)} %bitcast.13), calls=%async_computation.2 | async-start | bytes 1572864 | tf_op jit(solution)/shard_map/all_to_all | solution.py:168
  125.6 5.0 %shard_map.56 = bf16[768,512]{1,0:T(8,128)(2,1)} custom-call(s32[5]{0:T(128)S(1)} %get-tuple-element.18.where_ref, s32[16]{0:T(128)S(1)} %get-tuple-element.12.first_ref, s32[16]{0:T(128)S(1)} %get-tuple-element.11.second_ref, bf16[4,16,64,128]{3,2,1,0:T(8,128)(2,1)S(1)} %all-to-all-done.1.w_ref, bf16[1536,512]{1,0:T(8,128)(2,1)S(1)} %copy-done, ...), custom_call_target="tpu_custom_call" | custom-call | flops 805306368 | bytes 4194304 | tf_op jit(solution)/shard_map/pallas_call | solution.py:86
  130.6 3.5 %all-to-all-done.2 = bf16[4,192,512]{2,1,0:T(8,128)(2,1)S(1)} async-done(((bf16[4,192,512]{2,1,0:T(8,128)(2,1)}), bf16[4,192,512]{2,1,0:T(8,128)(2,1)S(1)}, u32[]{:S(2)}, u32[]{:S(2)}) %all-to-all-start.2) | async-done | bytes 786464 | tf_op jit(solution)/shard_map/all_to_all | solution.py:168
  134.1 6.1 %all-to-all-start.3 = ((bf16[4,192,512]{2,1,0:T(8,128)(2,1)}), bf16[4,192,512]{2,1,0:T(8,128)(2,1)S(1)}, u32[]{:S(2)}, u32[]{:S(2)}) async-start(bf16[4,192,512]{2,1,0:T(8,128)(2,1)} %bitcast.15), calls=%async_computation.3 | async-start | bytes 1572864 | tf_op jit(solution)/shard_map/all_to_all | solution.py:168
  140.2 0.1 reduce_sum.24
  140.4 4.6 %collective-permute-start.11 = (bf16[192,512]{1,0:T(8,128)(2,1)S(1)}, bf16[192,512]{1,0:T(8,128)(2,1)S(1)}, u32[]{:S(2)}, u32[]{:S(2)}) collective-permute-start(bf16[192,512]{1,0:T(8,128)(2,1)S(1)} %reduce_sum.24), channel_id=1, source_target_pairs={{0,256},{1,257},{2,258},{3,259},{4,320},{5,321},{6,322},{7,323},{8... | collective-permute-start | bytes 589832 | tf_op jit(solution)/shard_map/ppermute | solution.py:170
  145.0 4.6 %all-to-all-done.3 = bf16[4,192,512]{2,1,0:T(8,128)(2,1)S(1)} async-done(((bf16[4,192,512]{2,1,0:T(8,128)(2,1)}), bf16[4,192,512]{2,1,0:T(8,128)(2,1)S(1)}, u32[]{:S(2)}, u32[]{:S(2)}) %all-to-all-start.3) | async-done | bytes 786464 | tf_op jit(solution)/shard_map/all_to_all | solution.py:168
  149.6 0.1 reduce_sum.25
  149.8 1.9 %collective-permute-start.12 = (bf16[192,512]{1,0:T(8,128)(2,1)S(1)}, bf16[192,512]{1,0:T(8,128)(2,1)S(1)}, u32[]{:S(2)}, u32[]{:S(2)}) collective-permute-start(bf16[192,512]{1,0:T(8,128)(2,1)S(1)} %reduce_sum.25), channel_id=1, source_target_pairs={{0,284},{1,285},{2,286},{3,287},{4,348},{5,349},{6,350},{7,351},{8... | collective-permute-start | bytes 589832 | tf_op jit(solution)/shard_map/ppermute | solution.py:170
  151.7 7.3 %collective-permute-done.11 = bf16[192,512]{1,0:T(8,128)(2,1)S(1)} collective-permute-done((bf16[192,512]{1,0:T(8,128)(2,1)S(1)}, bf16[192,512]{1,0:T(8,128)(2,1)S(1)}, u32[]{:S(2)}, u32[]{:S(2)}) %collective-permute-start.11) | collective-permute-done | bytes 196640 | tf_op jit(solution)/shard_map/ppermute | solution.py:170
  159.0 19.4 %collective-permute-done.12 = bf16[192,512]{1,0:T(8,128)(2,1)S(1)} collective-permute-done((bf16[192,512]{1,0:T(8,128)(2,1)S(1)}, bf16[192,512]{1,0:T(8,128)(2,1)S(1)}, u32[]{:S(2)}, u32[]{:S(2)}) %collective-permute-start.12) | collective-permute-done | bytes 196640 | tf_op jit(solution)/shard_map/ppermute | solution.py:170
  178.4 0.1 add_convert_fusion
  178.4 0.7 reshape.32
  (16 shorter events, 0.2 us)
Async XLA Ops:
  6.5 85.3 %all-gather.2.cloned.1.call-start = ((), (), s32[]{:S(2)}) async-start(), calls=%async_computation.4 | async-start | bytes 1769472 | tf_op jit(solution)/shard_map/all_gather | solution.py:116
  8.2 46.8 %collective-permute-start.1 = (bf16[128,2048]{1,0:T(8,128)(2,1)}, bf16[128,2048]{1,0:T(8,128)(2,1)S(1)}, u32[]{:S(2)}, u32[]{:S(2)}) collective-permute-start(bf16[128,2048]{1,0:T(8,128)(2,1)} %param.7), channel_id=1, source_target_pairs={{0,32},{32,0},{1,33},{33,1},{2,34},{34,2},{3,35},{35,3},{4,36},{36... | collective-permute-start | bytes 1572872 | tf_op jit(solution)/shard_map/ppermute | solution.py:108
  11.7 23.4 %collective-permute-start.3 = (bf16[32,2048]{1,0:T(8,128)(2,1)S(1)}, bf16[32,2048]{1,0:T(8,128)(2,1)S(1)}, u32[]{:S(2)}, u32[]{:S(2)}) collective-permute-start(bf16[32,2048]{1,0:T(8,128)(2,1)S(1)} %constant_dynamic-slice_fusion), channel_id=1, source_target_pairs={{0,284},{4,280},{8,276},{12,272},{16,268},{20,264},{24,260},{28,25... | collective-permute-start | bytes 393224 | tf_op jit(solution)/shard_map/ppermute | solution.py:123
  25.6 28.5 %all-to-all-start = ((bf16[4,64,2176]{2,1,0:T(8,128)(2,1)}), bf16[4,64,2176]{2,1,0:T(8,128)(2,1)S(1)}, u32[]{:S(2)}, u32[]{:S(2)}) async-start(bf16[4,64,2176]{2,1,0:T(8,128)(2,1)} %broadcast_in_dim.9), calls=%async_computation | async-start | bytes 2228224 | tf_op jit(solution)/shard_map/all_to_all | solution.py:112
  35.2 15.7 %collective-permute-start.6 = (bf16[32,2048]{1,0:T(8,128)(2,1)S(1)}, bf16[32,2048]{1,0:T(8,128)(2,1)S(1)}, u32[]{:S(2)}, u32[]{:S(2)}) collective-permute-start(bf16[32,2048]{1,0:T(8,128)(2,1)S(1)} %collective-permute-done.3), channel_id=1, source_target_pairs={{0,3},{1,0},{2,1},{3,2},{4,7},{5,4},{6,5},{7,6},{8,11},{9,8},{10,9... | collective-permute-start | bytes 393224 | tf_op jit(solution)/shard_map/ppermute | solution.py:134
  39.8 11.0 %collective-permute-start.5 = (bf16[32,2048]{1,0:T(8,128)(2,1)S(1)}, bf16[32,2048]{1,0:T(8,128)(2,1)S(1)}, u32[]{:S(2)}, u32[]{:S(2)}) collective-permute-start(bf16[32,2048]{1,0:T(8,128)(2,1)S(1)} %collective-permute-done.3), channel_id=1, source_target_pairs={{0,2},{1,3},{2,0},{3,1},{4,6},{5,7},{6,4},{7,5},{8,10},{9,11},{10,... | collective-permute-start | bytes 393224 | tf_op jit(solution)/shard_map/ppermute | solution.py:134
  42.1 8.7 %collective-permute-start.4 = (bf16[32,2048]{1,0:T(8,128)(2,1)S(1)}, bf16[32,2048]{1,0:T(8,128)(2,1)S(1)}, u32[]{:S(2)}, u32[]{:S(2)}) collective-permute-start(bf16[32,2048]{1,0:T(8,128)(2,1)S(1)} %collective-permute-done.3), channel_id=1, source_target_pairs={{0,1},{1,2},{2,3},{3,0},{4,5},{5,6},{6,7},{7,4},{8,9},{9,10},{10,1... | collective-permute-start | bytes 393224 | tf_op jit(solution)/shard_map/ppermute | solution.py:134
  50.8 3.8 %copy-start.1 = (bf16[128,2048]{1,0:T(8,128)(2,1)S(1)}, bf16[128,2048]{1,0:T(8,128)(2,1)}, u32[]{:S(2)}) copy-start(bf16[128,2048]{1,0:T(8,128)(2,1)} %param.7) | copy-start | bytes 1572868
  50.8 4.8 %collective-permute-start.8 = (bf16[128,2048]{1,0:T(8,128)(2,1)S(1)}, bf16[128,2048]{1,0:T(8,128)(2,1)S(1)}, u32[]{:S(2)}, u32[]{:S(2)}) collective-permute-start(bf16[128,2048]{1,0:T(8,128)(2,1)S(1)} %constant_dynamic-update-slice_fusion), channel_id=1, source_target_pairs={{0,32},{32,0},{1,33},{33,1},{2,34},{34,2},{3,35},{35,3},{4,36},{36... | collective-permute-start | bytes 1572872 | tf_op jit(solution)/shard_map/ppermute | solution.py:108
  56.1 21.4 %collective-permute-start.9 = (bf16[272,128]{1,0:T(8,128)(2,1)S(1)}, bf16[272,128]{1,0:T(8,128)(2,1)S(1)}, u32[]{:S(2)}, u32[]{:S(2)}) collective-permute-start(bf16[272,128]{1,0:T(8,128)(2,1)S(1)} %get-tuple-element.16), channel_id=1, source_target_pairs={{0,32},{1,33},{2,34},{3,35},{4,96},{5,97},{6,98},{7,99},{8,160},{9... | collective-permute-start | bytes 208904 | tf_op jit(solution)/shard_map/ppermute | solution.py:145
  60.4 17.3 %collective-permute-start.7 = (bf16[272,128]{1,0:T(8,128)(2,1)S(1)}, bf16[272,128]{1,0:T(8,128)(2,1)S(1)}, u32[]{:S(2)}, u32[]{:S(2)}) collective-permute-start(bf16[272,128]{1,0:T(8,128)(2,1)S(1)} %get-tuple-element.15), channel_id=1, source_target_pairs={{0,0},{1,1},{2,2},{3,3},{4,64},{5,65},{6,66},{7,67},{8,128},{9,129... | collective-permute-start | bytes 208904 | tf_op jit(solution)/shard_map/ppermute | solution.py:145
  68.8 20.5 %collective-permute-start.2 = (bf16[272,128]{1,0:T(8,128)(2,1)S(1)}, bf16[272,128]{1,0:T(8,128)(2,1)S(1)}, u32[]{:S(2)}, u32[]{:S(2)}) collective-permute-start(bf16[272,128]{1,0:T(8,128)(2,1)S(1)} %get-tuple-element.14), channel_id=1, source_target_pairs={{0,40},{1,41},{2,42},{3,43},{4,104},{5,105},{6,106},{7,107},{8,168... | collective-permute-start | bytes 208904 | tf_op jit(solution)/shard_map/ppermute | solution.py:145
  72.8 18.0 %collective-permute-start = (bf16[272,128]{1,0:T(8,128)(2,1)S(1)}, bf16[272,128]{1,0:T(8,128)(2,1)S(1)}, u32[]{:S(2)}, u32[]{:S(2)}) collective-permute-start(bf16[272,128]{1,0:T(8,128)(2,1)S(1)} %get-tuple-element.13), channel_id=1, source_target_pairs={{0,8},{1,9},{2,10},{3,11},{4,72},{5,73},{6,74},{7,75},{8,136},{9,1... | collective-permute-start | bytes 208904 | tf_op jit(solution)/shard_map/ppermute | solution.py:145
  91.9 22.4 %collective-permute-start.10 = (bf16[1536,512]{1,0:T(8,128)(2,1)}, bf16[1536,512]{1,0:T(8,128)(2,1)}, u32[]{:S(2)}, u32[]{:S(2)}) collective-permute-start(bf16[1536,512]{1,0:T(8,128)(2,1)} %all-gather.2.cloned.1.call-done.near_ref), channel_id=1, source_target_pairs={{0,32},{32,0},{1,33},{33,1},{2,34},{34,2},{3,35},{35,3},{4,36},{36... | collective-permute-start | bytes 4718600 | tf_op jit(solution)/shard_map/ppermute | solution.py:108
  95.4 3.7 %copy-start.2 = (s32[1,4]{1,0:T(1,128)S(1)}, s32[1,4]{1,0:T(1,128)}, u32[]{:S(2)}) copy-start(s32[1,4]{1,0:T(1,128)} %constant.70) | copy-start | bytes 52
  95.4 3.7 %copy-start.3 = (s32[1,4]{1,0:T(1,128)S(1)}, s32[1,4]{1,0:T(1,128)}, u32[]{:S(2)}) copy-start(s32[1,4]{1,0:T(1,128)} %constant.69) | copy-start | bytes 52
  95.4 18.8 %copy-start = (bf16[1536,512]{1,0:T(8,128)(2,1)S(1)}, bf16[1536,512]{1,0:T(8,128)(2,1)}, u32[]{:S(2)}) copy-start(bf16[1536,512]{1,0:T(8,128)(2,1)} %all-gather.2.cloned.1.call-done.near_ref) | copy-start | bytes 4718596
  95.4 18.8 %all-to-all-start.1 = ((bf16[4,16,64,128]{3,2,1,0:T(8,128)(2,1)}), bf16[4,16,64,128]{3,2,1,0:T(8,128)(2,1)S(1)}, u32[]{:S(2)}, u32[]{:S(2)}) async-start(bf16[4,16,64,128]{3,2,1,0:T(8,128)(2,1)} %broadcast_in_dim.22), calls=%async_computation.1 | async-start | bytes 2097152 | tf_op jit(solution)/shard_map/all_to_all | solution.py:112
  119.3 14.9 %all-to-all-start.2 = ((bf16[4,192,512]{2,1,0:T(8,128)(2,1)}), bf16[4,192,512]{2,1,0:T(8,128)(2,1)S(1)}, u32[]{:S(2)}, u32[]{:S(2)}) async-start(bf16[4,192,512]{2,1,0:T(8,128)(2,1)} %bitcast.13), calls=%async_computation.2 | async-start | bytes 1572864 | tf_op jit(solution)/shard_map/all_to_all | solution.py:168
  134.1 15.5 %all-to-all-start.3 = ((bf16[4,192,512]{2,1,0:T(8,128)(2,1)}), bf16[4,192,512]{2,1,0:T(8,128)(2,1)S(1)}, u32[]{:S(2)}, u32[]{:S(2)}) async-start(bf16[4,192,512]{2,1,0:T(8,128)(2,1)} %bitcast.15), calls=%async_computation.3 | async-start | bytes 1572864 | tf_op jit(solution)/shard_map/all_to_all | solution.py:168
  140.4 18.7 %collective-permute-start.11 = (bf16[192,512]{1,0:T(8,128)(2,1)S(1)}, bf16[192,512]{1,0:T(8,128)(2,1)S(1)}, u32[]{:S(2)}, u32[]{:S(2)}) collective-permute-start(bf16[192,512]{1,0:T(8,128)(2,1)S(1)} %reduce_sum.24), channel_id=1, source_target_pairs={{0,256},{1,257},{2,258},{3,259},{4,320},{5,321},{6,322},{7,323},{8... | collective-permute-start | bytes 589832 | tf_op jit(solution)/shard_map/ppermute | solution.py:170
  149.8 28.6 %collective-permute-start.12 = (bf16[192,512]{1,0:T(8,128)(2,1)S(1)}, bf16[192,512]{1,0:T(8,128)(2,1)S(1)}, u32[]{:S(2)}, u32[]{:S(2)}) collective-permute-start(bf16[192,512]{1,0:T(8,128)(2,1)S(1)} %reduce_sum.25), channel_id=1, source_target_pairs={{0,284},{1,285},{2,286},{3,287},{4,348},{5,349},{6,350},{7,351},{8... | collective-permute-start | bytes 589832 | tf_op jit(solution)/shard_map/ppermute | solution.py:170
Sparse Core Ops, SparseCore 0:
  9.4 55.7 all-gather.1

commit v14 on v12

--- a/solution.py
+++ b/solution.py
@@ -142,11 +142,11 @@
 
     near = [weights(coefficients), weights(c_other)]
     far = [weights(c_far), weights(swap_core(c_far))]
-    w = [
-        lax.ppermute(jnp.concatenate([v, info], axis=0), AXES, weight_perm(k, d))
-        for k, pieces in enumerate((near, far))
-        for d, v in enumerate(pieces)
-    ]
+    w = []
+    for k, pieces in enumerate((near, far)):
+        v = jnp.stack([jnp.concatenate([v, info], axis=0) for v in pieces])
+        v = lax.ppermute(v, AXES, weight_perm(k, 0))
+        w += [v[0], swap_core(v[1])]
     w = jnp.stack(w)
     slots, n_b = H * C * X, X * rows
     pairs = w[:, n_b : n_b + X, :2].reshape(slots, 2).astype(jnp.int32)

time: 185 us -> 200 us (1.081)
  the two profiles are of different devices: /device:TPU:199 before, /device:TPU:5 now
where the time goes in v14:
time: 200 us
  starting transfers between devices  83.9 us (42%)
  waiting for transfers between devices  78.3 us (39%)
  between operations  13.8 us (7%)
  Pallas kernels  10.1 us (5%)
  local copies, waits for them, and re-layouts  8.08 us (4%)
  other arithmetic  3.66 us (2%)
    ppermute x2, waiting for transfers between devices, on_device(): v = lax.ppermute(v, AXES, weight_perm(k, 0))  27.5 us
    ppermute x2, waiting for transfers between devices, on_device(): total += lax.ppermute(v, AXES, result_perm(k)).astype(f32)  22.4 us
    ppermute x2, starting transfers between devices, on_device(): total += lax.ppermute(v, AXES, result_perm(k)).astype(f32)  16.5 us
    all_to_all x2, starting transfers between devices, on_device(): v = lax.all_to_all(v, 'x', split_axis=0, concat_axis=0, tiled=True)  16 us
    all_to_all x2, waiting for transfers between devices, gather(): return lax.all_to_all(v, axes, split_axis=0, concat_axis=0, tiled=True)  14.5 us
    ppermute x5, starting transfers between devices, swap_core(): return lax.ppermute(v, 'c', shift(C, 1))  12.5 us
    ppermute x1, starting transfers between devices, on_device(): piece = lax.ppermute(piece, ('h', 'l'), mirror)  11.1 us
    ppermute x2, starting transfers between devices, on_device(): v = lax.ppermute(v, AXES, weight_perm(k, 0))  10.4 us
  transfers between devices with their start and end apart: 18, of which 9 were waited for; matrix products, arithmetic and copies ran while one was open for 6% of the time, Pallas kernels for 3%

profile of v14, /device:TPU:5, one launch (start us, length us, event | category | flops | bytes accessed | tf_op | source)
XLA Modules:
  0.0 199.6 jit_solution(17276277537459338206)
XLA Ops:
  6.5 2.6 %collective-permute-start = (bf16[128,2048]{1,0:T(8,128)(2,1)}, bf16[128,2048]{1,0:T(8,128)(2,1)S(1)}, u32[]{:S(2)}, u32[]{:S(2)}) collective-permute-start(bf16[128,2048]{1,0:T(8,128)(2,1)} %param.7), channel_id=1, source_target_pairs={{0,32},{32,0},{1,33},{33,1},{2,34},{34,2},{3,35},{35,3},{4,36},{36... | collective-permute-start | bytes 1572872 | tf_op jit(solution)/shard_map/ppermute | solution.py:109
  9.1 0.9 constant_dynamic-slice_fusion
  10.0 11.1 %collective-permute-start.3 = (bf16[32,2048]{1,0:T(8,128)(2,1)S(1)}, bf16[32,2048]{1,0:T(8,128)(2,1)S(1)}, u32[]{:S(2)}, u32[]{:S(2)}) collective-permute-start(bf16[32,2048]{1,0:T(8,128)(2,1)S(1)} %constant_dynamic-slice_fusion), channel_id=1, source_target_pairs={{0,284},{4,280},{8,276},{12,272},{16,268},{20,264},{24,260},{28,25... | collective-permute-start | bytes 393224 | tf_op jit(solution)/shard_map/ppermute | solution.py:124
  21.2 1.6 copy.43
  22.8 0.0 all-gather.2.cloned.1.call-update
  22.8 0.7 convert_element_type.38
  23.5 1.0 fusion.5
  24.5 1.1 broadcast_in_dim.9
  25.6 4.2 %all-to-all-start = ((bf16[4,64,2176]{2,1,0:T(8,128)(2,1)}), bf16[4,64,2176]{2,1,0:T(8,128)(2,1)S(1)}, u32[]{:S(2)}, u32[]{:S(2)}) async-start(bf16[4,64,2176]{2,1,0:T(8,128)(2,1)} %broadcast_in_dim.9), calls=%async_computation | async-start | bytes 2228224 | tf_op jit(solution)/shard_map/all_to_all | solution.py:113
  29.8 3.6 %collective-permute-done.3 = bf16[32,2048]{1,0:T(8,128)(2,1)S(1)} collective-permute-done((bf16[32,2048]{1,0:T(8,128)(2,1)S(1)}, bf16[32,2048]{1,0:T(8,128)(2,1)S(1)}, u32[]{:S(2)}, u32[]{:S(2)}) %collective-permute-start.3) | collective-permute-done | bytes 131104 | tf_op jit(solution)/shard_map/ppermute | solution.py:124
  33.4 4.6 %collective-permute-start.6 = (bf16[32,2048]{1,0:T(8,128)(2,1)S(1)}, bf16[32,2048]{1,0:T(8,128)(2,1)S(1)}, u32[]{:S(2)}, u32[]{:S(2)}) collective-permute-start(bf16[32,2048]{1,0:T(8,128)(2,1)S(1)} %collective-permute-done.3), channel_id=1, source_target_pairs={{0,3},{1,0},{2,1},{3,2},{4,7},{5,4},{6,5},{7,6},{8,11},{9,8},{10,9... | collective-permute-start | bytes 393224 | tf_op jit(solution)/shard_map/ppermute | solution.py:135
  38.1 2.3 %collective-permute-start.5 = (bf16[32,2048]{1,0:T(8,128)(2,1)S(1)}, bf16[32,2048]{1,0:T(8,128)(2,1)S(1)}, u32[]{:S(2)}, u32[]{:S(2)}) collective-permute-start(bf16[32,2048]{1,0:T(8,128)(2,1)S(1)} %collective-permute-done.3), channel_id=1, source_target_pairs={{0,2},{1,3},{2,0},{3,1},{4,6},{5,7},{6,4},{7,5},{8,10},{9,11},{10,... | collective-permute-start | bytes 393224 | tf_op jit(solution)/shard_map/ppermute | solution.py:135
  40.4 2.6 %collective-permute-start.4 = (bf16[32,2048]{1,0:T(8,128)(2,1)S(1)}, bf16[32,2048]{1,0:T(8,128)(2,1)S(1)}, u32[]{:S(2)}, u32[]{:S(2)}) collective-permute-start(bf16[32,2048]{1,0:T(8,128)(2,1)S(1)} %collective-permute-done.3), channel_id=1, source_target_pairs={{0,1},{1,2},{2,3},{3,0},{4,5},{5,6},{6,7},{7,4},{8,9},{9,10},{10,1... | collective-permute-start | bytes 393224 | tf_op jit(solution)/shard_map/ppermute | solution.py:135
  43.0 5.9 %collective-permute-done.4 = bf16[32,2048]{1,0:T(8,128)(2,1)S(1)} collective-permute-done((bf16[32,2048]{1,0:T(8,128)(2,1)S(1)}, bf16[32,2048]{1,0:T(8,128)(2,1)S(1)}, u32[]{:S(2)}, u32[]{:S(2)}) %collective-permute-start.4) | collective-permute-done | bytes 131104 | tf_op jit(solution)/shard_map/ppermute | solution.py:135
  49.0 0.0 copy-start.1
  49.1 3.3 %collective-permute-start.7 = (bf16[128,2048]{1,0:T(8,128)(2,1)S(1)}, bf16[128,2048]{1,0:T(8,128)(2,1)S(1)}, u32[]{:S(2)}, u32[]{:S(2)}) collective-permute-start(bf16[128,2048]{1,0:T(8,128)(2,1)S(1)} %constant_dynamic-update-slice_fusion), channel_id=1, source_target_pairs={{0,32},{32,0},{1,33},{33,1},{2,34},{34,2},{3,35},{35,3},{4,36},{36... | collective-permute-start | bytes 1572872 | tf_op jit(solution)/shard_map/ppermute | solution.py:109
  52.4 0.0 all-to-all-done
  52.4 0.4 convolution_convert_fusion.1
  52.9 0.4 convolution_convert_fusion.3
  53.3 0.0 collective-permute-done
  53.3 0.4 convolution_convert_fusion.2
  53.8 0.1 collective-permute-done.7
  53.9 0.4 convolution_convert_fusion
  54.4 0.2 copy.33
  54.6 0.2 copy.34
  54.8 0.5 pad_maximum_fusion.4
  55.3 1.9 collective-permute-start.8
  57.2 0.2 copy.30
  57.4 0.2 copy.31
  57.6 0.5 pad_maximum_fusion.3
  58.1 8.5 %collective-permute-start.1 = (bf16[2,272,128]{1,0,2:T(2,128)(2,1)S(1)}, bf16[2,272,128]{1,0,2:T(2,128)(2,1)S(1)}, u32[]{:S(2)}, u32[]{:S(2)}) collective-permute-start(bf16[2,272,128]{1,0,2:T(2,128)(2,1)S(1)} %pad_maximum_fusion.3), channel_id=1, source_target_pairs={{0,8},{1,9},{2,10},{3,11},{4,72},{5,73},{6,74},{7,75},{8,136},{9,1... | collective-permute-start | bytes 417800 | tf_op jit(solution)/shard_map/ppermute | solution.py:148
  66.6 27.5 %collective-permute-done.8 = bf16[2,272,128]{1,0,2:T(2,128)(2,1)S(1)} collective-permute-done((bf16[2,272,128]{1,0,2:T(2,128)(2,1)S(1)}, bf16[2,272,128]{1,0,2:T(2,128)(2,1)S(1)}, u32[]{:S(2)}, u32[]{:S(2)}) %collective-permute-start.8) | collective-permute-done | bytes 139296 | tf_op jit(solution)/shard_map/ppermute | solution.py:148
  94.1 0.3 fusion.18
  94.4 0.2 copy.35
  94.5 2.6 %collective-permute-start.9 = (bf16[272,128]{1,0:T(8,128)(2,1)S(1)}, bf16[272,128]{1,0:T(8,128)(2,1)S(1)}, u32[]{:S(2)}, u32[]{:S(2)}) collective-permute-start(bf16[272,128]{1,0:T(8,128)(2,1)S(1)} %bitcast.49), channel_id=1, source_target_pairs={{0,32},{32,0},{1,33},{33,1},{2,34},{34,2},{3,35},{35,3},{4,36},{36... | collective-permute-start | bytes 208904 | tf_op jit(solution)/shard_map/ppermute | solution.py:109
  97.2 0.0 collective-permute-done.1
  97.2 0.3 fusion.17
  97.4 0.2 copy.32
  97.6 1.9 collective-permute-start.2
  99.6 0.2 copy.37
  99.8 1.0 collective-permute-done.2
  100.8 0.2 copy.36
  101.0 0.6 pad_maximum_fusion
  101.6 0.2 copy.38
  101.8 0.0 all-gather.2.cloned.1.call-done.near_ref
  101.9 2.1 %collective-permute-start.10 = (bf16[1536,512]{1,0:T(8,128)(2,1)}, bf16[1536,512]{1,0:T(8,128)(2,1)}, u32[]{:S(2)}, u32[]{:S(2)}) collective-permute-start(bf16[1536,512]{1,0:T(8,128)(2,1)} %all-gather.2.cloned.1.call-done.near_ref), channel_id=1, source_target_pairs={{0,32},{32,0},{1,33},{33,1},{2,34},{34,2},{3,35},{35,3},{4,36},{36... | collective-permute-start | bytes 4718600 | tf_op jit(solution)/shard_map/ppermute | solution.py:109
  103.9 1.2 broadcast_in_dim.22
  105.2 3.6 %all-to-all-start.1 = ((bf16[4,16,64,128]{3,2,1,0:T(8,128)(2,1)}), bf16[4,16,64,128]{3,2,1,0:T(8,128)(2,1)S(1)}, u32[]{:S(2)}, u32[]{:S(2)}) async-start(bf16[4,16,64,128]{3,2,1,0:T(8,128)(2,1)} %broadcast_in_dim.22), calls=%async_computation.1 | async-start | bytes 2097152 | tf_op jit(solution)/shard_map/all_to_all | solution.py:113
  108.8 0.1 pad_add_fusion
  108.9 0.1 reshape.33
  109.0 14.5 %all-to-all-done.1.w_ref = bf16[4,16,64,128]{3,2,1,0:T(8,128)(2,1)S(1)} async-done(((bf16[4,16,64,128]{3,2,1,0:T(8,128)(2,1)}), bf16[4,16,64,128]{3,2,1,0:T(8,128)(2,1)S(1)}, u32[]{:S(2)}, u32[]{:S(2)}) %all-to-all-start.1) | async-done | bytes 1048608 | tf_op jit(solution)/shard_map/all_to_all | solution.py:113
  123.5 5.0 %shard_map.55 = bf16[768,512]{1,0:T(8,128)(2,1)} custom-call(s32[5]{0:T(128)S(1)} %get-tuple-element.21.where_ref, s32[16]{0:T(128)S(1)} %get-tuple-element.16.first_ref, s32[16]{0:T(128)S(1)} %get-tuple-element.15.second_ref, bf16[4,16,64,128]{3,2,1,0:T(8,128)(2,1)S(1)} %all-to-all-done.1.w_ref, bf16[1536,512]{1,0:T(8,128)(2,1)S(1)} %copy-done, ...), custom_call_target="tpu_custom_call" | custom-call | flops 805306368 | bytes 4194304 | tf_op jit(solution)/shard_map/pallas_call | solution.py:87
  128.6 9.8 %all-to-all-start.2 = ((bf16[4,192,512]{2,1,0:T(8,128)(2,1)}), bf16[4,192,512]{2,1,0:T(8,128)(2,1)S(1)}, u32[]{:S(2)}, u32[]{:S(2)}) async-start(bf16[4,192,512]{2,1,0:T(8,128)(2,1)} %bitcast.17), calls=%async_computation.2 | async-start | bytes 1572864 | tf_op jit(solution)/shard_map/all_to_all | solution.py:169
  138.4 5.0 %shard_map.56 = bf16[768,512]{1,0:T(8,128)(2,1)} custom-call(s32[5]{0:T(128)S(1)} %get-tuple-element.22.where_ref, s32[16]{0:T(128)S(1)} %get-tuple-element.16.first_ref, s32[16]{0:T(128)S(1)} %get-tuple-element.15.second_ref, bf16[4,16,64,128]{3,2,1,0:T(8,128)(2,1)S(1)} %all-to-all-done.1.w_ref, bf16[1536,512]{1,0:T(8,128)(2,1)S(1)} %copy-done, ...), custom_call_target="tpu_custom_call" | custom-call | flops 805306368 | bytes 4194304 | tf_op jit(solution)/shard_map/pallas_call | solution.py:87
  143.4 3.1 %all-to-all-done.2 = bf16[4,192,512]{2,1,0:T(8,128)(2,1)S(1)} async-done(((bf16[4,192,512]{2,1,0:T(8,128)(2,1)}), bf16[4,192,512]{2,1,0:T(8,128)(2,1)S(1)}, u32[]{:S(2)}, u32[]{:S(2)}) %all-to-all-start.2) | async-done | bytes 786464 | tf_op jit(solution)/shard_map/all_to_all | solution.py:169
  146.5 6.2 %all-to-all-start.3 = ((bf16[4,192,512]{2,1,0:T(8,128)(2,1)}), bf16[4,192,512]{2,1,0:T(8,128)(2,1)S(1)}, u32[]{:S(2)}, u32[]{:S(2)}) async-start(bf16[4,192,512]{2,1,0:T(8,128)(2,1)} %bitcast.19), calls=%async_computation.3 | async-start | bytes 1572864 | tf_op jit(solution)/shard_map/all_to_all | solution.py:169
  152.7 0.1 reduce_sum.24
  152.8 7.5 %collective-permute-start.11 = (bf16[192,512]{1,0:T(8,128)(2,1)S(1)}, bf16[192,512]{1,0:T(8,128)(2,1)S(1)}, u32[]{:S(2)}, u32[]{:S(2)}) collective-permute-start(bf16[192,512]{1,0:T(8,128)(2,1)S(1)} %reduce_sum.24), channel_id=1, source_target_pairs={{0,448},{1,449},{2,450},{3,451},{4,384},{5,385},{6,386},{7,387},{8... | collective-permute-start | bytes 589832 | tf_op jit(solution)/shard_map/ppermute | solution.py:171
  160.3 0.1 reduce_sum.25
  160.5 9.0 %collective-permute-start.12 = (bf16[192,512]{1,0:T(8,128)(2,1)S(1)}, bf16[192,512]{1,0:T(8,128)(2,1)S(1)}, u32[]{:S(2)}, u32[]{:S(2)}) collective-permute-start(bf16[192,512]{1,0:T(8,128)(2,1)S(1)} %reduce_sum.25), channel_id=1, source_target_pairs={{0,476},{1,477},{2,478},{3,479},{4,412},{5,413},{6,414},{7,415},{8... | collective-permute-start | bytes 589832 | tf_op jit(solution)/shard_map/ppermute | solution.py:171
  169.5 1.7 collective-permute-done.11
  171.2 20.7 %collective-permute-done.12 = bf16[192,512]{1,0:T(8,128)(2,1)S(1)} collective-permute-done((bf16[192,512]{1,0:T(8,128)(2,1)S(1)}, bf16[192,512]{1,0:T(8,128)(2,1)S(1)}, u32[]{:S(2)}, u32[]{:S(2)}) %collective-permute-start.12) | collective-permute-done | bytes 196640 | tf_op jit(solution)/shard_map/ppermute | solution.py:171
  191.9 0.1 add_convert_fusion
  192.0 0.7 reshape.32
  (24 shorter events, 0.2 us)
Async XLA Ops:
  6.5 95.3 %all-gather.2.cloned.1.call-start = ((), (), s32[]{:S(2)}) async-start(), calls=%async_computation.4 | async-start | bytes 1769472 | tf_op jit(solution)/shard_map/all_gather | solution.py:117
  6.5 46.8 %collective-permute-start = (bf16[128,2048]{1,0:T(8,128)(2,1)}, bf16[128,2048]{1,0:T(8,128)(2,1)S(1)}, u32[]{:S(2)}, u32[]{:S(2)}) collective-permute-start(bf16[128,2048]{1,0:T(8,128)(2,1)} %param.7), channel_id=1, source_target_pairs={{0,32},{32,0},{1,33},{33,1},{2,34},{34,2},{3,35},{35,3},{4,36},{36... | collective-permute-start | bytes 1572872 | tf_op jit(solution)/shard_map/ppermute | solution.py:109
  10.0 23.4 %collective-permute-start.3 = (bf16[32,2048]{1,0:T(8,128)(2,1)S(1)}, bf16[32,2048]{1,0:T(8,128)(2,1)S(1)}, u32[]{:S(2)}, u32[]{:S(2)}) collective-permute-start(bf16[32,2048]{1,0:T(8,128)(2,1)S(1)} %constant_dynamic-slice_fusion), channel_id=1, source_target_pairs={{0,284},{4,280},{8,276},{12,272},{16,268},{20,264},{24,260},{28,25... | collective-permute-start | bytes 393224 | tf_op jit(solution)/shard_map/ppermute | solution.py:124
  25.6 26.8 %all-to-all-start = ((bf16[4,64,2176]{2,1,0:T(8,128)(2,1)}), bf16[4,64,2176]{2,1,0:T(8,128)(2,1)S(1)}, u32[]{:S(2)}, u32[]{:S(2)}) async-start(bf16[4,64,2176]{2,1,0:T(8,128)(2,1)} %broadcast_in_dim.9), calls=%async_computation | async-start | bytes 2228224 | tf_op jit(solution)/shard_map/all_to_all | solution.py:113
  33.4 15.6 %collective-permute-start.6 = (bf16[32,2048]{1,0:T(8,128)(2,1)S(1)}, bf16[32,2048]{1,0:T(8,128)(2,1)S(1)}, u32[]{:S(2)}, u32[]{:S(2)}) collective-permute-start(bf16[32,2048]{1,0:T(8,128)(2,1)S(1)} %collective-permute-done.3), channel_id=1, source_target_pairs={{0,3},{1,0},{2,1},{3,2},{4,7},{5,4},{6,5},{7,6},{8,11},{9,8},{10,9... | collective-permute-start | bytes 393224 | tf_op jit(solution)/shard_map/ppermute | solution.py:135
  38.1 10.9 %collective-permute-start.5 = (bf16[32,2048]{1,0:T(8,128)(2,1)S(1)}, bf16[32,2048]{1,0:T(8,128)(2,1)S(1)}, u32[]{:S(2)}, u32[]{:S(2)}) collective-permute-start(bf16[32,2048]{1,0:T(8,128)(2,1)S(1)} %collective-permute-done.3), channel_id=1, source_target_pairs={{0,2},{1,3},{2,0},{3,1},{4,6},{5,7},{6,4},{7,5},{8,10},{9,11},{10,... | collective-permute-start | bytes 393224 | tf_op jit(solution)/shard_map/ppermute | solution.py:135
  40.4 8.6 %collective-permute-start.4 = (bf16[32,2048]{1,0:T(8,128)(2,1)S(1)}, bf16[32,2048]{1,0:T(8,128)(2,1)S(1)}, u32[]{:S(2)}, u32[]{:S(2)}) collective-permute-start(bf16[32,2048]{1,0:T(8,128)(2,1)S(1)} %collective-permute-done.3), channel_id=1, source_target_pairs={{0,1},{1,2},{2,3},{3,0},{4,5},{5,6},{6,7},{7,4},{8,9},{9,10},{10,1... | collective-permute-start | bytes 393224 | tf_op jit(solution)/shard_map/ppermute | solution.py:135
  49.0 3.8 %copy-start.1 = (bf16[128,2048]{1,0:T(8,128)(2,1)S(1)}, bf16[128,2048]{1,0:T(8,128)(2,1)}, u32[]{:S(2)}) copy-start(bf16[128,2048]{1,0:T(8,128)(2,1)} %param.7) | copy-start | bytes 1572868
  49.1 4.8 %collective-permute-start.7 = (bf16[128,2048]{1,0:T(8,128)(2,1)S(1)}, bf16[128,2048]{1,0:T(8,128)(2,1)S(1)}, u32[]{:S(2)}, u32[]{:S(2)}) collective-permute-start(bf16[128,2048]{1,0:T(8,128)(2,1)S(1)} %constant_dynamic-update-slice_fusion), channel_id=1, source_target_pairs={{0,32},{32,0},{1,33},{33,1},{2,34},{34,2},{3,35},{35,3},{4,36},{36... | collective-permute-start | bytes 1572872 | tf_op jit(solution)/shard_map/ppermute | solution.py:109
  55.3 38.8 %collective-permute-start.8 = (bf16[2,272,128]{1,0,2:T(2,128)(2,1)S(1)}, bf16[2,272,128]{1,0,2:T(2,128)(2,1)S(1)}, u32[]{:S(2)}, u32[]{:S(2)}) collective-permute-start(bf16[2,272,128]{1,0,2:T(2,128)(2,1)S(1)} %pad_maximum_fusion.4), channel_id=1, source_target_pairs={{0,28},{1,29},{2,30},{3,31},{4,92},{5,93},{6,94},{7,95},{8,156},{9... | collective-permute-start | bytes 417800 | tf_op jit(solution)/shard_map/ppermute | solution.py:148
  58.1 39.1 %collective-permute-start.1 = (bf16[2,272,128]{1,0,2:T(2,128)(2,1)S(1)}, bf16[2,272,128]{1,0,2:T(2,128)(2,1)S(1)}, u32[]{:S(2)}, u32[]{:S(2)}) collective-permute-start(bf16[2,272,128]{1,0,2:T(2,128)(2,1)S(1)} %pad_maximum_fusion.3), channel_id=1, source_target_pairs={{0,8},{1,9},{2,10},{3,11},{4,72},{5,73},{6,74},{7,75},{8,136},{9,1... | collective-permute-start | bytes 417800 | tf_op jit(solution)/shard_map/ppermute | solution.py:148
  94.5 5.0 %collective-permute-start.9 = (bf16[272,128]{1,0:T(8,128)(2,1)S(1)}, bf16[272,128]{1,0:T(8,128)(2,1)S(1)}, u32[]{:S(2)}, u32[]{:S(2)}) collective-permute-start(bf16[272,128]{1,0:T(8,128)(2,1)S(1)} %bitcast.49), channel_id=1, source_target_pairs={{0,32},{32,0},{1,33},{33,1},{2,34},{34,2},{3,35},{35,3},{4,36},{36... | collective-permute-start | bytes 208904 | tf_op jit(solution)/shard_map/ppermute | solution.py:109
  97.6 3.2 %collective-permute-start.2 = (bf16[272,128]{1,0:T(8,128)(2,1)S(1)}, bf16[272,128]{1,0:T(8,128)(2,1)S(1)}, u32[]{:S(2)}, u32[]{:S(2)}) collective-permute-start(bf16[272,128]{1,0:T(8,128)(2,1)S(1)} %bitcast.51), channel_id=1, source_target_pairs={{0,32},{32,0},{1,33},{33,1},{2,34},{34,2},{3,35},{35,3},{4,36},{36... | collective-permute-start | bytes 208904 | tf_op jit(solution)/shard_map/ppermute | solution.py:109
  101.9 21.7 %collective-permute-start.10 = (bf16[1536,512]{1,0:T(8,128)(2,1)}, bf16[1536,512]{1,0:T(8,128)(2,1)}, u32[]{:S(2)}, u32[]{:S(2)}) collective-permute-start(bf16[1536,512]{1,0:T(8,128)(2,1)} %all-gather.2.cloned.1.call-done.near_ref), channel_id=1, source_target_pairs={{0,32},{32,0},{1,33},{33,1},{2,34},{34,2},{3,35},{35,3},{4,36},{36... | collective-permute-start | bytes 4718600 | tf_op jit(solution)/shard_map/ppermute | solution.py:109
  105.1 3.7 %copy-start.2 = (s32[1,4]{1,0:T(1,128)S(1)}, s32[1,4]{1,0:T(1,128)}, u32[]{:S(2)}) copy-start(s32[1,4]{1,0:T(1,128)} %constant.70) | copy-start | bytes 52
  105.2 3.7 %copy-start.3 = (s32[1,4]{1,0:T(1,128)S(1)}, s32[1,4]{1,0:T(1,128)}, u32[]{:S(2)}) copy-start(s32[1,4]{1,0:T(1,128)} %constant.69) | copy-start | bytes 52
  105.2 18.4 %copy-start = (bf16[1536,512]{1,0:T(8,128)(2,1)S(1)}, bf16[1536,512]{1,0:T(8,128)(2,1)}, u32[]{:S(2)}) copy-start(bf16[1536,512]{1,0:T(8,128)(2,1)} %all-gather.2.cloned.1.call-done.near_ref) | copy-start | bytes 4718596
  105.2 18.4 %all-to-all-start.1 = ((bf16[4,16,64,128]{3,2,1,0:T(8,128)(2,1)}), bf16[4,16,64,128]{3,2,1,0:T(8,128)(2,1)S(1)}, u32[]{:S(2)}, u32[]{:S(2)}) async-start(bf16[4,16,64,128]{3,2,1,0:T(8,128)(2,1)} %broadcast_in_dim.22), calls=%async_computation.1 | async-start | bytes 2097152 | tf_op jit(solution)/shard_map/all_to_all | solution.py:113
  128.6 18.0 %all-to-all-start.2 = ((bf16[4,192,512]{2,1,0:T(8,128)(2,1)}), bf16[4,192,512]{2,1,0:T(8,128)(2,1)S(1)}, u32[]{:S(2)}, u32[]{:S(2)}) async-start(bf16[4,192,512]{2,1,0:T(8,128)(2,1)} %bitcast.17), calls=%async_computation.2 | async-start | bytes 1572864 | tf_op jit(solution)/shard_map/all_to_all | solution.py:169
  146.5 13.8 %all-to-all-start.3 = ((bf16[4,192,512]{2,1,0:T(8,128)(2,1)}), bf16[4,192,512]{2,1,0:T(8,128)(2,1)S(1)}, u32[]{:S(2)}, u32[]{:S(2)}) async-start(bf16[4,192,512]{2,1,0:T(8,128)(2,1)} %bitcast.19), calls=%async_computation.3 | async-start | bytes 1572864 | tf_op jit(solution)/shard_map/all_to_all | solution.py:169
  152.8 18.4 %collective-permute-start.11 = (bf16[192,512]{1,0:T(8,128)(2,1)S(1)}, bf16[192,512]{1,0:T(8,128)(2,1)S(1)}, u32[]{:S(2)}, u32[]{:S(2)}) collective-permute-start(bf16[192,512]{1,0:T(8,128)(2,1)S(1)} %reduce_sum.24), channel_id=1, source_target_pairs={{0,448},{1,449},{2,450},{3,451},{4,384},{5,385},{6,386},{7,387},{8... | collective-permute-start | bytes 589832 | tf_op jit(solution)/shard_map/ppermute | solution.py:171
  160.5 31.4 %collective-permute-start.12 = (bf16[192,512]{1,0:T(8,128)(2,1)S(1)}, bf16[192,512]{1,0:T(8,128)(2,1)S(1)}, u32[]{:S(2)}, u32[]{:S(2)}) collective-permute-start(bf16[192,512]{1,0:T(8,128)(2,1)S(1)} %reduce_sum.25), channel_id=1, source_target_pairs={{0,476},{1,477},{2,478},{3,479},{4,412},{5,413},{6,414},{7,415},{8... | collective-permute-start | bytes 589832 | tf_op jit(solution)/shard_map/ppermute | solution.py:171
Sparse Core Ops, SparseCore 0:
  23.0 60.9 all-gather.1
